TPU v7x, 32 devices: a whole 2x2x4 slice. The times are simulated.
32 devices in a mesh: section: 2 (over core), dp: 16 (over z, y, x).
Axes of the slice: x: 2, y: 2, z: 4, core: 2. Of those that a mesh axis runs over, the one named last changes fastest.
Arguments:
- inputs: bfloat16 [2, 16, 512, 768], P(None, 'dp'), may hold values from -8 to 8
- cotangent: bfloat16 [2, 16, 512, 768], P(None, 'dp'), may hold values from -6 to 6
- lengths: int32 [2, 16, 2], P(None, 'dp'), may hold values from 0 to 512, as said below
- weight_in: bfloat16 [2, 5376, 768], P('section', 'dp'), may hold values from -0.21875 to 0.21875
- weight_out: bfloat16 [2, 3840, 768], P('section', 'dp'), may hold values from -1.6329932 to 1.6329932
- scales: bfloat16 [2, 896], P('section', 'dp'), may hold values from 0.099609375 to 1.8984375
Outputs:
- layer_outputs: bfloat16 [2, 2, 16, 512, 768], P('section', None, 'dp')
- input_grads: bfloat16 [2, 2, 16, 512, 768], P('section', None, 'dp')
- weight_in_grad: float32 [2, 5376, 768], P('section', 'dp')
- weight_out_grad: float32 [2, 3840, 768], P('section', 'dp')
- scales_grad: float32 [2, 896], P('section', 'dp')
- statistics: float32 [2, 3], P('section')
Inputs may be any that keep to these rules, and one draw needn't show every extreme that they name: lengths[m, s] = (a, b): the first image takes slots [0, a), the second [a, a + b), a >= 1 and a + b <= 512; every micro-batch has a buffer holding one image of 512 tokens and an empty second.
All inputs are finite; a program needn't handle non-finite values.
Results may differ from a plain program's by a relative error of at most 0.017.
Values may be sent and summed in bfloat16 or wider, within the bound.
No kernel may reach another device: no remote copies, remote signals or barrier semaphores. Data moves between devices by JAX's collectives and lax.ppermute only.
A program may use at most 256 MiB of HBM per device.

v0:
```python
import jax
import jax.numpy as jnp
from jax import lax
from jax.sharding import PartitionSpec as P

HEADS = 12
HEAD = 64


EPSILON = 1e-06
MASKED = -1e30


def shifted(value, axis, by):
    size = lax.axis_size(axis)
    pairs = [(i, i + by) for i in range(size) if 0 <= i + by < size]
    return lax.ppermute(value, axis, pairs)


def normalize(values, scale_vector):
    average = jnp.mean(values, axis=-1, keepdims=True)
    centred = values - average
    inverse = lax.rsqrt(jnp.mean(centred * centred, axis=-1, keepdims=True) + EPSILON)
    return centred * inverse * scale_vector


def exact_gelu(values):
    return jax.nn.gelu(values, approximate=False)


def segments_of(length_pairs, length):
    position = lax.broadcasted_iota(jnp.int32, (length_pairs.shape[0], length), 1)
    first_end = length_pairs[:, 0:1]
    second_end = first_end + length_pairs[:, 1:2]
    return (position >= first_end).astype(jnp.int32) + (position >= second_end).astype(jnp.int32)


def rows_product(left, right, contract):
    return lax.dot_general(left, right, (contract, ((), ())), preferred_element_type=jnp.float32)


def output_term(joined_rows, grad_rows, weight_now):
    contract = tuple(range(joined_rows.ndim - 1))
    return weight_now * rows_product(joined_rows, grad_rows, (contract, contract))


def recompute(layer_in, segment, weights, head_count, head_size, kept_total):
    weight_in_full, weight_out_full, scale_full = weights
    seq_count, length, model_width = layer_in.shape
    row_count = seq_count * length
    row_values = layer_in.reshape(row_count, model_width).astype(jnp.float32)
    scale_values = scale_full.astype(jnp.float32)
    gain_vector = scale_values[:model_width]
    query_scale = scale_values[model_width : model_width + head_size]
    key_scale = scale_values[model_width + head_size :]
    normed = normalize(row_values, gain_vector).astype(jnp.bfloat16)
    projected = rows_product(normed, weight_in_full, ((1,), (1,)))
    split_shape = (seq_count, length, head_count, head_size)
    query_raw = projected[:, :model_width].reshape(split_shape)
    key_raw = projected[:, model_width : 2 * model_width].reshape(split_shape)
    value_low = (
        projected[:, 2 * model_width : 3 * model_width].reshape(split_shape).astype(jnp.bfloat16)
    )
    feed_input = projected[:, 3 * model_width :]
    query_low = normalize(query_raw, query_scale).astype(jnp.bfloat16)
    key_low = normalize(key_raw, key_scale).astype(jnp.bfloat16)
    hidden = exact_gelu(feed_input)
    scores = jnp.einsum(
        "sqhd,skhd->shqk", query_low, key_low, preferred_element_type=jnp.float32
    ) * head_size ** (-0.5)
    allowed = (segment[:, :, None] == segment[:, None, :])[:, None, :, :]
    scores = jnp.where(allowed, scores, MASKED)
    if kept_total is None:
        row_peak = jnp.max(scores, axis=-1, keepdims=True)
        exponent = jnp.exp(scores - row_peak)
        totals = jnp.sum(exponent, axis=-1, keepdims=True)
        probabilities = exponent / totals
        log_total = row_peak + jnp.log(totals)
    else:
        log_total = kept_total
        probabilities = jnp.exp(scores - log_total)
    probability_low = probabilities.astype(jnp.bfloat16)
    attended = jnp.einsum(
        "shqk,skhd->sqhd", probability_low, value_low, preferred_element_type=jnp.float32
    )
    joined = jnp.concatenate([attended.reshape(row_count, model_width), hidden], axis=1).astype(
        jnp.bfloat16
    )
    return {
        "row_values": row_values,
        "gain_vector": gain_vector,
        "query_scale": query_scale,
        "key_scale": key_scale,
        "normed": normed,
        "query_raw": query_raw,
        "key_raw": key_raw,
        "query_low": query_low,
        "key_low": key_low,
        "value_low": value_low,
        "feed_input": feed_input,
        "probabilities": probabilities,
        "probability_low": probability_low,
        "log_total": log_total,
        "joined": joined,
    }


def layer_forward(layer_in, segment, weights, head_count, head_size):
    stored = recompute(layer_in, segment, weights, head_count, head_size, None)
    weight_out_full = weights[1]
    model_width = layer_in.shape[2]
    joined = stored["joined"]
    attend_branch = jnp.dot(
        joined[:, :model_width], weight_out_full[:model_width], preferred_element_type=jnp.float32
    )
    feed_branch = jnp.dot(
        joined[:, model_width:], weight_out_full[model_width:], preferred_element_type=jnp.float32
    )
    result = stored["row_values"] + attend_branch + feed_branch
    return (result, attend_branch, feed_branch, stored["log_total"])


def layer_backward(layer_in, segment, weights, head_count, head_size, kept_total, grad_out):
    stored = recompute(layer_in, segment, weights, head_count, head_size, kept_total)
    weight_in_full, weight_out_full, scale_full = weights
    seq_count, length, model_width = layer_in.shape
    row_count = seq_count * length
    split_shape = (seq_count, length, head_count, head_size)
    grad_joined = rows_product(grad_out, weight_out_full, ((1,), (1,))).astype(jnp.bfloat16)
    grad_attended = grad_joined[:, :model_width].reshape(split_shape)
    grad_hidden = grad_joined[:, model_width:].astype(jnp.float32)
    gelu_back = jax.vjp(exact_gelu, stored["feed_input"])[1]
    grad_feed = gelu_back(grad_hidden)[0]
    probabilities = stored["probabilities"]
    grad_weights = jnp.einsum(
        "sqhd,skhd->shqk", grad_attended, stored["value_low"], preferred_element_type=jnp.float32
    )
    grad_value = jnp.einsum(
        "shqk,sqhd->skhd",
        stored["probability_low"],
        grad_attended,
        preferred_element_type=jnp.float32,
    )
    row_delta = jnp.sum(probabilities * grad_weights, axis=-1, keepdims=True)
    grad_scores = (probabilities * (grad_weights - row_delta)).astype(jnp.bfloat16)
    factor = head_size ** (-0.5)
    grad_query = (
        jnp.einsum(
            "shqk,skhd->sqhd", grad_scores, stored["key_low"], preferred_element_type=jnp.float32
        )
        * factor
    )
    grad_key = (
        jnp.einsum(
            "shqk,sqhd->skhd", grad_scores, stored["query_low"], preferred_element_type=jnp.float32
        )
        * factor
    )
    query_back = jax.vjp(normalize, stored["query_raw"], stored["query_scale"])[1]
    grad_query_raw, grad_query_scale = query_back(grad_query)
    key_back = jax.vjp(normalize, stored["key_raw"], stored["key_scale"])[1]
    grad_key_raw, grad_key_scale = key_back(grad_key)
    grad_projected = jnp.concatenate(
        [
            grad_query_raw.reshape(row_count, model_width),
            grad_key_raw.reshape(row_count, model_width),
            grad_value.reshape(row_count, model_width),
            grad_feed,
        ],
        axis=1,
    ).astype(jnp.bfloat16)
    grad_normed = jnp.dot(grad_projected, weight_in_full, preferred_element_type=jnp.float32)
    front_back = jax.vjp(normalize, stored["row_values"], stored["gain_vector"])[1]
    grad_rows, grad_gain = front_back(grad_normed)
    grad_input = grad_out.astype(jnp.float32) + grad_rows
    grad_scales = jnp.concatenate([grad_gain, grad_query_scale, grad_key_scale])
    return (grad_input, grad_scales, stored["normed"], grad_projected, stored["joined"])


def body(inputs, cotangent, lengths, weight_in, weight_out, scales):
    micro_count, seq_count, length, model_width = inputs.shape
    head_count = HEADS
    head_size = HEAD
    row_count = seq_count * length
    section_index = lax.axis_index("section")
    weights = (
        lax.all_gather(weight_in[0], "dp", axis=0, tiled=True),
        lax.all_gather(weight_out[0], "dp", axis=0, tiled=True),
        lax.all_gather(scales[0], "dp", axis=0, tiled=True),
    )
    arriving = jnp.zeros((seq_count, length, model_width), jnp.bfloat16)
    kept_inputs = jnp.zeros((micro_count, seq_count, length, model_width), jnp.bfloat16)
    kept_outputs = jnp.zeros_like(kept_inputs)
    kept_totals = jnp.zeros((micro_count, seq_count, head_count, length, 1), jnp.float32)
    square_sums = jnp.zeros((3,), jnp.float32)
    for tick_index in range(micro_count + 1):
        current = tick_index - section_index
        active = jnp.logical_and(current >= 0, current < micro_count)
        active_weight = active.astype(jnp.float32)
        safe_index = jnp.clip(current, 0, micro_count - 1)
        layer_in = jnp.where(section_index == 0, inputs[min(tick_index, micro_count - 1)], arriving)
        segment = segments_of(lengths[safe_index], length)
        result, attend_branch, feed_branch, log_total = layer_forward(
            layer_in, segment, weights, head_count, head_size
        )
        result_low = result.astype(jnp.bfloat16).reshape(seq_count, length, model_width)
        if tick_index < micro_count:
            arriving = shifted(result_low, "section", 1)
        kept_inputs = jnp.where(active, kept_inputs.at[safe_index].set(layer_in), kept_inputs)
        kept_outputs = jnp.where(active, kept_outputs.at[safe_index].set(result_low), kept_outputs)
        kept_totals = jnp.where(active, kept_totals.at[safe_index].set(log_total), kept_totals)
        valid_rows = (segment < 2).reshape(row_count, 1).astype(jnp.float32)
        square_sums = square_sums + active_weight * jnp.stack(
            [
                jnp.sum(result * result * valid_rows),
                jnp.sum(attend_branch * attend_branch * valid_rows),
                jnp.sum(feed_branch * feed_branch * valid_rows),
            ]
        )
    token_count = jnp.sum(lengths).astype(jnp.float32) * model_width
    total_sums, total_count = lax.psum((square_sums, token_count), "dp")
    statistics = jnp.sqrt(total_sums / total_count)
    weights_back = (
        lax.all_gather(weight_in[0], "dp", axis=0, tiled=True),
        lax.all_gather(weight_out[0], "dp", axis=0, tiled=True),
        lax.all_gather(scales[0], "dp", axis=0, tiled=True),
    )
    arriving_grad = jnp.zeros((seq_count, length, model_width), jnp.bfloat16)
    kept_grads = jnp.zeros((micro_count, seq_count, length, model_width), jnp.bfloat16)
    stash_projected = jnp.zeros((micro_count, row_count, weights_back[0].shape[0]), jnp.bfloat16)
    stash_normed = jnp.zeros((micro_count, row_count, model_width), jnp.bfloat16)
    stash_joined = jnp.zeros((micro_count, row_count, weights_back[1].shape[0]), jnp.bfloat16)
    stash_grads = jnp.zeros((micro_count, row_count, model_width), jnp.bfloat16)
    scale_total = jnp.zeros((weights_back[2].shape[0],), jnp.float32)
    for tick_index in range(micro_count + 1):
        current = tick_index - 1 + section_index
        active = jnp.logical_and(current >= 0, current < micro_count)
        active_weight = active.astype(jnp.float32)
        safe_index = jnp.clip(current, 0, micro_count - 1)
        segment = segments_of(lengths[safe_index], length)
        valid_rows = (segment < 2).reshape(row_count, 1).astype(jnp.float32)
        own_grad = (
            cotangent[safe_index].reshape(row_count, model_width).astype(jnp.float32) * valid_rows
        ).astype(jnp.bfloat16)
        grad_out = jnp.where(
            section_index == 1, own_grad, arriving_grad.reshape(row_count, model_width)
        )
        grad_input, grad_scales, normed, grad_projected, joined = layer_backward(
            kept_inputs[safe_index],
            segment,
            weights_back,
            head_count,
            head_size,
            kept_totals[safe_index],
            grad_out,
        )
        grad_low = grad_input.astype(jnp.bfloat16).reshape(seq_count, length, model_width)
        if tick_index < micro_count:
            arriving_grad = shifted(grad_low, "section", -1)
        kept_grads = jnp.where(active, kept_grads.at[safe_index].set(grad_low), kept_grads)
        stash_projected = jnp.where(
            active, stash_projected.at[safe_index].set(grad_projected), stash_projected
        )
        stash_normed = jnp.where(active, stash_normed.at[safe_index].set(normed), stash_normed)
        stash_joined = jnp.where(active, stash_joined.at[safe_index].set(joined), stash_joined)
        stash_grads = jnp.where(active, stash_grads.at[safe_index].set(grad_out), stash_grads)
        scale_total = scale_total + active_weight * grad_scales
    summed_in = rows_product(stash_projected, stash_normed, ((0, 1), (0, 1)))
    weight_in_grad, scale_grad = (
        lax.psum_scatter(summed_in, "dp", scatter_dimension=0, tiled=True),
        lax.psum_scatter(scale_total, "dp", scatter_dimension=0, tiled=True),
    )
    weight_out_grad = lax.psum_scatter(
        output_term(stash_joined, stash_grads, 1.0), "dp", scatter_dimension=0, tiled=True
    )
    return (
        kept_outputs[None],
        kept_grads[None],
        weight_in_grad[None],
        weight_out_grad[None],
        scale_grad[None],
        statistics[None],
    )


def solution(mesh):
    return jax.shard_map(
        body,
        mesh=mesh,
        in_specs=(
            P(None, "dp", None, None),
            P(None, "dp", None, None),
            P(None, "dp", None),
            P("section", "dp", None),
            P("section", "dp", None),
            P("section", "dp"),
        ),
        out_specs=(
            P("section", None, "dp", None, None),
            P("section", None, "dp", None, None),
            P("section", "dp", None),
            P("section", "dp", None),
            P("section", "dp"),
            P("section", None),
        ),
        check_vma=False,
    )
```

profile of v0, /device:TPU:0, one launch (start us, length us, event | category | flops | bytes accessed | tf_op | source)
XLA Modules:
  0.0 1113.6 jit_solution(1215800434849585302)
XLA Ops:
  11.8 44.2 %all-reduce = bf16[896]{0:T(1024)(128)(2,1)S(1)} all-reduce(bf16[896]{0:T(1024)(128)(2,1)S(1)} %dynamic-update-slice.98), channel_id=2, replica_groups=mesh['section'=2,'dp'=16] {'dp'}, use_global_device_ids=true, to_apply=%add | all-reduce | flops 896 | bytes 3584
  88.5 37.0 %all-gather.6.cloned.1.call-done = bf16[1,5376,768]{2,1,0:T(8,128)(2,1)} async-done(((bf16[1,336,768]{2,1,0:T(8,128)(2,1)}), bf16[1,5376,768]{2,1,0:T(8,128)(2,1)}) %all-gather.6.cloned.1.call-update) | async-done | bytes 8257552 | tf_op jit(solution)/shard_map/all_gather | solution.py:187
  125.5 7.2 fusion.22
  132.8 4.2 copy-done.64
  149.7 4.8 fusion.322
  154.5 62.5 %all-gather.8.cloned.1.call-done = bf16[1,3840,768]{2,1,0:T(8,128)(2,1)} async-done(((bf16[1,240,768]{2,1,0:T(8,128)(2,1)}), bf16[1,3840,768]{2,1,0:T(8,128)(2,1)}) %all-gather.8.cloned.1.call-update) | async-done | bytes 5898256 | tf_op jit(solution)/shard_map/all_gather | solution.py:188
  217.0 18.0 %fusion.133 = f32[512,768]{1,0:T(8,128)S(1)} fusion(bf16[1,3840,768]{2,1,0:T(8,128)(2,1)} %all-gather.8.cloned.1.call-done, f32[512,5376]{1,0:T(8,128)} %copy-done.64), kind=kOutput, calls=%fused_computation.229 | convolution fusion | flops 2518155264 | bytes 12582912 | tf_op jit(solution)/shard_map/dot_general | solution.py:116
  235.0 4.2 multiply_reduce_fusion.11
  246.1 7.2 fusion.20
  253.4 4.1 copy-done.65
  269.3 3.7 fusion.1
  273.0 3.6 fusion.4
  276.7 3.6 fusion.321
  280.3 18.1 %fusion.132 = f32[512,768]{1,0:T(8,128)S(1)} fusion(bf16[1,3840,768]{2,1,0:T(8,128)(2,1)} %all-gather.8.cloned.1.call-done, f32[512,5376]{1,0:T(8,128)} %copy-done.65), kind=kOutput, calls=%fused_computation.228 | convolution fusion | flops 2518155264 | bytes 12582912 | tf_op jit(solution)/shard_map/dot_general | solution.py:116
  298.5 4.0 multiply_reduce_fusion.8
  305.1 6.5 convolution_convert_fusion.2
  322.1 7.0 fusion.16
  332.6 14.5 %fusion.134 = (bf16[1,512,3072]{2,1,0:T(8,128)(2,1)}, f32[512,3072]{1,0:T(8,128)}) fusion(f32[512,5376]{1,0:T(8,128)S(1)} %fusion.16), kind=kLoop, calls=%fused_computation.230 | loop fusion | flops 102236160 | bytes 15728640 | tf_op jit(solution)/shard_map/concatenate | solution.py:86
  347.7 7.5 fusion.18
  380.3 5.0 convolution_convert_fusion.8
  385.3 4.0 convolution_convert_fusion.5
  389.3 7.4 multiply_reduce_fusion.2
  397.2 6.4 fusion.32
  405.9 10.0 multiply_convert_fusion.2
  428.0 10.4 fusion.271
  438.5 7.0 fusion.12
  448.9 14.9 %fusion.135 = (bf16[1,512,3072]{2,1,0:T(8,128)(2,1)}, f32[512,3072]{1,0:T(8,128)}) fusion(f32[512,5376]{1,0:T(8,128)S(1)} %fusion.12), kind=kLoop, calls=%fused_computation.231 | loop fusion | flops 102236160 | bytes 15728640 | tf_op jit(solution)/shard_map/concatenate | solution.py:86
  482.3 4.6 convolution_convert_fusion.4
  487.1 3.9 broadcast_in_dim.141
  497.5 5.8 fusion.127
  503.4 6.3 convolution_convert_fusion.1
  514.8 8.9 convolution_convert_fusion.7
  523.7 9.6 multiply_reduce_fusion.1
  533.3 7.2 multiply_convert_fusion.1
  540.5 3.3 fusion.316
  547.7 5.8 fusion.39
  567.3 9.6 fusion.286
  576.9 7.2 fusion.8
  586.3 14.5 %fusion.136 = (bf16[1,512,3072]{2,1,0:T(8,128)(2,1)}, f32[512,3072]{1,0:T(8,128)}) fusion(f32[512,5376]{1,0:T(8,128)S(1)} %fusion.8), kind=kLoop, calls=%fused_computation.232 | loop fusion | flops 102236160 | bytes 15728640 | tf_op jit(solution)/shard_map/concatenate | solution.py:86
  601.6 3.8 fusion.331
  616.1 5.0 convolution_convert_fusion.3
  623.3 3.6 fusion.336
  626.9 6.0 fusion.128
  635.5 12.0 %convolution_bitcast_fusion.1 = f32[3840,768]{1,0:T(8,128)} fusion(bf16[2,512,3840]{2,1,0:T(8,128)(2,1)} %fusion.128, bf16[2,512,768]{2,1,0:T(8,128)(2,1)S(1)} %fusion.337), kind=kOutput, calls=%fused_computation.57 | convolution fusion | flops 6039797760 | bytes 21233664 | tf_op jit(solution)/shard_map/dot_general | solution.py:39
  658.7 3.4 fusion.334
  662.1 5.6 broadcast_in_dim.138
  667.7 4.2 fusion.126
  678.9 3.4 fusion.335
  682.3 8.9 fusion.102
  691.2 6.4 convolution_convert_fusion
  702.6 9.3 convolution_convert_fusion.6
  714.2 9.6 multiply_reduce_fusion
  723.8 7.3 multiply_convert_fusion
  737.6 4.9 fusion.314
  744.3 7.2 fusion.46
  753.1 7.6 fusion.103
  760.7 15.8 %convolution_bitcast_fusion = f32[5376,768]{1,0:T(8,128)} fusion(bf16[2,512,5376]{2,1,0:T(8,128)(2,1)} %fusion.103, bf16[2,512,768]{2,1,0:T(8,128)(2,1)} %fusion.335), kind=kOutput, calls=%fused_computation.18 | convolution fusion | flops 8455716864 | bytes 29097984 | tf_op jit(solution)/shard_map/dot_general | solution.py:39
  786.7 6.9 fusion.320
  795.7 19.2 %fusion.328 = (bf16[1,2,1,512,768]{4,3,1,2,0:T(8,128)(2,1)S(1)}, f32[512,768]{1,0:T(8,128)S(1)}) fusion(bf16[1,2,1,512,768]{4,3,1,2,0:T(8,128)(2,1)S(1)} %copy-done.61, s32[]{:T(128)} %min.35, bf16[2,1,512,768]{3,2,1,0:T(8,128)(2,1)S(1)} %fusion.326, pred[]{:T(512)} %get-tuple-element.349, pred[]{:T(512)S(6)} %and.131, f32[512,768]{1,0:T(8,128)S(1)} %fusion.323, ...), kind=kOutput, calls=%fused_computation.546 | convolution fusion | flops 2520514560 | bytes 16516097 | tf_op jit(solution)/shard_map/dot_general | solution.py:116
  816.7 5.6 fusion.430
  829.9 9.2 fusion.303
  841.2 43.1 %all-reduce.2 = (f32[896]{0:T(1024)S(1)}, f32[3]{0:T(128)S(1)}, f32[]{:T(128)}) all-reduce(f32[896]{0:T(1024)S(1)} %fusion.419, f32[3]{0:T(128)S(1)} %fusion.430, f32[]{:T(128)S(6)} %mul.1698), channel_id=7, replica_groups=mesh['section'=2,'dp'=16] {'dp'}, use_global_device_ids=true, to_apply=%region_86.87.clone | all-reduce | flops 900 | bytes 7200
  886.1 4.3 fusion.333
  890.4 216.5 %reduce-scatter.3.cloned.1.call-done = f32[336,768]{1,0:T(8,128)} async-done(((f32[5376,768]{1,0:T(8,128)}), f32[336,768]{1,0:T(8,128)}) %reduce-scatter.3.cloned.1.call-update) | async-done | bytes 1032208 | tf_op jit(solution)/shard_map/reduce_scatter | solution.py:270
  (533 shorter events, 245.3 us)
Async XLA Ops:
  7.2 118.3 %all-gather.6.cloned.1.call-start = ((), (), s32[]{:S(2)}) async-start(), calls=%async_computation.4 | async-start | bytes 8773632 | tf_op jit(solution)/shard_map/all_gather | solution.py:187
  7.9 209.1 %all-gather.8.cloned.1.call-start = ((), (), s32[]{:S(2)}) async-start(), calls=%async_computation.5 | async-start | bytes 6266880 | tf_op jit(solution)/shard_map/all_gather | solution.py:188
  8.6 881.7 %reduce-scatter.5.cloned.1.call-start = ((), (), s32[]{:S(2)}) async-start(), calls=%async_computation.3 | async-start | bytes 12533760 | tf_op jit(solution)/shard_map/reduce_scatter | solution.py:273
  70.3 234.7 %copy-start.116 = (f32[512]{0:T(512)}, f32[512]{0:T(512)S(1)}, u32[]{:S(2)}) copy-start(f32[512]{0:T(512)S(1)} %compare_convert_fusion.5) | copy-start | bytes 6148
  84.0 294.3 %copy-start.95 = (f32[64]{0:T(128)}, f32[64]{0:T(128)S(1)}, u32[]{:S(2)}) copy-start(f32[64]{0:T(128)S(1)} %get-tuple-element.396) | copy-start | bytes 772
  154.5 80.5 %copy-start.26 = (bf16[2,1,512,768]{3,2,1,0:T(8,128)(2,1)S(1)}, bf16[2,1,512,768]{3,2,1,0:T(8,128)(2,1)}, u32[]{:S(2)}) copy-start(bf16[2,1,512,768]{3,2,1,0:T(8,128)(2,1)} %param.54) | copy-start | bytes 4718596
  217.0 18.0 %copy-start.133 = (bf16[12,64,512]{2,1,0:T(8,128)(2,1)S(1)}, bf16[12,64,512]{2,1,0:T(8,128)(2,1)}, u32[]{:S(2)}) copy-start(bf16[12,64,512]{2,1,0:T(8,128)(2,1)} %fusion.322) | copy-start | bytes 2359300
  239.2 5.2 collective-permute-start
  242.3 124.6 %copy-start.58 = (pred[512,512]{0,1:T(8,128)(4,1)}, pred[512,512]{0,1:T(8,128)(4,1)S(1)}, u32[]{:S(2)}) copy-start(pred[512,512]{0,1:T(8,128)(4,1)S(1)} %broadcast_compare_fusion.3) | copy-start | bytes 786436
  245.6 7.8 copy-start.31
  280.3 18.1 %copy-start.32 = (bf16[1,512,768]{2,1,0:T(8,128)(2,1)S(1)}, bf16[1,512,768]{2,1,0:T(8,128)(2,1)}, u32[]{:S(2)}) copy-start(bf16[1,512,768]{2,1,0:T(8,128)(2,1)} %copy-done.31) | copy-start | bytes 2359300
  280.3 18.1 %copy-start.132 = (f32[512]{0:T(512)S(1)}, f32[512]{0:T(512)}, u32[]{:S(2)}) copy-start(f32[512]{0:T(512)} %compare_convert_fusion.1) | copy-start | bytes 6148
  302.5 14.2 %copy-start.69 = (f32[12,512]{1,0:T(8,128)S(1)}, f32[12,512]{1,0:T(8,128)}, u32[]{:S(2)}) copy-start(f32[12,512]{1,0:T(8,128)} %copy-done.68) | copy-start | bytes 73732
  302.5 17.0 %copy-start.27 = (bf16[2,1,512,768]{3,2,1,0:T(8,128)(2,1)S(1)}, bf16[2,1,512,768]{3,2,1,0:T(8,128)(2,1)}, u32[]{:S(2)}) copy-start(bf16[2,1,512,768]{3,2,1,0:T(8,128)(2,1)} %param.54) | copy-start | bytes 4718596
  302.5 17.0 %collective-permute-start.1 = (bf16[1,512,768]{2,1,0:T(8,128)(2,1)}, bf16[1,512,768]{2,1,0:T(8,128)(2,1)}, u32[]{:S(2)}, u32[]{:S(2)}) collective-permute-start(bf16[1,512,768]{2,1,0:T(8,128)(2,1)} %bitcast.708), channel_id=1, source_target_pairs={{0,16},{1,17},{2,18},{3,19},{4,20},{5,21},{6,22},{7,23},{8,24},{9,... | collective-permute-start | bytes 2359304 | tf_op jit(solution)/shard_map/ppermute | solution.py:17
  320.6 8.6 copy-start.3
  320.6 27.1 %copy-start.23 = (bf16[1,512,768]{2,1,0:T(8,128)(2,1)}, bf16[1,512,768]{2,1,0:T(8,128)(2,1)S(1)}, u32[]{:S(2)}) copy-start(bf16[1,512,768]{2,1,0:T(8,128)(2,1)S(1)} %get-tuple-element.375) | copy-start | bytes 2359300
  321.8 7.4 copy-start.99
  329.2 17.9 %copy-start.11 = (f32[512,5376]{1,0:T(8,128)}, f32[512,5376]{1,0:T(8,128)S(1)}, u32[]{:S(2)}) copy-start(f32[512,5376]{1,0:T(8,128)S(1)} %fusion.16) | copy-start | bytes 33030148
  366.8 7.5 copy-start.33
  380.3 9.0 copy-start.2
  385.3 11.9 %slice-start.5 = ((s8[6291456]{0:T(1024)(128)(4,1)}), s8[4194304]{0:T(1024)(128)(4,1)S(1)}, s32[]{:S(2)}) async-start(s8[6291456]{0:T(1024)(128)(4,1)} %bitcast.802), calls=%async_computation.11 | async-start | bytes 8388608
  389.3 8.0 slice-start.6
  405.9 10.0 copy-start.93
  445.5 18.4 %copy-start.10 = (f32[512,5376]{1,0:T(8,128)}, f32[512,5376]{1,0:T(8,128)S(1)}, u32[]{:S(2)}) copy-start(f32[512,5376]{1,0:T(8,128)S(1)} %fusion.12) | copy-start | bytes 33030148
  448.9 17.4 %copy-start.119 = (f32[512]{0:T(512)S(1)}, f32[512]{0:T(512)}, u32[]{:S(2)}) copy-start(f32[512]{0:T(512)} %copy-done.118) | copy-start | bytes 6148
  472.0 31.4 %collective-permute-start.2 = (bf16[1,512,768]{2,1,0:T(8,128)(2,1)}, bf16[1,512,768]{2,1,0:T(8,128)(2,1)}, u32[]{:S(2)}, u32[]{:S(2)}) collective-permute-start(bf16[1,512,768]{2,1,0:T(8,128)(2,1)} %bitcast.90), channel_id=1, source_target_pairs={{16,0},{17,1},{18,2},{19,3},{20,4},{21,5},{22,6},{23,7},{24,8},{25... | collective-permute-start | bytes 2359304 | tf_op jit(solution)/shard_map/ppermute | solution.py:17
  514.8 8.9 copy-start.46
  514.8 8.9 copy-start.49
  514.8 8.9 copy-start.87
  514.8 18.5 %slice-start = ((s8[12582912]{0:T(1024)(128)(4,1)}), s8[4194304]{0:T(1024)(128)(4,1)S(1)}, s32[]{:S(2)}) async-start(s8[12582912]{0:T(1024)(128)(4,1)} %bitcast.738), calls=%async_computation.6 | async-start | bytes 8388608
  514.8 18.5 %slice-start.1 = ((s8[12582912]{0:T(1024)(128)(4,1)}), s8[4194304]{0:T(1024)(128)(4,1)S(1)}, s32[]{:S(2)}) async-start(s8[12582912]{0:T(1024)(128)(4,1)} %bitcast.738), calls=%async_computation.7 | async-start | bytes 8388608
  523.7 9.6 slice-start.2
  547.7 8.2 copy-start.77
  547.7 8.2 copy-start.79
  584.2 16.7 %copy-start.9 = (f32[512,5376]{1,0:T(8,128)}, f32[512,5376]{1,0:T(8,128)S(1)}, u32[]{:S(2)}) copy-start(f32[512,5376]{1,0:T(8,128)S(1)} %fusion.8) | copy-start | bytes 33030148
  586.3 14.5 %copy-start.124 = (f32[512]{0:T(512)S(1)}, f32[512]{0:T(512)}, u32[]{:S(2)}) copy-start(f32[512]{0:T(512)} %copy-done.123) | copy-start | bytes 6148
  586.3 15.3 %copy-start.17 = (bf16[2,1,512,768]{3,2,1,0:T(8,128)(2,1)S(1)}, bf16[2,1,512,768]{3,2,1,0:T(8,128)(2,1)}, u32[]{:S(2)}) copy-start(bf16[2,1,512,768]{3,2,1,0:T(8,128)(2,1)} %param.55) | copy-start | bytes 4718596
  586.3 15.3 %copy-start.115 = (f32[512]{0:T(512)S(1)}, f32[512]{0:T(512)}, u32[]{:S(2)}) copy-start(f32[512]{0:T(512)} %compare_convert_fusion.4) | copy-start | bytes 6148
  605.5 27.5 %collective-permute-start.3 = (bf16[1,512,768]{2,1,0:T(8,128)(2,1)}, bf16[1,512,768]{2,1,0:T(8,128)(2,1)}, u32[]{:S(2)}, u32[]{:S(2)}) collective-permute-start(bf16[1,512,768]{2,1,0:T(8,128)(2,1)} %bitcast.116), channel_id=1, source_target_pairs={{16,0},{17,1},{18,2},{19,3},{20,4},{21,5},{22,6},{23,7},{24,8},{25... | collective-permute-start | bytes 2359304 | tf_op jit(solution)/shard_map/ppermute | solution.py:17
  647.5 459.4 %reduce-scatter.3.cloned.1.call-start = ((), (), s32[]{:S(2)}) async-start(), calls=%async_computation.2 | async-start | bytes 17547264 | tf_op jit(solution)/shard_map/reduce_scatter | solution.py:270
  682.3 8.9 copy-start.19
  682.3 8.9 copy-start.112
  714.2 9.6 copy-start.85
  744.0 7.5 copy-start.29
  744.2 8.9 copy-start.44
  744.3 8.8 copy-start.47
  786.7 9.0 copy-start.24
  786.7 9.0 copy-start.61
  815.0 12.4 %copy-start.28 = (bf16[1,512,12,64]{1,3,2,0:T(8,128)(2,1)S(1)}, bf16[1,512,12,64]{1,3,2,0:T(8,128)(2,1)}, u32[]{:S(2)}) copy-start(bf16[1,512,12,64]{1,3,2,0:T(8,128)(2,1)} %add_convert_fusion.2) | copy-start | bytes 2359300
  815.0 13.6 %copy-start.30 = (bf16[1,512,12,64]{1,3,2,0:T(8,128)(2,1)S(1)}, bf16[1,512,12,64]{1,3,2,0:T(8,128)(2,1)}, u32[]{:S(2)}) copy-start(bf16[1,512,12,64]{1,3,2,0:T(8,128)(2,1)} %copy-done.29) | copy-start | bytes 2359300
  815.0 14.8 %copy-start.6 = (bf16[2,1,512,768]{3,2,1,0:T(8,128)(2,1)S(1)}, bf16[2,1,512,768]{3,2,1,0:T(8,128)(2,1)}, u32[]{:S(2)}) copy-start(bf16[2,1,512,768]{3,2,1,0:T(8,128)(2,1)} %copy-done.3) | copy-start | bytes 4718596
  815.0 14.8 %copy-start.102 = (f32[512]{0:T(512)S(1)}, f32[512]{0:T(512)}, u32[]{:S(2)}) copy-start(f32[512]{0:T(512)} %broadcast_multiply_fusion.12) | copy-start | bytes 6148
  829.8 9.3 copy-start.122
  829.8 10.5 copy-start.104
  829.8 11.3 %copy-start.125 = (f32[768]{0:T(1024)S(1)}, f32[768]{0:T(1024)}, u32[]{:S(2)}) copy-start(f32[768]{0:T(1024)} %get-tuple-element.328) | copy-start | bytes 9220
  829.8 11.3 %copy-start.126 = (f32[768]{0:T(1024)S(1)}, f32[768]{0:T(1024)}, u32[]{:S(2)}) copy-start(f32[768]{0:T(1024)} %get-tuple-element.326) | copy-start | bytes 9220
  829.8 11.3 %copy-start.127 = (f32[64]{0:T(128)S(1)}, f32[64]{0:T(128)}, u32[]{:S(2)}) copy-start(f32[64]{0:T(128)} %get-tuple-element.322) | copy-start | bytes 772
  829.8 11.3 %copy-start.128 = (f32[64]{0:T(128)S(1)}, f32[64]{0:T(128)}, u32[]{:S(2)}) copy-start(f32[64]{0:T(128)} %get-tuple-element.320) | copy-start | bytes 772
  829.9 11.3 %copy-start.129 = (f32[64]{0:T(128)S(1)}, f32[64]{0:T(128)}, u32[]{:S(2)}) copy-start(f32[64]{0:T(128)} %get-tuple-element.318) | copy-start | bytes 772
  829.9 11.3 %copy-start.130 = (f32[64]{0:T(128)S(1)}, f32[64]{0:T(128)}, u32[]{:S(2)}) copy-start(f32[64]{0:T(128)} %get-tuple-element.316) | copy-start | bytes 772
  829.9 11.3 %copy-start.131 = (f32[64]{0:T(128)S(1)}, f32[64]{0:T(128)}, u32[]{:S(2)}) copy-start(f32[64]{0:T(128)} %get-tuple-element.312) | copy-start | bytes 772
  829.9 56.2 %copy-start.20 = (bf16[2,1,512,768]{3,2,1,0:T(8,128)(2,1)S(1)}, bf16[2,1,512,768]{3,2,1,0:T(8,128)(2,1)}, u32[]{:S(2)}) copy-start(bf16[2,1,512,768]{3,2,1,0:T(8,128)(2,1)} %param.55) | copy-start | bytes 4718596
  829.9 56.2 %copy-start.113 = (f32[512]{0:T(512)S(1)}, f32[512]{0:T(512)}, u32[]{:S(2)}) copy-start(f32[512]{0:T(512)} %compare_convert_fusion.3) | copy-start | bytes 6148
  (85 other events, 356.7 us)
Sparse Core Ops, SparseCore 0:
  10.8 114.6 all-gather.5
  128.3 88.6 all-gather.7
  647.6 194.6 reduce-scatter.4
  848.5 258.3 reduce-scatter.2
where the time goes:
time: 1130 us; the launch traced here: 1110 us
  waiting for transfers between devices  317 us (28%)
  matrix products  295 us (26%)
  other arithmetic  239 us (21%)
  local copies, waits for them, and re-layouts  142 us (13%)
  blocking collectives  87.3 us (8%)
  between operations  26 us (2%)
    reduce_scatter x1, waiting for transfers between devices, body(): lax.psum_scatter(summed_in, 'dp', scatter_dimension=0, tiled=True)  217 us
    dot_general x11, matrix products, rows_product(): lax.dot_general(left, right, (contract, ((), ())), preferred_element_type...  90.1 us
    unnamed x2, blocking collectives  87.3 us
    all_gather x1, waiting for transfers between devices, body(): lax.all_gather(weight_out[0], 'dp', axis=0, tiled=True)  62.5 us
    dot_general x3, matrix products, layer_forward(): jnp.dot(joined[:, model_width:], weight_out_full[model_width:], preferred...  55.3 us
    concatenate x3, other arithmetic, recompute(): jnp.concatenate([attended.reshape(row_count, model_width), hidden], axis=1)  44 us
    all_gather x1, waiting for transfers between devices, body(): lax.all_gather(weight_in[0], 'dp', axis=0, tiled=True)  37 us
    another operation x14, other arithmetic  35.5 us
  transfers between devices with their start and end apart: 8, of which 3 were waited for; matrix products, arithmetic and copies ran while one was open for 28% of the time, Pallas kernels for 0%

commit v1 on v0

v1 whole, which is shorter than its diff:
```python
import jax
import jax.numpy as jnp
from jax import lax
from jax.sharding import Mesh, PartitionSpec as P

HEADS = 12
HEAD = 64
EPSILON = 1e-06
MASKED = -1e30
F32 = jnp.float32
BF16 = jnp.bfloat16
DP = ("z", "y", "x")
ALL = ("section",) + DP


def normalize(values, scale_vector):
    average = jnp.mean(values, axis=-1, keepdims=True)
    centred = values - average
    inverse = lax.rsqrt(jnp.mean(centred * centred, axis=-1, keepdims=True) + EPSILON)
    return centred * inverse * scale_vector


def gelu(values):
    return jax.nn.gelu(values, approximate=False)


def dot(left, right, contract):
    return lax.dot_general(left, right, (contract, ((), ())), preferred_element_type=F32)


def forward(rows_in, allowed, weight_in, weight_out, scales):
    length, width = rows_in.shape
    rows = rows_in.astype(F32)
    gain, query_scale, key_scale = scales[:width], scales[width : width + HEAD], scales[width + HEAD :]
    normed = normalize(rows, gain).astype(BF16)
    projected = dot(normed, weight_in, ((1,), (1,)))
    heads = lambda v: v.reshape(length, HEADS, HEAD)
    query_raw, key_raw = heads(projected[:, :width]), heads(projected[:, width : 2 * width])
    value = heads(projected[:, 2 * width : 3 * width]).astype(BF16)
    feed = projected[:, 3 * width :]
    query = normalize(query_raw, query_scale).astype(BF16)
    key = normalize(key_raw, key_scale).astype(BF16)
    scores = jnp.einsum("qhd,khd->hqk", query, key, preferred_element_type=F32) * HEAD**-0.5
    probs = jax.nn.softmax(jnp.where(allowed[None], scores, MASKED), axis=-1)
    attended = jnp.einsum("hqk,khd->qhd", probs.astype(BF16), value, preferred_element_type=F32)
    joined = jnp.concatenate([attended.reshape(length, width), gelu(feed)], axis=1).astype(BF16)
    attend_branch = dot(joined[:, :width], weight_out[:width], ((1,), (0,)))
    feed_branch = dot(joined[:, width:], weight_out[width:], ((1,), (0,)))
    result = rows + attend_branch + feed_branch
    kept = (rows, gain, query_scale, key_scale, normed, query_raw, key_raw, query, key, value, feed, probs, joined)
    return result, attend_branch, feed_branch, kept


def backward(grad, kept, weight_in, weight_out):
    rows, gain, query_scale, key_scale, normed, query_raw, key_raw, query, key, value, feed, probs, joined = kept
    length, width = rows.shape
    grad_joined = dot(grad, weight_out, ((1,), (1,))).astype(BF16)
    grad_attended = grad_joined[:, :width].reshape(length, HEADS, HEAD)
    grad_feed = jax.vjp(gelu, feed)[1](grad_joined[:, width:].astype(F32))[0]
    grad_probs = jnp.einsum("qhd,khd->hqk", grad_attended, value, preferred_element_type=F32)
    grad_value = jnp.einsum("hqk,qhd->khd", probs.astype(BF16), grad_attended, preferred_element_type=F32)
    delta = jnp.sum(probs * grad_probs, axis=-1, keepdims=True)
    grad_scores = (probs * (grad_probs - delta)).astype(BF16)
    grad_query = jnp.einsum("hqk,khd->qhd", grad_scores, key, preferred_element_type=F32) * HEAD**-0.5
    grad_key = jnp.einsum("hqk,qhd->khd", grad_scores, query, preferred_element_type=F32) * HEAD**-0.5
    query_back, query_scale_back = jax.vjp(normalize, query_raw, query_scale)[1](grad_query)
    key_back, key_scale_back = jax.vjp(normalize, key_raw, key_scale)[1](grad_key)
    flat = lambda v: v.reshape(length, width)
    grad_projected = jnp.concatenate(
        [flat(query_back), flat(key_back), flat(grad_value), grad_feed], axis=1
    ).astype(BF16)
    grad_normed = dot(grad_projected, weight_in, ((1,), (0,)))
    grad_rows, grad_gain = jax.vjp(normalize, rows, gain)[1](grad_normed)
    grad_in = (grad.astype(F32) + grad_rows).astype(BF16)
    weight_in_grad = dot(grad_projected, normed, ((0,), (0,))).astype(BF16)
    weight_out_grad = dot(joined, grad, ((0,), (0,))).astype(BF16)
    return grad_in, weight_in_grad, weight_out_grad, jnp.concatenate([grad_gain, query_scale_back, key_scale_back])


def body(inputs, cotangent, lengths, weight_in, weight_out, scales):
    length, width = inputs.shape[2], inputs.shape[3]
    core = lax.axis_index("section")
    rows_first = lax.dynamic_index_in_dim(inputs, core, 0, False)[0]
    grad_last = lax.dynamic_index_in_dim(cotangent, core, 0, False)[0]
    pair = lax.dynamic_index_in_dim(lengths, core, 0, False)[0]
    position = lax.broadcasted_iota(jnp.int32, (length, 1), 0)
    segment = (position >= pair[0]).astype(jnp.int32) + (position >= pair[0] + pair[1]).astype(jnp.int32)
    allowed = segment == segment.reshape(1, length)
    valid = (segment < 2).astype(F32)
    gather = lambda v: lax.all_gather(v[0], ALL, axis=0, tiled=True).reshape((2, -1) + v.shape[2:])
    weight_in_all, weight_out_all = gather(weight_in), gather(weight_out)
    scales_all = gather(scales).astype(F32)
    outputs, kept, sums = [], [], []
    rows = rows_first
    for layer in range(2):
        result, attend, feed, keep = forward(rows, allowed, weight_in_all[layer], weight_out_all[layer], scales_all[layer])
        rows = result.astype(BF16)
        outputs.append(rows)
        kept.append(keep)
        sums.append(jnp.stack([jnp.sum(v * v * valid) for v in (result, attend, feed)]))
    grad = (grad_last.astype(F32) * valid).astype(BF16)
    grads, in_grads, out_grads, scale_grads = [None] * 2, [None] * 2, [None] * 2, [None] * 2
    for layer in (1, 0):
        grad, in_grads[layer], out_grads[layer], scale_grads[layer] = backward(
            grad, kept[layer], weight_in_all[layer], weight_out_all[layer]
        )
        grads[layer] = grad
    scatter = lambda pieces: lax.psum_scatter(
        jnp.concatenate(pieces, axis=0), ALL, scatter_dimension=0, tiled=True
    ).astype(F32)[None]
    small = jnp.concatenate([jnp.stack(sums).reshape(-1), jnp.sum(pair).astype(F32)[None]])
    for axis in ALL:
        small = lax.psum(small, axis)
    statistics = jnp.sqrt(lax.dynamic_slice(small, (3 * core,), (3,)) / (small[6] * width))
    def spread(pieces):
        mine = jnp.where(core == 0, pieces[0], pieces[1])
        other = jnp.where(core == 0, pieces[1], pieces[0])
        other = lax.ppermute(other, "section", [(0, 1), (1, 0)])
        return jnp.stack([jnp.where(core == 0, mine, other), jnp.where(core == 0, other, mine)])[None, :, None]
    return (
        spread(outputs),
        spread(grads),
        scatter(in_grads),
        scatter(out_grads),
        scatter(scale_grads),
        statistics[None],
    )


def solution(mesh):
    count = mesh.shape["dp"]
    fine = Mesh(mesh.devices.reshape(2, count // 4, 2, 2), ALL)
    return jax.shard_map(
        body,
        mesh=fine,
        in_specs=(
            P(None, DP, None, None),
            P(None, DP, None, None),
            P(None, DP, None),
            P("section", DP, None),
            P("section", DP, None),
            P("section", DP),
        ),
        out_specs=(
            P("section", None, DP, None, None),
            P("section", None, DP, None, None),
            P("section", DP, None),
            P("section", DP, None),
            P("section", DP),
            P("section", None),
        ),
        check_vma=False,
    )
```

time: 1130 us -> 759 us (0.67)
  matrix products: 295 us -> 155 us
  other arithmetic: 239 us -> 129 us
  local copies, waits for them, and re-layouts: 142 us -> 42 us
  blocking collectives: 87.3 us -> 103 us
  waiting for transfers between devices: 317 us -> 304 us
    dot_general x44 -> x24, matrix products: 295 us -> 137 us  [the longest x14 91.2 us: dot(): lax.dot_general(left, right, (contract, ((), ())), preferred_element_type...]
    select_n x23 -> x2, other arithmetic: 73 us -> 2.16 us  [spread(): other = jnp.where(core == 0, pieces[1], pieces[0])]
    reduce_scatter x2, waiting for transfers between devices: 217 us -> 151 us  [body(): lax.psum_scatter(jnp.concatenate(pieces, axis=0), ALL, scatter_dimension=...]
    all_gather x2, waiting for transfers between devices: 99.5 us -> 151 us  [body(): lax.all_gather(v[0], ALL, axis=0, tiled=True).reshape((2, -1) + v.shape[2:])]
    slice x41 -> x17, local copies, waits for them, and re-layouts: 54 us -> 12.9 us  [the longest x4 6.7 us: forward(): projected[:, width:2 * width]]
    concatenate x12 -> x1, local copies, waits for them, and re-layouts: 25.7 us -> 0.08 us  [body(): jnp.concatenate(pieces, axis=0)]
    slice x0 -> x2, other arithmetic: none -> 22.2 us  [forward(): feed_branch = dot(joined[:, width:], weight_out[width:], ((1,), (0,)))]
    psum x0 -> x4, blocking collectives: none -> 21.8 us  [body(): small = lax.psum(small, axis)]
  transfers between devices with their start and end apart: 8 -> 6, of which waited for: 3 -> 3; matrix products, arithmetic and copies ran while one was open for 28% -> 19% of each run, Pallas kernels for 0% -> 0%
where the time goes in v1:
time: 759 us; the launch traced here: 750 us
  waiting for transfers between devices  304 us (40%)
  matrix products  155 us (20%)
  other arithmetic  129 us (17%)
  blocking collectives  103 us (14%)
  local copies, waits for them, and re-layouts  42 us (6%)
  between operations  17.9 us (2%)
    all_gather x2, waiting for transfers between devices, body(): lax.all_gather(v[0], ALL, axis=0, tiled=True).reshape((2, -1) + v.shape[2:])  151 us
    reduce_scatter x2, waiting for transfers between devices, body(): lax.psum_scatter(jnp.concatenate(pieces, axis=0), ALL, scatter_dimension=...  151 us
    dot_general x14, matrix products, dot(): lax.dot_general(left, right, (contract, ((), ())), preferred_element_type...  91.2 us
    unnamed x2, blocking collectives  81 us
    another operation x6, other arithmetic  31.3 us
    concatenate x2, other arithmetic, body(): jnp.concatenate(pieces, axis=0)  26 us
    slice x2, other arithmetic, forward(): feed_branch = dot(joined[:, width:], weight_out[width:], ((1,), (0,)))  22.2 us
    psum x4, blocking collectives, body(): small = lax.psum(small, axis)  21.8 us
  transfers between devices with their start and end apart: 6, of which 3 were waited for; matrix products, arithmetic and copies ran while one was open for 19% of the time, Pallas kernels for 0%

profile of v1, /device:TPU:0, one launch (start us, length us, event | category | flops | bytes accessed | tf_op | source)
XLA Modules:
  0.0 750.4 jit_solution(18262357067822087953)
XLA Ops:
  9.6 42.4 %all-reduce = bf16[1792]{0:T(1024)(128)(2,1)S(1)} all-reduce(bf16[1792]{0:T(1024)(128)(2,1)S(1)} %dynamic-update-slice), channel_id=2, replica_groups=mesh['section'=2,'z'=4,'y'=2,'x'=2] {'section','z','y','x'}, use_global_device_ids=true, to_apply=%add | all-reduce | flops 1792 | bytes 7168
  57.9 1.5 fusion.74
  60.9 45.9 %all-gather.8.cloned.1.call-done = bf16[1,7680,768]{2,1,0:T(8,128)(2,1)} async-done(((bf16[1,240,768]{2,1,0:T(8,128)(2,1)}), bf16[1,7680,768]{2,1,0:T(8,128)(2,1)}) %all-gather.8.cloned.1.call-update) | async-done | bytes 11796496 | tf_op jit(solution)/shard_map/all_gather | solution.py:90
  106.9 6.2 convolution_convert_fusion.5
  113.1 1.9 copy-done.15
  116.2 105.6 %all-gather.6.cloned.1.call-done = bf16[1,10752,768]{2,1,0:T(8,128)(2,1)} async-done(((bf16[1,336,768]{2,1,0:T(8,128)(2,1)}), bf16[1,10752,768]{2,1,0:T(8,128)(2,1)}) %all-gather.6.cloned.1.call-update) | async-done | bytes 16515088 | tf_op jit(solution)/shard_map/all_gather | solution.py:90
  221.8 7.0 fusion.5
  228.9 1.6 fusion.142
  230.5 2.9 copy-done.5
  233.4 14.5 %multiply_convert_fusion.3 = (bf16[512,3072]{1,0:T(8,128)(2,1)}, f32[512,3072]{1,0:T(8,128)}) fusion(f32[512,5376]{1,0:T(8,128)S(1)} %fusion.5), kind=kLoop, calls=%fused_computation.60 | loop fusion | flops 102236160 | bytes 15728640 | tf_op jit(solution)/shard_map/slice | solution.py:48
  250.0 1.9 copy.70
  253.2 9.4 %fusion.144 = (f32[12,512]{1,0:T(8,128)}, f32[12,512,512]{1,2,0:T(8,128)}) fusion(pred[512,512]{0,1:T(8,128)(4,1)S(1)} %broadcast_compare_fusion, f32[512,12,64]{0,2,1:T(8,128)S(1)} %bitcast.238, f32[64]{0:T(128)} %get-tuple-element.72, f32[512,12]{0,1:T(8,128)S(1)} %fusion.108, f32[512,12]{0,1:T(8,128)S(1)} %broadcast_multiply_fusion.3, ...), kind=kOutput, calls=%fused_computation.282 | convolution fusion | flops 418382336 | bytes 16114176 | tf_op jit(solution)/shard_map/sub | solution.py:44
  262.5 6.1 fusion.89
  268.7 2.4 fusion.106
  271.1 6.7 convert_reduce_fusion
  278.2 7.0 fusion.7
  286.7 4.1 copy-done.6
  290.8 16.1 %fusion.13 = (bf16[512,3072]{1,0:T(8,128)(2,1)}, f32[512,3072]{1,0:T(8,128)}) fusion(f32[512,5376]{1,0:T(8,128)S(1)} %fusion.7, bf16[512,3840]{1,0:T(8,128)(2,1)S(1)} %copy-done.16), kind=kLoop, calls=%fused_computation.35 | loop fusion | flops 114819072 | bytes 18874368 | tf_op jit(solution)/shard_map/convert.15
  309.1 1.9 copy.74
  311.5 8.5 %fusion.145 = (f32[12,512]{1,0:T(8,128)S(1)}, f32[12,512,512]{1,2,0:T(8,128)}) fusion(pred[512,512]{0,1:T(8,128)(4,1)} %copy-done.54, f32[512,12,64]{0,2,1:T(8,128)S(1)} %bitcast.252, f32[64]{0:T(128)S(1)} %copy-done.71, f32[512,12]{0,1:T(8,128)S(1)} %fusion.110, f32[512,12]{0,1:T(8,128)S(1)} %broadcast_multiply_fusion.1, ...), kind=kOutput, calls=%fused_computation.283 | convolution fusion | flops 418382336 | bytes 16114176 | tf_op jit(solution)/shard_map/sub | solution.py:44
  319.9 7.1 fusion.95
  327.0 1.6 copy-done.11
  328.8 2.9 fusion.98
  331.7 5.6 multiply_reduce_fusion.1
  337.3 2.3 copy.90
  339.7 7.7 %multiply_convert_fusion.2 = bf16[512,3072]{1,0:T(8,128)(2,1)} fusion(f32[512,3072]{1,0:T(8,128)} %get-tuple-element.52, f32[512,5376]{1,0:T(8,128)} %copy-done.6), kind=kLoop, calls=%fused_computation.46 | loop fusion | flops 4718592 | bytes 15728640 | tf_op jit(solution)/shard_map/slice | solution.py:48
  347.4 2.3 copy.82
  349.7 10.0 %multiply_convert_fusion.1 = bf16[12,512,512]{1,2,0:T(8,128)(2,1)S(1)} fusion(f32[12,512,512]{1,2,0:T(8,128)} %get-tuple-element.81, f32[12,512]{1,0:T(8,128)S(1)} %get-tuple-element.80, f32[12,512,512]{1,2,0:T(8,128)} %get-tuple-element.79, f32[12,512]{1,0:T(8,128)S(1)} %get-tuple-element.78), kind=kLoop, calls=%fused_computation.5 | loop fusion | flops 12582912 | bytes 31506432 | tf_op jit(solution)/shard_map/convert_element_type | solution.py:63
  359.7 2.1 fusion.87
  363.3 2.5 fusion.81
  365.8 1.4 add_convert_fusion.4
  367.3 2.3 copy.81
  369.6 2.0 add_convert_fusion.5
  371.9 9.6 %fusion.78 = (f32[512]{0:T(512)S(1)}, f32[512,768]{1,0:T(8,128)S(1)}) fusion(bf16[512,768]{1,0:T(8,128)(2,1)S(1)} %copy-done.8, f32[768]{0:T(1024)S(1)} %get-tuple-element.41, f32[512]{0:T(512)S(1)} %broadcast_multiply_fusion.4, bf16[1,10752,768]{2,1,0:T(8,128)(2,1)} %all-gather.6.cloned.1.call-done, bf16[512,3072]{1,0:T(8,128)(2,1)} %get-tuple-element.51, ...), kind=kOutput, calls=%fused_computation.141 | convolution fusion | flops 4251844096 | bytes 16129024 | tf_op jit(solution)/shard_map/dot_general | solution.py:28
  383.4 5.8 convolution_convert_fusion.2
  389.2 3.6 convolution_convert_fusion.3
  392.8 5.4 pad_maximum_fusion.1
  398.3 6.2 convolution_convert_fusion.4
  404.5 1.9 copy-done.14
  407.1 7.4 fusion.92
  415.7 6.6 multiply_reduce_fusion
  422.3 7.7 %multiply_convert_fusion = bf16[12,512,512]{1,2,0:T(8,128)(2,1)S(1)} fusion(f32[12,512,512]{1,2,0:T(8,128)S(1)} %get-tuple-element.89, f32[12,512]{1,0:T(8,128)S(1)} %get-tuple-element.88, f32[12,512,512]{1,2,0:T(8,128)} %get-tuple-element.76, f32[12,512]{1,0:T(8,128)S(1)} %copy-done.55), kind=kLoop, calls=%fused_computation.3 | loop fusion | flops 12582912 | bytes 31506432 | tf_op jit(solution)/shard_map/convert_element_type | solution.py:63
  430.2 2.1 fusion.85
  433.6 1.4 add_convert_fusion.1
  435.1 2.3 copy.88
  437.4 4.3 fusion.86
  444.3 9.9 %fusion.20 = bf16[512,3072]{1,0:T(8,128)(2,1)} fusion(f32[512,3072]{1,0:T(8,128)} %get-tuple-element.56, f32[512,5376]{1,0:T(8,128)} %copy-done.5, bf16[512,3840]{1,0:T(8,128)(2,1)} %copy-done.14), kind=kLoop, calls=%fused_computation.42 | loop fusion | flops 23592960 | bytes 18874368 | tf_op jit(solution)/shard_map/convert.7
  454.2 7.1 convolution_convert_fusion.1
  461.3 8.8 %convolution_convert_fusion = bf16[5376,768]{1,0:T(8,128)(2,1)} fusion(bf16[512,3072]{1,0:T(8,128)(2,1)} %get-tuple-element.51, bf16[512,768]{1,0:T(8,128)(2,1)S(1)} %copy-done.33, bf16[512,768]{1,0:T(8,128)(2,1)S(1)} %copy-done.34, bf16[512,768]{1,0:T(8,128)(2,1)S(1)} %copy-done.38, bf16[512,768]{1,0:T(8,128)(2,1)S(1)} %copy-done.9, ...), kind=kOutput, calls=%fused_computation.12 | convolution fusion | flops 4255973376 | bytes 14556160 | tf_op jit(solution)/shard_map/dot_general | solution.py:28
  470.1 20.6 %pad_maximum_fusion = bf16[10752,768]{1,0:T(8,128)(2,1)} fusion(bf16[5376,768]{1,0:T(8,128)(2,1)} %convolution_convert_fusion, bf16[5376,768]{1,0:T(8,128)(2,1)S(1)} %convolution_convert_fusion.1), kind=kLoop, calls=%fused_computation.2 | loop fusion | flops 33030144 | bytes 33030144 | tf_op jit(solution)/shard_map/concatenate | solution.py:109
  491.9 3.4 fusion.105
  495.4 6.3 fusion.40
  501.7 11.1 %multiply_reduce_fusion.7 = (f32[]{:T(128)}, f32[]{:T(128)}, f32[]{:T(128)}, f32[512]{0:T(512)S(1)}, f32[768]{0:T(1024)S(1)}, /*index=5*/f32[]{:T(128)}, f32[]{:...) fusion(f32[512]{0:T(512)S(1)} %compare_convert_fusion, f32[512,768]{1,0:T(8,128)} %get-tuple-element.77, ...), kind=kOutput, calls=%fused_computation.174 | convolution fusion | flops 4262460160 | bytes 24000540 | tf_op jit(solution)/shard_map/dot_general | solution.py:28
  516.3 1.9 maximum_bitcast_fusion.3
  518.2 2.0 maximum_bitcast_fusion.2
  520.4 2.4 psum.28
  522.8 9.5 %psum.29 = f32[7]{0:T(128)S(1)} all-reduce(f32[7]{0:T(128)S(1)} %psum.28), channel_id=1, replica_groups=mesh['section'=2,'z'=4,'y'=2,'x'=2] {'z'}, use_global_device_ids=true, to_apply=%region_47.48 | all-reduce | flops 7 | bytes 56 | tf_op jit(solution)/shard_map/psum | solution.py:113
  532.3 4.9 psum.30
  537.2 4.9 psum.31
  543.4 38.6 %all-reduce.1 = f32[1792]{0:T(1024)S(1)} all-reduce(f32[1792]{0:T(1024)S(1)} %concatenate.34), channel_id=7, replica_groups=mesh['section'=2,'z'=4,'y'=2,'x'=2] {'section','z','y','x'}, use_global_device_ids=true, to_apply=%region_38.39.clone | all-reduce | flops 1792 | bytes 14336
  585.8 1.7 select_bitcast_fusion.1
  588.8 2.0 bitcast_convert_fusion.1
  590.7 150.9 %reduce-scatter.3.cloned.1.call-done = bf16[336,768]{1,0:T(8,128)(2,1)} async-done(((bf16[10752,768]{1,0:T(8,128)(2,1)}), bf16[336,768]{1,0:T(8,128)(2,1)}) %reduce-scatter.3.cloned.1.call-update) | async-done | bytes 516112 | tf_op jit(solution)/shard_map/reduce_scatter | solution.py:108
  741.6 2.1 bitcast_convert_fusion
  (235 shorter events, 36.7 us)
Async XLA Ops:
  7.2 99.7 %all-gather.8.cloned.1.call-start = ((), (), s32[]{:S(2)}) async-start(), calls=%async_computation.5 | async-start | bytes 12165120 | tf_op jit(solution)/shard_map/all_gather | solution.py:90
  7.9 213.9 %all-gather.6.cloned.1.call-start = ((), (), s32[]{:S(2)}) async-start(), calls=%async_computation.4 | async-start | bytes 17031168 | tf_op jit(solution)/shard_map/all_gather | solution.py:90
  8.6 580.1 %reduce-scatter.5.cloned.1.call-start = ((), (), s32[]{:S(2)}) async-start(), calls=%async_computation.3 | async-start | bytes 12165120 | tf_op jit(solution)/shard_map/reduce_scatter | solution.py:108
  57.9 163.9 %copy-start.60 = (f32[768]{0:T(1024)}, f32[768]{0:T(1024)S(1)}, u32[]{:S(2)}) copy-start(f32[768]{0:T(1024)S(1)} %get-tuple-element.42) | copy-start | bytes 9220
  57.9 163.9 %copy-start.56 = (f32[512]{0:T(512)}, f32[512]{0:T(512)S(1)}, u32[]{:S(2)}) copy-start(f32[512]{0:T(512)S(1)} %broadcast_multiply_fusion.5) | copy-start | bytes 6148
  59.4 53.6 %copy-start.58 = (f32[512]{0:T(512)}, f32[512]{0:T(512)S(1)}, u32[]{:S(2)}) copy-start(f32[512]{0:T(512)S(1)} %fusion.74) | copy-start | bytes 6148
  60.7 161.1 %copy-start.62 = (f32[512]{0:T(512)}, f32[512]{0:T(512)S(1)}, u32[]{:S(2)}) copy-start(f32[512]{0:T(512)S(1)} %fusion.112) | copy-start | bytes 6148
  60.9 192.2 %copy-start.54 = (pred[512,512]{0,1:T(8,128)(4,1)}, pred[512,512]{0,1:T(8,128)(4,1)S(1)}, u32[]{:S(2)}) copy-start(pred[512,512]{0,1:T(8,128)(4,1)S(1)} %broadcast_compare_fusion) | copy-start | bytes 786436
  115.0 106.8 %copy-start.17 = (bf16[2,1,512,768]{3,2,1,0:T(8,128)(2,1)S(1)}, bf16[2,1,512,768]{3,2,1,0:T(8,128)(2,1)}, u32[]{:S(2)}) copy-start(bf16[2,1,512,768]{3,2,1,0:T(8,128)(2,1)} %param.6) | copy-start | bytes 4718596
  228.8 4.6 copy-start.5
  249.5 3.6 copy-start
  249.7 3.4 copy-start.26
  250.0 3.1 copy-start.45
  252.0 10.6 %copy-start.2 = (f32[512,768]{0,1:T(8,128)}, f32[512,768]{0,1:T(8,128)S(1)}, u32[]{:S(2)}) copy-start(f32[512,768]{0,1:T(8,128)S(1)} %copy.70) | copy-start | bytes 4718596
  252.2 10.3 %copy-start.28 = (f32[512,12]{0,1:T(8,128)}, f32[512,12]{0,1:T(8,128)S(1)}, u32[]{:S(2)}) copy-start(f32[512,12]{0,1:T(8,128)S(1)} %broadcast_multiply_fusion.2) | copy-start | bytes 73732
  253.1 9.4 %copy-start.47 = (f32[512,12]{0,1:T(8,128)}, f32[512,12]{0,1:T(8,128)S(1)}, u32[]{:S(2)}) copy-start(f32[512,12]{0,1:T(8,128)S(1)} %fusion.109) | copy-start | bytes 73732
  262.5 8.5 %copy-start.24 = (bf16[512,3072]{1,0:T(8,128)(2,1)S(1)}, bf16[512,3072]{1,0:T(8,128)(2,1)}, u32[]{:S(2)}) copy-start(bf16[512,3072]{1,0:T(8,128)(2,1)} %get-tuple-element.55) | copy-start | bytes 9437188
  268.6 9.1 %copy-start.43 = (bf16[12,64,512]{2,1,0:T(8,128)(2,1)}, bf16[12,64,512]{2,1,0:T(8,128)(2,1)S(1)}, u32[]{:S(2)}) copy-start(bf16[12,64,512]{2,1,0:T(8,128)(2,1)S(1)} %fusion.89) | copy-start | bytes 2359300
  271.1 6.7 copy-start.72
  277.8 7.4 copy-start.7
  285.2 5.6 copy-start.6
  285.3 5.5 copy-start.16
  319.9 8.7 %copy-start.11 = (f32[12,512,512]{1,2,0:T(8,128)S(1)}, f32[12,512,512]{1,2,0:T(8,128)}, u32[]{:S(2)}) copy-start(f32[12,512,512]{1,2,0:T(8,128)} %get-tuple-element.79) | copy-start | bytes 37748740
  319.9 8.8 %copy-start.40 = (bf16[512,768]{0,1:T(8,128)(2,1)S(1)}, bf16[512,768]{0,1:T(8,128)(2,1)}, u32[]{:S(2)}) copy-start(bf16[512,768]{0,1:T(8,128)(2,1)} %copy.76) | copy-start | bytes 2359300
  328.8 3.0 copy-start.44
  371.9 9.6 %copy-start.37 = (bf16[512,768]{1,0:T(8,128)(2,1)}, bf16[512,768]{1,0:T(8,128)(2,1)S(1)}, u32[]{:S(2)}) copy-start(bf16[512,768]{1,0:T(8,128)(2,1)S(1)} %copy.80) | copy-start | bytes 2359300
  371.9 10.5 %copy-start.49 = (bf16[2,1,512,768]{3,2,1,0:T(8,128)(2,1)S(1)}, bf16[2,1,512,768]{3,2,1,0:T(8,128)(2,1)}, u32[]{:S(2)}) copy-start(bf16[2,1,512,768]{3,2,1,0:T(8,128)(2,1)} %param.7) | copy-start | bytes 4718596
  383.1 15.2 %copy-start.12 = (bf16[512,768]{1,0:T(8,128)(2,1)}, bf16[512,768]{1,0:T(8,128)(2,1)S(1)}, u32[]{:S(2)}) copy-start(bf16[512,768]{1,0:T(8,128)(2,1)S(1)} %add_convert_fusion.3) | copy-start | bytes 2359300
  383.4 5.8 copy-start.25
  383.4 5.8 copy-start.41
  398.2 343.4 %reduce-scatter.3.cloned.1.call-start = ((), (), s32[]{:S(2)}) async-start(), calls=%async_computation.2 | async-start | bytes 17031168 | tf_op jit(solution)/shard_map/reduce_scatter | solution.py:108
  407.1 8.6 %copy-start.32 = (bf16[512,768]{0,1:T(8,128)(2,1)S(1)}, bf16[512,768]{0,1:T(8,128)(2,1)}, u32[]{:S(2)}) copy-start(bf16[512,768]{0,1:T(8,128)(2,1)} %copy.68) | copy-start | bytes 2359300
  422.3 7.8 %copy-start.1 = (f32[512,768]{0,1:T(8,128)S(1)}, f32[512,768]{0,1:T(8,128)}, u32[]{:S(2)}) copy-start(f32[512,768]{0,1:T(8,128)} %copy-done) | copy-start | bytes 4718596
  422.3 7.8 %copy-start.3 = (f32[512,768]{0,1:T(8,128)S(1)}, f32[512,768]{0,1:T(8,128)}, u32[]{:S(2)}) copy-start(f32[512,768]{0,1:T(8,128)} %copy-done.2) | copy-start | bytes 4718596
  422.3 7.8 %copy-start.27 = (f32[512,12]{0,1:T(8,128)S(1)}, f32[512,12]{0,1:T(8,128)}, u32[]{:S(2)}) copy-start(f32[512,12]{0,1:T(8,128)} %copy-done.26) | copy-start | bytes 73732
  422.3 7.8 %copy-start.29 = (f32[512,12]{0,1:T(8,128)S(1)}, f32[512,12]{0,1:T(8,128)}, u32[]{:S(2)}) copy-start(f32[512,12]{0,1:T(8,128)} %copy-done.28) | copy-start | bytes 73732
  422.3 7.8 %copy-start.46 = (f32[512,12]{0,1:T(8,128)S(1)}, f32[512,12]{0,1:T(8,128)}, u32[]{:S(2)}) copy-start(f32[512,12]{0,1:T(8,128)} %copy-done.45) | copy-start | bytes 73732
  422.3 7.8 %copy-start.65 = (f32[64]{0:T(128)S(1)}, f32[64]{0:T(128)}, u32[]{:S(2)}) copy-start(f32[64]{0:T(128)} %get-tuple-element.67) | copy-start | bytes 772
  422.3 7.8 %copy-start.69 = (f32[64]{0:T(128)S(1)}, f32[64]{0:T(128)}, u32[]{:S(2)}) copy-start(f32[64]{0:T(128)} %get-tuple-element.72) | copy-start | bytes 772
  430.1 2.6 copy-start.4
  433.6 3.8 copy-start.64
  433.6 3.8 copy-start.68
  437.4 4.4 copy-start.51
  444.2 9.9 %copy-start.19 = (bf16[2,1,512,768]{3,2,1,0:T(8,128)(2,1)S(1)}, bf16[2,1,512,768]{3,2,1,0:T(8,128)(2,1)}, u32[]{:S(2)}) copy-start(bf16[2,1,512,768]{3,2,1,0:T(8,128)(2,1)} %param.6) | copy-start | bytes 4718596
  444.2 9.9 %copy-start.35 = (bf16[512,768]{1,0:T(8,128)(2,1)S(1)}, bf16[512,768]{1,0:T(8,128)(2,1)}, u32[]{:S(2)}) copy-start(bf16[512,768]{1,0:T(8,128)(2,1)} %copy.89) | copy-start | bytes 2359300
  444.2 9.9 %copy-start.57 = (f32[512]{0:T(512)S(1)}, f32[512]{0:T(512)}, u32[]{:S(2)}) copy-start(f32[512]{0:T(512)} %copy-done.56) | copy-start | bytes 6148
  444.2 9.9 %copy-start.61 = (f32[768]{0:T(1024)S(1)}, f32[768]{0:T(1024)}, u32[]{:S(2)}) copy-start(f32[768]{0:T(1024)} %copy-done.60) | copy-start | bytes 9220
  444.2 9.9 %copy-start.63 = (f32[512]{0:T(512)S(1)}, f32[512]{0:T(512)}, u32[]{:S(2)}) copy-start(f32[512]{0:T(512)} %copy-done.62) | copy-start | bytes 6148
  454.2 7.1 copy-start.9
  454.2 7.1 copy-start.33
  454.2 7.1 copy-start.34
  454.2 7.1 copy-start.38
  491.9 3.5 copy-start.23
  495.4 6.3 copy-start.21
  495.4 6.3 copy-start.36
  495.4 6.3 copy-start.39
  495.4 6.3 copy-start.42
  495.4 6.3 copy-start.73
  501.7 12.3 %copy-start.59 = (f32[512]{0:T(512)S(1)}, f32[512]{0:T(512)}, u32[]{:S(2)}) copy-start(f32[512]{0:T(512)} %copy-done.58) | copy-start | bytes 6148
  501.7 12.3 %copy-start.20 = (bf16[2,1,512,768]{3,2,1,0:T(8,128)(2,1)S(1)}, bf16[2,1,512,768]{3,2,1,0:T(8,128)(2,1)}, u32[]{:S(2)}) copy-start(bf16[2,1,512,768]{3,2,1,0:T(8,128)(2,1)} %param.6) | copy-start | bytes 4718596
  513.8 69.4 %collective-permute-start = (bf16[512,768]{1,0:T(8,128)(2,1)}, bf16[512,768]{1,0:T(8,128)(2,1)}, u32[]{:S(2)}, u32[]{:S(2)}) collective-permute-start(bf16[512,768]{1,0:T(8,128)(2,1)} %broadcast_select_fusion.2), channel_id=1, source_target_pairs={{0,16},{16,0},{1,17},{17,1},{2,18},{18,2},{3,19},{19,3},{4,20},{20... | collective-permute-start | bytes 2359304 | tf_op jit(solution)/shard_map/ppermute | solution.py:118
  514.0 29.3 %copy-start.66 = (f32[64]{0:T(128)S(1)}, f32[64]{0:T(128)}, u32[]{:S(2)}) copy-start(f32[64]{0:T(128)} %get-tuple-element.24) | copy-start | bytes 772
  514.0 29.3 %copy-start.67 = (f32[64]{0:T(128)S(1)}, f32[64]{0:T(128)}, u32[]{:S(2)}) copy-start(f32[64]{0:T(128)} %get-tuple-element.96) | copy-start | bytes 772
  516.0 69.8 %collective-permute-start.1 = (bf16[512,768]{1,0:T(8,128)(2,1)}, bf16[512,768]{1,0:T(8,128)(2,1)}, u32[]{:S(2)}, u32[]{:S(2)}) collective-permute-start(bf16[512,768]{1,0:T(8,128)(2,1)} %broadcast_select_fusion), channel_id=1, source_target_pairs={{0,16},{16,0},{1,17},{17,1},{2,18},{18,2},{3,19},{19,3},{4,20},{20... | collective-permute-start | bytes 2359304 | tf_op jit(solution)/shard_map/ppermute | solution.py:118
  (16 other events, 30.9 us)
Sparse Core Ops, SparseCore 0:
  10.9 95.9 all-gather.7
  109.8 111.9 all-gather.5
  398.3 145.9 reduce-scatter.4
  551.7 189.8 reduce-scatter.2

commit v2 on v1

v2 whole, which is shorter than its diff:
```python
import functools

import jax
import jax.numpy as jnp
from jax import lax
from jax.experimental import pallas as pl
from jax.experimental.pallas import tpu as pltpu
from jax.sharding import Mesh, PartitionSpec as P

HEADS = 12
HEAD = 64
GROUP = 4
GROUPS = HEADS // GROUP
LANES = GROUP * HEAD
EPSILON = 1e-06
MASKED = -1e30
FACTOR = HEAD**-0.5
F32 = jnp.float32
BF16 = jnp.bfloat16
DP = ("z", "y", "x")
ALL = ("section",) + DP
VMEM_MIB = 56
ANY = pl.BlockSpec(memory_space=pl.ANY)
VMEM = pl.BlockSpec(memory_space=pltpu.VMEM)


def nn(left, right):
    return lax.dot_general(left, right, (((1,), (0,)), ((), ())), preferred_element_type=F32)


def nt(left, right):
    return lax.dot_general(left, right, (((1,), (1,)), ((), ())), preferred_element_type=F32)


def tn(left, right):
    return lax.dot_general(left, right, (((0,), (0,)), ((), ())), preferred_element_type=F32)


def launch(kernel, values, *, name, micros, grid=(), in_specs, out_specs, out_shape, scratch=()):
    return pl.pallas_call(
        kernel,
        grid=grid,
        in_specs=in_specs,
        out_specs=out_specs,
        out_shape=out_shape,
        scratch_shapes=scratch,
        cost_estimate=pl.CostEstimate(flops=int(micros * 1150000000.0), bytes_accessed=int(micros * 1000000.0), transcendentals=0),
        compiler_params=pltpu.CompilerParams(
            vmem_limit_bytes=VMEM_MIB * 1024 * 1024, dimension_semantics=("arbitrary",) * len(grid)
        ),
        name=name,
    )(*values)


def array(shape, dtype=BF16):
    return jax.ShapeDtypeStruct(shape, dtype)


def row_norm(rows):
    average = jnp.mean(rows, axis=1, keepdims=True)
    centred = rows - average
    inverse = lax.rsqrt(jnp.mean(centred * centred, axis=1, keepdims=True) + EPSILON)
    return centred * inverse, inverse


def column_norm(columns):
    average = jnp.mean(columns, axis=0, keepdims=True)
    centred = columns - average
    inverse = lax.rsqrt(jnp.mean(centred * centred, axis=0, keepdims=True) + EPSILON)
    return centred * inverse, inverse


def norm_back(normal, inverse, grad, scale, axis):
    scaled = grad * scale
    average = jnp.mean(scaled, axis=axis, keepdims=True)
    along_normal = jnp.mean(scaled * normal, axis=axis, keepdims=True)
    return inverse * (scaled - average - normal * along_normal)


def segment_at(pair_ref, position):
    first_end = pair_ref[0, 0]
    second_end = first_end + pair_ref[0, 1]
    return (position >= first_end).astype(jnp.int32) + (position >= second_end).astype(jnp.int32)


def fill_bias(pair_ref, bias_ref):
    length = bias_ref.shape[0]
    down = segment_at(pair_ref, lax.broadcasted_iota(jnp.int32, (length, length), 0))
    sideways = segment_at(pair_ref, lax.broadcasted_iota(jnp.int32, (length, length), 1))
    bias_ref[...] = jnp.where(down == sideways, 0.0, MASKED).astype(F32)


def whole(*shape):
    return pl.BlockSpec(shape, lambda *_: (0,) * len(shape))


def attend_kernel(
    pair_ref, rows_ref, gain_ref, query_scale_ref, key_scale_ref, weight_ref,
    normed_ref, raw_ref, value_ref, attended_ref, log_ref, bias_ref,
):
    @pl.when(pl.program_id(0) == 0)
    def _():
        normal, _ = row_norm(rows_ref[...].astype(F32))
        normed_ref[...] = (normal * gain_ref[...]).astype(BF16)
        fill_bias(pair_ref, bias_ref)

    normed = normed_ref[...]
    width = normed.shape[1]
    projected = nt(weight_ref[...].reshape(3 * LANES, width), normed)
    raw_ref[...] = projected[: 2 * LANES].reshape(raw_ref.shape)
    value_ref[...] = projected[2 * LANES :].astype(BF16)
    for head in range(GROUP):
        at = slice(head * HEAD, (head + 1) * HEAD)
        query = column_norm(projected[:LANES][at])[0] * query_scale_ref[...]
        query = query.astype(BF16) * BF16(FACTOR)
        key = (column_norm(projected[LANES : 2 * LANES][at])[0] * key_scale_ref[...]).astype(BF16)
        scores = tn(key, query) + bias_ref[...]
        peak = jnp.max(scores, axis=0, keepdims=True)
        exponent = jnp.exp(scores - peak)
        total = jnp.sum(exponent, axis=0, keepdims=True)
        attended = nn(value_ref[at, :], exponent.astype(BF16)) * (1.0 / total)
        attended_ref[at, :] = attended.astype(BF16)
        log_ref[0, head : head + 1, :] = peak + jnp.log(total)


def attend(layer, pair, rows, gain, query_scale, key_scale, weight_in):
    length, width = rows.shape
    return launch(
        attend_kernel,
        (pair, rows, gain, query_scale, key_scale, weight_in.reshape(2, -1, GROUPS, LANES, width)),
        name="attend",
        micros=12,
        grid=(GROUPS,),
        in_specs=[
            pl.BlockSpec(memory_space=pltpu.SMEM),
            whole(length, width),
            whole(1, width),
            whole(HEAD, 1),
            whole(HEAD, 1),
            pl.BlockSpec((1, 3, 1, LANES, width), lambda g: (layer, 0, g, 0, 0)),
        ],
        out_specs=[
            whole(length, width),
            pl.BlockSpec((2, 1, LANES, length), lambda g: (0, g, 0, 0)),
            pl.BlockSpec((LANES, length), lambda g: (g, 0)),
            pl.BlockSpec((LANES, length), lambda g: (g, 0)),
            pl.BlockSpec((1, 8, length), lambda g: (g, 0, 0)),
        ],
        out_shape=[
            array((length, width)),
            array((2, GROUPS, LANES, length), F32),
            array((width, length)),
            array((width, length)),
            array((GROUPS, 8, length), F32),
        ],
        scratch=[pltpu.VMEM((length, length), F32)],
    )


def hidden_kernel(normed_ref, weight_ref, hidden_ref, slope_ref):
    feed = nt(weight_ref[...], normed_ref[...])
    half = 0.5 * lax.erf(feed * (0.5**0.5)) + 0.5
    hidden_ref[...] = (feed * half).astype(BF16)
    density = jnp.exp(feed * feed * -0.5) * ((2.0 * jnp.pi) ** -0.5)
    slope_ref[...] = (half + feed * density).astype(BF16)


def hidden(layer, normed, weight_in):
    length, width = normed.shape
    blocks = weight_in.shape[0] // width // 2
    first, count = layer * blocks + 3, blocks - 3
    return launch(
        hidden_kernel,
        (normed, weight_in),
        name="hidden",
        micros=8,
        grid=(count,),
        in_specs=[whole(length, width), pl.BlockSpec((width, width), lambda i: (i + first, 0))],
        out_specs=[pl.BlockSpec((width, length), lambda i: (i, 0))] * 2,
        out_shape=[array((count * width, length))] * 2,
    )


def output_kernel(pair_ref, rows_ref, attended_ref, hidden_ref, weight_ref, result_ref, sums_ref, attend_ref, feed_ref):
    step = pl.program_id(0)

    @pl.when(step == 0)
    def _():
        attend_ref[...] = tn(attended_ref[...], weight_ref[...])

    @pl.when(step == 1)
    def _():
        feed_ref[...] = tn(hidden_ref[...], weight_ref[...])

    @pl.when(step > 1)
    def _():
        feed_ref[...] += tn(hidden_ref[...], weight_ref[...])

    @pl.when(step == pl.num_programs(0) - 1)
    def _():
        length, width = attend_ref.shape
        position = lax.broadcasted_iota(jnp.int32, (length, 1), 0)
        valid = (segment_at(pair_ref, position) < 2).astype(F32)
        branch, feed = attend_ref[...], feed_ref[...]
        result = rows_ref[...].astype(F32) + branch + feed
        result_ref[...] = result.astype(BF16)
        for at, value in enumerate((result, branch, feed)):
            squares = (value * value * valid).reshape(length // 8, 8, width)
            sums_ref[at] = jnp.sum(squares, axis=0)


def output(pair, rows, attended, hid, weight):
    length, width = rows.shape
    count = weight.shape[0] // width
    return launch(
        output_kernel,
        (pair, rows, attended, hid, weight),
        name="output",
        micros=9,
        grid=(count,),
        in_specs=[
            pl.BlockSpec(memory_space=pltpu.SMEM),
            whole(length, width),
            whole(width, length),
            pl.BlockSpec((width, length), lambda i: (jnp.maximum(i - 1, 0), 0)),
            pl.BlockSpec((width, width), lambda i: (i, 0)),
        ],
        out_specs=[whole(length, width), whole(3, 8, width)],
        out_shape=[array((length, width)), array((3, 8, width), F32)],
        scratch=[pltpu.VMEM((length, width), F32)] * 2,
    )


def feed_back_kernel(grad_ref, slope_ref, weight_in_ref, weight_out_ref, grad_normed_ref, grad_feed_ref):
    step = pl.program_id(0)
    grad_hidden = nt(weight_out_ref[...], grad_ref[...]).astype(BF16).astype(F32)
    grad_feed = (grad_hidden * slope_ref[...].astype(F32)).astype(BF16)
    grad_feed_ref[...] = grad_feed
    part = tn(grad_feed, weight_in_ref[...])

    @pl.when(step == 0)
    def _():
        grad_normed_ref[...] = part

    @pl.when(step > 0)
    def _():
        grad_normed_ref[...] += part


def feed_back(layer, grad, slope, weight_in, weight_out):
    length, width = grad.shape
    count = slope.shape[0] // width
    first = layer * (weight_in.shape[0] // width // 2) + 3
    rows = pl.BlockSpec((width, length), lambda i: (i, 0))
    return launch(
        feed_back_kernel,
        (grad, slope, weight_in, weight_out),
        name="feed_back",
        micros=11,
        grid=(count,),
        in_specs=[
            whole(length, width),
            rows,
            pl.BlockSpec((width, width), lambda i: (i + first, 0)),
            pl.BlockSpec((width, width), lambda i: (i + 1, 0)),
        ],
        out_specs=[whole(length, width), rows],
        out_shape=[array((length, width), F32), array(slope.shape)],
    )


def attend_back_kernel(
    pair_ref, rows_ref, grad_ref, gain_ref, query_scale_ref, key_scale_ref, raw_ref, value_ref,
    attended_ref, log_ref, weight_out_ref, weight_in_ref, feed_grad_ref,
    projected_ref, grad_in_ref, gain_grad_ref, scale_grad_ref, bias_ref, grad_normed_ref,
):
    step = pl.program_id(0)

    @pl.when(step == 0)
    def _():
        fill_bias(pair_ref, bias_ref)
        grad_normed_ref[...] = feed_grad_ref[...]
        scale_grad_ref[...] = jnp.zeros_like(scale_grad_ref)

    length, width = grad_ref.shape
    query_scale, key_scale = query_scale_ref[...], key_scale_ref[...]
    grad_attended = nt(weight_out_ref[0], grad_ref[...]).astype(BF16)
    for head in range(GROUP):
        at = slice(head * HEAD, (head + 1) * HEAD)
        query_normal, query_inverse = column_norm(raw_ref[0, 0, at, :])
        key_normal, key_inverse = column_norm(raw_ref[1, 0, at, :])
        query = (query_normal * query_scale).astype(BF16) * BF16(FACTOR)
        key = (key_normal * key_scale).astype(BF16)
        value = value_ref[at, :]
        probs = jnp.exp(tn(key, query) + bias_ref[...] - log_ref[0, head : head + 1, :])
        grad_out = grad_attended[at]
        grad_probs = tn(value, grad_out)
        grad_value = nt(grad_out, probs.astype(BF16))
        delta = jnp.sum(grad_out.astype(F32) * attended_ref[at, :].astype(F32), axis=0, keepdims=True)
        grad_scores = (probs * (grad_probs - delta)).astype(BF16)
        grad_query = nn(key, grad_scores) * FACTOR
        grad_key = nt(query, grad_scores)
        for place_at, term in enumerate((grad_query * query_normal, grad_key * key_normal)):
            for lane in range(0, length, 128):
                scale_grad_ref[place_at] += term[:, lane : lane + 128]
        projected_ref[0, 0, at, :] = norm_back(query_normal, query_inverse, grad_query, query_scale, 0).astype(BF16)
        projected_ref[1, 0, at, :] = norm_back(key_normal, key_inverse, grad_key, key_scale, 0).astype(BF16)
        projected_ref[2, 0, at, :] = grad_value.astype(BF16)
    projected = projected_ref[...].reshape(3 * LANES, length)
    grad_normed_ref[...] += tn(projected, weight_in_ref[...].reshape(3 * LANES, width))

    @pl.when(step == pl.num_programs(0) - 1)
    def _():
        normal, inverse = row_norm(rows_ref[...].astype(F32))
        grad_normed = grad_normed_ref[...]
        grad_rows = norm_back(normal, inverse, grad_normed, gain_ref[...], 1)
        grad_in_ref[...] = (grad_ref[...].astype(F32) + grad_rows).astype(BF16)
        gain_grad_ref[...] = jnp.sum((grad_normed * normal).reshape(length // 8, 8, width), axis=0)


def attend_back(layer, pair, rows, grad, gain, query_scale, key_scale, raw, value, attended, logs, weight_out,
                weight_in, feed_grad):
    length, width = grad.shape
    group_rows = pl.BlockSpec((LANES, length), lambda g: (g, 0))
    projected, *others = launch(
        attend_back_kernel,
        (pair, rows, grad, gain, query_scale, key_scale, raw, value, attended, logs,
         weight_out.reshape(-1, LANES, width), weight_in.reshape(2, -1, GROUPS, LANES, width), feed_grad),
        name="attend_back",
        micros=17,
        grid=(GROUPS,),
        in_specs=[
            pl.BlockSpec(memory_space=pltpu.SMEM),
            whole(length, width),
            whole(length, width),
            whole(1, width),
            whole(HEAD, 1),
            whole(HEAD, 1),
            pl.BlockSpec((2, 1, LANES, length), lambda g: (0, g, 0, 0)),
            group_rows,
            group_rows,
            pl.BlockSpec((1, 8, length), lambda g: (g, 0, 0)),
            pl.BlockSpec((1, LANES, width), lambda g: (g, 0, 0)),
            pl.BlockSpec((1, 3, 1, LANES, width), lambda g: (layer, 0, g, 0, 0)),
            whole(length, width),
        ],
        out_specs=[
            pl.BlockSpec((3, 1, LANES, length), lambda g: (0, g, 0, 0)),
            whole(length, width),
            whole(8, width),
            whole(2, HEAD, 128),
        ],
        out_shape=[
            array((3, GROUPS, LANES, length)),
            array((length, width)),
            array((8, width), F32),
            array((2, HEAD, 128), F32),
        ],
        scratch=[pltpu.VMEM((length, length), F32), pltpu.VMEM((length, width), F32)],
    )
    return projected.reshape(3 * width, length), *others


def sends(fine, first, second):
    _, depth, high, wide = fine
    number = lambda c, z, y, x: ((c * depth + z) * high + y) * wide + x
    return [
        (number(c, z, y, x), number(c, *(first, second)[c](z, y, x)))
        for c in range(2)
        for z in range(depth)
        for y in range(high)
        for x in range(wide)
    ]


def next_x(z, y, x):
    return z, y, 1 - x


def next_y(z, y, x):
    return z, 1 - y, x


def sideways(value, fine):
    return lax.ppermute(value, ALL, sends(fine, next_x, next_y))


def turned(value, fine):
    return lax.ppermute(value, ALL, sends(fine, next_y, next_x))


def along(value, fine):
    depth = fine[1]
    return lax.ppermute(
        value, ALL, sends(fine, lambda z, y, x: ((z + 1) % depth, y, x), lambda z, y, x: ((z - 1) % depth, y, x))
    )


def opposite(value, fine):
    depth = fine[1]
    return lax.ppermute(value, "z", [(z, (z + 2) % depth) for z in range(depth)])


def swap(value):
    return lax.ppermute(value, "section", [(0, 1), (1, 0)])


def place():
    return [lax.axis_index(axis) for axis in ALL]


def either(condition, make_first, make_second):
    @pl.when(condition)
    def _():
        make_first().start()

    @pl.when(jnp.logical_not(condition))
    def _():
        make_second().start()


def slot_copy(slot, keep_ref, pass_ref, owner, target, sem, rows=None):
    index = slot % 2 if isinstance(slot, int) else lax.rem(slot, 2)
    view = (lambda ref: ref.at[index]) if rows is None else (lambda ref: ref.at[index, rows])
    kept = pltpu.make_async_copy(view(keep_ref), target, sem)
    either(slot // 2 == owner, lambda: kept, lambda: pltpu.make_async_copy(view(pass_ref), target, sem))
    return kept


def half_of(rows):
    return -(-rows // 32) * 16


def pick_kernel(layer, own_ref, other_ref, *refs):
    extra, (shard_ref, half_ref, sem) = refs[:-3], refs[-3:]
    core = lax.axis_index("section")
    count, rows, half = own_ref.shape[0], shard_ref.shape[0], half_ref.shape[0]
    goal = shard_ref.at[pl.ds(0, count)]
    copy = pltpu.make_async_copy(own_ref, goal, sem)
    either(core == layer, lambda: copy, lambda: pltpu.make_async_copy(other_ref, goal, sem))
    if extra:
        shard_ref[count:] = extra[0][...]
    copy.wait()

    @pl.when(core == 0)
    def _():
        half_ref[...] = shard_ref[:half]

    @pl.when(core == 1)
    def _():
        half_ref[...] = shard_ref[rows - half :]


def pick(layer, own, other, *extra):
    rows, width = own.shape[0] + sum(value.shape[0] for value in extra), own.shape[1]
    return launch(
        functools.partial(pick_kernel, layer), (own, other, *extra), name="pick", micros=1.5,
        in_specs=[ANY] * 2 + [VMEM] * len(extra), out_specs=[VMEM] * 2,
        out_shape=[array((rows, width)), array((half_of(rows), width))],
        scratch=[pltpu.SemaphoreType.DMA],
    )


def line_kernel(own_ref, near_ref, other_ref, far_ref, far_other_ref, keep_ref, pass_ref, line_ref, sems):
    core, z = lax.axis_index("section"), lax.axis_index("z")
    depth = line_ref.shape[0]
    half = far_ref.shape[0]
    below, above, far = lax.rem(z + depth - 1, depth), lax.rem(z + 1, depth), lax.rem(z + 2, depth)
    near_at, other_at = jnp.where(core == 0, below, above), jnp.where(core == 0, above, below)
    rest = own_ref.shape[0] - half
    first, second = pl.multiple_of(core * rest, 16), pl.multiple_of((1 - core) * half, 16)
    skipped = pl.multiple_of((1 - core) * (half - rest), 16)
    copies = [
        pltpu.make_async_copy(own_ref, line_ref.at[z], sems.at[0]),
        pltpu.make_async_copy(near_ref, line_ref.at[near_at], sems.at[1]),
        pltpu.make_async_copy(other_ref, line_ref.at[other_at], sems.at[2]),
        pltpu.make_async_copy(far_ref, line_ref.at[far, pl.ds(first, half)], sems.at[3]),
        pltpu.make_async_copy(far_other_ref.at[pl.ds(skipped, rest)], line_ref.at[far, pl.ds(second, rest)], sems.at[4]),
    ]
    for copy in copies:
        copy.start()
    for copy in copies:
        copy.wait()
    keep_ref[...] = line_ref[pl.ds(2 * core, 2)]
    pass_ref[...] = line_ref[pl.ds(2 - 2 * core, 2)]


def line_of(own, near, near_other, far, far_other):
    rows, width = own.shape
    return launch(
        line_kernel, (own, near, near_other, far, far_other), name="line", micros=2.5,
        in_specs=[ANY] * 5, out_specs=[VMEM] * 2, out_shape=[array((2, rows, width))] * 2,
        scratch=[pltpu.VMEM((4, rows, width), BF16), pltpu.SemaphoreType.DMA((5,))],
    )


def place_kernel(
    line_keep, line_pass, side_keep, side_pass, turn_keep, turn_pass, corner, corner_other, full_ref, sems
):
    core, y, x = lax.axis_index("section"), lax.axis_index("y"), lax.axis_index("x")
    at = pl.program_id(0)
    take = pl.ds(line_keep.shape[1] - full_ref.shape[3], full_ref.shape[3])
    side_y, side_x = jnp.where(core == 0, y, 1 - y), jnp.where(core == 0, 1 - x, x)
    copies = [
        slot_copy(at, line_keep, line_pass, core, full_ref.at[0, y, x], sems.at[0], take),
        slot_copy(at, side_keep, side_pass, core, full_ref.at[0, side_y, side_x], sems.at[1], take),
        slot_copy(at, turn_keep, turn_pass, 1 - core, full_ref.at[0, 1 - side_y, 1 - side_x], sems.at[2], take),
        slot_copy(at, corner_other, corner, core, full_ref.at[0, 1 - y, 1 - x], sems.at[3], take),
    ]
    for copy in copies:
        copy.wait()


def placed(pieces, fine, rows):
    width = pieces[0].shape[-1]
    full = launch(
        place_kernel, pieces, name="place", micros=5, grid=(fine[1],),
        in_specs=[ANY] * 8,
        out_specs=pl.BlockSpec((1, *fine[2:], rows, width), lambda i: (i, 0, 0, 0, 0)),
        out_shape=array((*fine[1:], rows, width)),
        scratch=[pltpu.SemaphoreType.DMA((4,))],
    )
    return full.reshape(-1, width)


def rows_copy(low_ref, high_ref, start, count, target_ref, at, sem, crossing):
    split = low_ref.shape[0]
    goal = target_ref.at[pl.ds(at, count)]
    copy = pltpu.make_async_copy(low_ref.at[pl.ds(0, count)], goal, sem)

    @pl.when(start + count <= split)
    def _():
        pltpu.make_async_copy(low_ref.at[pl.ds(pl.multiple_of(start, 16), count)], goal, sem).start()

    @pl.when(start >= split)
    def _():
        pltpu.make_async_copy(high_ref.at[pl.ds(pl.multiple_of(start - split, 16), count)], goal, sem).start()

    for first in crossing:
        if first < split < first + count:
            low = split - first

            @pl.when(start == first)
            def _():
                pltpu.make_async_copy(low_ref.at[pl.ds(first, low)], target_ref.at[pl.ds(at, low)], sem).start()
                rest = target_ref.at[pl.ds(at + low, count - low)]
                pltpu.make_async_copy(high_ref.at[pl.ds(0, count - low)], rest, sem).start()

    return copy


def partial_kernel(
    fine, own_low, own_high, other_low, other_high, right_ref, right_other_ref,
    turn_ref, keep_ref, pass_ref, near_ref, half_ref, left_ref, sems,
):
    core, z, y, x = place()
    depth, high, wide = fine[1:]
    split = own_low.shape[0]
    rows = keep_ref.shape[1]
    half = half_ref.shape[1]
    step = pl.program_id(0)
    side_y, side_x = jnp.where(core == 0, y, 1 - y), jnp.where(core == 0, 1 - x, x)
    near, far = lax.rem(z + jnp.where(core == 0, 1, depth - 1), depth), lax.rem(z + 2, depth)
    whole_at = (split // rows) * rows
    crossing = (whole_at, whole_at + rows - half)

    def row(slot, line_y, line_x):
        return ((slot * high + line_y) * wide + line_x) * rows

    kept, passed = 2 * core, 2 - 2 * core
    parts = [(row(passed + at, 1 - y, 1 - x), rows) for at in range(2)]
    parts += [(row(kept + at, side_y, side_x), rows) for at in range(2)]
    parts += [(row(passed + at, side_y, side_x), rows) for at in range(2)]
    parts += [(row(near, y, x), rows)]
    parts += [(row(slot, y, x) + core * (rows - half), half) for slot in (z, far)]
    sides = ((own_low, own_high), (other_low, other_high))

    def copies():
        at = 0
        for index, (start, count) in enumerate(parts):
            for side, (low, up) in enumerate(sides):
                yield index, low, up, start, count, left_ref.at[side], at, sems.at[side, index]
            at += count

    @pl.when(step == 0)
    def _():
        for _, *what in copies():
            rows_copy(*what, crossing)

    def wait(indices):
        for index, low, _, _, count, target, at, sem in copies():
            if index in indices:
                pltpu.make_async_copy(low.at[pl.ds(0, count)], target.at[pl.ds(at, count)], sem).wait()

    def product(first, count):
        own = nn(left_ref[0, first : first + count], right_ref[...])
        return (own + nn(left_ref[1, first : first + count], right_other_ref[...])).astype(BF16)

    for at, out in enumerate((turn_ref, keep_ref, pass_ref)):

        @pl.when(step == at)
        def _():
            wait((2 * at, 2 * at + 1))
            out[...] = product(2 * at * rows, 2 * rows).reshape(out.shape)

    @pl.when(step == 3)
    def _():
        wait((6, 7, 8))
        last = product(6 * rows, rows + 2 * half)
        near_ref[...] = last[:rows]
        half_ref[...] = last[rows:].reshape(half_ref.shape)


def partial(fine, own_low, own_high, other_low, other_high, right, right_other):
    length, width = right.shape
    features = own_low.shape[0] + own_high.shape[0]
    rows = features // (fine[1] * fine[2] * fine[3])
    half = half_of(rows)
    shapes = [(2, rows, width)] * 3 + [(rows, width), (2, half, width)]
    return launch(
        functools.partial(partial_kernel, fine), (own_low, own_high, other_low, other_high, right, right_other),
        name="partial", micros=features / 700, grid=(4,),
        in_specs=[ANY] * 4 + [whole(length, width)] * 2,
        out_specs=[whole(*shape) for shape in shapes],
        out_shape=[array(shape) for shape in shapes],
        scratch=[pltpu.VMEM((2, 7 * rows + 2 * half, length), BF16), pltpu.SemaphoreType.DMA((2, 9))],
    )


def depth_kernel(
    near_ref, half_ref, keep_ref, pass_ref, keep_other, pass_other,
    near_out, far_out, own_out, near_got, half_got, sems,
):
    core, z = lax.axis_index("section"), lax.axis_index("z")
    depth = 4
    half = half_ref.shape[1]
    near = lax.rem(z + jnp.where(core == 0, 1, depth - 1), depth)
    part = pl.ds(pl.multiple_of(core * (near_ref.shape[0] - half), 16), half)
    copies = []
    for at, (keep, pass_, owner) in enumerate(((keep_ref, pass_ref, core), (keep_other, pass_other, 1 - core))):
        copies.append(slot_copy(near, keep, pass_, owner, near_got.at[at], sems.at[3 * at]))
        for index, slot in enumerate((z, lax.rem(z + 2, depth))):
            copies.append(slot_copy(slot, keep, pass_, owner, half_got.at[at, index], sems.at[3 * at + 1 + index], part))
    for copy in copies:
        copy.wait()
    near_total = near_ref[...].astype(F32) + near_got[0].astype(F32) + near_got[1].astype(F32)
    near_out[...] = near_total.astype(BF16)
    for index, out in enumerate((own_out, far_out)):
        total = half_ref[index].astype(F32) + half_got[0, index].astype(F32) + half_got[1, index].astype(F32)
        out[...] = total.astype(BF16)


def depth_sums(near, halves, keep, passed, keep_other, passed_other):
    rows, width = near.shape
    half = halves.shape[1]
    return launch(
        depth_kernel, (near, halves, keep, passed, keep_other, passed_other), name="depth", micros=2,
        in_specs=[VMEM] * 2 + [ANY] * 4, out_specs=[VMEM] * 3,
        out_shape=[array((rows, width)), array((half, width)), array((half, width))],
        scratch=[
            pltpu.VMEM((2, rows, width), BF16),
            pltpu.VMEM((2, 2, half, width), BF16),
            pltpu.SemaphoreType.DMA((6,)),
        ],
    )


def total_kernel(near_ref, near_other, far_ref, far_other, own_ref, own_other, *refs):
    second, out_ref = refs[:-1], refs[-1]
    core = lax.axis_index("section")
    rows, half = near_ref.shape[0], far_ref.shape[0]
    near = near_ref[...].astype(F32) + near_other[...].astype(F32)
    mine = far_ref[...].astype(F32) + own_ref[...].astype(F32)
    other = far_other[...].astype(F32) + own_other[...].astype(F32)
    low, high = jnp.where(core == 0, mine, other), jnp.where(core == 0, other, mine)
    out_ref[:half] = near[:half] + low
    out_ref[half:] = near[half:] + high[2 * half - rows :]
    if second:

        @pl.when(core == 1)
        def _():
            out_ref[...] = second[0][...]


def total(near, near_other, far, far_other, own, own_other, *second):
    values = (near, near_other, far, far_other, own, own_other, *second)
    return launch(
        total_kernel, values, name="total", micros=1.5,
        in_specs=[VMEM] * len(values), out_specs=VMEM, out_shape=array(near.shape, F32),
    )


class Order:
    def __init__(self, first):
        self.last = first
        self.moving = []

    def run(self, function, *values):
        values, _ = lax.optimization_barrier((values, self.last))
        return self.fence(function(*values))

    def fence(self, *result):
        due = [value for value, left in self.moving if left == 0]
        self.moving = [(value, left - 1) for value, left in self.moving if left > 0]
        result, self.last, _ = lax.optimization_barrier((result, self.last, due))
        if result:
            self.last = jax.tree.leaves(result)[0]
            return result[0]

    def move(self, way, *values, count=1):
        values, _ = lax.optimization_barrier((values, self.last))
        moved = [way(value) for value in values]
        self.moving += [(value, count - 1) for value in moved]
        return moved if len(values) > 1 else moved[0]

    def swap(self, *values, count=1):
        return self.move(swap, *values, count=count)


def total_along(value, axis, size):
    return sum([lax.ppermute(value, axis, [(i, (i + k) % size) for i in range(size)]) for k in range(1, size)], value)


def total_of(value, fine):
    for axis, size in zip(ALL, fine):
        value = total_along(value, axis, size) if size < 8 else lax.psum(value, axis)
    return value


def added(first, second):
    return (first.astype(F32) + second.astype(F32)).astype(BF16)


class Gather:
    def __init__(self, order, fine, shard, half):
        self.order, self.fine, self.shard, self.half = order, fine, shard, half

    def along(self):
        self.near = self.order.move(functools.partial(along, fine=self.fine), self.shard)
        self.far = self.order.move(functools.partial(opposite, fine=self.fine), self.half)

    def across(self):
        self.near_other, self.far_other = self.order.swap(self.near, self.far)

    def line(self):
        self.keep, self.passed = self.order.run(
            line_of, self.shard, self.near, self.near_other, self.far, self.far_other
        )

    def side(self):
        self.side_passed = self.order.move(functools.partial(sideways, fine=self.fine), self.passed)
        self.side_keep = self.order.move(functools.partial(sideways, fine=self.fine), self.keep)

    def turn(self):
        self.corner = self.order.move(functools.partial(turned, fine=self.fine), self.side_passed)
        self.turn_keep, self.turn_passed = self.order.swap(self.side_keep, self.side_passed)

    def meet(self):
        self.corner_other = self.order.swap(self.corner)

    def place(self):
        pieces = (
            self.keep, self.passed, self.side_keep, self.side_passed, self.turn_keep, self.turn_passed,
            self.corner, self.corner_other,
        )
        return self.order.run(lambda *values: placed(values, self.fine, self.shard.shape[0]), *pieces)


class Scatter:
    def __init__(self, order, fine, values):
        self.order, self.fine = order, fine
        self.turn, self.keep, self.passed, self.near, self.halves = values

    def start(self):
        self.turn = self.order.move(functools.partial(turned, fine=self.fine), self.turn)
        self.keep = self.order.move(functools.partial(sideways, fine=self.fine), self.keep)

    def add(self):
        self.passed = self.order.run(added, self.passed, self.turn)

    def pass_on(self):
        self.passed = self.order.move(functools.partial(sideways, fine=self.fine), self.passed)
        self.keep_other = self.order.swap(self.keep)

    def meet(self):
        self.passed_other = self.order.swap(self.passed)

    def parts(self):
        return self.near, self.halves, self.keep, self.passed, self.keep_other, self.passed_other

    def along(self, values, count=1):
        near, far, self.own = values
        self.near = self.order.move(functools.partial(along, fine=self.fine), near, count=count)
        self.far = self.order.move(functools.partial(opposite, fine=self.fine), far, count=count)
        self.own_other = self.order.swap(self.own)

    def across(self):
        self.near_other, self.far_other = self.order.swap(self.near, self.far)

    def ends(self):
        return self.near, self.near_other, self.far, self.far_other, self.own, self.own_other


def body(fine, inputs, cotangent, lengths, weight_in, weight_out, scales):
    length, width = inputs.shape[2], inputs.shape[3]
    core, z, y, x = place()
    depth = fine[1]
    device = (z * fine[2] + y) * fine[3] + x
    pair = lax.dynamic_index_in_dim(lengths, core, 0, False)
    scale_count = scales.shape[1]
    whole_scales = scale_count * depth * fine[2] * fine[3]
    by_core = lambda first, second: (jnp.where(core == 0, first, second), jnp.where(core == 0, second, first))

    shift = lambda axis: lambda value: lax.ppermute(value, axis, [(0, 1), (1, 0)])
    spread = lambda mine, other: jnp.stack(by_core(mine, other))[None, :, None]
    chip = functools.partial(partial, fine)

    weight_in_all = lax.all_gather(weight_in[0], ALL, axis=0, tiled=True)

    def padded(flat):
        return jnp.pad(flat, (0, -flat.shape[0] % 1024)).reshape(-1, 128)

    own_scales = lax.dynamic_update_slice(
        jnp.zeros((2 * whole_scales,), F32), scales[0].astype(F32), (core * whole_scales + device * scale_count,)
    )
    scale = total_of(padded(own_scales), fine).reshape(-1)[: 2 * whole_scales].reshape(2, whole_scales)
    vectors_0, vectors_1 = [(s[None, :width], s[width : width + HEAD, None], s[width + HEAD :, None]) for s in scale]
    rows_0 = lax.dynamic_index_in_dim(inputs, core, 0, False)[0]
    grad = lax.dynamic_index_in_dim(cotangent, core, 0, False)[0]
    position = lax.broadcasted_iota(jnp.int32, (length, 1), 0)
    grad_1 = jnp.where(position < pair[0, 0] + pair[0, 1], grad, jnp.zeros_like(grad))

    order = Order(grad_1)
    if depth == 4:
        other_out = order.swap(weight_out[0])
        grad_1_other = order.swap(grad_1)
        order.fence()
        first = Gather(order, fine, *order.run(functools.partial(pick, 0), weight_out[0], other_out))
        first.along()
        second = Gather(order, fine, *order.run(functools.partial(pick, 1), weight_out[0], other_out))
        first.across()
        order.fence()
        first.line()
        first.side()
        second.along()
        order.fence()
        first.turn()
        second.across()
        order.fence()
        first.meet()
        second.line()
        second.side()
        weight_out_0 = first.place()
        second.turn()
        order.fence()
        second.meet()
        order.fence()
        weight_out_1 = second.place()
    else:
        weight_out_0, weight_out_1 = jnp.split(lax.all_gather(weight_out[0], ALL, axis=0, tiled=True), 2)
    out = functools.partial(output, pair)
    normed_0, raw_0, value_0, attended_0, logs_0 = order.run(
        functools.partial(attend, 0, pair), rows_0, *vectors_0, weight_in_all
    )
    attended_0_other, normed_0_other = order.swap(attended_0, normed_0)
    hidden_0, slope_0 = order.run(functools.partial(hidden, 0), normed_0, weight_in_all)
    hidden_0_other = order.swap(hidden_0)
    rows_1, squares_0 = order.run(out, rows_0, attended_0, hidden_0, weight_out_0)
    normed_1, raw_1, value_1, attended_1, logs_1 = order.run(
        functools.partial(attend, 1, pair), rows_1, *vectors_1, weight_in_all
    )
    attended_1_other, normed_1_other = order.swap(attended_1, normed_1)
    hidden_1, slope_1 = order.run(functools.partial(hidden, 1), normed_1, weight_in_all)
    back_1, back_0 = functools.partial(attend_back, 1, pair), functools.partial(attend_back, 0, pair)
    kept_1 = (rows_1, grad_1, *vectors_1, raw_1, value_1, attended_1, logs_1, weight_out_1, weight_in_all)

    def small_sums(squares_0, squares_1, gain_0, heads_0, gain_1, heads_1):
        sums = [jnp.sum(squares, axis=(1, 2)) for squares in (squares_0, squares_1)]
        scale_grads = [
            jnp.concatenate([jnp.sum(gain, axis=0), jnp.sum(heads, axis=2).reshape(-1)])
            for gain, heads in ((gain_0, heads_0), (gain_1, heads_1))
        ]
        return padded(jnp.concatenate([jnp.sum(pair).astype(F32)[None], *sums, *scale_grads]))

    if depth == 4:
        hidden_1_other = order.swap(hidden_1)
        feed_1, low_1 = order.run(functools.partial(feed_back, 1), grad_1, slope_1, weight_in_all, weight_out_1)
        low_1_other = order.swap(low_1)
        out_1 = Scatter(order, fine, order.run(
            chip, attended_1, hidden_1, attended_1_other, hidden_1_other, grad_1, grad_1_other
        ))
        out_1.start()
        top_1, grad_0, gain_1, heads_1 = order.run(back_1, *kept_1, feed_1)
        grad_0_other, top_1_other = order.swap(grad_0, top_1, count=2)
        out_1.add()
        out_1.pass_on()
        feed_0, low_0 = order.run(functools.partial(feed_back, 0), grad_0, slope_0, weight_in_all, weight_out_0)
        low_0_other = order.swap(low_0)
        out_1.meet()
        out_0 = Scatter(order, fine, order.run(
            chip, attended_0, hidden_0, attended_0_other, hidden_0_other, grad_0, grad_0_other
        ))
        out_0.start()
        in_1, ends = order.run(
            lambda values, parts: (chip(*values), depth_sums(*parts)),
            (top_1, low_1, top_1_other, low_1_other, normed_1, normed_1_other), out_1.parts(),
        )
        in_1 = Scatter(order, fine, in_1)
        out_0.add()
        out_0.pass_on()
        in_1.start()
        out_1.along(ends)
        kept_0 = (rows_0, grad_0, *vectors_0, raw_0, value_0, attended_0, logs_0, weight_out_0, weight_in_all)
        (top_0, grad_first, gain_0, heads_0), (result_1, squares_1) = order.run(
            lambda kept, late: (back_0(*kept), out(*late)), (*kept_0, feed_0), (rows_1, attended_1, hidden_1, weight_out_1)
        )
        top_0_other = order.swap(top_0, count=2)
        in_1.add()
        in_1.pass_on()
        out_0.meet()
        out_1.across()
        small, (rows_kept, rows_given), (grads_kept, grads_given) = order.run(
            lambda *values: (small_sums(*values[:6]), by_core(*values[6:8]), by_core(*values[8:])),
            squares_0, squares_1, gain_0, heads_0, gain_1, heads_1, rows_1, result_1, grad_first, grad_0,
        )
        in_1.meet()
        in_0, ends = order.run(
            lambda values, parts: (chip(*values), depth_sums(*parts)),
            (top_0, low_0, top_0_other, low_0_other, normed_0, normed_0_other), out_0.parts(),
        )
        in_0 = Scatter(order, fine, in_0)
        in_0.start()
        out_0.along(ends)
        small_other = order.move(shift("x"), small)
        rows_got, grads_got = order.swap(rows_given, grads_given)
        ends, out_grad_1 = order.run(
            lambda parts, sums: (depth_sums(*parts), total(*sums)), in_1.parts(), out_1.ends()
        )
        small = small + small_other
        small_other = order.move(shift("y"), small)
        in_0.add()
        in_0.pass_on()
        in_1.along(ends, count=2)
        out_0.across()
        outputs, input_grads = order.run(lambda *v: (spread(*v[:2]), spread(*v[2:])), rows_kept, rows_got, grads_kept, grads_got)
        in_0.meet()
        out_grad = order.run(total, *out_0.ends(), out_grad_1)
        ends = order.run(depth_sums, *in_0.parts())
        in_0.along(ends)
        in_1.across()
        small = small + small_other
        ring = [
            order.move(lambda v, k=k: lax.ppermute(v, "z", [(i, (i + k) % depth) for i in range(depth)]), small)
            for k in range(1, depth)
        ]
        order.fence()
        in_0.across()
        small = sum(ring, small)
        small_other = order.swap(small)
        in_grad_1 = order.run(total, *in_1.ends())
        in_grad = order.run(total, *in_0.ends(), in_grad_1)[None]
        out_grad = out_grad[None]
        small = small + small_other
    else:
        feed_1, low_1 = order.run(functools.partial(feed_back, 1), grad_1, slope_1, weight_in_all, weight_out_1)
        top_1, grad_0, gain_1, heads_1 = order.run(back_1, *kept_1, feed_1)
        feed_0, low_0 = order.run(functools.partial(feed_back, 0), grad_0, slope_0, weight_in_all, weight_out_0)
        kept_0 = (rows_0, grad_0, *vectors_0, raw_0, value_0, attended_0, logs_0, weight_out_0, weight_in_all)
        top_0, grad_first, gain_0, heads_0 = order.run(back_0, *kept_0, feed_0)
        result_1, squares_1 = order.run(out, rows_1, attended_1, hidden_1, weight_out_1)
        own = lambda low, high, right: nn(jnp.concatenate([low, high]), right).astype(BF16)
        summed = lambda first, second: lax.psum_scatter(
            jnp.concatenate([first, second]), ALL, scatter_dimension=0, tiled=True
        ).astype(F32)[None]
        in_grad = summed(own(top_0, low_0, normed_0), own(top_1, low_1, normed_1))
        out_grad = summed(own(attended_0, hidden_0, grad_0), own(attended_1, hidden_1, grad_1))
        small = small_sums(squares_0, squares_1, gain_0, heads_0, gain_1, heads_1)
        for axis in ALL:
            small = lax.psum(small, axis)
        outputs, input_grads = [
            spread(mine, swap(given)) for mine, given in (by_core(rows_1, result_1), by_core(grad_first, grad_0))
        ]
    small = small.reshape(-1)
    statistics = jnp.sqrt(lax.dynamic_slice(small, (1 + 3 * core,), (3,)) / (small[0] * width))
    scale_grad = lax.dynamic_slice(small, (7 + core * whole_scales + device * scale_count,), (scale_count,))
    return outputs, input_grads, in_grad, out_grad, scale_grad[None], statistics[None]


def solution(mesh):
    count = mesh.shape["dp"]
    fine = Mesh(mesh.devices.reshape(2, count // 4, 2, 2), ALL)
    return jax.shard_map(
        functools.partial(body, (2, count // 4, 2, 2)),
        mesh=fine,
        in_specs=(
            P(None, DP, None, None),
            P(None, DP, None, None),
            P(None, DP, None),
            P("section", DP, None),
            P("section", DP, None),
            P("section", DP),
        ),
        out_specs=(
            P("section", None, DP, None, None),
            P("section", None, DP, None, None),
            P("section", DP, None),
            P("section", DP, None),
            P("section", DP),
            P("section", None),
        ),
        check_vma=False,
    )
```

time: 759 us -> 546 us (0.72)
  Pallas kernels: 0 us -> 209 us
  matrix products: 155 us -> 0 us
  other arithmetic: 129 us -> 11.9 us
  waiting for transfers between devices: 304 us -> 187 us
  blocking collectives: 103 us -> 0 us
  starting transfers between devices: 0.67 us -> 94.6 us
  local copies, waits for them, and re-layouts: 42 us -> 20.5 us
    pallas_call x0 -> x28, Pallas kernels: none -> 209 us  [launch(): pl.pallas_call(kernel, grid=grid, in_specs=in_specs, out_specs=out_specs,...]
    ppermute x2 -> x87, waiting for transfers between devices: 0.01 us -> 187 us  [the longest x6 83.5 us: opposite(): lax.ppermute(value, 'z', [(z, (z + 2) % depth) for z in range(depth)])]
    all_gather x2 -> x1, waiting for transfers between devices: 151 us -> 0.02 us  [body(): weight_in_all = lax.all_gather(weight_in[0], ALL, axis=0, tiled=True)]
    reduce_scatter x2 -> x0, waiting for transfers between devices: 151 us -> none  [body(): lax.psum_scatter(jnp.concatenate(pieces, axis=0), ALL, scatter_dimension=...]
    dot_general x24 -> x0, matrix products: 137 us -> none  [the longest x14 91.2 us: dot(): lax.dot_general(left, right, (contract, ((), ())), preferred_element_type...]
    ppermute x2 -> x87, starting transfers between devices: 0.51 us -> 94.5 us  [the longest x46 40.2 us: swap(): return lax.ppermute(value, 'section', [(0, 1), (1, 0)])]
    unnamed x2 -> x0, blocking collectives: 81 us -> none
    another operation x11 -> x2, other arithmetic: 38.2 us -> 0.21 us  [body(): spread = lambda mine, other: jnp.stack(by_core(mine, other))[None, :, None]]
  transfers between devices with their start and end apart: 6 -> 88, of which waited for: 3 -> 31; matrix products, arithmetic and copies ran while one was open for 19% -> 3% of each run, Pallas kernels for 0% -> 33%
where the time goes in v2:
time: 546 us; the launch traced here: 541 us
  Pallas kernels  209 us (38%)
  waiting for transfers between devices  187 us (34%)
  starting transfers between devices  94.6 us (17%)
  local copies, waits for them, and re-layouts  20.5 us (4%)
  between operations  18 us (3%)
  other arithmetic  11.9 us (2%)
    pallas_call x28, Pallas kernels, launch(): pl.pallas_call(kernel, grid=grid, in_specs=in_specs, out_specs=out_specs,...  209 us
    ppermute x6, waiting for transfers between devices, opposite(): lax.ppermute(value, 'z', [(z, (z + 2) % depth) for z in range(depth)])  83.5 us
    ppermute x46, starting transfers between devices, swap(): return lax.ppermute(value, 'section', [(0, 1), (1, 0)])  40.2 us
    ppermute x12, waiting for transfers between devices, sideways(): return lax.ppermute(value, ALL, sends(fine, next_x, next_y))  37.4 us
    ppermute x2, waiting for transfers between devices, body(): lax.ppermute(value, axis, [(0, 1), (1, 0)])  24.2 us
    ppermute x46, waiting for transfers between devices, swap(): return lax.ppermute(value, 'section', [(0, 1), (1, 0)])  13.7 us
    ppermute x12, starting transfers between devices, sideways(): return lax.ppermute(value, ALL, sends(fine, next_x, next_y))  13.5 us
    ppermute x6, waiting for transfers between devices, total_along(): lax.ppermute(value, axis, [(i, (i + k) % size) for i in range(size)])  13.2 us
  transfers between devices with their start and end apart: 88, of which 31 were waited for; matrix products, arithmetic and copies ran while one was open for 3% of the time, Pallas kernels for 33%

profile of v2, /device:TPU:0, one launch (start us, length us, event | category | flops | bytes accessed | tf_op | source)
XLA Modules:
  0.0 541.1 jit_solution(18221946268348358917)
XLA Ops:
  13.0 2.6 collective-permute-done.6.other_ref
  16.3 2.0 pick.2
  18.4 3.0 collective-permute-start.8
  21.4 2.6 collective-permute-start.9
  24.0 1.8 pick.3
  25.8 21.9 %collective-permute-done.9.far_ref = bf16[128,768]{1,0:T(8,128)(2,1)S(1)} collective-permute-done((bf16[128,768]{1,0:T(8,128)(2,1)}, bf16[128,768]{1,0:T(8,128)(2,1)S(1)}, u32[]{:S(2)}, u32[]{:S(2)}) %collective-permute-start.9) | collective-permute-done | bytes 196640 | tf_op jit(solution)/shard_map/ppermute | solution.py:401
  47.7 3.4 collective-permute-start.10
  54.1 2.7 line.2
  59.9 3.6 collective-permute-start.13
  63.5 22.3 %collective-permute-done.13.far_ref = bf16[128,768]{1,0:T(8,128)(2,1)S(1)} collective-permute-done((bf16[128,768]{1,0:T(8,128)(2,1)S(1)}, bf16[128,768]{1,0:T(8,128)(2,1)S(1)}, u32[]{:S(2)}, u32[]{:S(2)}) %collective-permute-start.13) | collective-permute-done | bytes 196640 | tf_op jit(solution)/shard_map/ppermute | solution.py:401
  85.9 1.9 collective-permute-done.14.side_pass
  89.2 8.5 %collective-permute-start.19 = (bf16[2,240,768]{2,1,0:T(8,128)(2,1)S(1)}, bf16[2,240,768]{2,1,0:T(8,128)(2,1)S(1)}, u32[]{:S(2)}, u32[]{:S(2)}) collective-permute-start(bf16[2,240,768]{2,1,0:T(8,128)(2,1)S(1)} %collective-permute-done.15.side_keep), channel_id=1, source_target_pairs={{0,16},{16,0},{1,17},{17,1},{2,18},{18,2},{3,19},{19,3},{4,20},{20... | collective-permute-start | bytes 2211848 | tf_op jit(solution)/shard_map/ppermute | solution.py:405
  98.2 4.0 collective-permute-done.17.far_other_ref
  102.3 15.9 %collective-permute-start.21 = (bf16[2,240,768]{2,1,0:T(8,128)(2,1)S(1)}, bf16[2,240,768]{2,1,0:T(8,128)(2,1)S(1)}, u32[]{:S(2)}, u32[]{:S(2)}) collective-permute-start(bf16[2,240,768]{2,1,0:T(8,128)(2,1)S(1)} %collective-permute-done.18.corner), channel_id=1, source_target_pairs={{0,16},{16,0},{1,17},{17,1},{2,18},{18,2},{3,19},{19,3},{4,20},{20... | collective-permute-start | bytes 2211848 | tf_op jit(solution)/shard_map/ppermute | solution.py:405
  118.2 2.6 line.3
  121.7 2.6 collective-permute-start.22
  124.4 8.1 %place.2 = bf16[4,2,2,240,768]{4,3,2,1,0:T(8,128)(2,1)} custom-call(bf16[2,240,768]{2,1,0:T(8,128)(2,1)} %get-tuple-element.481.line_keep, bf16[2,240,768]{2,1,0:T(8,128)(2,1)} %get-tuple-element.482.line_pass, bf16[2,240,768]{2,1,0:T(8,128)(2,1)} %copy-done.31, bf16[2,240,768]{2,1,0:T(8,128)(2,1)} %copy-done.32, bf16[2,240,768]{2,1,0:T(8,128)(2,1)} %copy-done.37, ...), custom_call_target="tpu_custom_call" | custom-call | flops 5750000128 | bytes 5000000 | tf_op jit(solution)/shard_map/place/pallas_call | solution.py:40
  132.5 11.9 %collective-permute-done.22.side_keep = bf16[2,240,768]{2,1,0:T(8,128)(2,1)S(1)} collective-permute-done((bf16[2,240,768]{2,1,0:T(8,128)(2,1)}, bf16[2,240,768]{2,1,0:T(8,128)(2,1)S(1)}, u32[]{:S(2)}, u32[]{:S(2)}) %collective-permute-start.22) | collective-permute-done | bytes 737312 | tf_op jit(solution)/shard_map/ppermute | solution.py:385
  144.4 7.9 %collective-permute-done.23.side_pass = bf16[2,240,768]{2,1,0:T(8,128)(2,1)S(1)} collective-permute-done((bf16[2,240,768]{2,1,0:T(8,128)(2,1)}, bf16[2,240,768]{2,1,0:T(8,128)(2,1)S(1)}, u32[]{:S(2)}, u32[]{:S(2)}) %collective-permute-start.23) | collective-permute-done | bytes 737312 | tf_op jit(solution)/shard_map/ppermute | solution.py:385
  154.4 2.2 collective-permute-done
  156.6 2.2 collective-permute-start.3
  158.9 2.3 collective-permute-done.2
  161.2 5.4 %collective-permute-done.1 = f32[16,128]{1,0:T(8,128)S(1)} collective-permute-done((f32[16,128]{1,0:T(8,128)S(1)}, f32[16,128]{1,0:T(8,128)S(1)}, u32[]{:S(2)}, u32[]{:S(2)}) %collective-permute-start.1) | collective-permute-done | bytes 8224 | tf_op jit(solution)/shard_map/ppermute | solution.py:721
  168.2 2.2 collective-permute-done.4
  177.3 8.5 %place.3 = bf16[4,2,2,240,768]{4,3,2,1,0:T(8,128)(2,1)} custom-call(bf16[2,240,768]{2,1,0:T(8,128)(2,1)} %get-tuple-element.496.line_keep, bf16[2,240,768]{2,1,0:T(8,128)(2,1)} %get-tuple-element.497.line_pass, bf16[2,240,768]{2,1,0:T(8,128)(2,1)} %copy-done.28, bf16[2,240,768]{2,1,0:T(8,128)(2,1)} %copy-done.29, bf16[2,240,768]{2,1,0:T(8,128)(2,1)} %copy-done.33, ...), custom_call_target="tpu_custom_call" | custom-call | flops 5750000128 | bytes 5000000 | tf_op jit(solution)/shard_map/place/pallas_call | solution.py:40
  187.2 12.4 %attend.2 = (bf16[512,768]{1,0:T(8,128)(2,1)}, f32[2,3,256,512]{3,2,1,0:T(8,128)}, bf16[768,512]{1,0:T(8,128)(2,1)}, bf16[768,512]{1,0:T(8,128)(2,1)}, f32[3,8,512]{2,1,0:T(8,128)}) custom-call(s32[1,2]{1,0:T(1,128)} %copy-done.13, bf16[512,768]{1,0:T(8,128)(2,1)} %dynamic-slice_bitcast_fusion.rows_ref, f32[1,768]{1,0:T(1,128)} %get-tuple-element.665.gain_ref, ...), custom_call_target="tpu_custom_call" | custom-call | flops 13799999488 | bytes 12000000 | tf_op jit(solution)/shard_map/attend/pallas_call | solution.py:40
  200.2 8.4 %hidden.2 = (bf16[3072,512]{1,0:T(8,128)(2,1)}, bf16[3072,512]{1,0:T(8,128)(2,1)}) custom-call(bf16[512,768]{1,0:T(8,128)(2,1)} %get-tuple-element.734.normed_ref.right_ref, bf16[10752,768]{1,0:T(8,128)(2,1)} %bitcast.79), custom_call_target="tpu_custom_call" | custom-call | flops 9200000000 | bytes 8000000 | tf_op jit(solution)/shard_map/hidden/pallas_call | solution.py:40
  208.9 9.5 %output.2 = (bf16[512,768]{1,0:T(8,128)(2,1)}, f32[3,8,768]{2,1,0:T(8,128)}) custom-call(s32[1,2]{1,0:T(1,128)} %copy-done.13, bf16[512,768]{1,0:T(8,128)(2,1)} %dynamic-slice_bitcast_fusion.rows_ref, bf16[768,512]{1,0:T(8,128)(2,1)} %get-tuple-element.670.attended_ref.own_low, bf16[3072,512]{1,0:T(8,128)(2,1)} %get-tuple-element.619.hidden_ref.own_high, ...), custom_call_target="tpu_custom_call" | custom-call | flops 10350000128 | bytes 9000000 | tf_op jit(solution)/shard_map/output/pallas_call | solution.py:40
  219.8 12.4 %attend.3 = (bf16[512,768]{1,0:T(8,128)(2,1)}, f32[2,3,256,512]{3,2,1,0:T(8,128)}, bf16[768,512]{1,0:T(8,128)(2,1)}, bf16[768,512]{1,0:T(8,128)(2,1)}, f32[3,8,512]{2,1,0:T(8,128)}) custom-call(s32[1,2]{1,0:T(1,128)} %copy-done.13, bf16[512,768]{1,0:T(8,128)(2,1)} %get-tuple-element.714.rows_ref, f32[1,768]{1,0:T(1,128)} %get-tuple-element.580.gain_ref, ...), custom_call_target="tpu_custom_call" | custom-call | flops 13799999488 | bytes 12000000 | tf_op jit(solution)/shard_map/attend/pallas_call | solution.py:40
  232.7 8.4 %hidden.3 = (bf16[3072,512]{1,0:T(8,128)(2,1)}, bf16[3072,512]{1,0:T(8,128)(2,1)}) custom-call(bf16[512,768]{1,0:T(8,128)(2,1)} %get-tuple-element.641.normed_ref.right_ref, bf16[10752,768]{1,0:T(8,128)(2,1)} %bitcast.81), custom_call_target="tpu_custom_call" | custom-call | flops 9200000000 | bytes 8000000 | tf_op jit(solution)/shard_map/hidden/pallas_call | solution.py:40
  241.4 12.1 %feed_back.2 = (f32[512,768]{1,0:T(8,128)}, bf16[3072,512]{1,0:T(8,128)(2,1)}) custom-call(bf16[512,768]{1,0:T(8,128)(2,1)} %copy-done.4, bf16[3072,512]{1,0:T(8,128)(2,1)} %get-tuple-element.557.slope_ref, bf16[10752,768]{1,0:T(8,128)(2,1)} %bitcast.82, bf16[3840,768]{1,0:T(8,128)(2,1)} %bitcast.94), custom_call_target="tpu_custom_call" | custom-call | flops 12650000384 | bytes 11000000 | tf_op jit(solution)/shard_map/feed_back/pallas_call | solution.py:40
  255.2 8.4 %partial.4 = (bf16[2,240,768]{2,1,0:T(8,128)(2,1)}, bf16[2,240,768]{2,1,0:T(8,128)(2,1)}, bf16[2,240,768]{2,1,0:T(8,128)(2,1)}, bf16[240,768]{1,0:T(8,128)(2,1)}, bf16[2,128,768]{2,1,0:T(8,128)(2,1)}) custom-call(bf16[768,512]{1,0:T(8,128)(2,1)} %get-tuple-element.680.own_low.attended_ref, bf16[3072,512]{1,0:T(8,128)(2,1)} %get-tuple-element.681.own_high.hidden_ref, ...), custom_call_target="tpu_custom_call" | custom-call | flops 6308571648 | bytes 5485714 | tf_op jit(solution)/shard_map/partial/pallas_call | solution.py:40
  268.0 17.5 %attend_back.2 = (bf16[3,3,256,512]{3,2,1,0:T(8,128)(2,1)}, bf16[512,768]{1,0:T(8,128)(2,1)}, f32[8,768]{1,0:T(8,128)}, f32[2,64,128]{2,1,0:T(8,128)}) custom-call(s32[1,2]{1,0:T(1,128)} %copy-done.13, bf16[512,768]{1,0:T(8,128)(2,1)} %get-tuple-element.714.rows_ref, bf16[512,768]{1,0:T(8,128)(2,1)} %copy-done.4, f32[1,768]{1,0:T(1,128)} %get-tuple-element.580.gain_ref, ...), custom_call_target="tpu_custom_call" | custom-call | flops 19549999104 | bytes 17000000 | tf_op jit(solution)/shard_map/attend_back/pallas_call | solution.py:40
  286.9 11.8 %feed_back.3 = (f32[512,768]{1,0:T(8,128)}, bf16[3072,512]{1,0:T(8,128)(2,1)}) custom-call(bf16[512,768]{1,0:T(8,128)(2,1)} %get-tuple-element.717.grad_ref.right_ref, bf16[3072,512]{1,0:T(8,128)(2,1)} %get-tuple-element.608.slope_ref, bf16[10752,768]{1,0:T(8,128)(2,1)} %bitcast.84, bf16[3840,768]{1,0:T(8,128)(2,1)} %bitcast.92), custom_call_target="tpu_custom_call" | custom-call | flops 12650000384 | bytes 11000000 | tf_op jit(solution)/shard_map/feed_back/pallas_call | solution.py:40
  300.4 8.8 %partial.5 = (bf16[2,240,768]{2,1,0:T(8,128)(2,1)}, bf16[2,240,768]{2,1,0:T(8,128)(2,1)}, bf16[2,240,768]{2,1,0:T(8,128)(2,1)}, bf16[240,768]{1,0:T(8,128)(2,1)}, bf16[2,128,768]{2,1,0:T(8,128)(2,1)}) custom-call(bf16[768,512]{1,0:T(8,128)(2,1)} %get-tuple-element.670.attended_ref.own_low, bf16[3072,512]{1,0:T(8,128)(2,1)} %get-tuple-element.619.hidden_ref.own_high, ...), custom_call_target="tpu_custom_call" | custom-call | flops 6308571648 | bytes 5485714 | tf_op jit(solution)/shard_map/partial/pallas_call | solution.py:40
  309.3 1.7 copy-done.14
  313.2 3.5 depth.4
  316.8 10.1 %partial.6 = (bf16[2,336,768]{2,1,0:T(8,128)(2,1)}, bf16[2,336,768]{2,1,0:T(8,128)(2,1)}, bf16[2,336,768]{2,1,0:T(8,128)(2,1)}, bf16[336,768]{1,0:T(8,128)(2,1)}, bf16[2,176,768]{2,1,0:T(8,128)(2,1)}) custom-call(bf16[2304,512]{1,0:T(8,128)(2,1)} %bitcast.87, bf16[3072,512]{1,0:T(8,128)(2,1)} %get-tuple-element.638.own_high, bf16[2304,512]{1,0:T(8,128)(2,1)} %copy-done.16, ...), custom_call_target="tpu_custom_call" | custom-call | flops 8832000000 | bytes 7680000 | tf_op jit(solution)/shard_map/partial/pallas_call | solution.py:40
  326.9 3.4 collective-permute-done.43
  334.4 17.5 %attend_back.3 = (bf16[3,3,256,512]{3,2,1,0:T(8,128)(2,1)}, bf16[512,768]{1,0:T(8,128)(2,1)}, f32[8,768]{1,0:T(8,128)}, f32[2,64,128]{2,1,0:T(8,128)}) custom-call(s32[1,2]{1,0:T(1,128)} %copy-done.13, bf16[512,768]{1,0:T(8,128)(2,1)} %dynamic-slice_bitcast_fusion.rows_ref, bf16[512,768]{1,0:T(8,128)(2,1)} %get-tuple-element.717.grad_ref.right_ref, ...), custom_call_target="tpu_custom_call" | custom-call | flops 19549999104 | bytes 17000000 | tf_op jit(solution)/shard_map/attend_back/pallas_call | solution.py:40
  354.2 9.2 %output.3 = (bf16[512,768]{1,0:T(8,128)(2,1)}, f32[3,8,768]{2,1,0:T(8,128)}) custom-call(s32[1,2]{1,0:T(1,128)} %copy-done.13, bf16[512,768]{1,0:T(8,128)(2,1)} %get-tuple-element.714.rows_ref, bf16[768,512]{1,0:T(8,128)(2,1)} %get-tuple-element.680.own_low.attended_ref, bf16[3072,512]{1,0:T(8,128)(2,1)} %get-tuple-element.681.own_high.hidden_ref, ...), custom_call_target="tpu_custom_call" | custom-call | flops 10350000128 | bytes 9000000 | tf_op jit(solution)/shard_map/output/pallas_call | solution.py:40
  376.0 5.1 collective-permute-done.53.pass_ref
  381.1 3.6 depth.5
  384.7 10.2 %partial.7 = (bf16[2,336,768]{2,1,0:T(8,128)(2,1)}, bf16[2,336,768]{2,1,0:T(8,128)(2,1)}, bf16[2,336,768]{2,1,0:T(8,128)(2,1)}, bf16[336,768]{1,0:T(8,128)(2,1)}, bf16[2,176,768]{2,1,0:T(8,128)(2,1)}) custom-call(bf16[2304,512]{1,0:T(8,128)(2,1)} %bitcast.24.own_low, bf16[3072,512]{1,0:T(8,128)(2,1)} %get-tuple-element.731.own_high, ...), custom_call_target="tpu_custom_call" | custom-call | flops 8832000000 | bytes 7680000 | tf_op jit(solution)/shard_map/partial/pallas_call | solution.py:40
  398.6 22.0 %collective-permute-done.66 = f32[16,128]{1,0:T(8,128)S(1)} collective-permute-done((f32[16,128]{1,0:T(8,128)S(1)}, f32[16,128]{1,0:T(8,128)S(1)}, u32[]{:S(2)}, u32[]{:S(2)}) %collective-permute-start.66) | collective-permute-done | bytes 8224 | tf_op jit(solution)/shard_map/ppermute | solution.py:814
  422.1 2.7 collective-permute-start.64
  424.8 9.4 %collective-permute-done.64.far_ref = bf16[128,768]{1,0:T(8,128)(2,1)S(1)} collective-permute-done((bf16[128,768]{1,0:T(8,128)(2,1)S(1)}, bf16[128,768]{1,0:T(8,128)(2,1)S(1)}, u32[]{:S(2)}, u32[]{:S(2)}) %collective-permute-start.64) | collective-permute-done | bytes 196640 | tf_op jit(solution)/shard_map/ppermute | solution.py:401
  434.2 2.5 total.4.refs_0_
  436.7 4.0 depth.6
  440.7 3.2 collective-permute-done.63.near_ref
  445.5 2.2 collective-permute-done.67
  452.5 9.8 %collective-permute-done.68.pass_ref = bf16[2,336,768]{2,1,0:T(8,128)(2,1)S(1)} collective-permute-done((bf16[2,336,768]{2,1,0:T(8,128)(2,1)S(1)}, bf16[2,336,768]{2,1,0:T(8,128)(2,1)S(1)}, u32[]{:S(2)}, u32[]{:S(2)}) %collective-permute-start.68) | collective-permute-done | bytes 1032224 | tf_op jit(solution)/shard_map/ppermute | solution.py:385
  462.4 1.8 collective-permute-start.74
  464.2 2.1 collective-permute-start.75
  466.3 2.7 total.5
  469.0 16.5 %collective-permute-done.75.far_ref = bf16[176,768]{1,0:T(8,128)(2,1)S(1)} collective-permute-done((bf16[176,768]{1,0:T(8,128)(2,1)S(1)}, bf16[176,768]{1,0:T(8,128)(2,1)S(1)}, u32[]{:S(2)}, u32[]{:S(2)}) %collective-permute-start.75) | collective-permute-done | bytes 270368 | tf_op jit(solution)/shard_map/ppermute | solution.py:401
  486.4 3.9 depth.7
  490.4 2.7 collective-permute-start.76
  494.2 1.8 collective-permute-start.83
  498.5 6.8 %collective-permute-done.83 = f32[16,128]{1,0:T(8,128)S(1)} collective-permute-done((f32[16,128]{1,0:T(8,128)S(1)}, f32[16,128]{1,0:T(8,128)S(1)}, u32[]{:S(2)}, u32[]{:S(2)}) %collective-permute-start.83) | collective-permute-done | bytes 8224 | tf_op jit(solution)/shard_map/ppermute | solution.py:953
  505.3 3.0 collective-permute-start.80
  510.1 13.4 %collective-permute-done.77.far_ref = bf16[176,768]{1,0:T(8,128)(2,1)S(1)} collective-permute-done((bf16[176,768]{1,0:T(8,128)(2,1)}, bf16[176,768]{1,0:T(8,128)(2,1)S(1)}, u32[]{:S(2)}, u32[]{:S(2)}) %collective-permute-start.77) | collective-permute-done | bytes 270368 | tf_op jit(solution)/shard_map/ppermute | solution.py:401
  524.3 2.8 total.6.refs_0_
  531.0 3.1 total.7
  (365 shorter events, 80.5 us)
Async XLA Ops:
  7.2 178.6 %all-gather.3.cloned.1.call-start = ((), (), s32[]{:S(2)}) async-start(), calls=%async_computation | async-start | bytes 17031168 | tf_op jit(solution)/shard_map/all_gather | solution.py:818
  18.4 29.3 %collective-permute-start.8 = (bf16[240,768]{1,0:T(8,128)(2,1)}, bf16[240,768]{1,0:T(8,128)(2,1)S(1)}, u32[]{:S(2)}, u32[]{:S(2)}) collective-permute-start(bf16[240,768]{1,0:T(8,128)(2,1)} %get-tuple-element.448.own_ref), channel_id=1, source_target_pairs={{0,4},{1,5},{2,6},{3,7},{4,8},{5,9},{6,10},{7,11},{8,12},{9,13},{1... | collective-permute-start | bytes 1105928 | tf_op jit(solution)/shard_map/ppermute | solution.py:394
  21.4 26.3 %collective-permute-start.9 = (bf16[128,768]{1,0:T(8,128)(2,1)}, bf16[128,768]{1,0:T(8,128)(2,1)S(1)}, u32[]{:S(2)}, u32[]{:S(2)}) collective-permute-start(bf16[128,768]{1,0:T(8,128)(2,1)} %get-tuple-element.443), channel_id=1, source_target_pairs={{0,8},{4,12},{8,0},{12,4},{1,9},{5,13},{9,1},{13,5},{2,10},{6,14},... | collective-permute-start | bytes 589832 | tf_op jit(solution)/shard_map/ppermute | solution.py:401
  56.8 29.0 %collective-permute-start.15 = (bf16[2,240,768]{2,1,0:T(8,128)(2,1)}, bf16[2,240,768]{2,1,0:T(8,128)(2,1)S(1)}, u32[]{:S(2)}, u32[]{:S(2)}) collective-permute-start(bf16[2,240,768]{2,1,0:T(8,128)(2,1)} %get-tuple-element.481.line_keep), channel_id=1, source_target_pairs={{0,1},{1,0},{2,3},{3,2},{4,5},{5,4},{6,7},{7,6},{8,9},{9,8},{10,11... | collective-permute-start | bytes 2211848 | tf_op jit(solution)/shard_map/ppermute | solution.py:385
  58.2 29.5 %collective-permute-start.14 = (bf16[2,240,768]{2,1,0:T(8,128)(2,1)}, bf16[2,240,768]{2,1,0:T(8,128)(2,1)S(1)}, u32[]{:S(2)}, u32[]{:S(2)}) collective-permute-start(bf16[2,240,768]{2,1,0:T(8,128)(2,1)} %get-tuple-element.482.line_pass), channel_id=1, source_target_pairs={{0,1},{1,0},{2,3},{3,2},{4,5},{5,4},{6,7},{7,6},{8,9},{9,8},{10,11... | collective-permute-start | bytes 2211848 | tf_op jit(solution)/shard_map/ppermute | solution.py:385
  58.9 26.9 %collective-permute-start.12 = (bf16[240,768]{1,0:T(8,128)(2,1)S(1)}, bf16[240,768]{1,0:T(8,128)(2,1)S(1)}, u32[]{:S(2)}, u32[]{:S(2)}) collective-permute-start(bf16[240,768]{1,0:T(8,128)(2,1)S(1)} %copy-done.54), channel_id=1, source_target_pairs={{0,4},{1,5},{2,6},{3,7},{4,8},{5,9},{6,10},{7,11},{8,12},{9,13},{1... | collective-permute-start | bytes 1105928 | tf_op jit(solution)/shard_map/ppermute | solution.py:394
  59.9 26.0 %collective-permute-start.13 = (bf16[128,768]{1,0:T(8,128)(2,1)S(1)}, bf16[128,768]{1,0:T(8,128)(2,1)S(1)}, u32[]{:S(2)}, u32[]{:S(2)}) collective-permute-start(bf16[128,768]{1,0:T(8,128)(2,1)S(1)} %copy-done.81), channel_id=1, source_target_pairs={{0,8},{4,12},{8,0},{12,4},{1,9},{5,13},{9,1},{13,5},{2,10},{6,14},... | collective-permute-start | bytes 589832 | tf_op jit(solution)/shard_map/ppermute | solution.py:401
  87.7 14.5 %collective-permute-start.18 = (bf16[2,240,768]{2,1,0:T(8,128)(2,1)S(1)}, bf16[2,240,768]{2,1,0:T(8,128)(2,1)S(1)}, u32[]{:S(2)}, u32[]{:S(2)}) collective-permute-start(bf16[2,240,768]{2,1,0:T(8,128)(2,1)S(1)} %collective-permute-done.14.side_pass), channel_id=1, source_target_pairs={{0,2},{1,3},{2,0},{3,1},{4,6},{5,7},{6,4},{7,5},{8,10},{9,11},{10,... | collective-permute-start | bytes 2211848 | tf_op jit(solution)/shard_map/ppermute | solution.py:389
  89.2 13.0 %collective-permute-start.19 = (bf16[2,240,768]{2,1,0:T(8,128)(2,1)S(1)}, bf16[2,240,768]{2,1,0:T(8,128)(2,1)S(1)}, u32[]{:S(2)}, u32[]{:S(2)}) collective-permute-start(bf16[2,240,768]{2,1,0:T(8,128)(2,1)S(1)} %collective-permute-done.15.side_keep), channel_id=1, source_target_pairs={{0,16},{16,0},{1,17},{17,1},{2,18},{18,2},{3,19},{19,3},{4,20},{20... | collective-permute-start | bytes 2211848 | tf_op jit(solution)/shard_map/ppermute | solution.py:405
  102.3 18.6 %collective-permute-start.21 = (bf16[2,240,768]{2,1,0:T(8,128)(2,1)S(1)}, bf16[2,240,768]{2,1,0:T(8,128)(2,1)S(1)}, u32[]{:S(2)}, u32[]{:S(2)}) collective-permute-start(bf16[2,240,768]{2,1,0:T(8,128)(2,1)S(1)} %collective-permute-done.18.corner), channel_id=1, source_target_pairs={{0,16},{16,0},{1,17},{17,1},{2,18},{18,2},{3,19},{19,3},{4,20},{20... | collective-permute-start | bytes 2211848 | tf_op jit(solution)/shard_map/ppermute | solution.py:405
  121.7 22.6 %collective-permute-start.22 = (bf16[2,240,768]{2,1,0:T(8,128)(2,1)}, bf16[2,240,768]{2,1,0:T(8,128)(2,1)S(1)}, u32[]{:S(2)}, u32[]{:S(2)}) collective-permute-start(bf16[2,240,768]{2,1,0:T(8,128)(2,1)} %get-tuple-element.496.line_keep), channel_id=1, source_target_pairs={{0,1},{1,0},{2,3},{3,2},{4,5},{5,4},{6,7},{7,6},{8,9},{9,8},{10,11... | collective-permute-start | bytes 2211848 | tf_op jit(solution)/shard_map/ppermute | solution.py:385
  124.3 27.9 %collective-permute-start.23 = (bf16[2,240,768]{2,1,0:T(8,128)(2,1)}, bf16[2,240,768]{2,1,0:T(8,128)(2,1)S(1)}, u32[]{:S(2)}, u32[]{:S(2)}) collective-permute-start(bf16[2,240,768]{2,1,0:T(8,128)(2,1)} %get-tuple-element.497.line_pass), channel_id=1, source_target_pairs={{0,1},{1,0},{2,3},{3,2},{4,5},{5,4},{6,7},{7,6},{8,9},{9,8},{10,11... | collective-permute-start | bytes 2211848 | tf_op jit(solution)/shard_map/ppermute | solution.py:385
  152.3 21.7 %collective-permute-start.24 = (bf16[2,240,768]{2,1,0:T(8,128)(2,1)S(1)}, bf16[2,240,768]{2,1,0:T(8,128)(2,1)S(1)}, u32[]{:S(2)}, u32[]{:S(2)}) collective-permute-start(bf16[2,240,768]{2,1,0:T(8,128)(2,1)S(1)} %collective-permute-done.22.side_keep), channel_id=1, source_target_pairs={{0,16},{16,0},{1,17},{17,1},{2,18},{18,2},{3,19},{19,3},{4,20},{20... | collective-permute-start | bytes 2211848 | tf_op jit(solution)/shard_map/ppermute | solution.py:405
  152.3 21.7 %collective-permute-start.25 = (bf16[2,240,768]{2,1,0:T(8,128)(2,1)S(1)}, bf16[2,240,768]{2,1,0:T(8,128)(2,1)S(1)}, u32[]{:S(2)}, u32[]{:S(2)}) collective-permute-start(bf16[2,240,768]{2,1,0:T(8,128)(2,1)S(1)} %collective-permute-done.23.side_pass), channel_id=1, source_target_pairs={{0,16},{16,0},{1,17},{17,1},{2,18},{18,2},{3,19},{19,3},{4,20},{20... | collective-permute-start | bytes 2211848 | tf_op jit(solution)/shard_map/ppermute | solution.py:405
  152.8 21.3 %collective-permute-start.26 = (bf16[2,240,768]{2,1,0:T(8,128)(2,1)S(1)}, bf16[2,240,768]{2,1,0:T(8,128)(2,1)S(1)}, u32[]{:S(2)}, u32[]{:S(2)}) collective-permute-start(bf16[2,240,768]{2,1,0:T(8,128)(2,1)S(1)} %collective-permute-done.23.side_pass), channel_id=1, source_target_pairs={{0,2},{1,3},{2,0},{3,1},{4,6},{5,7},{6,4},{7,5},{8,10},{9,11},{10,... | collective-permute-start | bytes 2211848 | tf_op jit(solution)/shard_map/ppermute | solution.py:389
  161.2 5.4 %collective-permute-start.1 = (f32[16,128]{1,0:T(8,128)S(1)}, f32[16,128]{1,0:T(8,128)S(1)}, u32[]{:S(2)}, u32[]{:S(2)}) collective-permute-start(f32[16,128]{1,0:T(8,128)S(1)} %fusion.2), channel_id=1, source_target_pairs={{0,4},{4,8},{8,12},{12,0},{1,5},{5,9},{9,13},{13,1},{2,6},{6,10},{... | collective-permute-start | bytes 24584 | tf_op jit(solution)/shard_map/ppermute | solution.py:721
  199.6 9.0 %collective-permute-start.28 = (bf16[768,512]{1,0:T(8,128)(2,1)}, bf16[768,512]{1,0:T(8,128)(2,1)S(1)}, u32[]{:S(2)}, u32[]{:S(2)}) collective-permute-start(bf16[768,512]{1,0:T(8,128)(2,1)} %get-tuple-element.670.attended_ref.own_low), channel_id=1, source_target_pairs={{0,16},{16,0},{1,17},{17,1},{2,18},{18,2},{3,19},{19,3},{4,20},{20... | collective-permute-start | bytes 2359304 | tf_op jit(solution)/shard_map/ppermute | solution.py:405
  199.8 8.8 %collective-permute-start.29 = (bf16[512,768]{1,0:T(8,128)(2,1)}, bf16[512,768]{1,0:T(8,128)(2,1)S(1)}, u32[]{:S(2)}, u32[]{:S(2)}) collective-permute-start(bf16[512,768]{1,0:T(8,128)(2,1)} %get-tuple-element.734.normed_ref.right_ref), channel_id=1, source_target_pairs={{0,16},{16,0},{1,17},{17,1},{2,18},{18,2},{3,19},{19,3},{4,20},{20... | collective-permute-start | bytes 2359304 | tf_op jit(solution)/shard_map/ppermute | solution.py:405
  208.6 9.8 %collective-permute-start.30 = (bf16[3072,512]{1,0:T(8,128)(2,1)}, bf16[3072,512]{1,0:T(8,128)(2,1)}, u32[]{:S(2)}, u32[]{:S(2)}) collective-permute-start(bf16[3072,512]{1,0:T(8,128)(2,1)} %get-tuple-element.619.hidden_ref.own_high), channel_id=1, source_target_pairs={{0,16},{16,0},{1,17},{17,1},{2,18},{18,2},{3,19},{19,3},{4,20},{20... | collective-permute-start | bytes 9437192 | tf_op jit(solution)/shard_map/ppermute | solution.py:405
  232.2 9.0 %collective-permute-start.31 = (bf16[768,512]{1,0:T(8,128)(2,1)}, bf16[768,512]{1,0:T(8,128)(2,1)S(1)}, u32[]{:S(2)}, u32[]{:S(2)}) collective-permute-start(bf16[768,512]{1,0:T(8,128)(2,1)} %get-tuple-element.680.own_low.attended_ref), channel_id=1, source_target_pairs={{0,16},{16,0},{1,17},{17,1},{2,18},{18,2},{3,19},{19,3},{4,20},{20... | collective-permute-start | bytes 2359304 | tf_op jit(solution)/shard_map/ppermute | solution.py:405
  232.3 8.8 %collective-permute-start.32 = (bf16[512,768]{1,0:T(8,128)(2,1)}, bf16[512,768]{1,0:T(8,128)(2,1)S(1)}, u32[]{:S(2)}, u32[]{:S(2)}) collective-permute-start(bf16[512,768]{1,0:T(8,128)(2,1)} %get-tuple-element.641.normed_ref.right_ref), channel_id=1, source_target_pairs={{0,16},{16,0},{1,17},{17,1},{2,18},{18,2},{3,19},{19,3},{4,20},{20... | collective-permute-start | bytes 2359304 | tf_op jit(solution)/shard_map/ppermute | solution.py:405
  241.2 12.3 %collective-permute-start.33 = (bf16[3072,512]{1,0:T(8,128)(2,1)}, bf16[3072,512]{1,0:T(8,128)(2,1)S(1)}, u32[]{:S(2)}, u32[]{:S(2)}) collective-permute-start(bf16[3072,512]{1,0:T(8,128)(2,1)} %get-tuple-element.681.own_high.hidden_ref), channel_id=1, source_target_pairs={{0,16},{16,0},{1,17},{17,1},{2,18},{18,2},{3,19},{19,3},{4,20},{20... | collective-permute-start | bytes 9437192 | tf_op jit(solution)/shard_map/ppermute | solution.py:405
  253.5 10.1 %collective-permute-start.34 = (bf16[3072,512]{1,0:T(8,128)(2,1)}, bf16[3072,512]{1,0:T(8,128)(2,1)}, u32[]{:S(2)}, u32[]{:S(2)}) collective-permute-start(bf16[3072,512]{1,0:T(8,128)(2,1)} %get-tuple-element.638.own_high), channel_id=1, source_target_pairs={{0,16},{16,0},{1,17},{17,1},{2,18},{18,2},{3,19},{19,3},{4,20},{20... | collective-permute-start | bytes 9437192 | tf_op jit(solution)/shard_map/ppermute | solution.py:405
  265.0 20.5 %collective-permute-start.35 = (bf16[2,240,768]{2,1,0:T(8,128)(2,1)}, bf16[2,240,768]{2,1,0:T(8,128)(2,1)S(1)}, u32[]{:S(2)}, u32[]{:S(2)}) collective-permute-start(bf16[2,240,768]{2,1,0:T(8,128)(2,1)} %get-tuple-element.594), channel_id=1, source_target_pairs={{0,2},{1,3},{2,0},{3,1},{4,6},{5,7},{6,4},{7,5},{8,10},{9,11},{10,... | collective-permute-start | bytes 2211848 | tf_op jit(solution)/shard_map/ppermute | solution.py:389
  266.5 19.0 %collective-permute-start.36 = (bf16[2,240,768]{2,1,0:T(8,128)(2,1)}, bf16[2,240,768]{2,1,0:T(8,128)(2,1)S(1)}, u32[]{:S(2)}, u32[]{:S(2)}) collective-permute-start(bf16[2,240,768]{2,1,0:T(8,128)(2,1)} %get-tuple-element.596), channel_id=1, source_target_pairs={{0,1},{1,0},{2,3},{3,2},{4,5},{5,4},{6,7},{7,6},{8,9},{9,8},{10,11... | collective-permute-start | bytes 2211848 | tf_op jit(solution)/shard_map/ppermute | solution.py:385
  285.5 13.3 %collective-permute-start.38 = (bf16[2304,512]{1,0:T(8,128)(2,1)}, bf16[2304,512]{1,0:T(8,128)(2,1)S(1)}, u32[]{:S(2)}, u32[]{:S(2)}) collective-permute-start(bf16[2304,512]{1,0:T(8,128)(2,1)} %bitcast.86), channel_id=1, source_target_pairs={{0,16},{16,0},{1,17},{17,1},{2,18},{18,2},{3,19},{19,3},{4,20},{20... | collective-permute-start | bytes 7077896 | tf_op jit(solution)/shard_map/ppermute | solution.py:405
  285.8 13.0 %collective-permute-start.39 = (bf16[2,240,768]{2,1,0:T(8,128)(2,1)S(1)}, bf16[2,240,768]{2,1,0:T(8,128)(2,1)S(1)}, u32[]{:S(2)}, u32[]{:S(2)}) collective-permute-start(bf16[2,240,768]{2,1,0:T(8,128)(2,1)S(1)} %add_convert_fusion.3), channel_id=1, source_target_pairs={{0,1},{1,0},{2,3},{3,2},{4,5},{5,4},{6,7},{7,6},{8,9},{9,8},{10,11... | collective-permute-start | bytes 2211848 | tf_op jit(solution)/shard_map/ppermute | solution.py:385
  286.4 12.4 %collective-permute-start.40 = (bf16[2,240,768]{2,1,0:T(8,128)(2,1)S(1)}, bf16[2,240,768]{2,1,0:T(8,128)(2,1)S(1)}, u32[]{:S(2)}, u32[]{:S(2)}) collective-permute-start(bf16[2,240,768]{2,1,0:T(8,128)(2,1)S(1)} %collective-permute-done.36.keep_ref), channel_id=1, source_target_pairs={{0,16},{16,0},{1,17},{17,1},{2,18},{18,2},{3,19},{19,3},{4,20},{20... | collective-permute-start | bytes 2211848 | tf_op jit(solution)/shard_map/ppermute | solution.py:405
  286.9 11.9 %collective-permute-start.37 = (bf16[512,768]{1,0:T(8,128)(2,1)S(1)}, bf16[512,768]{1,0:T(8,128)(2,1)S(1)}, u32[]{:S(2)}, u32[]{:S(2)}) collective-permute-start(bf16[512,768]{1,0:T(8,128)(2,1)S(1)} %copy-done.6), channel_id=1, source_target_pairs={{0,16},{16,0},{1,17},{17,1},{2,18},{18,2},{3,19},{19,3},{4,20},{20... | collective-permute-start | bytes 2359304 | tf_op jit(solution)/shard_map/ppermute | solution.py:405
  299.9 9.4 %collective-permute-start.41 = (bf16[3072,512]{1,0:T(8,128)(2,1)}, bf16[3072,512]{1,0:T(8,128)(2,1)S(1)}, u32[]{:S(2)}, u32[]{:S(2)}) collective-permute-start(bf16[3072,512]{1,0:T(8,128)(2,1)} %get-tuple-element.731.own_high), channel_id=1, source_target_pairs={{0,16},{16,0},{1,17},{17,1},{2,18},{18,2},{3,19},{19,3},{4,20},{20... | collective-permute-start | bytes 9437192 | tf_op jit(solution)/shard_map/ppermute | solution.py:405
  300.4 8.9 %collective-permute-start.42 = (bf16[2,240,768]{2,1,0:T(8,128)(2,1)}, bf16[2,240,768]{2,1,0:T(8,128)(2,1)S(1)}, u32[]{:S(2)}, u32[]{:S(2)}) collective-permute-start(bf16[2,240,768]{2,1,0:T(8,128)(2,1)} %copy-done.41), channel_id=1, source_target_pairs={{0,16},{16,0},{1,17},{17,1},{2,18},{18,2},{3,19},{19,3},{4,20},{20... | collective-permute-start | bytes 2211848 | tf_op jit(solution)/shard_map/ppermute | solution.py:405
  311.0 19.3 %collective-permute-start.43 = (bf16[2,240,768]{2,1,0:T(8,128)(2,1)}, bf16[2,240,768]{2,1,0:T(8,128)(2,1)S(1)}, u32[]{:S(2)}, u32[]{:S(2)}) collective-permute-start(bf16[2,240,768]{2,1,0:T(8,128)(2,1)} %get-tuple-element.634), channel_id=1, source_target_pairs={{0,2},{1,3},{2,0},{3,1},{4,6},{5,7},{6,4},{7,5},{8,10},{9,11},{10,... | collective-permute-start | bytes 2211848 | tf_op jit(solution)/shard_map/ppermute | solution.py:389
  312.2 18.2 %collective-permute-start.44 = (bf16[2,240,768]{2,1,0:T(8,128)(2,1)}, bf16[2,240,768]{2,1,0:T(8,128)(2,1)}, u32[]{:S(2)}, u32[]{:S(2)}) collective-permute-start(bf16[2,240,768]{2,1,0:T(8,128)(2,1)} %get-tuple-element.658), channel_id=1, source_target_pairs={{0,1},{1,0},{2,3},{3,2},{4,5},{5,4},{6,7},{7,6},{8,9},{9,8},{10,11... | collective-permute-start | bytes 2211848 | tf_op jit(solution)/shard_map/ppermute | solution.py:385
  332.0 20.8 %collective-permute-start.50 = (bf16[128,768]{1,0:T(8,128)(2,1)S(1)}, bf16[128,768]{1,0:T(8,128)(2,1)S(1)}, u32[]{:S(2)}, u32[]{:S(2)}) collective-permute-start(bf16[128,768]{1,0:T(8,128)(2,1)S(1)} %copy-done.77), channel_id=1, source_target_pairs={{0,8},{4,12},{8,0},{12,4},{1,9},{5,13},{9,1},{13,5},{2,10},{6,14},... | collective-permute-start | bytes 589832 | tf_op jit(solution)/shard_map/ppermute | solution.py:401
  332.0 22.2 %collective-permute-start.51 = (bf16[128,768]{1,0:T(8,128)(2,1)S(1)}, bf16[128,768]{1,0:T(8,128)(2,1)}, u32[]{:S(2)}, u32[]{:S(2)}) collective-permute-start(bf16[128,768]{1,0:T(8,128)(2,1)S(1)} %copy-done.71), channel_id=1, source_target_pairs={{0,16},{16,0},{1,17},{17,1},{2,18},{18,2},{3,19},{19,3},{4,20},{20... | collective-permute-start | bytes 589832 | tf_op jit(solution)/shard_map/ppermute | solution.py:405
  332.2 33.3 %collective-permute-start.47 = (bf16[2,336,768]{2,1,0:T(8,128)(2,1)}, bf16[2,336,768]{2,1,0:T(8,128)(2,1)S(1)}, u32[]{:S(2)}, u32[]{:S(2)}) collective-permute-start(bf16[2,336,768]{2,1,0:T(8,128)(2,1)} %get-tuple-element.687), channel_id=1, source_target_pairs={{0,2},{1,3},{2,0},{3,1},{4,6},{5,7},{6,4},{7,5},{8,10},{9,11},{10,... | collective-permute-start | bytes 3096584 | tf_op jit(solution)/shard_map/ppermute | solution.py:389
  333.3 32.1 %collective-permute-start.48 = (bf16[2,336,768]{2,1,0:T(8,128)(2,1)S(1)}, bf16[2,336,768]{2,1,0:T(8,128)(2,1)}, u32[]{:S(2)}, u32[]{:S(2)}) collective-permute-start(bf16[2,336,768]{2,1,0:T(8,128)(2,1)S(1)} %copy-done.17), channel_id=1, source_target_pairs={{0,1},{1,0},{2,3},{3,2},{4,5},{5,4},{6,7},{7,6},{8,9},{9,8},{10,11... | collective-permute-start | bytes 3096584 | tf_op jit(solution)/shard_map/ppermute | solution.py:385
  351.9 12.8 %collective-permute-start.49 = (bf16[240,768]{1,0:T(8,128)(2,1)S(1)}, bf16[240,768]{1,0:T(8,128)(2,1)S(1)}, u32[]{:S(2)}, u32[]{:S(2)}) collective-permute-start(bf16[240,768]{1,0:T(8,128)(2,1)S(1)} %copy-done.55), channel_id=1, source_target_pairs={{0,4},{1,5},{2,6},{3,7},{4,8},{5,9},{6,10},{7,11},{8,12},{9,13},{1... | collective-permute-start | bytes 1105928 | tf_op jit(solution)/shard_map/ppermute | solution.py:394
  352.8 12.7 %collective-permute-start.45 = (bf16[2,240,768]{2,1,0:T(8,128)(2,1)S(1)}, bf16[2,240,768]{2,1,0:T(8,128)(2,1)}, u32[]{:S(2)}, u32[]{:S(2)}) collective-permute-start(bf16[2,240,768]{2,1,0:T(8,128)(2,1)S(1)} %add_convert_fusion.2), channel_id=1, source_target_pairs={{0,1},{1,0},{2,3},{3,2},{4,5},{5,4},{6,7},{7,6},{8,9},{9,8},{10,11... | collective-permute-start | bytes 2211848 | tf_op jit(solution)/shard_map/ppermute | solution.py:385
  354.2 11.3 %collective-permute-start.46 = (bf16[2,240,768]{2,1,0:T(8,128)(2,1)}, bf16[2,240,768]{2,1,0:T(8,128)(2,1)S(1)}, u32[]{:S(2)}, u32[]{:S(2)}) collective-permute-start(bf16[2,240,768]{2,1,0:T(8,128)(2,1)} %collective-permute-done.44.keep_ref), channel_id=1, source_target_pairs={{0,16},{16,0},{1,17},{17,1},{2,18},{18,2},{3,19},{19,3},{4,20},{20... | collective-permute-start | bytes 2211848 | tf_op jit(solution)/shard_map/ppermute | solution.py:405
  365.5 15.6 %collective-permute-start.52 = (bf16[2304,512]{1,0:T(8,128)(2,1)}, bf16[2304,512]{1,0:T(8,128)(2,1)}, u32[]{:S(2)}, u32[]{:S(2)}) collective-permute-start(bf16[2304,512]{1,0:T(8,128)(2,1)} %bitcast.24.own_low), channel_id=1, source_target_pairs={{0,16},{16,0},{1,17},{17,1},{2,18},{18,2},{3,19},{19,3},{4,20},{20... | collective-permute-start | bytes 7077896 | tf_op jit(solution)/shard_map/ppermute | solution.py:405
  366.3 14.8 %collective-permute-start.53 = (bf16[2,336,768]{2,1,0:T(8,128)(2,1)S(1)}, bf16[2,336,768]{2,1,0:T(8,128)(2,1)}, u32[]{:S(2)}, u32[]{:S(2)}) collective-permute-start(bf16[2,336,768]{2,1,0:T(8,128)(2,1)S(1)} %add_convert_fusion.1), channel_id=1, source_target_pairs={{0,1},{1,0},{2,3},{3,2},{4,5},{5,4},{6,7},{7,6},{8,9},{9,8},{10,11... | collective-permute-start | bytes 3096584 | tf_op jit(solution)/shard_map/ppermute | solution.py:385
  367.5 13.6 %collective-permute-start.54 = (bf16[2,336,768]{2,1,0:T(8,128)(2,1)}, bf16[2,336,768]{2,1,0:T(8,128)(2,1)}, u32[]{:S(2)}, u32[]{:S(2)}) collective-permute-start(bf16[2,336,768]{2,1,0:T(8,128)(2,1)} %collective-permute-done.48.keep_ref), channel_id=1, source_target_pairs={{0,16},{16,0},{1,17},{17,1},{2,18},{18,2},{3,19},{19,3},{4,20},{20... | collective-permute-start | bytes 3096584 | tf_op jit(solution)/shard_map/ppermute | solution.py:405
  367.5 8.5 %collective-permute-start.55 = (bf16[2,240,768]{2,1,0:T(8,128)(2,1)}, bf16[2,240,768]{2,1,0:T(8,128)(2,1)}, u32[]{:S(2)}, u32[]{:S(2)}) collective-permute-start(bf16[2,240,768]{2,1,0:T(8,128)(2,1)} %collective-permute-done.45.pass_ref), channel_id=1, source_target_pairs={{0,16},{16,0},{1,17},{17,1},{2,18},{18,2},{3,19},{19,3},{4,20},{20... | collective-permute-start | bytes 2211848 | tf_op jit(solution)/shard_map/ppermute | solution.py:405
  381.1 13.8 %collective-permute-start.58 = (bf16[2,336,768]{2,1,0:T(8,128)(2,1)}, bf16[2,336,768]{2,1,0:T(8,128)(2,1)S(1)}, u32[]{:S(2)}, u32[]{:S(2)}) collective-permute-start(bf16[2,336,768]{2,1,0:T(8,128)(2,1)} %collective-permute-done.53.pass_ref), channel_id=1, source_target_pairs={{0,16},{16,0},{1,17},{17,1},{2,18},{18,2},{3,19},{19,3},{4,20},{20... | collective-permute-start | bytes 3096584 | tf_op jit(solution)/shard_map/ppermute | solution.py:405
  394.9 49.0 %collective-permute-start.61 = (bf16[2,336,768]{2,1,0:T(8,128)(2,1)}, bf16[2,336,768]{2,1,0:T(8,128)(2,1)S(1)}, u32[]{:S(2)}, u32[]{:S(2)}) collective-permute-start(bf16[2,336,768]{2,1,0:T(8,128)(2,1)} %get-tuple-element.756), channel_id=1, source_target_pairs={{0,2},{1,3},{2,0},{3,1},{4,6},{5,7},{6,4},{7,5},{8,10},{9,11},{10,... | collective-permute-start | bytes 3096584 | tf_op jit(solution)/shard_map/ppermute | solution.py:389
  396.1 47.9 %collective-permute-start.62 = (bf16[2,336,768]{2,1,0:T(8,128)(2,1)}, bf16[2,336,768]{2,1,0:T(8,128)(2,1)}, u32[]{:S(2)}, u32[]{:S(2)}) collective-permute-start(bf16[2,336,768]{2,1,0:T(8,128)(2,1)} %get-tuple-element.775), channel_id=1, source_target_pairs={{0,1},{1,0},{2,3},{3,2},{4,5},{5,4},{6,7},{7,6},{8,9},{9,8},{10,11... | collective-permute-start | bytes 3096584 | tf_op jit(solution)/shard_map/ppermute | solution.py:385
  397.1 46.8 %collective-permute-start.59 = (bf16[512,768]{1,0:T(8,128)(2,1)S(1)}, bf16[512,768]{1,0:T(8,128)(2,1)S(1)}, u32[]{:S(2)}, u32[]{:S(2)}) collective-permute-start(bf16[512,768]{1,0:T(8,128)(2,1)S(1)} %get-tuple-element.752), channel_id=1, source_target_pairs={{0,16},{16,0},{1,17},{17,1},{2,18},{18,2},{3,19},{19,3},{4,20},{20... | collective-permute-start | bytes 2359304 | tf_op jit(solution)/shard_map/ppermute | solution.py:405
  397.2 46.8 %collective-permute-start.60 = (bf16[512,768]{1,0:T(8,128)(2,1)S(1)}, bf16[512,768]{1,0:T(8,128)(2,1)S(1)}, u32[]{:S(2)}, u32[]{:S(2)}) collective-permute-start(bf16[512,768]{1,0:T(8,128)(2,1)S(1)} %get-tuple-element.754), channel_id=1, source_target_pairs={{0,16},{16,0},{1,17},{17,1},{2,18},{18,2},{3,19},{19,3},{4,20},{20... | collective-permute-start | bytes 2359304 | tf_op jit(solution)/shard_map/ppermute | solution.py:405
  397.7 23.0 %collective-permute-start.66 = (f32[16,128]{1,0:T(8,128)S(1)}, f32[16,128]{1,0:T(8,128)S(1)}, u32[]{:S(2)}, u32[]{:S(2)}) collective-permute-start(f32[16,128]{1,0:T(8,128)S(1)} %pad_bitcast_fusion), channel_id=1, source_target_pairs={{0,1},{1,0},{2,3},{3,2},{4,5},{5,4},{6,7},{7,6},{8,9},{9,8},{10,11... | collective-permute-start | bytes 24584 | tf_op jit(solution)/shard_map/ppermute | solution.py:814
  422.1 12.1 %collective-permute-start.64 = (bf16[128,768]{1,0:T(8,128)(2,1)S(1)}, bf16[128,768]{1,0:T(8,128)(2,1)S(1)}, u32[]{:S(2)}, u32[]{:S(2)}) collective-permute-start(bf16[128,768]{1,0:T(8,128)(2,1)S(1)} %copy-done.79), channel_id=1, source_target_pairs={{0,8},{4,12},{8,0},{12,4},{1,9},{5,13},{9,1},{13,5},{2,10},{6,14},... | collective-permute-start | bytes 589832 | tf_op jit(solution)/shard_map/ppermute | solution.py:401
  434.2 9.8 %collective-permute-start.63 = (bf16[240,768]{1,0:T(8,128)(2,1)S(1)}, bf16[240,768]{1,0:T(8,128)(2,1)S(1)}, u32[]{:S(2)}, u32[]{:S(2)}) collective-permute-start(bf16[240,768]{1,0:T(8,128)(2,1)S(1)} %copy-done.56), channel_id=1, source_target_pairs={{0,4},{1,5},{2,6},{3,7},{4,8},{5,9},{6,10},{7,11},{8,12},{9,13},{1... | collective-permute-start | bytes 1105928 | tf_op jit(solution)/shard_map/ppermute | solution.py:394
  447.7 14.6 %collective-permute-start.68 = (bf16[2,336,768]{2,1,0:T(8,128)(2,1)S(1)}, bf16[2,336,768]{2,1,0:T(8,128)(2,1)S(1)}, u32[]{:S(2)}, u32[]{:S(2)}) collective-permute-start(bf16[2,336,768]{2,1,0:T(8,128)(2,1)S(1)} %add_convert_fusion), channel_id=1, source_target_pairs={{0,1},{1,0},{2,3},{3,2},{4,5},{5,4},{6,7},{7,6},{8,9},{9,8},{10,11... | collective-permute-start | bytes 3096584 | tf_op jit(solution)/shard_map/ppermute | solution.py:385
  448.7 13.7 %collective-permute-start.69 = (bf16[2,336,768]{2,1,0:T(8,128)(2,1)}, bf16[2,336,768]{2,1,0:T(8,128)(2,1)S(1)}, u32[]{:S(2)}, u32[]{:S(2)}) collective-permute-start(bf16[2,336,768]{2,1,0:T(8,128)(2,1)} %collective-permute-done.62.keep_ref), channel_id=1, source_target_pairs={{0,16},{16,0},{1,17},{17,1},{2,18},{18,2},{3,19},{19,3},{4,20},{20... | collective-permute-start | bytes 3096584 | tf_op jit(solution)/shard_map/ppermute | solution.py:405
  462.3 23.1 %collective-permute-start.73 = (bf16[2,336,768]{2,1,0:T(8,128)(2,1)S(1)}, bf16[2,336,768]{2,1,0:T(8,128)(2,1)S(1)}, u32[]{:S(2)}, u32[]{:S(2)}) collective-permute-start(bf16[2,336,768]{2,1,0:T(8,128)(2,1)S(1)} %collective-permute-done.68.pass_ref), channel_id=1, source_target_pairs={{0,16},{16,0},{1,17},{17,1},{2,18},{18,2},{3,19},{19,3},{4,20},{20... | collective-permute-start | bytes 3096584 | tf_op jit(solution)/shard_map/ppermute | solution.py:405
  462.4 23.0 %collective-permute-start.74 = (bf16[336,768]{1,0:T(8,128)(2,1)S(1)}, bf16[336,768]{1,0:T(8,128)(2,1)S(1)}, u32[]{:S(2)}, u32[]{:S(2)}) collective-permute-start(bf16[336,768]{1,0:T(8,128)(2,1)S(1)} %copy-done.47), channel_id=1, source_target_pairs={{0,4},{1,5},{2,6},{3,7},{4,8},{5,9},{6,10},{7,11},{8,12},{9,13},{1... | collective-permute-start | bytes 1548296 | tf_op jit(solution)/shard_map/ppermute | solution.py:394
  464.2 21.2 %collective-permute-start.75 = (bf16[176,768]{1,0:T(8,128)(2,1)S(1)}, bf16[176,768]{1,0:T(8,128)(2,1)S(1)}, u32[]{:S(2)}, u32[]{:S(2)}) collective-permute-start(bf16[176,768]{1,0:T(8,128)(2,1)S(1)} %copy-done.66), channel_id=1, source_target_pairs={{0,8},{4,12},{8,0},{12,4},{1,9},{5,13},{9,1},{13,5},{2,10},{6,14},... | collective-permute-start | bytes 811016 | tf_op jit(solution)/shard_map/ppermute | solution.py:401
  490.4 33.2 %collective-permute-start.76 = (bf16[336,768]{1,0:T(8,128)(2,1)}, bf16[336,768]{1,0:T(8,128)(2,1)S(1)}, u32[]{:S(2)}, u32[]{:S(2)}) collective-permute-start(bf16[336,768]{1,0:T(8,128)(2,1)} %get-tuple-element.833), channel_id=1, source_target_pairs={{0,4},{1,5},{2,6},{3,7},{4,8},{5,9},{6,10},{7,11},{8,12},{9,13},{1... | collective-permute-start | bytes 1548296 | tf_op jit(solution)/shard_map/ppermute | solution.py:394
  493.1 30.4 %collective-permute-start.79 = (bf16[336,768]{1,0:T(8,128)(2,1)S(1)}, bf16[336,768]{1,0:T(8,128)(2,1)S(1)}, u32[]{:S(2)}, u32[]{:S(2)}) collective-permute-start(bf16[336,768]{1,0:T(8,128)(2,1)S(1)} %collective-permute-done.74.near_ref), channel_id=1, source_target_pairs={{0,16},{16,0},{1,17},{17,1},{2,18},{18,2},{3,19},{19,3},{4,20},{20... | collective-permute-start | bytes 1548296 | tf_op jit(solution)/shard_map/ppermute | solution.py:405
  494.2 11.1 %collective-permute-start.83 = (f32[16,128]{1,0:T(8,128)S(1)}, f32[16,128]{1,0:T(8,128)S(1)}, u32[]{:S(2)}, u32[]{:S(2)}) collective-permute-start(f32[16,128]{1,0:T(8,128)S(1)} %add.106), channel_id=1, source_target_pairs={{0,12},{4,0},{8,4},{12,8},{1,13},{5,1},{9,5},{13,9},{2,14},{6,2},{... | collective-permute-start | bytes 24584 | tf_op jit(solution)/shard_map/ppermute | solution.py:953
  496.1 12.3 %collective-permute-start.82 = (f32[16,128]{1,0:T(8,128)S(1)}, f32[16,128]{1,0:T(8,128)S(1)}, u32[]{:S(2)}, u32[]{:S(2)}) collective-permute-start(f32[16,128]{1,0:T(8,128)S(1)} %add.106), channel_id=1, source_target_pairs={{0,8},{4,12},{8,0},{12,4},{1,9},{5,13},{9,1},{13,5},{2,10},{6,14},... | collective-permute-start | bytes 24584 | tf_op jit(solution)/shard_map/ppermute | solution.py:953
  497.3 11.0 %collective-permute-start.81 = (f32[16,128]{1,0:T(8,128)S(1)}, f32[16,128]{1,0:T(8,128)S(1)}, u32[]{:S(2)}, u32[]{:S(2)}) collective-permute-start(f32[16,128]{1,0:T(8,128)S(1)} %add.106), channel_id=1, source_target_pairs={{0,4},{4,8},{8,12},{12,0},{1,5},{5,9},{9,13},{13,1},{2,6},{6,10},{... | collective-permute-start | bytes 24584 | tf_op jit(solution)/shard_map/ppermute | solution.py:953
  508.4 15.2 %collective-permute-start.77 = (bf16[176,768]{1,0:T(8,128)(2,1)}, bf16[176,768]{1,0:T(8,128)(2,1)S(1)}, u32[]{:S(2)}, u32[]{:S(2)}) collective-permute-start(bf16[176,768]{1,0:T(8,128)(2,1)} %get-tuple-element.827), channel_id=1, source_target_pairs={{0,8},{4,12},{8,0},{12,4},{1,9},{5,13},{9,1},{13,5},{2,10},{6,14},... | collective-permute-start | bytes 811016 | tf_op jit(solution)/shard_map/ppermute | solution.py:401
  523.7 5.8 %collective-permute-start.85 = (bf16[176,768]{1,0:T(8,128)(2,1)S(1)}, bf16[176,768]{1,0:T(8,128)(2,1)S(1)}, u32[]{:S(2)}, u32[]{:S(2)}) collective-permute-start(bf16[176,768]{1,0:T(8,128)(2,1)S(1)} %collective-permute-done.77.far_ref), channel_id=1, source_target_pairs={{0,16},{16,0},{1,17},{17,1},{2,18},{18,2},{3,19},{19,3},{4,20},{20... | collective-permute-start | bytes 811016 | tf_op jit(solution)/shard_map/ppermute | solution.py:405
  (110 other events, 1139.7 us)
Sparse Core Ops, SparseCore 0:
  10.9 152.6 all-gather.2

commit v3 on v2

--- a/solution.py
+++ b/solution.py
@@ -94,19 +94,26 @@
     return pl.BlockSpec(shape, lambda *_: (0,) * len(shape))
 
 
-def attend_kernel(
-    pair_ref, rows_ref, gain_ref, query_scale_ref, key_scale_ref, weight_ref,
-    normed_ref, raw_ref, value_ref, attended_ref, log_ref, bias_ref,
-):
-    @pl.when(pl.program_id(0) == 0)
+def attend_kernel(in_rows, pair_ref, rows_ref, gain_ref, query_scale_ref, key_scale_ref, *refs):
+    step = pl.program_id(0)
+    if in_rows is None:
+        weight_ref, normed_ref, raw_ref, value_ref, attended_ref, log_ref, bias_ref = refs
+        weight = weight_ref[...].reshape(3 * LANES, rows_ref.shape[1])
+    else:
+        pieces, refs = refs[:8], refs[8:]
+        normed_ref, raw_ref, value_ref, attended_ref, log_ref, full_ref, bias_ref, weight_ref, sems, full_sems = refs
+        load_weight(step, pieces, weight_ref, sems, in_rows, full_ref, full_sems, (0, 0, 1, 1))
+        starts = [pl.multiple_of(rows_ref.shape[1] * third + LANES * step, LANES) for third in range(3)]
+        weight = jnp.concatenate([weight_ref[pl.ds(start, LANES)] for start in starts])
+
+    @pl.when(step == 0)
     def _():
         normal, _ = row_norm(rows_ref[...].astype(F32))
         normed_ref[...] = (normal * gain_ref[...]).astype(BF16)
         fill_bias(pair_ref, bias_ref)
 
     normed = normed_ref[...]
-    width = normed.shape[1]
-    projected = nt(weight_ref[...].reshape(3 * LANES, width), normed)
+    projected = nt(weight, normed)
     raw_ref[...] = projected[: 2 * LANES].reshape(raw_ref.shape)
     value_ref[...] = projected[2 * LANES :].astype(BF16)
     for head in range(GROUP):
@@ -123,13 +130,17 @@
         log_ref[0, head : head + 1, :] = peak + jnp.log(total)
 
 
-def attend(layer, pair, rows, gain, query_scale, key_scale, weight_in):
+def attend(in_rows, pair, rows, gain, query_scale, key_scale, *weights):
     length, width = rows.shape
+    gathered = in_rows is not None
+    features = 16 * in_rows if gathered else weights[0].shape[0]
+    if not gathered:
+        weights = (weights[0].reshape(-1, GROUPS, LANES, width),)
     return launch(
-        attend_kernel,
-        (pair, rows, gain, query_scale, key_scale, weight_in.reshape(2, -1, GROUPS, LANES, width)),
+        functools.partial(attend_kernel, in_rows),
+        (pair, rows, gain, query_scale, key_scale, *weights),
         name="attend",
-        micros=12,
+        micros=13,
         grid=(GROUPS,),
         in_specs=[
             pl.BlockSpec(memory_space=pltpu.SMEM),
@@ -137,7 +148,7 @@
             whole(1, width),
             whole(HEAD, 1),
             whole(HEAD, 1),
-            pl.BlockSpec((1, 3, 1, LANES, width), lambda g: (layer, 0, g, 0, 0)),
+            *([ANY] * 8 if gathered else [pl.BlockSpec((3, 1, LANES, width), lambda g: (0, g, 0, 0))]),
         ],
         out_specs=[
             whole(length, width),
@@ -145,6 +156,7 @@
             pl.BlockSpec((LANES, length), lambda g: (g, 0)),
             pl.BlockSpec((LANES, length), lambda g: (g, 0)),
             pl.BlockSpec((1, 8, length), lambda g: (g, 0, 0)),
+            *[ANY] * gathered,
         ],
         out_shape=[
             array((length, width)),
@@ -152,8 +164,12 @@
             array((width, length)),
             array((width, length)),
             array((GROUPS, 8, length), F32),
+            *[array((features, width))] * gathered,
         ],
-        scratch=[pltpu.VMEM((length, length), F32)],
+        scratch=[
+            pltpu.VMEM((length, length), F32),
+            *(weight_scratch(features, width) if gathered else ()),
+        ],
     )
 
 
@@ -165,40 +181,72 @@
     slope_ref[...] = (half + feed * density).astype(BF16)
 
 
-def hidden(layer, normed, weight_in):
+def hidden(normed, weight_in):
     length, width = normed.shape
-    blocks = weight_in.shape[0] // width // 2
-    first, count = layer * blocks + 3, blocks - 3
+    count = weight_in.shape[0] // width - 3
     return launch(
         hidden_kernel,
         (normed, weight_in),
         name="hidden",
         micros=8,
         grid=(count,),
-        in_specs=[whole(length, width), pl.BlockSpec((width, width), lambda i: (i + first, 0))],
+        in_specs=[whole(length, width), pl.BlockSpec((width, width), lambda i: (i + 3, 0))],
         out_specs=[pl.BlockSpec((width, length), lambda i: (i, 0))] * 2,
         out_shape=[array((count * width, length))] * 2,
     )
 
 
-def output_kernel(pair_ref, rows_ref, attended_ref, hidden_ref, weight_ref, result_ref, sums_ref, attend_ref, feed_ref):
-    step = pl.program_id(0)
-
+def load_weight(step, pieces, target, sems, rows, full_ref, full_sems, steps):
     @pl.when(step == 0)
     def _():
-        attend_ref[...] = tn(attended_ref[...], weight_ref[...])
+        piece_copies(pieces, target, sems, rows)
+
+    size = 4 * rows
+    out = [
+        pltpu.make_async_copy(target.at[pl.ds(size * slot, size)], full_ref.at[pl.ds(size * slot, size)], full_sems.at[slot])
+        for slot in range(4)
+    ]
+    for slot in range(4):
+
+        @pl.when(step == steps[slot])
+        def _():
+            for at in range(4):
+                goal = target.at[pl.ds(size * slot + rows * at, rows)]
+                pltpu.make_async_copy(pieces[0].at[0, pl.ds(0, rows)], goal, sems.at[4 * slot + at]).wait()
+            out[slot].start()
+
+    @pl.when(step == pl.num_programs(0) - 1)
+    def _():
+        for copy in out:
+            copy.wait()
+
+
+def output_kernel(out_rows, pair_ref, rows_ref, attended_ref, hidden_ref, *refs):
+    step, last = pl.program_id(0), pl.num_programs(0) - 1
+    width = rows_ref.shape[1]
+    if out_rows is None:
+        weight_ref, result_ref, sums_ref, attend_ref, feed_ref = refs
+        weight = weight_ref[...]
+    else:
+        pieces, (result_ref, sums_ref, full_ref, attend_ref, feed_ref, all_ref, sems, full_sems) = refs[:8], refs[8:]
+        load_weight(step, pieces, all_ref, sems, out_rows, full_ref, full_sems, (0, 1, 2, 3))
+        weight = all_ref[pl.ds(pl.multiple_of(step * width, width), width)]
+
+    @pl.when(step == 0)
+    def _():
+        attend_ref[...] = tn(attended_ref[...], weight)
 
     @pl.when(step == 1)
     def _():
-        feed_ref[...] = tn(hidden_ref[...], weight_ref[...])
+        feed_ref[...] = tn(hidden_ref[...], weight)
 
     @pl.when(step > 1)
     def _():
-        feed_ref[...] += tn(hidden_ref[...], weight_ref[...])
-
-    @pl.when(step == pl.num_programs(0) - 1)
-    def _():
-        length, width = attend_ref.shape
+        feed_ref[...] += tn(hidden_ref[...], weight)
+
+    @pl.when(step == last)
+    def _():
+        length = attend_ref.shape[0]
         position = lax.broadcasted_iota(jnp.int32, (length, 1), 0)
         valid = (segment_at(pair_ref, position) < 2).astype(F32)
         branch, feed = attend_ref[...], feed_ref[...]
@@ -209,12 +257,18 @@
             sums_ref[at] = jnp.sum(squares, axis=0)
 
 
-def output(pair, rows, attended, hid, weight):
+def weight_scratch(features, width):
+    return [pltpu.VMEM((features, width), BF16), pltpu.SemaphoreType.DMA((16,)), pltpu.SemaphoreType.DMA((4,))]
+
+
+def output(pair, out_rows, rows, attended, hid, *weights):
     length, width = rows.shape
-    count = weight.shape[0] // width
+    features = hid.shape[0] + width
+    count = features // width
+    gathered = out_rows is not None
     return launch(
-        output_kernel,
-        (pair, rows, attended, hid, weight),
+        functools.partial(output_kernel, out_rows),
+        (pair, rows, attended, hid, *weights),
         name="output",
         micros=9,
         grid=(count,),
@@ -223,17 +277,28 @@
             whole(length, width),
             whole(width, length),
             pl.BlockSpec((width, length), lambda i: (jnp.maximum(i - 1, 0), 0)),
-            pl.BlockSpec((width, width), lambda i: (i, 0)),
+            *([ANY] * 8 if gathered else [pl.BlockSpec((width, width), lambda i: (i, 0))]),
         ],
-        out_specs=[whole(length, width), whole(3, 8, width)],
-        out_shape=[array((length, width)), array((3, 8, width), F32)],
-        scratch=[pltpu.VMEM((length, width), F32)] * 2,
-    )
-
-
-def feed_back_kernel(grad_ref, slope_ref, weight_in_ref, weight_out_ref, grad_normed_ref, grad_feed_ref):
+        out_specs=[whole(length, width), whole(3, 8, width), *[ANY] * gathered],
+        out_shape=[array((length, width)), array((3, 8, width), F32), *[array((features, width))] * gathered],
+        scratch=[
+            *[pltpu.VMEM((length, width), F32)] * 2,
+            *(weight_scratch(features, width) if gathered else ()),
+        ],
+    )
+
+
+def feed_back_kernel(out_rows, grad_ref, slope_ref, weight_in_ref, *refs):
     step = pl.program_id(0)
-    grad_hidden = nt(weight_out_ref[...], grad_ref[...]).astype(BF16).astype(F32)
+    width = grad_ref.shape[1]
+    if out_rows is None:
+        weight_ref, grad_normed_ref, grad_feed_ref = refs
+        weight_out = weight_ref[...]
+    else:
+        pieces, (grad_normed_ref, grad_feed_ref, full_ref, all_ref, sems, full_sems) = refs[:8], refs[8:]
+        load_weight(step, pieces, all_ref, sems, out_rows, full_ref, full_sems, (0, 0, 1, 2))
+        weight_out = all_ref[pl.ds(pl.multiple_of((step + 1) * width, width), width)]
+    grad_hidden = nt(weight_out, grad_ref[...]).astype(BF16).astype(F32)
     grad_feed = (grad_hidden * slope_ref[...].astype(F32)).astype(BF16)
     grad_feed_ref[...] = grad_feed
     part = tn(grad_feed, weight_in_ref[...])
@@ -247,25 +312,27 @@
         grad_normed_ref[...] += part
 
 
-def feed_back(layer, grad, slope, weight_in, weight_out):
+def feed_back(out_rows, grad, slope, weight_in, *weights):
     length, width = grad.shape
+    features = slope.shape[0] + width
     count = slope.shape[0] // width
-    first = layer * (weight_in.shape[0] // width // 2) + 3
+    gathered = out_rows is not None
     rows = pl.BlockSpec((width, length), lambda i: (i, 0))
     return launch(
-        feed_back_kernel,
-        (grad, slope, weight_in, weight_out),
+        functools.partial(feed_back_kernel, out_rows),
+        (grad, slope, weight_in, *weights),
         name="feed_back",
         micros=11,
         grid=(count,),
         in_specs=[
             whole(length, width),
             rows,
-            pl.BlockSpec((width, width), lambda i: (i + first, 0)),
-            pl.BlockSpec((width, width), lambda i: (i + 1, 0)),
+            pl.BlockSpec((width, width), lambda i: (i + 3, 0)),
+            *([ANY] * 8 if gathered else [pl.BlockSpec((width, width), lambda i: (i + 1, 0))]),
         ],
-        out_specs=[whole(length, width), rows],
-        out_shape=[array((length, width), F32), array(slope.shape)],
+        out_specs=[whole(length, width), rows, *[ANY] * gathered],
+        out_shape=[array((length, width), F32), array(slope.shape), *[array((features, width))] * gathered],
+        scratch=weight_scratch(features, width) if gathered else (),
     )
 
 
@@ -318,14 +385,14 @@
         gain_grad_ref[...] = jnp.sum((grad_normed * normal).reshape(length // 8, 8, width), axis=0)
 
 
-def attend_back(layer, pair, rows, grad, gain, query_scale, key_scale, raw, value, attended, logs, weight_out,
+def attend_back(pair, rows, grad, gain, query_scale, key_scale, raw, value, attended, logs, weight_out,
                 weight_in, feed_grad):
     length, width = grad.shape
     group_rows = pl.BlockSpec((LANES, length), lambda g: (g, 0))
     projected, *others = launch(
         attend_back_kernel,
         (pair, rows, grad, gain, query_scale, key_scale, raw, value, attended, logs,
-         weight_out.reshape(-1, LANES, width), weight_in.reshape(2, -1, GROUPS, LANES, width), feed_grad),
+         weight_out.reshape(-1, LANES, width), weight_in.reshape(-1, GROUPS, LANES, width), feed_grad),
         name="attend_back",
         micros=17,
         grid=(GROUPS,),
@@ -341,7 +408,7 @@
             group_rows,
             pl.BlockSpec((1, 8, length), lambda g: (g, 0, 0)),
             pl.BlockSpec((1, LANES, width), lambda g: (g, 0, 0)),
-            pl.BlockSpec((1, 3, 1, LANES, width), lambda g: (layer, 0, g, 0, 0)),
+            pl.BlockSpec((3, 1, LANES, width), lambda g: (0, g, 0, 0)),
             whole(length, width),
         ],
         out_specs=[
@@ -494,33 +561,25 @@
     )
 
 
-def place_kernel(
-    line_keep, line_pass, side_keep, side_pass, turn_keep, turn_pass, corner, corner_other, full_ref, sems
-):
-    core, y, x = lax.axis_index("section"), lax.axis_index("y"), lax.axis_index("x")
-    at = pl.program_id(0)
-    take = pl.ds(line_keep.shape[1] - full_ref.shape[3], full_ref.shape[3])
+def piece_copies(pieces, target, sems, rows):
+    line_keep, line_pass, side_keep, side_pass, turn_keep, turn_pass, corner, corner_other = pieces
+    core, _, y, x = place()
+    high, wide = 2, 2
+    take = pl.ds(0, rows)
     side_y, side_x = jnp.where(core == 0, y, 1 - y), jnp.where(core == 0, 1 - x, x)
-    copies = [
-        slot_copy(at, line_keep, line_pass, core, full_ref.at[0, y, x], sems.at[0], take),
-        slot_copy(at, side_keep, side_pass, core, full_ref.at[0, side_y, side_x], sems.at[1], take),
-        slot_copy(at, turn_keep, turn_pass, 1 - core, full_ref.at[0, 1 - side_y, 1 - side_x], sems.at[2], take),
-        slot_copy(at, corner_other, corner, core, full_ref.at[0, 1 - y, 1 - x], sems.at[3], take),
-    ]
-    for copy in copies:
-        copy.wait()
-
-
-def placed(pieces, fine, rows):
-    width = pieces[0].shape[-1]
-    full = launch(
-        place_kernel, pieces, name="place", micros=5, grid=(fine[1],),
-        in_specs=[ANY] * 8,
-        out_specs=pl.BlockSpec((1, *fine[2:], rows, width), lambda i: (i, 0, 0, 0, 0)),
-        out_shape=array((*fine[1:], rows, width)),
-        scratch=[pltpu.SemaphoreType.DMA((4,))],
-    )
-    return full.reshape(-1, width)
+    copies = []
+    for slot in range(4):
+        lines = (
+            (line_keep, line_pass, core, y, x),
+            (side_keep, side_pass, core, side_y, side_x),
+            (turn_keep, turn_pass, 1 - core, 1 - side_y, 1 - side_x),
+            (corner_other, corner, core, 1 - y, 1 - x),
+        )
+        for at, (keep, passed, owner, line_y, line_x) in enumerate(lines):
+            start = pl.multiple_of(((slot * high + line_y) * wide + line_x) * rows, 8)
+            goal = target.at[pl.ds(start, rows)]
+            copies.append(slot_copy(slot, keep, passed, owner, goal, sems.at[4 * slot + at], take))
+    return copies
 
 
 def rows_copy(low_ref, high_ref, start, count, target_ref, at, sem, crossing):
@@ -735,35 +794,36 @@
     def __init__(self, order, fine, shard, half):
         self.order, self.fine, self.shard, self.half = order, fine, shard, half
 
-    def along(self):
-        self.near = self.order.move(functools.partial(along, fine=self.fine), self.shard)
-        self.far = self.order.move(functools.partial(opposite, fine=self.fine), self.half)
-
-    def across(self):
-        self.near_other, self.far_other = self.order.swap(self.near, self.far)
+    def along(self, count=1):
+        self.near = self.order.move(functools.partial(along, fine=self.fine), self.shard, count=count)
+        self.far = self.order.move(functools.partial(opposite, fine=self.fine), self.half, count=count)
+
+    def across(self, count=1):
+        self.near_other, self.far_other = self.order.swap(self.near, self.far, count=count)
 
     def line(self):
         self.keep, self.passed = self.order.run(
             line_of, self.shard, self.near, self.near_other, self.far, self.far_other
         )
 
-    def side(self):
-        self.side_passed = self.order.move(functools.partial(sideways, fine=self.fine), self.passed)
-        self.side_keep = self.order.move(functools.partial(sideways, fine=self.fine), self.keep)
-
-    def turn(self):
-        self.corner = self.order.move(functools.partial(turned, fine=self.fine), self.side_passed)
-        self.turn_keep, self.turn_passed = self.order.swap(self.side_keep, self.side_passed)
+    def side(self, count=1):
+        self.side_passed = self.order.move(functools.partial(sideways, fine=self.fine), self.passed, count=count)
+        self.side_keep = self.order.move(functools.partial(sideways, fine=self.fine), self.keep, count=count)
+
+    def turn(self, count=1):
+        self.corner = self.order.move(functools.partial(turned, fine=self.fine), self.side_passed, count=count)
+
+    def rest(self, count=1):
+        self.turn_keep, self.turn_passed = self.order.swap(self.side_keep, self.side_passed, count=count)
 
     def meet(self):
         self.corner_other = self.order.swap(self.corner)
 
-    def place(self):
-        pieces = (
+    def pieces(self):
+        return (
             self.keep, self.passed, self.side_keep, self.side_passed, self.turn_keep, self.turn_passed,
             self.corner, self.corner_other,
         )
-        return self.order.run(lambda *values: placed(values, self.fine, self.shard.shape[0]), *pieces)
 
 
 class Scatter:
@@ -771,15 +831,17 @@
         self.order, self.fine = order, fine
         self.turn, self.keep, self.passed, self.near, self.halves = values
 
-    def start(self):
-        self.turn = self.order.move(functools.partial(turned, fine=self.fine), self.turn)
-        self.keep = self.order.move(functools.partial(sideways, fine=self.fine), self.keep)
+    def start(self, count=1):
+        self.turn = self.order.move(functools.partial(turned, fine=self.fine), self.turn, count=count)
+        self.keep = self.order.move(functools.partial(sideways, fine=self.fine), self.keep, count=count)
 
     def add(self):
         self.passed = self.order.run(added, self.passed, self.turn)
 
     def pass_on(self):
         self.passed = self.order.move(functools.partial(sideways, fine=self.fine), self.passed)
+
+    def keep_across(self):
         self.keep_other = self.order.swap(self.keep)
 
     def meet(self):
@@ -792,6 +854,8 @@
         near, far, self.own = values
         self.near = self.order.move(functools.partial(along, fine=self.fine), near, count=count)
         self.far = self.order.move(functools.partial(opposite, fine=self.fine), far, count=count)
+
+    def own_across(self):
         self.own_other = self.order.swap(self.own)
 
     def across(self):
@@ -815,64 +879,113 @@
     spread = lambda mine, other: jnp.stack(by_core(mine, other))[None, :, None]
     chip = functools.partial(partial, fine)
 
-    weight_in_all = lax.all_gather(weight_in[0], ALL, axis=0, tiled=True)
-
     def padded(flat):
         return jnp.pad(flat, (0, -flat.shape[0] % 1024)).reshape(-1, 128)
 
     own_scales = lax.dynamic_update_slice(
         jnp.zeros((2 * whole_scales,), F32), scales[0].astype(F32), (core * whole_scales + device * scale_count,)
     )
-    scale = total_of(padded(own_scales), fine).reshape(-1)[: 2 * whole_scales].reshape(2, whole_scales)
-    vectors_0, vectors_1 = [(s[None, :width], s[width : width + HEAD, None], s[width + HEAD :, None]) for s in scale]
-    rows_0 = lax.dynamic_index_in_dim(inputs, core, 0, False)[0]
-    grad = lax.dynamic_index_in_dim(cotangent, core, 0, False)[0]
-    position = lax.broadcasted_iota(jnp.int32, (length, 1), 0)
-    grad_1 = jnp.where(position < pair[0, 0] + pair[0, 1], grad, jnp.zeros_like(grad))
-
-    order = Order(grad_1)
+    scale = padded(own_scales)
+
+    def vectors_of(scale):
+        scale = scale.reshape(-1)[: 2 * whole_scales].reshape(2, whole_scales)
+        return [(s[None, :width], s[width : width + HEAD, None], s[width + HEAD :, None]) for s in scale]
+
+    def own_rows(inputs, cotangent):
+        rows = lax.dynamic_index_in_dim(inputs, core, 0, False)[0]
+        grad = lax.dynamic_index_in_dim(cotangent, core, 0, False)[0]
+        position = lax.broadcasted_iota(jnp.int32, (length, 1), 0)
+        return rows, jnp.where(position < pair[0, 0] + pair[0, 1], grad, jnp.zeros_like(grad))
+
+    order = Order(scale)
+    butterfly = lambda by: lambda value: lax.ppermute(value, "z", [(i, i ^ by) for i in range(depth)])
+    out = functools.partial(output, pair)
     if depth == 4:
-        other_out = order.swap(weight_out[0])
-        grad_1_other = order.swap(grad_1)
+        in_rows, out_rows = weight_in.shape[1], weight_out.shape[1]
+        gather = lambda values: Gather(order, fine, *values)
+        other_in, other_out, got = order.swap(weight_in[0], weight_out[0], scale)
         order.fence()
-        first = Gather(order, fine, *order.run(functools.partial(pick, 0), weight_out[0], other_out))
+        first = gather(order.run(functools.partial(pick, 0), weight_in[0], other_in))
         first.along()
-        second = Gather(order, fine, *order.run(functools.partial(pick, 1), weight_out[0], other_out))
+        scale = scale + got
+        got = order.move(shift("x"), scale)
+        picked = order.run(
+            lambda own_in, other_in, own_out, other_out, *values: (
+                pick(0, own_out, other_out), pick(1, own_in, other_in), pick(1, own_out, other_out), own_rows(*values)
+            ),
+            weight_in[0], other_in, weight_out[0], other_out, inputs, cotangent,
+        )
+        second, third, fourth = [gather(values) for values in picked[:3]]
+        rows_0, grad_1 = picked[3]
         first.across()
+        scale = scale + got
+        got = order.move(shift("y"), scale)
         order.fence()
         first.line()
         first.side()
         second.along()
+        scale = scale + got
+        got = order.move(butterfly(1), scale)
         order.fence()
-        first.turn()
+        first.turn(count=3)
         second.across()
+        first.rest(count=2)
         order.fence()
+        scale = scale + got
+        got = order.move(butterfly(2), scale)
+        second.line()
+        vectors_0, vectors_1 = order.run(vectors_of, scale + got)
+        second.side(count=2)
+        third.along(count=2)
         first.meet()
-        second.line()
-        second.side()
-        weight_out_0 = first.place()
+        order.fence()
+        front, out = functools.partial(attend, in_rows, pair), functools.partial(output, pair, out_rows)
+        normed_0, raw_0, value_0, attended_0, logs_0, weight_in_0 = order.run(front, rows_0, *vectors_0, *first.pieces())
         second.turn()
+        second.rest()
+        third.across()
+        hidden_0, slope_0 = order.run(hidden, normed_0, weight_in_0)
+        second.meet()
+        third.line()
+        third.side()
+        fourth.along()
+        rows_1, squares_0, weight_out_0 = order.run(out, rows_0, attended_0, hidden_0, *second.pieces())
+        third.turn(count=3)
+        fourth.across()
+        third.rest(count=2)
         order.fence()
-        second.meet()
+        fourth.line()
+        grad_1_other = order.swap(grad_1)
         order.fence()
-        weight_out_1 = second.place()
+        fourth.side(count=2)
+        third.meet()
+        order.fence()
+        attended_0_other, normed_0_other, hidden_0_other = order.swap(attended_0, normed_0, hidden_0)
+        normed_1, raw_1, value_1, attended_1, logs_1, weight_in_1 = order.run(front, rows_1, *vectors_1, *third.pieces())
+        fourth.turn()
+        fourth.rest()
+        attended_1_other, normed_1_other = order.swap(attended_1, normed_1)
+        hidden_1, slope_1 = order.run(hidden, normed_1, weight_in_1)
+        fourth.meet()
+        order.fence()
+        hidden_1_other, rows_1_other = order.swap(hidden_1, rows_1)
+        feed_1, low_1, weight_out_1 = order.run(
+            functools.partial(feed_back, out_rows), grad_1, slope_1, weight_in_1, *fourth.pieces()
+        )
     else:
+        weight_in_0, weight_in_1 = jnp.split(lax.all_gather(weight_in[0], ALL, axis=0, tiled=True), 2)
         weight_out_0, weight_out_1 = jnp.split(lax.all_gather(weight_out[0], ALL, axis=0, tiled=True), 2)
-    out = functools.partial(output, pair)
-    normed_0, raw_0, value_0, attended_0, logs_0 = order.run(
-        functools.partial(attend, 0, pair), rows_0, *vectors_0, weight_in_all
-    )
-    attended_0_other, normed_0_other = order.swap(attended_0, normed_0)
-    hidden_0, slope_0 = order.run(functools.partial(hidden, 0), normed_0, weight_in_all)
-    hidden_0_other = order.swap(hidden_0)
-    rows_1, squares_0 = order.run(out, rows_0, attended_0, hidden_0, weight_out_0)
-    normed_1, raw_1, value_1, attended_1, logs_1 = order.run(
-        functools.partial(attend, 1, pair), rows_1, *vectors_1, weight_in_all
-    )
-    attended_1_other, normed_1_other = order.swap(attended_1, normed_1)
-    hidden_1, slope_1 = order.run(functools.partial(hidden, 1), normed_1, weight_in_all)
-    back_1, back_0 = functools.partial(attend_back, 1, pair), functools.partial(attend_back, 0, pair)
-    kept_1 = (rows_1, grad_1, *vectors_1, raw_1, value_1, attended_1, logs_1, weight_out_1, weight_in_all)
+        vectors_0, vectors_1 = vectors_of(total_of(scale, fine))
+        rows_0, grad_1 = own_rows(inputs, cotangent)
+        front, out = functools.partial(attend, None, pair), functools.partial(output, pair, None)
+        normed_0, raw_0, value_0, attended_0, logs_0 = order.run(front, rows_0, *vectors_0, weight_in_0)
+        hidden_0, slope_0 = order.run(hidden, normed_0, weight_in_0)
+        rows_1, squares_0 = order.run(out, rows_0, attended_0, hidden_0, weight_out_0)
+        normed_1, raw_1, value_1, attended_1, logs_1 = order.run(front, rows_1, *vectors_1, weight_in_1)
+        hidden_1, slope_1 = order.run(hidden, normed_1, weight_in_1)
+        feed_1, low_1 = order.run(functools.partial(feed_back, None), grad_1, slope_1, weight_in_1, weight_out_1)
+    out, back, feed = functools.partial(output, pair, None), functools.partial(attend_back, pair), functools.partial(feed_back, None)
+    kept_1 = (rows_1, grad_1, *vectors_1, raw_1, value_1, attended_1, logs_1, weight_out_1, weight_in_1)
 
     def small_sums(squares_0, squares_1, gain_0, heads_0, gain_1, heads_1):
         sums = [jnp.sum(squares, axis=(1, 2)) for squares in (squares_0, squares_1)]
@@ -883,90 +996,98 @@
         return padded(jnp.concatenate([jnp.sum(pair).astype(F32)[None], *sums, *scale_grads]))
 
     if depth == 4:
-        hidden_1_other = order.swap(hidden_1)
-        feed_1, low_1 = order.run(functools.partial(feed_back, 1), grad_1, slope_1, weight_in_all, weight_out_1)
         low_1_other = order.swap(low_1)
         out_1 = Scatter(order, fine, order.run(
             chip, attended_1, hidden_1, attended_1_other, hidden_1_other, grad_1, grad_1_other
         ))
         out_1.start()
-        top_1, grad_0, gain_1, heads_1 = order.run(back_1, *kept_1, feed_1)
-        grad_0_other, top_1_other = order.swap(grad_0, top_1, count=2)
+        top_1, grad_0, gain_1, heads_1 = order.run(back, *kept_1, feed_1)
+        grad_0_other = order.swap(grad_0)
+        top_1_other = order.swap(top_1, count=3)
         out_1.add()
         out_1.pass_on()
-        feed_0, low_0 = order.run(functools.partial(feed_back, 0), grad_0, slope_0, weight_in_all, weight_out_0)
-        low_0_other = order.swap(low_0)
-        out_1.meet()
+        out_1.keep_across()
         out_0 = Scatter(order, fine, order.run(
             chip, attended_0, hidden_0, attended_0_other, hidden_0_other, grad_0, grad_0_other
         ))
         out_0.start()
+        out_1.meet()
+        feed_0, low_0 = order.run(feed, grad_0, slope_0, weight_in_0, weight_out_0)
+        out_0.add()
+        out_0.pass_on()
+        out_0.keep_across()
+        low_0_other = order.swap(low_0)
         in_1, ends = order.run(
             lambda values, parts: (chip(*values), depth_sums(*parts)),
             (top_1, low_1, top_1_other, low_1_other, normed_1, normed_1_other), out_1.parts(),
         )
         in_1 = Scatter(order, fine, in_1)
-        out_0.add()
-        out_0.pass_on()
         in_1.start()
         out_1.along(ends)
-        kept_0 = (rows_0, grad_0, *vectors_0, raw_0, value_0, attended_0, logs_0, weight_out_0, weight_in_all)
-        (top_0, grad_first, gain_0, heads_0), (result_1, squares_1) = order.run(
-            lambda kept, late: (back_0(*kept), out(*late)), (*kept_0, feed_0), (rows_1, attended_1, hidden_1, weight_out_1)
+        out_0.meet()
+        kept_0 = (rows_0, grad_0, *vectors_0, raw_0, value_0, attended_0, logs_0, weight_out_0, weight_in_0)
+        top_0, grad_first, gain_0, heads_0 = order.run(back, *kept_0, feed_0)
+        top_0_other = order.swap(top_0)
+        ends, in_1.passed = order.run(
+            lambda parts, first, second: (depth_sums(*parts), added(first, second)), out_0.parts(), in_1.passed, in_1.turn
         )
-        top_0_other = order.swap(top_0, count=2)
-        in_1.add()
         in_1.pass_on()
-        out_0.meet()
+        out_0.along(ends)
+        in_1.keep_across()
+        in_0 = Scatter(order, fine, order.run(chip, top_0, low_0, top_0_other, low_0_other, normed_0, normed_0_other))
+        in_1.meet()
         out_1.across()
-        small, (rows_kept, rows_given), (grads_kept, grads_given) = order.run(
-            lambda *values: (small_sums(*values[:6]), by_core(*values[6:8]), by_core(*values[8:])),
-            squares_0, squares_1, gain_0, heads_0, gain_1, heads_1, rows_1, result_1, grad_first, grad_0,
-        )
-        in_1.meet()
-        in_0, ends = order.run(
-            lambda values, parts: (chip(*values), depth_sums(*parts)),
-            (top_0, low_0, top_0_other, low_0_other, normed_0, normed_0_other), out_0.parts(),
-        )
-        in_0 = Scatter(order, fine, in_0)
+        order.fence()
+        ends = order.run(depth_sums, *in_1.parts())
         in_0.start()
-        out_0.along(ends)
-        small_other = order.move(shift("x"), small)
-        rows_got, grads_got = order.swap(rows_given, grads_given)
-        ends, out_grad_1 = order.run(
-            lambda parts, sums: (depth_sums(*parts), total(*sums)), in_1.parts(), out_1.ends()
-        )
-        small = small + small_other
-        small_other = order.move(shift("y"), small)
+        in_1.along(ends)
+        out_1.own_across()
+        result_1, squares_1 = order.run(out, rows_1, attended_1, hidden_1, weight_out_1)
         in_0.add()
         in_0.pass_on()
-        in_1.along(ends, count=2)
+        in_0.keep_across()
         out_0.across()
-        outputs, input_grads = order.run(lambda *v: (spread(*v[:2]), spread(*v[2:])), rows_kept, rows_got, grads_kept, grads_got)
+        out_0.own_across()
+        small, out_grad_1 = order.run(
+            lambda sums, values: (small_sums(*values), total(*sums)),
+            out_1.ends(), (squares_0, squares_1, gain_0, heads_0, gain_1, heads_1),
+        )
         in_0.meet()
-        out_grad = order.run(total, *out_0.ends(), out_grad_1)
+        got = order.move(shift("x"), small)
+        order.fence()
+        small = small + got
+        got = order.move(shift("y"), small)
+        in_1.across()
+        in_1.own_across()
         ends = order.run(depth_sums, *in_0.parts())
         in_0.along(ends)
-        in_1.across()
-        small = small + small_other
-        ring = [
-            order.move(lambda v, k=k: lax.ppermute(v, "z", [(i, (i + k) % depth) for i in range(depth)]), small)
-            for k in range(1, depth)
-        ]
-        order.fence()
+        small = small + got
+        result_1_other, grad_first_other = order.swap(result_1, grad_first)
+        in_0.own_across()
+        def spread_both(rows_1, rows_other, result, result_other, first, first_other, grad_0, grad_other):
+            outputs = jnp.where(core == 0, rows_1, result), jnp.where(core == 0, rows_other, result_other)
+            grads = jnp.where(core == 0, first, grad_0), jnp.where(core == 0, first_other, grad_other)
+            return spread(*outputs), spread(*grads)
+
+        out_grad, in_grad_1 = order.run(
+            lambda first, second: (total(*first), total(*second)), (*out_0.ends(), out_grad_1), in_1.ends()
+        )
         in_0.across()
-        small = sum(ring, small)
-        small_other = order.swap(small)
-        in_grad_1 = order.run(total, *in_1.ends())
+        got = order.move(butterfly(1), small)
+        outputs, input_grads = order.run(
+            spread_both, rows_1, rows_1_other, result_1, result_1_other, grad_first, grad_first_other, grad_0, grad_0_other
+        )
+        small = small + got
+        got = order.move(butterfly(2), small)
         in_grad = order.run(total, *in_0.ends(), in_grad_1)[None]
+        small = small + got
+        small = small + order.swap(small)
         out_grad = out_grad[None]
-        small = small + small_other
     else:
-        feed_1, low_1 = order.run(functools.partial(feed_back, 1), grad_1, slope_1, weight_in_all, weight_out_1)
-        top_1, grad_0, gain_1, heads_1 = order.run(back_1, *kept_1, feed_1)
-        feed_0, low_0 = order.run(functools.partial(feed_back, 0), grad_0, slope_0, weight_in_all, weight_out_0)
-        kept_0 = (rows_0, grad_0, *vectors_0, raw_0, value_0, attended_0, logs_0, weight_out_0, weight_in_all)
-        top_0, grad_first, gain_0, heads_0 = order.run(back_0, *kept_0, feed_0)
+        top_1, grad_0, gain_1, heads_1 = order.run(back, *kept_1, feed_1)
+        feed_0, low_0 = order.run(feed, grad_0, slope_0, weight_in_0, weight_out_0)
+        kept_0 = (rows_0, grad_0, *vectors_0, raw_0, value_0, attended_0, logs_0, weight_out_0, weight_in_0)
+        top_0, grad_first, gain_0, heads_0 = order.run(back, *kept_0, feed_0)
         result_1, squares_1 = order.run(out, rows_1, attended_1, hidden_1, weight_out_1)
         own = lambda low, high, right: nn(jnp.concatenate([low, high]), right).astype(BF16)
         summed = lambda first, second: lax.psum_scatter(

time: 546 us -> 473 us (0.87)
  waiting for transfers between devices: 187 us -> 114 us
  between operations: 18 us -> 5.01 us
  starting transfers between devices: 94.6 us -> 103 us
    ppermute x6 -> x8, waiting for transfers between devices: 83.5 us -> 44 us  [opposite(): lax.ppermute(value, 'z', [(z, (z + 2) % depth) for z in range(depth)])]
    ppermute x46 -> x59, starting transfers between devices: 40.2 us -> 16.2 us  [swap(): return lax.ppermute(value, 'section', [(0, 1), (1, 0)])]
    ppermute x2 -> x4, waiting for transfers between devices: 24.2 us -> 3.77 us  [body(): lax.ppermute(value, axis, [(0, 1), (1, 0)])]
    ppermute x12 -> x16, waiting for transfers between devices: 37.4 us -> 21.3 us  [sideways(): return lax.ppermute(value, ALL, sends(fine, next_x, next_y))]
    ppermute x6 -> x8, waiting for transfers between devices: 3.44 us -> 18.7 us  [turned(): return lax.ppermute(value, ALL, sends(fine, next_y, next_x))]
    ppermute x6 -> x8, starting transfers between devices: 11.7 us -> 27 us  [opposite(): lax.ppermute(value, 'z', [(z, (z + 2) % depth) for z in range(depth)])]
    ppermute x9 -> x4, waiting for transfers between devices: 20.1 us -> 6.45 us  [body(): lax.ppermute(value, 'z', [(i, i ^ by) for i in range(depth)])]
    ppermute x2 -> x4, starting transfers between devices: 2.25 us -> 8.05 us  [body(): lax.ppermute(value, axis, [(0, 1), (1, 0)])]
  transfers between devices with their start and end apart: 88 -> 107, of which waited for: 31 -> 33; matrix products, arithmetic and copies ran while one was open for 3% -> 3% of each run, Pallas kernels for 33% -> 43%
where the time goes in v3:
time: 473 us; the launch traced here: 465 us
  Pallas kernels  211 us (45%)
  waiting for transfers between devices  114 us (24%)
  starting transfers between devices  103 us (22%)
  local copies, waits for them, and re-layouts  23.9 us (5%)
  other arithmetic  8.27 us (2%)
  between operations  5.01 us (1%)
    pallas_call x30, Pallas kernels, launch(): pl.pallas_call(kernel, grid=grid, in_specs=in_specs, out_specs=out_specs,...  211 us
    ppermute x8, waiting for transfers between devices, opposite(): lax.ppermute(value, 'z', [(z, (z + 2) % depth) for z in range(depth)])  44 us
    ppermute x8, starting transfers between devices, opposite(): lax.ppermute(value, 'z', [(z, (z + 2) % depth) for z in range(depth)])  27 us
    ppermute x16, waiting for transfers between devices, sideways(): return lax.ppermute(value, ALL, sends(fine, next_x, next_y))  21.3 us
    ppermute x8, waiting for transfers between devices, turned(): return lax.ppermute(value, ALL, sends(fine, next_y, next_x))  18.7 us
    ppermute x16, starting transfers between devices, sideways(): return lax.ppermute(value, ALL, sends(fine, next_x, next_y))  17.2 us
    ppermute x59, starting transfers between devices, swap(): return lax.ppermute(value, 'section', [(0, 1), (1, 0)])  16.2 us
    ppermute x59, waiting for transfers between devices, swap(): return lax.ppermute(value, 'section', [(0, 1), (1, 0)])  15.1 us
  transfers between devices with their start and end apart: 107, of which 33 were waited for; matrix products, arithmetic and copies ran while one was open for 3% of the time, Pallas kernels for 43%

profile of v3, /device:TPU:0, one launch (start us, length us, event | category | flops | bytes accessed | tf_op | source)
XLA Modules:
  0.0 465.3 jit_solution(16883084748840673027)
XLA Ops:
  6.7 1.9 pick.4
  8.6 1.8 pick.7
  10.5 2.0 pick.5
  12.5 2.6 collective-permute-start.5
  15.2 2.6 collective-permute-start.4
  19.5 2.2 pick.6
  22.7 13.2 %collective-permute-done.4.far_ref = bf16[176,768]{1,0:T(8,128)(2,1)S(1)} collective-permute-done((bf16[176,768]{1,0:T(8,128)(2,1)S(1)}, bf16[176,768]{1,0:T(8,128)(2,1)S(1)}, u32[]{:S(2)}, u32[]{:S(2)}) %collective-permute-start.4) | collective-permute-done | bytes 270368 | tf_op jit(solution)/shard_map/ppermute | solution.py:468
  38.9 2.1 collective-permute-done.6
  42.5 3.0 line.4
  47.6 5.4 %collective-permute-start.12 = (bf16[240,768]{1,0:T(8,128)(2,1)S(1)}, bf16[240,768]{1,0:T(8,128)(2,1)S(1)}, u32[]{:S(2)}, u32[]{:S(2)}) collective-permute-start(bf16[240,768]{1,0:T(8,128)(2,1)S(1)} %copy-done.77), channel_id=1, source_target_pairs={{0,4},{1,5},{2,6},{3,7},{4,8},{5,9},{6,10},{7,11},{8,12},{9,13},{1... | collective-permute-start | bytes 1105928 | tf_op jit(solution)/shard_map/ppermute | solution.py:461
  53.0 2.0 collective-permute-start.13
  55.5 6.2 %collective-permute-done.9 = f32[16,128]{1,0:T(8,128)S(1)} collective-permute-done((f32[16,128]{1,0:T(8,128)S(1)}, f32[16,128]{1,0:T(8,128)S(1)}, u32[]{:S(2)}, u32[]{:S(2)}) %collective-permute-start.9) | collective-permute-done | bytes 8224 | tf_op jit(solution)/shard_map/ppermute | solution.py:901
  61.7 4.7 %collective-permute-done.13.far_ref = bf16[128,768]{1,0:T(8,128)(2,1)S(1)} collective-permute-done((bf16[128,768]{1,0:T(8,128)(2,1)S(1)}, bf16[128,768]{1,0:T(8,128)(2,1)S(1)}, u32[]{:S(2)}, u32[]{:S(2)}) %collective-permute-start.13) | collective-permute-done | bytes 196640 | tf_op jit(solution)/shard_map/ppermute | solution.py:468
  66.5 4.9 %collective-permute-done.10.refs_3_ = bf16[2,336,768]{2,1,0:T(8,128)(2,1)S(1)} collective-permute-done((bf16[2,336,768]{2,1,0:T(8,128)(2,1)}, bf16[2,336,768]{2,1,0:T(8,128)(2,1)S(1)}, u32[]{:S(2)}, u32[]{:S(2)}) %collective-permute-start.10) | collective-permute-done | bytes 1032224 | tf_op jit(solution)/shard_map/ppermute | solution.py:452
  74.0 2.4 collective-permute-done.15.far_other_ref
  76.4 7.3 %collective-permute-start.16 = (f32[16,128]{1,0:T(8,128)S(1)}, f32[16,128]{1,0:T(8,128)S(1)}, u32[]{:S(2)}, u32[]{:S(2)}) collective-permute-start(f32[16,128]{1,0:T(8,128)S(1)} %add.92), channel_id=1, source_target_pairs={{0,8},{4,12},{8,0},{12,4},{1,9},{5,13},{9,1},{13,5},{2,10},{6,14},... | collective-permute-start | bytes 24584 | tf_op jit(solution)/shard_map/ppermute | solution.py:901
  83.7 2.6 line.5
  88.9 6.5 %collective-permute-start.24 = (bf16[176,768]{1,0:T(8,128)(2,1)}, bf16[176,768]{1,0:T(8,128)(2,1)}, u32[]{:S(2)}, u32[]{:S(2)}) collective-permute-start(bf16[176,768]{1,0:T(8,128)(2,1)} %get-tuple-element.606), channel_id=1, source_target_pairs={{0,8},{4,12},{8,0},{12,4},{1,9},{5,13},{9,1},{13,5},{2,10},{6,14},... | collective-permute-start | bytes 811016 | tf_op jit(solution)/shard_map/ppermute | solution.py:468
  99.0 14.5 %attend.2 = (bf16[512,768]{1,0:T(8,128)(2,1)}, f32[2,3,256,512]{3,2,1,0:T(8,128)}, bf16[768,512]{1,0:T(8,128)(2,1)}, bf16[768,512]{1,0:T(8,128)(2,1)}, f32[3,8,512]{2,1,0:T(8,128)}, /*index=5*/bf16[5376,768]{1,0:T(8,128)(2,1)}) custom-call(s32[1,2]{1,0:T(1,128)} %copy-done.21, bf16[512,768]{1,0:T(8,128)(2,1)} %dynamic-slice_bitcast_fusion.rows_ref, ...), custom_call_target="tpu_custom_call" | custom-call | flops 14949999616 | bytes 13000000 | tf_op jit(solution)/shard_map/attend/pallas_call | solution.py:40
  117.6 8.4 %hidden.2 = (bf16[3072,512]{1,0:T(8,128)(2,1)}, bf16[3072,512]{1,0:T(8,128)(2,1)}) custom-call(bf16[512,768]{1,0:T(8,128)(2,1)} %get-tuple-element.886.normed_ref.right_ref, bf16[5376,768]{1,0:T(8,128)(2,1)} %get-tuple-element.855.weight_ref.weight_in_ref), custom_call_target="tpu_custom_call" | custom-call | flops 9200000000 | bytes 8000000 | tf_op jit(solution)/shard_map/hidden/pallas_call | solution.py:40
  127.4 3.8 line.6
  133.4 4.2 collective-permute-start.34
  138.3 11.0 %output.2 = (bf16[512,768]{1,0:T(8,128)(2,1)}, f32[3,8,768]{2,1,0:T(8,128)}, bf16[3840,768]{1,0:T(8,128)(2,1)}) custom-call(s32[1,2]{1,0:T(1,128)} %copy-done.21, bf16[512,768]{1,0:T(8,128)(2,1)} %dynamic-slice_bitcast_fusion.rows_ref, bf16[768,512]{1,0:T(8,128)(2,1)} %get-tuple-element.852.attended_ref.own_low, ...), custom_call_target="tpu_custom_call" | custom-call | flops 10350000128 | bytes 9000000 | tf_op jit(solution)/shard_map/output/pallas_call | solution.py:40
  149.3 2.9 collective-permute-done.33.near_ref
  152.3 5.0 %collective-permute-done.31.refs_3_ = bf16[2,336,768]{2,1,0:T(8,128)(2,1)S(1)} collective-permute-done((bf16[2,336,768]{2,1,0:T(8,128)(2,1)}, bf16[2,336,768]{2,1,0:T(8,128)(2,1)S(1)}, u32[]{:S(2)}, u32[]{:S(2)}) %collective-permute-start.31) | collective-permute-done | bytes 1032224 | tf_op jit(solution)/shard_map/ppermute | solution.py:452
  159.8 2.4 collective-permute-done.39.far_other_ref
  163.7 2.5 line.7
  166.5 6.5 %collective-permute-done.37.refs_6_ = bf16[2,336,768]{2,1,0:T(8,128)(2,1)S(1)} collective-permute-done((bf16[2,336,768]{2,1,0:T(8,128)(2,1)S(1)}, bf16[2,336,768]{2,1,0:T(8,128)(2,1)S(1)}, u32[]{:S(2)}, u32[]{:S(2)}) %collective-permute-start.37) | collective-permute-done | bytes 1032224 | tf_op jit(solution)/shard_map/ppermute | solution.py:456
  179.7 14.5 %attend.3 = (bf16[512,768]{1,0:T(8,128)(2,1)}, f32[2,3,256,512]{3,2,1,0:T(8,128)}, bf16[768,512]{1,0:T(8,128)(2,1)}, bf16[768,512]{1,0:T(8,128)(2,1)}, f32[3,8,512]{2,1,0:T(8,128)}, /*index=5*/bf16[5376,768]{1,0:T(8,128)(2,1)}) custom-call(s32[1,2]{1,0:T(1,128)} %copy-done.21, bf16[512,768]{1,0:T(8,128)(2,1)} %get-tuple-element.998.rows_ref, ...), custom_call_target="tpu_custom_call" | custom-call | flops 14949999616 | bytes 13000000 | tf_op jit(solution)/shard_map/attend/pallas_call | solution.py:40
  199.7 8.4 %hidden.3 = (bf16[3072,512]{1,0:T(8,128)(2,1)}, bf16[3072,512]{1,0:T(8,128)(2,1)}) custom-call(bf16[512,768]{1,0:T(8,128)(2,1)} %get-tuple-element.812.normed_ref.right_ref, bf16[5376,768]{1,0:T(8,128)(2,1)} %get-tuple-element.758.weight_ref.weight_in_ref), custom_call_target="tpu_custom_call" | custom-call | flops 9200000000 | bytes 8000000 | tf_op jit(solution)/shard_map/hidden/pallas_call | solution.py:40
  209.0 2.2 collective-permute-done.52.refs_7_
  212.2 13.5 %feed_back.2 = (f32[512,768]{1,0:T(8,128)}, bf16[3072,512]{1,0:T(8,128)(2,1)}, bf16[3840,768]{1,0:T(8,128)(2,1)}) custom-call(bf16[512,768]{1,0:T(8,128)(2,1)} %copy-done.11, bf16[3072,512]{1,0:T(8,128)(2,1)} %get-tuple-element.715.slope_ref, bf16[5376,768]{1,0:T(8,128)(2,1)} %get-tuple-element.758.weight_ref.weight_in_ref, ...), custom_call_target="tpu_custom_call" | custom-call | flops 12650000384 | bytes 11000000 | tf_op jit(solution)/shard_map/feed_back/pallas_call | solution.py:40
  227.4 8.6 %partial.4 = (bf16[2,240,768]{2,1,0:T(8,128)(2,1)}, bf16[2,240,768]{2,1,0:T(8,128)(2,1)}, bf16[2,240,768]{2,1,0:T(8,128)(2,1)}, bf16[240,768]{1,0:T(8,128)(2,1)}, bf16[2,128,768]{2,1,0:T(8,128)(2,1)}) custom-call(bf16[768,512]{1,0:T(8,128)(2,1)} %get-tuple-element.912.own_low.attended_ref, bf16[3072,512]{1,0:T(8,128)(2,1)} %get-tuple-element.913.own_high.hidden_ref, ...), custom_call_target="tpu_custom_call" | custom-call | flops 6308571648 | bytes 5485714 | tf_op jit(solution)/shard_map/partial/pallas_call | solution.py:40
  239.5 17.6 %attend_back.2 = (bf16[3,3,256,512]{3,2,1,0:T(8,128)(2,1)}, bf16[512,768]{1,0:T(8,128)(2,1)}, f32[8,768]{1,0:T(8,128)}, f32[2,64,128]{2,1,0:T(8,128)}) custom-call(s32[1,2]{1,0:T(1,128)} %copy-done.21, bf16[512,768]{1,0:T(8,128)(2,1)} %get-tuple-element.998.rows_ref, bf16[512,768]{1,0:T(8,128)(2,1)} %copy-done.11, f32[1,768]{1,0:T(1,128)} %bitcast.79, ...), custom_call_target="tpu_custom_call" | custom-call | flops 19549999104 | bytes 17000000 | tf_op jit(solution)/shard_map/attend_back/pallas_call | solution.py:40
  261.2 8.5 %partial.5 = (bf16[2,240,768]{2,1,0:T(8,128)(2,1)}, bf16[2,240,768]{2,1,0:T(8,128)(2,1)}, bf16[2,240,768]{2,1,0:T(8,128)(2,1)}, bf16[240,768]{1,0:T(8,128)(2,1)}, bf16[2,128,768]{2,1,0:T(8,128)(2,1)}) custom-call(bf16[768,512]{1,0:T(8,128)(2,1)} %get-tuple-element.852.attended_ref.own_low, bf16[3072,512]{1,0:T(8,128)(2,1)} %get-tuple-element.780.hidden_ref.own_high, ...), custom_call_target="tpu_custom_call" | custom-call | flops 6308571648 | bytes 5485714 | tf_op jit(solution)/shard_map/partial/pallas_call | solution.py:40
  274.1 12.2 %feed_back.3 = (f32[512,768]{1,0:T(8,128)}, bf16[3072,512]{1,0:T(8,128)(2,1)}) custom-call(bf16[512,768]{1,0:T(8,128)(2,1)} %get-tuple-element.1003.right_ref.grad_ref, bf16[3072,512]{1,0:T(8,128)(2,1)} %get-tuple-element.797.slope_ref, bf16[5376,768]{1,0:T(8,128)(2,1)} %get-tuple-element.855.weight_ref.weight_in_ref, ...), custom_call_target="tpu_custom_call" | custom-call | flops 12650000384 | bytes 11000000 | tf_op jit(solution)/shard_map/feed_back/pallas_call | solution.py:40
  286.3 4.6 collective-permute-done.63
  293.3 3.5 depth.4
  296.9 10.1 %partial.6 = (bf16[2,336,768]{2,1,0:T(8,128)(2,1)}, bf16[2,336,768]{2,1,0:T(8,128)(2,1)}, bf16[2,336,768]{2,1,0:T(8,128)(2,1)}, bf16[336,768]{1,0:T(8,128)(2,1)}, bf16[2,176,768]{2,1,0:T(8,128)(2,1)}) custom-call(bf16[2304,512]{1,0:T(8,128)(2,1)} %bitcast.81, bf16[3072,512]{1,0:T(8,128)(2,1)} %get-tuple-element.809.own_high, bf16[2304,512]{1,0:T(8,128)(2,1)} %copy-done.24, ...), custom_call_target="tpu_custom_call" | custom-call | flops 8832000000 | bytes 7680000 | tf_op jit(solution)/shard_map/partial/pallas_call | solution.py:40
  309.3 4.2 collective-permute-start.72
  314.0 2.3 collective-permute-start.69
  318.0 17.7 %attend_back.3 = (bf16[3,3,256,512]{3,2,1,0:T(8,128)(2,1)}, bf16[512,768]{1,0:T(8,128)(2,1)}, f32[8,768]{1,0:T(8,128)}, f32[2,64,128]{2,1,0:T(8,128)}) custom-call(s32[1,2]{1,0:T(1,128)} %copy-done.21, bf16[512,768]{1,0:T(8,128)(2,1)} %dynamic-slice_bitcast_fusion.rows_ref, bf16[512,768]{1,0:T(8,128)(2,1)} %get-tuple-element.1003.right_ref.grad_ref, ...), custom_call_target="tpu_custom_call" | custom-call | flops 19549999104 | bytes 17000000 | tf_op jit(solution)/shard_map/attend_back/pallas_call | solution.py:40
  335.7 5.7 %collective-permute-done.70 = bf16[2,336,768]{2,1,0:T(8,128)(2,1)S(1)} collective-permute-done((bf16[2,336,768]{2,1,0:T(8,128)(2,1)}, bf16[2,336,768]{2,1,0:T(8,128)(2,1)S(1)}, u32[]{:S(2)}, u32[]{:S(2)}) %collective-permute-start.70) | collective-permute-done | bytes 1032224 | tf_op jit(solution)/shard_map/ppermute | solution.py:456
  341.5 4.0 depth.5
  349.1 10.0 %partial.7 = (bf16[2,336,768]{2,1,0:T(8,128)(2,1)}, bf16[2,336,768]{2,1,0:T(8,128)(2,1)}, bf16[2,336,768]{2,1,0:T(8,128)(2,1)}, bf16[336,768]{1,0:T(8,128)(2,1)}, bf16[2,176,768]{2,1,0:T(8,128)(2,1)}) custom-call(bf16[2304,512]{1,0:T(8,128)(2,1)} %bitcast.83, bf16[3072,512]{1,0:T(8,128)(2,1)} %get-tuple-element.883.own_high, bf16[2304,512]{1,0:T(8,128)(2,1)} %copy-done.25, ...), custom_call_target="tpu_custom_call" | custom-call | flops 8832000000 | bytes 7680000 | tf_op jit(solution)/shard_map/partial/pallas_call | solution.py:40
  359.1 3.5 collective-permute-done.77.far_ref
  363.4 2.8 collective-permute-done.80.far_other
  367.3 3.9 depth.6
  373.1 5.3 %collective-permute-start.84 = (bf16[176,768]{1,0:T(8,128)(2,1)}, bf16[176,768]{1,0:T(8,128)(2,1)S(1)}, u32[]{:S(2)}, u32[]{:S(2)}) collective-permute-start(bf16[176,768]{1,0:T(8,128)(2,1)} %get-tuple-element.922), channel_id=1, source_target_pairs={{0,8},{4,12},{8,0},{12,4},{1,9},{5,13},{9,1},{13,5},{2,10},{6,14},... | collective-permute-start | bytes 811016 | tf_op jit(solution)/shard_map/ppermute | solution.py:468
  378.4 9.6 %output.3 = (bf16[512,768]{1,0:T(8,128)(2,1)}, f32[3,8,768]{2,1,0:T(8,128)}) custom-call(s32[1,2]{1,0:T(1,128)} %copy-done.21, bf16[512,768]{1,0:T(8,128)(2,1)} %get-tuple-element.998.rows_ref, bf16[768,512]{1,0:T(8,128)(2,1)} %get-tuple-element.912.own_low.attended_ref, bf16[3072,512]{1,0:T(8,128)(2,1)} %get-tuple-element.913.own_high.hidden_ref, ...), custom_call_target="tpu_custom_call" | custom-call | flops 10350000128 | bytes 9000000 | tf_op jit(solution)/shard_map/output/pallas_call | solution.py:40
  388.1 8.8 %collective-permute-done.84.far_ref = bf16[176,768]{1,0:T(8,128)(2,1)S(1)} collective-permute-done((bf16[176,768]{1,0:T(8,128)(2,1)}, bf16[176,768]{1,0:T(8,128)(2,1)S(1)}, u32[]{:S(2)}, u32[]{:S(2)}) %collective-permute-start.84) | collective-permute-done | bytes 270368 | tf_op jit(solution)/shard_map/ppermute | solution.py:468
  397.9 2.2 collective-permute-start.86
  402.6 2.5 total.4.refs_0_
  405.1 7.7 %collective-permute-done.86.pass_ref = bf16[2,336,768]{2,1,0:T(8,128)(2,1)} collective-permute-done((bf16[2,336,768]{2,1,0:T(8,128)(2,1)S(1)}, bf16[2,336,768]{2,1,0:T(8,128)(2,1)}, u32[]{:S(2)}, u32[]{:S(2)}) %collective-permute-start.86) | collective-permute-done | bytes 1032224 | tf_op jit(solution)/shard_map/ppermute | solution.py:452
  412.8 2.0 collective-permute-start.92
  417.2 1.8 collective-permute-start.93
  419.0 3.9 depth.7
  424.4 3.9 collective-permute-start.99
  429.6 2.8 total.6.refs_0_
  432.4 2.8 total.5
  435.2 12.8 %collective-permute-done.100.far_ref = bf16[176,768]{1,0:T(8,128)(2,1)S(1)} collective-permute-done((bf16[176,768]{1,0:T(8,128)(2,1)}, bf16[176,768]{1,0:T(8,128)(2,1)S(1)}, u32[]{:S(2)}, u32[]{:S(2)}) %collective-permute-start.100) | collective-permute-done | bytes 270368 | tf_op jit(solution)/shard_map/ppermute | solution.py:468
  448.1 2.1 collective-permute-start.104
  450.2 2.5 collective-permute-start.103
  458.2 3.1 total.7
  (454 shorter events, 93.6 us)
Async XLA Ops:
  15.2 20.7 %collective-permute-start.4 = (bf16[176,768]{1,0:T(8,128)(2,1)S(1)}, bf16[176,768]{1,0:T(8,128)(2,1)S(1)}, u32[]{:S(2)}, u32[]{:S(2)}) collective-permute-start(bf16[176,768]{1,0:T(8,128)(2,1)S(1)} %copy-done.95), channel_id=1, source_target_pairs={{0,8},{4,12},{8,0},{12,4},{1,9},{5,13},{9,1},{13,5},{2,10},{6,14},... | collective-permute-start | bytes 811016 | tf_op jit(solution)/shard_map/ppermute | solution.py:468
  17.7 19.0 %collective-permute-start.3 = (bf16[336,768]{1,0:T(8,128)(2,1)S(1)}, bf16[336,768]{1,0:T(8,128)(2,1)S(1)}, u32[]{:S(2)}, u32[]{:S(2)}) collective-permute-start(bf16[336,768]{1,0:T(8,128)(2,1)S(1)} %copy-done.67), channel_id=1, source_target_pairs={{0,4},{1,5},{2,6},{3,7},{4,8},{5,9},{6,10},{7,11},{8,12},{9,13},{1... | collective-permute-start | bytes 1548296 | tf_op jit(solution)/shard_map/ppermute | solution.py:461
  45.5 21.0 %collective-permute-start.11 = (bf16[2,336,768]{2,1,0:T(8,128)(2,1)}, bf16[2,336,768]{2,1,0:T(8,128)(2,1)S(1)}, u32[]{:S(2)}, u32[]{:S(2)}) collective-permute-start(bf16[2,336,768]{2,1,0:T(8,128)(2,1)} %get-tuple-element.586.refs_0_), channel_id=1, source_target_pairs={{0,1},{1,0},{2,3},{3,2},{4,5},{5,4},{6,7},{7,6},{8,9},{9,8},{10,11... | collective-permute-start | bytes 3096584 | tf_op jit(solution)/shard_map/ppermute | solution.py:452
  46.1 25.4 %collective-permute-start.10 = (bf16[2,336,768]{2,1,0:T(8,128)(2,1)}, bf16[2,336,768]{2,1,0:T(8,128)(2,1)S(1)}, u32[]{:S(2)}, u32[]{:S(2)}) collective-permute-start(bf16[2,336,768]{2,1,0:T(8,128)(2,1)} %get-tuple-element.587.refs_1_), channel_id=1, source_target_pairs={{0,1},{1,0},{2,3},{3,2},{4,5},{5,4},{6,7},{7,6},{8,9},{9,8},{10,11... | collective-permute-start | bytes 3096584 | tf_op jit(solution)/shard_map/ppermute | solution.py:452
  47.6 18.9 %collective-permute-start.12 = (bf16[240,768]{1,0:T(8,128)(2,1)S(1)}, bf16[240,768]{1,0:T(8,128)(2,1)S(1)}, u32[]{:S(2)}, u32[]{:S(2)}) collective-permute-start(bf16[240,768]{1,0:T(8,128)(2,1)S(1)} %copy-done.77), channel_id=1, source_target_pairs={{0,4},{1,5},{2,6},{3,7},{4,8},{5,9},{6,10},{7,11},{8,12},{9,13},{1... | collective-permute-start | bytes 1105928 | tf_op jit(solution)/shard_map/ppermute | solution.py:461
  53.0 13.5 %collective-permute-start.13 = (bf16[128,768]{1,0:T(8,128)(2,1)S(1)}, bf16[128,768]{1,0:T(8,128)(2,1)S(1)}, u32[]{:S(2)}, u32[]{:S(2)}) collective-permute-start(bf16[128,768]{1,0:T(8,128)(2,1)S(1)} %copy-done.104), channel_id=1, source_target_pairs={{0,8},{4,12},{8,0},{12,4},{1,9},{5,13},{9,1},{13,5},{2,10},{6,14},... | collective-permute-start | bytes 589832 | tf_op jit(solution)/shard_map/ppermute | solution.py:468
  71.5 14.9 %collective-permute-start.17 = (bf16[2,336,768]{2,1,0:T(8,128)(2,1)S(1)}, bf16[2,336,768]{2,1,0:T(8,128)(2,1)S(1)}, u32[]{:S(2)}, u32[]{:S(2)}) collective-permute-start(bf16[2,336,768]{2,1,0:T(8,128)(2,1)S(1)} %collective-permute-done.11.refs_2_), channel_id=1, source_target_pairs={{0,16},{16,0},{1,17},{17,1},{2,18},{18,2},{3,19},{19,3},{4,20},{20... | collective-permute-start | bytes 3096584 | tf_op jit(solution)/shard_map/ppermute | solution.py:472
  71.5 14.9 %collective-permute-start.18 = (bf16[2,336,768]{2,1,0:T(8,128)(2,1)S(1)}, bf16[2,336,768]{2,1,0:T(8,128)(2,1)S(1)}, u32[]{:S(2)}, u32[]{:S(2)}) collective-permute-start(bf16[2,336,768]{2,1,0:T(8,128)(2,1)S(1)} %collective-permute-done.10.refs_3_), channel_id=1, source_target_pairs={{0,16},{16,0},{1,17},{17,1},{2,18},{18,2},{3,19},{19,3},{4,20},{20... | collective-permute-start | bytes 3096584 | tf_op jit(solution)/shard_map/ppermute | solution.py:472
  72.5 15.4 %collective-permute-start.19 = (bf16[2,336,768]{2,1,0:T(8,128)(2,1)S(1)}, bf16[2,336,768]{2,1,0:T(8,128)(2,1)S(1)}, u32[]{:S(2)}, u32[]{:S(2)}) collective-permute-start(bf16[2,336,768]{2,1,0:T(8,128)(2,1)S(1)} %collective-permute-done.10.refs_3_), channel_id=1, source_target_pairs={{0,2},{1,3},{2,0},{3,1},{4,6},{5,7},{6,4},{7,5},{8,10},{9,11},{10,... | collective-permute-start | bytes 3096584 | tf_op jit(solution)/shard_map/ppermute | solution.py:456
  88.9 25.5 %collective-permute-start.24 = (bf16[176,768]{1,0:T(8,128)(2,1)}, bf16[176,768]{1,0:T(8,128)(2,1)}, u32[]{:S(2)}, u32[]{:S(2)}) collective-permute-start(bf16[176,768]{1,0:T(8,128)(2,1)} %get-tuple-element.606), channel_id=1, source_target_pairs={{0,8},{4,12},{8,0},{12,4},{1,9},{5,13},{9,1},{13,5},{2,10},{6,14},... | collective-permute-start | bytes 811016 | tf_op jit(solution)/shard_map/ppermute | solution.py:468
  95.4 19.0 %collective-permute-start.23 = (bf16[336,768]{1,0:T(8,128)(2,1)S(1)}, bf16[336,768]{1,0:T(8,128)(2,1)}, u32[]{:S(2)}, u32[]{:S(2)}) collective-permute-start(bf16[336,768]{1,0:T(8,128)(2,1)S(1)} %copy-done.65), channel_id=1, source_target_pairs={{0,4},{1,5},{2,6},{3,7},{4,8},{5,9},{6,10},{7,11},{8,12},{9,13},{1... | collective-permute-start | bytes 1548296 | tf_op jit(solution)/shard_map/ppermute | solution.py:461
  95.4 19.0 %collective-permute-start.21 = (bf16[2,240,768]{2,1,0:T(8,128)(2,1)}, bf16[2,240,768]{2,1,0:T(8,128)(2,1)}, u32[]{:S(2)}, u32[]{:S(2)}) collective-permute-start(bf16[2,240,768]{2,1,0:T(8,128)(2,1)} %get-tuple-element.633.refs_1_), channel_id=1, source_target_pairs={{0,1},{1,0},{2,3},{3,2},{4,5},{5,4},{6,7},{7,6},{8,9},{9,8},{10,11... | collective-permute-start | bytes 2211848 | tf_op jit(solution)/shard_map/ppermute | solution.py:452
  96.0 19.1 %collective-permute-start.22 = (bf16[2,240,768]{2,1,0:T(8,128)(2,1)}, bf16[2,240,768]{2,1,0:T(8,128)(2,1)}, u32[]{:S(2)}, u32[]{:S(2)}) collective-permute-start(bf16[2,240,768]{2,1,0:T(8,128)(2,1)} %get-tuple-element.632.refs_0_), channel_id=1, source_target_pairs={{0,1},{1,0},{2,3},{3,2},{4,5},{5,4},{6,7},{7,6},{8,9},{9,8},{10,11... | collective-permute-start | bytes 2211848 | tf_op jit(solution)/shard_map/ppermute | solution.py:452
  115.1 10.9 %collective-permute-start.29 = (bf16[176,768]{1,0:T(8,128)(2,1)}, bf16[176,768]{1,0:T(8,128)(2,1)S(1)}, u32[]{:S(2)}, u32[]{:S(2)}) collective-permute-start(bf16[176,768]{1,0:T(8,128)(2,1)} %collective-permute-done.24.far_ref), channel_id=1, source_target_pairs={{0,16},{16,0},{1,17},{17,1},{2,18},{18,2},{3,19},{19,3},{4,20},{20... | collective-permute-start | bytes 811016 | tf_op jit(solution)/shard_map/ppermute | solution.py:472
  115.1 11.0 %collective-permute-start.28 = (bf16[336,768]{1,0:T(8,128)(2,1)}, bf16[336,768]{1,0:T(8,128)(2,1)S(1)}, u32[]{:S(2)}, u32[]{:S(2)}) collective-permute-start(bf16[336,768]{1,0:T(8,128)(2,1)} %collective-permute-done.23.near_ref), channel_id=1, source_target_pairs={{0,16},{16,0},{1,17},{17,1},{2,18},{18,2},{3,19},{19,3},{4,20},{20... | collective-permute-start | bytes 1548296 | tf_op jit(solution)/shard_map/ppermute | solution.py:472
  115.6 11.7 %collective-permute-start.25 = (bf16[2,240,768]{2,1,0:T(8,128)(2,1)}, bf16[2,240,768]{2,1,0:T(8,128)(2,1)S(1)}, u32[]{:S(2)}, u32[]{:S(2)}) collective-permute-start(bf16[2,240,768]{2,1,0:T(8,128)(2,1)} %collective-permute-done.21.refs_3_), channel_id=1, source_target_pairs={{0,2},{1,3},{2,0},{3,1},{4,6},{5,7},{6,4},{7,5},{8,10},{9,11},{10,... | collective-permute-start | bytes 2211848 | tf_op jit(solution)/shard_map/ppermute | solution.py:456
  117.1 10.2 %collective-permute-start.26 = (bf16[2,240,768]{2,1,0:T(8,128)(2,1)}, bf16[2,240,768]{2,1,0:T(8,128)(2,1)S(1)}, u32[]{:S(2)}, u32[]{:S(2)}) collective-permute-start(bf16[2,240,768]{2,1,0:T(8,128)(2,1)} %collective-permute-done.22.refs_2_), channel_id=1, source_target_pairs={{0,16},{16,0},{1,17},{17,1},{2,18},{18,2},{3,19},{19,3},{4,20},{20... | collective-permute-start | bytes 2211848 | tf_op jit(solution)/shard_map/ppermute | solution.py:472
  117.1 10.2 %collective-permute-start.27 = (bf16[2,240,768]{2,1,0:T(8,128)(2,1)}, bf16[2,240,768]{2,1,0:T(8,128)(2,1)S(1)}, u32[]{:S(2)}, u32[]{:S(2)}) collective-permute-start(bf16[2,240,768]{2,1,0:T(8,128)(2,1)} %collective-permute-done.21.refs_3_), channel_id=1, source_target_pairs={{0,16},{16,0},{1,17},{17,1},{2,18},{18,2},{3,19},{19,3},{4,20},{20... | collective-permute-start | bytes 2211848 | tf_op jit(solution)/shard_map/ppermute | solution.py:472
  131.3 20.9 %collective-permute-start.32 = (bf16[2,336,768]{2,1,0:T(8,128)(2,1)}, bf16[2,336,768]{2,1,0:T(8,128)(2,1)S(1)}, u32[]{:S(2)}, u32[]{:S(2)}) collective-permute-start(bf16[2,336,768]{2,1,0:T(8,128)(2,1)} %get-tuple-element.677.refs_0_), channel_id=1, source_target_pairs={{0,1},{1,0},{2,3},{3,2},{4,5},{5,4},{6,7},{7,6},{8,9},{9,8},{10,11... | collective-permute-start | bytes 3096584 | tf_op jit(solution)/shard_map/ppermute | solution.py:452
  131.9 25.4 %collective-permute-start.31 = (bf16[2,336,768]{2,1,0:T(8,128)(2,1)}, bf16[2,336,768]{2,1,0:T(8,128)(2,1)S(1)}, u32[]{:S(2)}, u32[]{:S(2)}) collective-permute-start(bf16[2,336,768]{2,1,0:T(8,128)(2,1)} %get-tuple-element.678.refs_1_), channel_id=1, source_target_pairs={{0,1},{1,0},{2,3},{3,2},{4,5},{5,4},{6,7},{7,6},{8,9},{9,8},{10,11... | collective-permute-start | bytes 3096584 | tf_op jit(solution)/shard_map/ppermute | solution.py:452
  133.4 15.9 %collective-permute-start.34 = (bf16[128,768]{1,0:T(8,128)(2,1)S(1)}, bf16[128,768]{1,0:T(8,128)(2,1)S(1)}, u32[]{:S(2)}, u32[]{:S(2)}) collective-permute-start(bf16[128,768]{1,0:T(8,128)(2,1)S(1)} %copy-done.97), channel_id=1, source_target_pairs={{0,8},{4,12},{8,0},{12,4},{1,9},{5,13},{9,1},{13,5},{2,10},{6,14},... | collective-permute-start | bytes 589832 | tf_op jit(solution)/shard_map/ppermute | solution.py:468
  137.6 14.6 %collective-permute-start.33 = (bf16[240,768]{1,0:T(8,128)(2,1)S(1)}, bf16[240,768]{1,0:T(8,128)(2,1)S(1)}, u32[]{:S(2)}, u32[]{:S(2)}) collective-permute-start(bf16[240,768]{1,0:T(8,128)(2,1)S(1)} %copy-done.74), channel_id=1, source_target_pairs={{0,4},{1,5},{2,6},{3,7},{4,8},{5,9},{6,10},{7,11},{8,12},{9,13},{1... | collective-permute-start | bytes 1105928 | tf_op jit(solution)/shard_map/ppermute | solution.py:461
  158.3 14.6 %collective-permute-start.37 = (bf16[2,336,768]{2,1,0:T(8,128)(2,1)S(1)}, bf16[2,336,768]{2,1,0:T(8,128)(2,1)S(1)}, u32[]{:S(2)}, u32[]{:S(2)}) collective-permute-start(bf16[2,336,768]{2,1,0:T(8,128)(2,1)S(1)} %collective-permute-done.31.refs_3_), channel_id=1, source_target_pairs={{0,2},{1,3},{2,0},{3,1},{4,6},{5,7},{6,4},{7,5},{8,10},{9,11},{10,... | collective-permute-start | bytes 3096584 | tf_op jit(solution)/shard_map/ppermute | solution.py:456
  175.7 19.8 %collective-permute-start.46 = (bf16[3072,512]{1,0:T(8,128)(2,1)}, bf16[3072,512]{1,0:T(8,128)(2,1)S(1)}, u32[]{:S(2)}, u32[]{:S(2)}) collective-permute-start(bf16[3072,512]{1,0:T(8,128)(2,1)} %get-tuple-element.780.hidden_ref.own_high), channel_id=1, source_target_pairs={{0,16},{16,0},{1,17},{17,1},{2,18},{18,2},{3,19},{19,3},{4,20},{20... | collective-permute-start | bytes 9437192 | tf_op jit(solution)/shard_map/ppermute | solution.py:472
  175.8 18.4 %collective-permute-start.42 = (bf16[2,240,768]{2,1,0:T(8,128)(2,1)}, bf16[2,240,768]{2,1,0:T(8,128)(2,1)}, u32[]{:S(2)}, u32[]{:S(2)}) collective-permute-start(bf16[2,240,768]{2,1,0:T(8,128)(2,1)} %get-tuple-element.718.refs_1_), channel_id=1, source_target_pairs={{0,1},{1,0},{2,3},{3,2},{4,5},{5,4},{6,7},{7,6},{8,9},{9,8},{10,11... | collective-permute-start | bytes 2211848 | tf_op jit(solution)/shard_map/ppermute | solution.py:452
  176.6 18.9 %collective-permute-start.43 = (bf16[2,240,768]{2,1,0:T(8,128)(2,1)}, bf16[2,240,768]{2,1,0:T(8,128)(2,1)}, u32[]{:S(2)}, u32[]{:S(2)}) collective-permute-start(bf16[2,240,768]{2,1,0:T(8,128)(2,1)} %get-tuple-element.717.refs_0_), channel_id=1, source_target_pairs={{0,1},{1,0},{2,3},{3,2},{4,5},{5,4},{6,7},{7,6},{8,9},{9,8},{10,11... | collective-permute-start | bytes 2211848 | tf_op jit(solution)/shard_map/ppermute | solution.py:452
  179.2 16.3 %collective-permute-start.44 = (bf16[768,512]{1,0:T(8,128)(2,1)}, bf16[768,512]{1,0:T(8,128)(2,1)S(1)}, u32[]{:S(2)}, u32[]{:S(2)}) collective-permute-start(bf16[768,512]{1,0:T(8,128)(2,1)} %get-tuple-element.852.attended_ref.own_low), channel_id=1, source_target_pairs={{0,16},{16,0},{1,17},{17,1},{2,18},{18,2},{3,19},{19,3},{4,20},{20... | collective-permute-start | bytes 2359304 | tf_op jit(solution)/shard_map/ppermute | solution.py:472
  179.4 16.1 %collective-permute-start.45 = (bf16[512,768]{1,0:T(8,128)(2,1)}, bf16[512,768]{1,0:T(8,128)(2,1)S(1)}, u32[]{:S(2)}, u32[]{:S(2)}) collective-permute-start(bf16[512,768]{1,0:T(8,128)(2,1)} %get-tuple-element.886.normed_ref.right_ref), channel_id=1, source_target_pairs={{0,16},{16,0},{1,17},{17,1},{2,18},{18,2},{3,19},{19,3},{4,20},{20... | collective-permute-start | bytes 2359304 | tf_op jit(solution)/shard_map/ppermute | solution.py:472
  197.2 11.7 %collective-permute-start.47 = (bf16[2,240,768]{2,1,0:T(8,128)(2,1)}, bf16[2,240,768]{2,1,0:T(8,128)(2,1)S(1)}, u32[]{:S(2)}, u32[]{:S(2)}) collective-permute-start(bf16[2,240,768]{2,1,0:T(8,128)(2,1)} %collective-permute-done.42.refs_3_), channel_id=1, source_target_pairs={{0,2},{1,3},{2,0},{3,1},{4,6},{5,7},{6,4},{7,5},{8,10},{9,11},{10,... | collective-permute-start | bytes 2211848 | tf_op jit(solution)/shard_map/ppermute | solution.py:456
  198.7 10.2 %collective-permute-start.48 = (bf16[2,240,768]{2,1,0:T(8,128)(2,1)}, bf16[2,240,768]{2,1,0:T(8,128)(2,1)S(1)}, u32[]{:S(2)}, u32[]{:S(2)}) collective-permute-start(bf16[2,240,768]{2,1,0:T(8,128)(2,1)} %collective-permute-done.43.refs_2_), channel_id=1, source_target_pairs={{0,16},{16,0},{1,17},{17,1},{2,18},{18,2},{3,19},{19,3},{4,20},{20... | collective-permute-start | bytes 2211848 | tf_op jit(solution)/shard_map/ppermute | solution.py:472
  198.7 10.2 %collective-permute-start.49 = (bf16[2,240,768]{2,1,0:T(8,128)(2,1)}, bf16[2,240,768]{2,1,0:T(8,128)(2,1)S(1)}, u32[]{:S(2)}, u32[]{:S(2)}) collective-permute-start(bf16[2,240,768]{2,1,0:T(8,128)(2,1)} %collective-permute-done.42.refs_3_), channel_id=1, source_target_pairs={{0,16},{16,0},{1,17},{17,1},{2,18},{18,2},{3,19},{19,3},{4,20},{20... | collective-permute-start | bytes 2211848 | tf_op jit(solution)/shard_map/ppermute | solution.py:472
  211.2 14.5 %collective-permute-start.54 = (bf16[3072,512]{1,0:T(8,128)(2,1)}, bf16[3072,512]{1,0:T(8,128)(2,1)S(1)}, u32[]{:S(2)}, u32[]{:S(2)}) collective-permute-start(bf16[3072,512]{1,0:T(8,128)(2,1)} %get-tuple-element.913.own_high.hidden_ref), channel_id=1, source_target_pairs={{0,16},{16,0},{1,17},{17,1},{2,18},{18,2},{3,19},{19,3},{4,20},{20... | collective-permute-start | bytes 9437192 | tf_op jit(solution)/shard_map/ppermute | solution.py:472
  212.1 13.7 %collective-permute-start.53 = (bf16[512,768]{1,0:T(8,128)(2,1)S(1)}, bf16[512,768]{1,0:T(8,128)(2,1)S(1)}, u32[]{:S(2)}, u32[]{:S(2)}) collective-permute-start(bf16[512,768]{1,0:T(8,128)(2,1)S(1)} %copy-done.4), channel_id=1, source_target_pairs={{0,16},{16,0},{1,17},{17,1},{2,18},{18,2},{3,19},{19,3},{4,20},{20... | collective-permute-start | bytes 2359304 | tf_op jit(solution)/shard_map/ppermute | solution.py:472
  225.8 10.3 %collective-permute-start.55 = (bf16[3072,512]{1,0:T(8,128)(2,1)}, bf16[3072,512]{1,0:T(8,128)(2,1)}, u32[]{:S(2)}, u32[]{:S(2)}) collective-permute-start(bf16[3072,512]{1,0:T(8,128)(2,1)} %get-tuple-element.809.own_high), channel_id=1, source_target_pairs={{0,16},{16,0},{1,17},{17,1},{2,18},{18,2},{3,19},{19,3},{4,20},{20... | collective-permute-start | bytes 9437192 | tf_op jit(solution)/shard_map/ppermute | solution.py:472
  237.5 19.6 %collective-permute-start.56 = (bf16[2,240,768]{2,1,0:T(8,128)(2,1)}, bf16[2,240,768]{2,1,0:T(8,128)(2,1)S(1)}, u32[]{:S(2)}, u32[]{:S(2)}) collective-permute-start(bf16[2,240,768]{2,1,0:T(8,128)(2,1)} %get-tuple-element.764), channel_id=1, source_target_pairs={{0,2},{1,3},{2,0},{3,1},{4,6},{5,7},{6,4},{7,5},{8,10},{9,11},{10,... | collective-permute-start | bytes 2211848 | tf_op jit(solution)/shard_map/ppermute | solution.py:456
  239.0 18.1 %collective-permute-start.57 = (bf16[2,240,768]{2,1,0:T(8,128)(2,1)}, bf16[2,240,768]{2,1,0:T(8,128)(2,1)S(1)}, u32[]{:S(2)}, u32[]{:S(2)}) collective-permute-start(bf16[2,240,768]{2,1,0:T(8,128)(2,1)} %get-tuple-element.766), channel_id=1, source_target_pairs={{0,1},{1,0},{2,3},{3,2},{4,5},{5,4},{6,7},{7,6},{8,9},{9,8},{10,11... | collective-permute-start | bytes 2211848 | tf_op jit(solution)/shard_map/ppermute | solution.py:452
  257.2 34.0 %collective-permute-start.58 = (bf16[2304,512]{1,0:T(8,128)(2,1)}, bf16[2304,512]{1,0:T(8,128)(2,1)S(1)}, u32[]{:S(2)}, u32[]{:S(2)}) collective-permute-start(bf16[2304,512]{1,0:T(8,128)(2,1)} %bitcast.80), channel_id=1, source_target_pairs={{0,16},{16,0},{1,17},{17,1},{2,18},{18,2},{3,19},{19,3},{4,20},{20... | collective-permute-start | bytes 7077896 | tf_op jit(solution)/shard_map/ppermute | solution.py:472
  259.7 11.5 %collective-permute-start.60 = (bf16[2,240,768]{2,1,0:T(8,128)(2,1)S(1)}, bf16[2,240,768]{2,1,0:T(8,128)(2,1)S(1)}, u32[]{:S(2)}, u32[]{:S(2)}) collective-permute-start(bf16[2,240,768]{2,1,0:T(8,128)(2,1)S(1)} %add_convert_fusion.3), channel_id=1, source_target_pairs={{0,1},{1,0},{2,3},{3,2},{4,5},{5,4},{6,7},{7,6},{8,9},{9,8},{10,11... | collective-permute-start | bytes 2211848 | tf_op jit(solution)/shard_map/ppermute | solution.py:452
  272.1 14.2 %collective-permute-start.62 = (bf16[2,240,768]{2,1,0:T(8,128)(2,1)S(1)}, bf16[2,240,768]{2,1,0:T(8,128)(2,1)S(1)}, u32[]{:S(2)}, u32[]{:S(2)}) collective-permute-start(bf16[2,240,768]{2,1,0:T(8,128)(2,1)S(1)} %collective-permute-done.60.pass_ref), channel_id=1, source_target_pairs={{0,16},{16,0},{1,17},{17,1},{2,18},{18,2},{3,19},{19,3},{4,20},{20... | collective-permute-start | bytes 2211848 | tf_op jit(solution)/shard_map/ppermute | solution.py:472
  272.1 18.9 %collective-permute-start.63 = (bf16[2,240,768]{2,1,0:T(8,128)(2,1)}, bf16[2,240,768]{2,1,0:T(8,128)(2,1)S(1)}, u32[]{:S(2)}, u32[]{:S(2)}) collective-permute-start(bf16[2,240,768]{2,1,0:T(8,128)(2,1)} %get-tuple-element.793), channel_id=1, source_target_pairs={{0,2},{1,3},{2,0},{3,1},{4,6},{5,7},{6,4},{7,5},{8,10},{9,11},{10,... | collective-permute-start | bytes 2211848 | tf_op jit(solution)/shard_map/ppermute | solution.py:456
  273.1 18.1 %collective-permute-start.64 = (bf16[2,240,768]{2,1,0:T(8,128)(2,1)}, bf16[2,240,768]{2,1,0:T(8,128)(2,1)S(1)}, u32[]{:S(2)}, u32[]{:S(2)}) collective-permute-start(bf16[2,240,768]{2,1,0:T(8,128)(2,1)} %get-tuple-element.803), channel_id=1, source_target_pairs={{0,1},{1,0},{2,3},{3,2},{4,5},{5,4},{6,7},{7,6},{8,9},{9,8},{10,11... | collective-permute-start | bytes 2211848 | tf_op jit(solution)/shard_map/ppermute | solution.py:452
  291.4 16.6 %collective-permute-start.67 = (bf16[3072,512]{1,0:T(8,128)(2,1)}, bf16[3072,512]{1,0:T(8,128)(2,1)}, u32[]{:S(2)}, u32[]{:S(2)}) collective-permute-start(bf16[3072,512]{1,0:T(8,128)(2,1)} %get-tuple-element.883.own_high), channel_id=1, source_target_pairs={{0,16},{16,0},{1,17},{17,1},{2,18},{18,2},{3,19},{19,3},{4,20},{20... | collective-permute-start | bytes 9437192 | tf_op jit(solution)/shard_map/ppermute | solution.py:472
  291.7 15.3 %collective-permute-start.65 = (bf16[2,240,768]{2,1,0:T(8,128)(2,1)S(1)}, bf16[2,240,768]{2,1,0:T(8,128)(2,1)}, u32[]{:S(2)}, u32[]{:S(2)}) collective-permute-start(bf16[2,240,768]{2,1,0:T(8,128)(2,1)S(1)} %add_convert_fusion.2), channel_id=1, source_target_pairs={{0,1},{1,0},{2,3},{3,2},{4,5},{5,4},{6,7},{7,6},{8,9},{9,8},{10,11... | collective-permute-start | bytes 2211848 | tf_op jit(solution)/shard_map/ppermute | solution.py:452
  293.3 13.7 %collective-permute-start.66 = (bf16[2,240,768]{2,1,0:T(8,128)(2,1)S(1)}, bf16[2,240,768]{2,1,0:T(8,128)(2,1)S(1)}, u32[]{:S(2)}, u32[]{:S(2)}) collective-permute-start(bf16[2,240,768]{2,1,0:T(8,128)(2,1)S(1)} %collective-permute-done.64.keep_ref), channel_id=1, source_target_pairs={{0,16},{16,0},{1,17},{17,1},{2,18},{18,2},{3,19},{19,3},{4,20},{20... | collective-permute-start | bytes 2211848 | tf_op jit(solution)/shard_map/ppermute | solution.py:472
  309.3 26.3 %collective-permute-start.72 = (bf16[128,768]{1,0:T(8,128)(2,1)S(1)}, bf16[128,768]{1,0:T(8,128)(2,1)S(1)}, u32[]{:S(2)}, u32[]{:S(2)}) collective-permute-start(bf16[128,768]{1,0:T(8,128)(2,1)S(1)} %copy-done.106), channel_id=1, source_target_pairs={{0,8},{4,12},{8,0},{12,4},{1,9},{5,13},{9,1},{13,5},{2,10},{6,14},... | collective-permute-start | bytes 589832 | tf_op jit(solution)/shard_map/ppermute | solution.py:468
  313.5 22.1 %collective-permute-start.71 = (bf16[240,768]{1,0:T(8,128)(2,1)S(1)}, bf16[240,768]{1,0:T(8,128)(2,1)S(1)}, u32[]{:S(2)}, u32[]{:S(2)}) collective-permute-start(bf16[240,768]{1,0:T(8,128)(2,1)S(1)} %copy-done.79), channel_id=1, source_target_pairs={{0,4},{1,5},{2,6},{3,7},{4,8},{5,9},{6,10},{7,11},{8,12},{9,13},{1... | collective-permute-start | bytes 1105928 | tf_op jit(solution)/shard_map/ppermute | solution.py:461
  314.0 21.6 %collective-permute-start.69 = (bf16[2,240,768]{2,1,0:T(8,128)(2,1)}, bf16[2,240,768]{2,1,0:T(8,128)(2,1)S(1)}, u32[]{:S(2)}, u32[]{:S(2)}) collective-permute-start(bf16[2,240,768]{2,1,0:T(8,128)(2,1)} %collective-permute-done.65.pass_ref), channel_id=1, source_target_pairs={{0,16},{16,0},{1,17},{17,1},{2,18},{18,2},{3,19},{19,3},{4,20},{20... | collective-permute-start | bytes 2211848 | tf_op jit(solution)/shard_map/ppermute | solution.py:472
  316.3 25.1 %collective-permute-start.70 = (bf16[2,336,768]{2,1,0:T(8,128)(2,1)}, bf16[2,336,768]{2,1,0:T(8,128)(2,1)S(1)}, u32[]{:S(2)}, u32[]{:S(2)}) collective-permute-start(bf16[2,336,768]{2,1,0:T(8,128)(2,1)} %get-tuple-element.841), channel_id=1, source_target_pairs={{0,2},{1,3},{2,0},{3,1},{4,6},{5,7},{6,4},{7,5},{8,10},{9,11},{10,... | collective-permute-start | bytes 3096584 | tf_op jit(solution)/shard_map/ppermute | solution.py:456
  316.7 24.7 %collective-permute-start.68 = (bf16[2,336,768]{2,1,0:T(8,128)(2,1)}, bf16[2,336,768]{2,1,0:T(8,128)(2,1)S(1)}, u32[]{:S(2)}, u32[]{:S(2)}) collective-permute-start(bf16[2,336,768]{2,1,0:T(8,128)(2,1)} %get-tuple-element.836), channel_id=1, source_target_pairs={{0,1},{1,0},{2,3},{3,2},{4,5},{5,4},{6,7},{7,6},{8,9},{9,8},{10,11... | collective-permute-start | bytes 3096584 | tf_op jit(solution)/shard_map/ppermute | solution.py:452
  346.2 16.4 %collective-permute-start.75 = (bf16[2,336,768]{2,1,0:T(8,128)(2,1)S(1)}, bf16[2,336,768]{2,1,0:T(8,128)(2,1)S(1)}, u32[]{:S(2)}, u32[]{:S(2)}) collective-permute-start(bf16[2,336,768]{2,1,0:T(8,128)(2,1)S(1)} %collective-permute-done.68.keep_ref), channel_id=1, source_target_pairs={{0,16},{16,0},{1,17},{17,1},{2,18},{18,2},{3,19},{19,3},{4,20},{20... | collective-permute-start | bytes 3096584 | tf_op jit(solution)/shard_map/ppermute | solution.py:472
  346.4 16.3 %collective-permute-start.74 = (bf16[2,336,768]{2,1,0:T(8,128)(2,1)S(1)}, bf16[2,336,768]{2,1,0:T(8,128)(2,1)S(1)}, u32[]{:S(2)}, u32[]{:S(2)}) collective-permute-start(bf16[2,336,768]{2,1,0:T(8,128)(2,1)S(1)} %add_convert_fusion.1), channel_id=1, source_target_pairs={{0,1},{1,0},{2,3},{3,2},{4,5},{5,4},{6,7},{7,6},{8,9},{9,8},{10,11... | collective-permute-start | bytes 3096584 | tf_op jit(solution)/shard_map/ppermute | solution.py:452
  347.3 15.4 %collective-permute-start.77 = (bf16[128,768]{1,0:T(8,128)(2,1)}, bf16[128,768]{1,0:T(8,128)(2,1)}, u32[]{:S(2)}, u32[]{:S(2)}) collective-permute-start(bf16[128,768]{1,0:T(8,128)(2,1)} %get-tuple-element.895), channel_id=1, source_target_pairs={{0,8},{4,12},{8,0},{12,4},{1,9},{5,13},{9,1},{13,5},{2,10},{6,14},... | collective-permute-start | bytes 589832 | tf_op jit(solution)/shard_map/ppermute | solution.py:468
  348.1 14.6 %collective-permute-start.76 = (bf16[240,768]{1,0:T(8,128)(2,1)}, bf16[240,768]{1,0:T(8,128)(2,1)S(1)}, u32[]{:S(2)}, u32[]{:S(2)}) collective-permute-start(bf16[240,768]{1,0:T(8,128)(2,1)} %get-tuple-element.893), channel_id=1, source_target_pairs={{0,4},{1,5},{2,6},{3,7},{4,8},{5,9},{6,10},{7,11},{8,12},{9,13},{1... | collective-permute-start | bytes 1105928 | tf_op jit(solution)/shard_map/ppermute | solution.py:461
  371.3 26.1 %collective-permute-start.81 = (bf16[2,336,768]{2,1,0:T(8,128)(2,1)S(1)}, bf16[2,336,768]{2,1,0:T(8,128)(2,1)S(1)}, u32[]{:S(2)}, u32[]{:S(2)}) collective-permute-start(bf16[2,336,768]{2,1,0:T(8,128)(2,1)S(1)} %copy-done.34), channel_id=1, source_target_pairs={{0,2},{1,3},{2,0},{3,1},{4,6},{5,7},{6,4},{7,5},{8,10},{9,11},{10,... | collective-permute-start | bytes 3096584 | tf_op jit(solution)/shard_map/ppermute | solution.py:456
  372.7 24.7 %collective-permute-start.82 = (bf16[2,336,768]{2,1,0:T(8,128)(2,1)S(1)}, bf16[2,336,768]{2,1,0:T(8,128)(2,1)}, u32[]{:S(2)}, u32[]{:S(2)}) collective-permute-start(bf16[2,336,768]{2,1,0:T(8,128)(2,1)S(1)} %copy-done.33), channel_id=1, source_target_pairs={{0,1},{1,0},{2,3},{3,2},{4,5},{5,4},{6,7},{7,6},{8,9},{9,8},{10,11... | collective-permute-start | bytes 3096584 | tf_op jit(solution)/shard_map/ppermute | solution.py:452
  373.1 15.1 %collective-permute-start.85 = (bf16[128,768]{1,0:T(8,128)(2,1)S(1)}, bf16[128,768]{1,0:T(8,128)(2,1)S(1)}, u32[]{:S(2)}, u32[]{:S(2)}) collective-permute-start(bf16[128,768]{1,0:T(8,128)(2,1)S(1)} %copy-done.99), channel_id=1, source_target_pairs={{0,16},{16,0},{1,17},{17,1},{2,18},{18,2},{3,19},{19,3},{4,20},{20... | collective-permute-start | bytes 589832 | tf_op jit(solution)/shard_map/ppermute | solution.py:472
  373.1 23.8 %collective-permute-start.84 = (bf16[176,768]{1,0:T(8,128)(2,1)}, bf16[176,768]{1,0:T(8,128)(2,1)S(1)}, u32[]{:S(2)}, u32[]{:S(2)}) collective-permute-start(bf16[176,768]{1,0:T(8,128)(2,1)} %get-tuple-element.922), channel_id=1, source_target_pairs={{0,8},{4,12},{8,0},{12,4},{1,9},{5,13},{9,1},{13,5},{2,10},{6,14},... | collective-permute-start | bytes 811016 | tf_op jit(solution)/shard_map/ppermute | solution.py:468
  378.4 19.0 %collective-permute-start.83 = (bf16[336,768]{1,0:T(8,128)(2,1)}, bf16[336,768]{1,0:T(8,128)(2,1)S(1)}, u32[]{:S(2)}, u32[]{:S(2)}) collective-permute-start(bf16[336,768]{1,0:T(8,128)(2,1)} %get-tuple-element.920), channel_id=1, source_target_pairs={{0,4},{1,5},{2,6},{3,7},{4,8},{5,9},{6,10},{7,11},{8,12},{9,13},{1... | collective-permute-start | bytes 1548296 | tf_op jit(solution)/shard_map/ppermute | solution.py:461
  397.9 14.9 %collective-permute-start.86 = (bf16[2,336,768]{2,1,0:T(8,128)(2,1)S(1)}, bf16[2,336,768]{2,1,0:T(8,128)(2,1)}, u32[]{:S(2)}, u32[]{:S(2)}) collective-permute-start(bf16[2,336,768]{2,1,0:T(8,128)(2,1)S(1)} %add_convert_fusion), channel_id=1, source_target_pairs={{0,1},{1,0},{2,3},{3,2},{4,5},{5,4},{6,7},{7,6},{8,9},{9,8},{10,11... | collective-permute-start | bytes 3096584 | tf_op jit(solution)/shard_map/ppermute | solution.py:452
  400.1 12.7 %collective-permute-start.87 = (bf16[2,336,768]{2,1,0:T(8,128)(2,1)}, bf16[2,336,768]{2,1,0:T(8,128)(2,1)}, u32[]{:S(2)}, u32[]{:S(2)}) collective-permute-start(bf16[2,336,768]{2,1,0:T(8,128)(2,1)} %collective-permute-done.82.keep_ref), channel_id=1, source_target_pairs={{0,16},{16,0},{1,17},{17,1},{2,18},{18,2},{3,19},{19,3},{4,20},{20... | collective-permute-start | bytes 3096584 | tf_op jit(solution)/shard_map/ppermute | solution.py:472
  423.9 24.2 %collective-permute-start.97 = (bf16[512,768]{1,0:T(8,128)(2,1)S(1)}, bf16[512,768]{1,0:T(8,128)(2,1)S(1)}, u32[]{:S(2)}, u32[]{:S(2)}) collective-permute-start(bf16[512,768]{1,0:T(8,128)(2,1)S(1)} %copy-done.10), channel_id=1, source_target_pairs={{0,16},{16,0},{1,17},{17,1},{2,18},{18,2},{3,19},{19,3},{4,20},{20... | collective-permute-start | bytes 2359304 | tf_op jit(solution)/shard_map/ppermute | solution.py:472
  424.0 24.0 %collective-permute-start.98 = (bf16[512,768]{1,0:T(8,128)(2,1)S(1)}, bf16[512,768]{1,0:T(8,128)(2,1)}, u32[]{:S(2)}, u32[]{:S(2)}) collective-permute-start(bf16[512,768]{1,0:T(8,128)(2,1)S(1)} %copy-done.9), channel_id=1, source_target_pairs={{0,16},{16,0},{1,17},{17,1},{2,18},{18,2},{3,19},{19,3},{4,20},{20... | collective-permute-start | bytes 2359304 | tf_op jit(solution)/shard_map/ppermute | solution.py:472
  424.4 23.6 %collective-permute-start.99 = (bf16[336,768]{1,0:T(8,128)(2,1)}, bf16[336,768]{1,0:T(8,128)(2,1)}, u32[]{:S(2)}, u32[]{:S(2)}) collective-permute-start(bf16[336,768]{1,0:T(8,128)(2,1)} %get-tuple-element.992), channel_id=1, source_target_pairs={{0,4},{1,5},{2,6},{3,7},{4,8},{5,9},{6,10},{7,11},{8,12},{9,13},{1... | collective-permute-start | bytes 1548296 | tf_op jit(solution)/shard_map/ppermute | solution.py:461
  428.3 19.8 %collective-permute-start.100 = (bf16[176,768]{1,0:T(8,128)(2,1)}, bf16[176,768]{1,0:T(8,128)(2,1)S(1)}, u32[]{:S(2)}, u32[]{:S(2)}) collective-permute-start(bf16[176,768]{1,0:T(8,128)(2,1)} %get-tuple-element.994), channel_id=1, source_target_pairs={{0,8},{4,12},{8,0},{12,4},{1,9},{5,13},{9,1},{13,5},{2,10},{6,14},... | collective-permute-start | bytes 811016 | tf_op jit(solution)/shard_map/ppermute | solution.py:468
  (154 other events, 1381.1 us)

commit v4 on v3

--- a/solution.py
+++ b/solution.py
@@ -19,7 +19,7 @@
 BF16 = jnp.bfloat16
 DP = ("z", "y", "x")
 ALL = ("section",) + DP
-VMEM_MIB = 56
+VMEM_MIB = 60
 ANY = pl.BlockSpec(memory_space=pl.ANY)
 VMEM = pl.BlockSpec(memory_space=pltpu.VMEM)
 
@@ -528,28 +528,31 @@
     )
 
 
-def line_kernel(own_ref, near_ref, other_ref, far_ref, far_other_ref, keep_ref, pass_ref, line_ref, sems):
+def line_kernel(own_ref, near_ref, other_ref, far_ref, far_other_ref, keep_ref, pass_ref, sems):
     core, z = lax.axis_index("section"), lax.axis_index("z")
-    depth = line_ref.shape[0]
-    half = far_ref.shape[0]
+    depth = 4
+    rows, half = own_ref.shape[0], far_ref.shape[0]
     below, above, far = lax.rem(z + depth - 1, depth), lax.rem(z + 1, depth), lax.rem(z + 2, depth)
     near_at, other_at = jnp.where(core == 0, below, above), jnp.where(core == 0, above, below)
-    rest = own_ref.shape[0] - half
+    rest = rows - half
     first, second = pl.multiple_of(core * rest, 16), pl.multiple_of((1 - core) * half, 16)
     skipped = pl.multiple_of((1 - core) * (half - rest), 16)
-    copies = [
-        pltpu.make_async_copy(own_ref, line_ref.at[z], sems.at[0]),
-        pltpu.make_async_copy(near_ref, line_ref.at[near_at], sems.at[1]),
-        pltpu.make_async_copy(other_ref, line_ref.at[other_at], sems.at[2]),
-        pltpu.make_async_copy(far_ref, line_ref.at[far, pl.ds(first, half)], sems.at[3]),
-        pltpu.make_async_copy(far_other_ref.at[pl.ds(skipped, rest)], line_ref.at[far, pl.ds(second, rest)], sems.at[4]),
-    ]
-    for copy in copies:
-        copy.start()
+    moves = (
+        (own_ref, z, pl.ds(0, rows)),
+        (near_ref, near_at, pl.ds(0, rows)),
+        (other_ref, other_at, pl.ds(0, rows)),
+        (far_ref, far, pl.ds(first, half)),
+        (far_other_ref.at[pl.ds(skipped, rest)], far, pl.ds(second, rest)),
+    )
+    copies = []
+    for at, (source, slot, part) in enumerate(moves):
+        index = lax.rem(slot, 2)
+        kept = pltpu.make_async_copy(source, keep_ref.at[index, part], sems.at[at])
+        passed = pltpu.make_async_copy(source, pass_ref.at[index, part], sems.at[at])
+        either(slot // 2 == core, lambda: kept, lambda: passed)
+        copies.append(kept)
     for copy in copies:
         copy.wait()
-    keep_ref[...] = line_ref[pl.ds(2 * core, 2)]
-    pass_ref[...] = line_ref[pl.ds(2 - 2 * core, 2)]
 
 
 def line_of(own, near, near_other, far, far_other):
@@ -557,7 +560,7 @@
     return launch(
         line_kernel, (own, near, near_other, far, far_other), name="line", micros=2.5,
         in_specs=[ANY] * 5, out_specs=[VMEM] * 2, out_shape=[array((2, rows, width))] * 2,
-        scratch=[pltpu.VMEM((4, rows, width), BF16), pltpu.SemaphoreType.DMA((5,))],
+        scratch=[pltpu.SemaphoreType.DMA((5,))],
     )
 
 
@@ -610,10 +613,17 @@
 
 def partial_kernel(
     fine, own_low, own_high, other_low, other_high, right_ref, right_other_ref,
-    turn_ref, keep_ref, pass_ref, near_ref, half_ref, left_ref, sems,
+    turn_any, keep_any, pass_any, near_any, half_any, turn_ref, keep_ref, pass_ref, near_ref, half_ref, left_ref, sems,
+    out_sems,
 ):
     core, z, y, x = place()
     depth, high, wide = fine[1:]
+    outs = [
+        pltpu.make_async_copy(source, goal, out_sems.at[at])
+        for at, (source, goal) in enumerate(
+            ((turn_ref, turn_any), (keep_ref, keep_any), (pass_ref, pass_any), (near_ref, near_any), (half_ref, half_any))
+        )
+    ]
     split = own_low.shape[0]
     rows = keep_ref.shape[1]
     half = half_ref.shape[1]
@@ -661,6 +671,7 @@
         def _():
             wait((2 * at, 2 * at + 1))
             out[...] = product(2 * at * rows, 2 * rows).reshape(out.shape)
+            outs[at].start()
 
     @pl.when(step == 3)
     def _():
@@ -668,6 +679,10 @@
         last = product(6 * rows, rows + 2 * half)
         near_ref[...] = last[:rows]
         half_ref[...] = last[rows:].reshape(half_ref.shape)
+        outs[3].start()
+        outs[4].start()
+        for copy in outs:
+            copy.wait()
 
 
 def partial(fine, own_low, own_high, other_low, other_high, right, right_other):
@@ -680,9 +695,14 @@
         functools.partial(partial_kernel, fine), (own_low, own_high, other_low, other_high, right, right_other),
         name="partial", micros=features / 700, grid=(4,),
         in_specs=[ANY] * 4 + [whole(length, width)] * 2,
-        out_specs=[whole(*shape) for shape in shapes],
+        out_specs=[ANY] * 5,
         out_shape=[array(shape) for shape in shapes],
-        scratch=[pltpu.VMEM((2, 7 * rows + 2 * half, length), BF16), pltpu.SemaphoreType.DMA((2, 9))],
+        scratch=[
+            *[pltpu.VMEM(shape, BF16) for shape in shapes],
+            pltpu.VMEM((2, 7 * rows + 2 * half, length), BF16),
+            pltpu.SemaphoreType.DMA((2, 9)),
+            pltpu.SemaphoreType.DMA((5,)),
+        ],
     )
 
 
@@ -909,31 +929,31 @@
         first.along()
         scale = scale + got
         got = order.move(shift("x"), scale)
-        picked = order.run(
+        order.fence()
+        first.across()
+        scale = scale + got
+        got = order.move(shift("y"), scale)
+        second = gather(order.run(functools.partial(pick, 0), weight_out[0], other_out))
+        first.line()
+        first.side()
+        second.along()
+        third, fourth, (rows_0, grad_1) = order.run(
             lambda own_in, other_in, own_out, other_out, *values: (
-                pick(0, own_out, other_out), pick(1, own_in, other_in), pick(1, own_out, other_out), own_rows(*values)
+                pick(1, own_in, other_in), pick(1, own_out, other_out), own_rows(*values)
             ),
             weight_in[0], other_in, weight_out[0], other_out, inputs, cotangent,
         )
-        second, third, fourth = [gather(values) for values in picked[:3]]
-        rows_0, grad_1 = picked[3]
-        first.across()
-        scale = scale + got
-        got = order.move(shift("y"), scale)
-        order.fence()
-        first.line()
-        first.side()
-        second.along()
-        scale = scale + got
-        got = order.move(butterfly(1), scale)
-        order.fence()
+        third, fourth = gather(third), gather(fourth)
         first.turn(count=3)
         second.across()
         first.rest(count=2)
+        scale = scale + got
+        got = order.move(butterfly(1), scale, count=2)
         order.fence()
+        second.line()
         scale = scale + got
         got = order.move(butterfly(2), scale)
-        second.line()
+        order.fence()
         vectors_0, vectors_1 = order.run(vectors_of, scale + got)
         second.side(count=2)
         third.along(count=2)
@@ -1034,6 +1054,7 @@
         in_1.pass_on()
         out_0.along(ends)
         in_1.keep_across()
+        out_0.own_across()
         in_0 = Scatter(order, fine, order.run(chip, top_0, low_0, top_0_other, low_0_other, normed_0, normed_0_other))
         in_1.meet()
         out_1.across()
@@ -1042,47 +1063,52 @@
         in_0.start()
         in_1.along(ends)
         out_1.own_across()
-        result_1, squares_1 = order.run(out, rows_1, attended_1, hidden_1, weight_out_1)
+        grad_first_other = order.swap(grad_first)
+
+        def last_output(values, squares_0, *others):
+            result, squares = out(*values)
+            return result, small_sums(squares_0, squares, *others)
+
+        result_1, small = order.run(
+            last_output, (rows_1, attended_1, hidden_1, weight_out_1), squares_0, gain_0, heads_0, gain_1, heads_1
+        )
         in_0.add()
         in_0.pass_on()
         in_0.keep_across()
         out_0.across()
-        out_0.own_across()
-        small, out_grad_1 = order.run(
-            lambda sums, values: (small_sums(*values), total(*sums)),
-            out_1.ends(), (squares_0, squares_1, gain_0, heads_0, gain_1, heads_1),
-        )
+        got = order.move(shift("x"), small)
+        out_grad_1 = order.run(total, *out_1.ends())
+        small = small + got
         in_0.meet()
-        got = order.move(shift("x"), small)
         order.fence()
-        small = small + got
         got = order.move(shift("y"), small)
+        result_1_other = order.swap(result_1)
         in_1.across()
         in_1.own_across()
         ends = order.run(depth_sums, *in_0.parts())
         in_0.along(ends)
         small = small + got
-        result_1_other, grad_first_other = order.swap(result_1, grad_first)
+        got = order.move(butterfly(1), small)
         in_0.own_across()
         def spread_both(rows_1, rows_other, result, result_other, first, first_other, grad_0, grad_other):
             outputs = jnp.where(core == 0, rows_1, result), jnp.where(core == 0, rows_other, result_other)
             grads = jnp.where(core == 0, first, grad_0), jnp.where(core == 0, first_other, grad_other)
             return spread(*outputs), spread(*grads)
 
-        out_grad, in_grad_1 = order.run(
-            lambda first, second: (total(*first), total(*second)), (*out_0.ends(), out_grad_1), in_1.ends()
+        out_grad, in_grad_1, (outputs, input_grads) = order.run(
+            lambda first, second, values: (total(*first), total(*second), spread_both(*values)),
+            (*out_0.ends(), out_grad_1), in_1.ends(),
+            (rows_1, rows_1_other, result_1, result_1_other, grad_first, grad_first_other, grad_0, grad_0_other),
         )
         in_0.across()
-        got = order.move(butterfly(1), small)
-        outputs, input_grads = order.run(
-            spread_both, rows_1, rows_1_other, result_1, result_1_other, grad_first, grad_first_other, grad_0, grad_0_other
-        )
         small = small + got
         got = order.move(butterfly(2), small)
+        order.fence()
+        small = small + got
+        got = order.swap(small)
         in_grad = order.run(total, *in_0.ends(), in_grad_1)[None]
+        out_grad = out_grad[None]
         small = small + got
-        small = small + order.swap(small)
-        out_grad = out_grad[None]
     else:
         top_1, grad_0, gain_1, heads_1 = order.run(back, *kept_1, feed_1)
         feed_0, low_0 = order.run(feed, grad_0, slope_0, weight_in_0, weight_out_0)

time: 473 us -> 455 us (0.962)
  starting transfers between devices: 103 us -> 94.8 us
  local copies, waits for them, and re-layouts: 23.9 us -> 17.7 us
  Pallas kernels: 211 us -> 206 us
    ppermute x4, starting transfers between devices: 11.4 us -> 3.74 us  [body(): lax.ppermute(value, 'z', [(i, i ^ by) for i in range(depth)])]
    ppermute x8, waiting for transfers between devices: 18.7 us -> 11.4 us  [turned(): return lax.ppermute(value, ALL, sends(fine, next_y, next_x))]
    ppermute x4, waiting for transfers between devices: 3.77 us -> 10.7 us  [body(): lax.ppermute(value, axis, [(0, 1), (1, 0)])]
    unnamed x225 -> x155, local copies, waits for them, and re-layouts: 15.1 us -> 8.56 us
    ppermute x59, starting transfers between devices: 16.2 us -> 22.2 us  [swap(): return lax.ppermute(value, 'section', [(0, 1), (1, 0)])]
    pallas_call x30, Pallas kernels: 211 us -> 206 us  [launch(): pl.pallas_call(kernel, grid=grid, in_specs=in_specs, out_specs=out_specs,...]
    ppermute x16, waiting for transfers between devices: 21.3 us -> 16.3 us  [sideways(): return lax.ppermute(value, ALL, sends(fine, next_x, next_y))]
  transfers between devices with their start and end apart: 107 -> 107, of which waited for: 33 -> 32; matrix products, arithmetic and copies ran while one was open for 3% -> 3% of each run, Pallas kernels for 43% -> 44%
where the time goes in v4:
time: 455 us; the launch traced here: 447 us
  Pallas kernels  206 us (45%)
  waiting for transfers between devices  114 us (25%)
  starting transfers between devices  94.8 us (21%)
  local copies, waits for them, and re-layouts  17.7 us (4%)
  other arithmetic  9.67 us (2%)
  between operations  4.84 us (1%)
    pallas_call x30, Pallas kernels, launch(): pl.pallas_call(kernel, grid=grid, in_specs=in_specs, out_specs=out_specs,...  206 us
    ppermute x8, waiting for transfers between devices, opposite(): lax.ppermute(value, 'z', [(z, (z + 2) % depth) for z in range(depth)])  46.7 us
    ppermute x8, starting transfers between devices, opposite(): lax.ppermute(value, 'z', [(z, (z + 2) % depth) for z in range(depth)])  26.2 us
    ppermute x59, starting transfers between devices, swap(): return lax.ppermute(value, 'section', [(0, 1), (1, 0)])  22.2 us
    ppermute x59, waiting for transfers between devices, swap(): return lax.ppermute(value, 'section', [(0, 1), (1, 0)])  18.6 us
    ppermute x16, starting transfers between devices, sideways(): return lax.ppermute(value, ALL, sends(fine, next_x, next_y))  16.8 us
    ppermute x16, waiting for transfers between devices, sideways(): return lax.ppermute(value, ALL, sends(fine, next_x, next_y))  16.3 us
    ppermute x8, waiting for transfers between devices, turned(): return lax.ppermute(value, ALL, sends(fine, next_y, next_x))  11.4 us
  transfers between devices with their start and end apart: 107, of which 32 were waited for; matrix products, arithmetic and copies ran while one was open for 3% of the time, Pallas kernels for 44%

profile of v4, /device:TPU:0, one launch (start us, length us, event | category | flops | bytes accessed | tf_op | source)
XLA Modules:
  0.0 447.0 jit_solution(6574128734730492872)
XLA Ops:
  5.2 1.9 pick.4
  7.1 3.0 collective-permute-start.3
  10.1 2.6 collective-permute-start.4
  14.2 2.2 collective-permute-done.5
  16.4 15.1 %collective-permute-done.4.far_ref = bf16[176,768]{1,0:T(8,128)(2,1)S(1)} collective-permute-done((bf16[176,768]{1,0:T(8,128)(2,1)}, bf16[176,768]{1,0:T(8,128)(2,1)S(1)}, u32[]{:S(2)}, u32[]{:S(2)}) %collective-permute-start.4) | collective-permute-done | bytes 270368 | tf_op jit(solution)/shard_map/ppermute | solution.py:468
  31.5 3.5 collective-permute-start.6
  39.7 2.9 line.4
  48.5 3.3 collective-permute-start.12
  53.1 2.2 pick.6
  58.1 7.4 %collective-permute-done.12.far_ref = bf16[128,768]{1,0:T(8,128)(2,1)S(1)} collective-permute-done((bf16[128,768]{1,0:T(8,128)(2,1)S(1)}, bf16[128,768]{1,0:T(8,128)(2,1)S(1)}, u32[]{:S(2)}, u32[]{:S(2)}) %collective-permute-start.12) | collective-permute-done | bytes 196640 | tf_op jit(solution)/shard_map/ppermute | solution.py:468
  65.5 3.1 collective-permute-done.10.refs_2_
  71.9 2.5 collective-permute-done.13
  76.2 2.5 line.5
  78.7 2.5 collective-permute-start.18
  81.2 2.9 collective-permute-done.19.refs_6_
  88.1 3.3 collective-permute-start.24
  92.8 14.5 %attend.2 = (bf16[512,768]{1,0:T(8,128)(2,1)}, f32[2,3,256,512]{3,2,1,0:T(8,128)}, bf16[768,512]{1,0:T(8,128)(2,1)}, bf16[768,512]{1,0:T(8,128)(2,1)}, f32[3,8,512]{2,1,0:T(8,128)}, /*index=5*/bf16[5376,768]{1,0:T(8,128)(2,1)}) custom-call(s32[1,2]{1,0:T(1,128)} %copy-done.23, bf16[512,768]{1,0:T(8,128)(2,1)} %dynamic-slice_bitcast_fusion.rows_ref, ...), custom_call_target="tpu_custom_call" | custom-call | flops 14949999616 | bytes 13000000 | tf_op jit(solution)/shard_map/attend/pallas_call | solution.py:40
  107.3 2.7 collective-permute-done.24.far_ref
  111.6 2.2 collective-permute-start.26
  114.4 8.4 %hidden.2 = (bf16[3072,512]{1,0:T(8,128)(2,1)}, bf16[3072,512]{1,0:T(8,128)(2,1)}) custom-call(bf16[512,768]{1,0:T(8,128)(2,1)} %get-tuple-element.887.normed_ref.right_ref, bf16[5376,768]{1,0:T(8,128)(2,1)} %get-tuple-element.854.weight_ref.weight_in_ref), custom_call_target="tpu_custom_call" | custom-call | flops 9200000000 | bytes 8000000 | tf_op jit(solution)/shard_map/hidden/pallas_call | solution.py:40
  123.7 2.9 line.6
  130.6 3.4 collective-permute-start.32
  134.0 11.0 %output.2 = (bf16[512,768]{1,0:T(8,128)(2,1)}, f32[3,8,768]{2,1,0:T(8,128)}, bf16[3840,768]{1,0:T(8,128)(2,1)}) custom-call(s32[1,2]{1,0:T(1,128)} %copy-done.23, bf16[512,768]{1,0:T(8,128)(2,1)} %dynamic-slice_bitcast_fusion.rows_ref, bf16[768,512]{1,0:T(8,128)(2,1)} %get-tuple-element.851.attended_ref.own_low, ...), custom_call_target="tpu_custom_call" | custom-call | flops 10350000128 | bytes 9000000 | tf_op jit(solution)/shard_map/output/pallas_call | solution.py:40
  145.0 2.9 collective-permute-done.32.far_ref
  148.0 4.7 %collective-permute-done.34.refs_2_ = bf16[2,336,768]{2,1,0:T(8,128)(2,1)S(1)} collective-permute-done((bf16[2,336,768]{2,1,0:T(8,128)(2,1)}, bf16[2,336,768]{2,1,0:T(8,128)(2,1)S(1)}, u32[]{:S(2)}, u32[]{:S(2)}) %collective-permute-start.34) | collective-permute-done | bytes 1032224 | tf_op jit(solution)/shard_map/ppermute | solution.py:452
  158.3 2.5 line.7
  161.0 7.3 %collective-permute-done.39.refs_6_ = bf16[2,336,768]{2,1,0:T(8,128)(2,1)} collective-permute-done((bf16[2,336,768]{2,1,0:T(8,128)(2,1)S(1)}, bf16[2,336,768]{2,1,0:T(8,128)(2,1)}, u32[]{:S(2)}, u32[]{:S(2)}) %collective-permute-start.39) | collective-permute-done | bytes 1032224 | tf_op jit(solution)/shard_map/ppermute | solution.py:456
  168.4 2.8 collective-permute-done.41.refs_7_
  175.3 14.5 %attend.3 = (bf16[512,768]{1,0:T(8,128)(2,1)}, f32[2,3,256,512]{3,2,1,0:T(8,128)}, bf16[768,512]{1,0:T(8,128)(2,1)}, bf16[768,512]{1,0:T(8,128)(2,1)}, f32[3,8,512]{2,1,0:T(8,128)}, /*index=5*/bf16[5376,768]{1,0:T(8,128)(2,1)}) custom-call(s32[1,2]{1,0:T(1,128)} %copy-done.23, bf16[512,768]{1,0:T(8,128)(2,1)} %get-tuple-element.993.rows_ref, ...), custom_call_target="tpu_custom_call" | custom-call | flops 14949999616 | bytes 13000000 | tf_op jit(solution)/shard_map/attend/pallas_call | solution.py:40
  194.5 8.5 %hidden.3 = (bf16[3072,512]{1,0:T(8,128)(2,1)}, bf16[3072,512]{1,0:T(8,128)(2,1)}) custom-call(bf16[512,768]{1,0:T(8,128)(2,1)} %get-tuple-element.819.normed_ref.right_ref, bf16[5376,768]{1,0:T(8,128)(2,1)} %get-tuple-element.761.weight_ref.weight_in_ref), custom_call_target="tpu_custom_call" | custom-call | flops 9200000000 | bytes 8000000 | tf_op jit(solution)/shard_map/hidden/pallas_call | solution.py:40
  203.8 2.4 collective-permute-done.52.refs_7_
  207.1 13.4 %feed_back.2 = (f32[512,768]{1,0:T(8,128)}, bf16[3072,512]{1,0:T(8,128)(2,1)}, bf16[3840,768]{1,0:T(8,128)(2,1)}) custom-call(bf16[512,768]{1,0:T(8,128)(2,1)} %copy-done.15, bf16[3072,512]{1,0:T(8,128)(2,1)} %get-tuple-element.720.slope_ref, bf16[5376,768]{1,0:T(8,128)(2,1)} %get-tuple-element.761.weight_ref.weight_in_ref, ...), custom_call_target="tpu_custom_call" | custom-call | flops 12650000384 | bytes 11000000 | tf_op jit(solution)/shard_map/feed_back/pallas_call | solution.py:40
  220.8 7.8 %partial.4 = (bf16[2,240,768]{2,1,0:T(8,128)(2,1)}, bf16[2,240,768]{2,1,0:T(8,128)(2,1)}, bf16[2,240,768]{2,1,0:T(8,128)(2,1)}, bf16[240,768]{1,0:T(8,128)(2,1)}, bf16[2,128,768]{2,1,0:T(8,128)(2,1)}) custom-call(bf16[768,512]{1,0:T(8,128)(2,1)} %get-tuple-element.924.own_low.attended_ref, bf16[3072,512]{1,0:T(8,128)(2,1)} %get-tuple-element.925.own_high.hidden_ref, ...), custom_call_target="tpu_custom_call" | custom-call | flops 6308571648 | bytes 5485714 | tf_op jit(solution)/shard_map/partial/pallas_call | solution.py:40
  232.6 17.5 %attend_back.2 = (bf16[3,3,256,512]{3,2,1,0:T(8,128)(2,1)}, bf16[512,768]{1,0:T(8,128)(2,1)}, f32[8,768]{1,0:T(8,128)}, f32[2,64,128]{2,1,0:T(8,128)}) custom-call(s32[1,2]{1,0:T(1,128)} %copy-done.23, bf16[512,768]{1,0:T(8,128)(2,1)} %get-tuple-element.993.rows_ref, bf16[512,768]{1,0:T(8,128)(2,1)} %copy-done.15, f32[1,768]{1,0:T(1,128)} %get-tuple-element.753.gain_ref, ...), custom_call_target="tpu_custom_call" | custom-call | flops 19549999104 | bytes 17000000 | tf_op jit(solution)/shard_map/attend_back/pallas_call | solution.py:40
  250.9 2.1 collective-permute-done.58.right_other_ref
  254.1 7.6 %partial.5 = (bf16[2,240,768]{2,1,0:T(8,128)(2,1)}, bf16[2,240,768]{2,1,0:T(8,128)(2,1)}, bf16[2,240,768]{2,1,0:T(8,128)(2,1)}, bf16[240,768]{1,0:T(8,128)(2,1)}, bf16[2,128,768]{2,1,0:T(8,128)(2,1)}) custom-call(bf16[768,512]{1,0:T(8,128)(2,1)} %get-tuple-element.851.attended_ref.own_low, bf16[3072,512]{1,0:T(8,128)(2,1)} %get-tuple-element.778.hidden_ref.own_high, ...), custom_call_target="tpu_custom_call" | custom-call | flops 6308571648 | bytes 5485714 | tf_op jit(solution)/shard_map/partial/pallas_call | solution.py:40
  261.8 2.7 collective-permute-done.59.pass_ref
  267.0 12.2 %feed_back.3 = (f32[512,768]{1,0:T(8,128)}, bf16[3072,512]{1,0:T(8,128)(2,1)}) custom-call(bf16[512,768]{1,0:T(8,128)(2,1)} %get-tuple-element.998.right_ref.grad_ref, bf16[3072,512]{1,0:T(8,128)(2,1)} %get-tuple-element.800.slope_ref, bf16[5376,768]{1,0:T(8,128)(2,1)} %get-tuple-element.854.weight_ref.weight_in_ref, ...), custom_call_target="tpu_custom_call" | custom-call | flops 12650000384 | bytes 11000000 | tf_op jit(solution)/shard_map/feed_back/pallas_call | solution.py:40
  279.3 4.6 %collective-permute-done.61.keep_ref = bf16[2,240,768]{2,1,0:T(8,128)(2,1)S(1)} collective-permute-done((bf16[2,240,768]{2,1,0:T(8,128)(2,1)}, bf16[2,240,768]{2,1,0:T(8,128)(2,1)S(1)}, u32[]{:S(2)}, u32[]{:S(2)}) %collective-permute-start.61) | collective-permute-done | bytes 737312 | tf_op jit(solution)/shard_map/ppermute | solution.py:452
  285.8 3.5 depth.4
  289.3 9.0 %partial.6 = (bf16[2,336,768]{2,1,0:T(8,128)(2,1)}, bf16[2,336,768]{2,1,0:T(8,128)(2,1)}, bf16[2,336,768]{2,1,0:T(8,128)(2,1)}, bf16[336,768]{1,0:T(8,128)(2,1)}, bf16[2,176,768]{2,1,0:T(8,128)(2,1)}) custom-call(bf16[2304,512]{1,0:T(8,128)(2,1)} %bitcast.75, bf16[3072,512]{1,0:T(8,128)(2,1)} %get-tuple-element.816.own_high, ...), custom_call_target="tpu_custom_call" | custom-call | flops 8832000000 | bytes 7680000 | tf_op jit(solution)/shard_map/partial/pallas_call | solution.py:40
  304.2 3.4 collective-permute-start.72
  307.6 17.7 %attend_back.3 = (bf16[3,3,256,512]{3,2,1,0:T(8,128)(2,1)}, bf16[512,768]{1,0:T(8,128)(2,1)}, f32[8,768]{1,0:T(8,128)}, f32[2,64,128]{2,1,0:T(8,128)}) custom-call(s32[1,2]{1,0:T(1,128)} %copy-done.23, bf16[512,768]{1,0:T(8,128)(2,1)} %dynamic-slice_bitcast_fusion.rows_ref, bf16[512,768]{1,0:T(8,128)(2,1)} %get-tuple-element.998.right_ref.grad_ref, ...), custom_call_target="tpu_custom_call" | custom-call | flops 19549999104 | bytes 17000000 | tf_op jit(solution)/shard_map/attend_back/pallas_call | solution.py:40
  326.4 3.6 depth.5
  332.5 3.4 collective-permute-start.75
  335.9 8.9 %partial.7 = (bf16[2,336,768]{2,1,0:T(8,128)(2,1)}, bf16[2,336,768]{2,1,0:T(8,128)(2,1)}, bf16[2,336,768]{2,1,0:T(8,128)(2,1)}, bf16[336,768]{1,0:T(8,128)(2,1)}, bf16[2,176,768]{2,1,0:T(8,128)(2,1)}) custom-call(bf16[2304,512]{1,0:T(8,128)(2,1)} %bitcast.77, bf16[3072,512]{1,0:T(8,128)(2,1)} %get-tuple-element.884.own_high, ...), custom_call_target="tpu_custom_call" | custom-call | flops 8832000000 | bytes 7680000 | tf_op jit(solution)/shard_map/partial/pallas_call | solution.py:40
  344.8 5.4 %collective-permute-done.75.far_ref = bf16[128,768]{1,0:T(8,128)(2,1)} collective-permute-done((bf16[128,768]{1,0:T(8,128)(2,1)}, bf16[128,768]{1,0:T(8,128)(2,1)}, u32[]{:S(2)}, u32[]{:S(2)}) %collective-permute-start.75) | collective-permute-done | bytes 196640 | tf_op jit(solution)/shard_map/ppermute | solution.py:468
  352.1 2.8 collective-permute-done.81.far_other
  354.9 4.1 depth.6
  362.9 3.4 collective-permute-start.85
  366.4 9.7 %output.3 = (bf16[512,768]{1,0:T(8,128)(2,1)}, f32[3,8,768]{2,1,0:T(8,128)}) custom-call(s32[1,2]{1,0:T(1,128)} %copy-done.23, bf16[512,768]{1,0:T(8,128)(2,1)} %get-tuple-element.993.rows_ref, bf16[768,512]{1,0:T(8,128)(2,1)} %get-tuple-element.924.own_low.attended_ref, bf16[3072,512]{1,0:T(8,128)(2,1)} %get-tuple-element.925.own_high.hidden_ref, ...), custom_call_target="tpu_custom_call" | custom-call | flops 10350000128 | bytes 9000000 | tf_op jit(solution)/shard_map/output/pallas_call | solution.py:40
  377.7 7.6 %collective-permute-done.85.far_ref = bf16[176,768]{1,0:T(8,128)(2,1)} collective-permute-done((bf16[176,768]{1,0:T(8,128)(2,1)}, bf16[176,768]{1,0:T(8,128)(2,1)}, u32[]{:S(2)}, u32[]{:S(2)}) %collective-permute-start.85) | collective-permute-done | bytes 270368 | tf_op jit(solution)/shard_map/ppermute | solution.py:468
  390.1 2.4 total.4.refs_0_
  392.5 8.3 %collective-permute-done.92 = f32[16,128]{1,0:T(8,128)S(1)} collective-permute-done((f32[16,128]{1,0:T(8,128)S(1)}, f32[16,128]{1,0:T(8,128)S(1)}, u32[]{:S(2)}, u32[]{:S(2)}) %collective-permute-start.92) | collective-permute-done | bytes 8224 | tf_op jit(solution)/shard_map/ppermute | solution.py:898
  401.4 2.3 collective-permute-done.93.pass_other
  405.5 4.0 depth.7
  411.1 3.4 collective-permute-start.100
  416.1 2.8 total.6.refs_0_
  418.9 2.7 total.5
  424.1 3.5 collective-permute-done.101
  427.6 5.6 %collective-permute-done.100.far_ref = bf16[176,768]{1,0:T(8,128)(2,1)} collective-permute-done((bf16[176,768]{1,0:T(8,128)(2,1)}, bf16[176,768]{1,0:T(8,128)(2,1)}, u32[]{:S(2)}, u32[]{:S(2)}) %collective-permute-start.100) | collective-permute-done | bytes 270368 | tf_op jit(solution)/shard_map/ppermute | solution.py:468
  433.2 2.6 collective-permute-start.103
  435.9 4.5 %collective-permute-done.105 = f32[16,128]{1,0:T(8,128)S(1)} collective-permute-done((f32[16,128]{1,0:T(8,128)S(1)}, f32[16,128]{1,0:T(8,128)S(1)}, u32[]{:S(2)}, u32[]{:S(2)}) %collective-permute-start.105) | collective-permute-done | bytes 8224 | tf_op jit(solution)/shard_map/ppermute | solution.py:921
  441.3 3.1 total.7
  (385 shorter events, 94.7 us)
Async XLA Ops:
  7.1 24.4 %collective-permute-start.3 = (bf16[336,768]{1,0:T(8,128)(2,1)}, bf16[336,768]{1,0:T(8,128)(2,1)S(1)}, u32[]{:S(2)}, u32[]{:S(2)}) collective-permute-start(bf16[336,768]{1,0:T(8,128)(2,1)} %get-tuple-element.537.own_ref), channel_id=1, source_target_pairs={{0,4},{1,5},{2,6},{3,7},{4,8},{5,9},{6,10},{7,11},{8,12},{9,13},{1... | collective-permute-start | bytes 1548296 | tf_op jit(solution)/shard_map/ppermute | solution.py:461
  10.1 21.4 %collective-permute-start.4 = (bf16[176,768]{1,0:T(8,128)(2,1)}, bf16[176,768]{1,0:T(8,128)(2,1)S(1)}, u32[]{:S(2)}, u32[]{:S(2)}) collective-permute-start(bf16[176,768]{1,0:T(8,128)(2,1)} %get-tuple-element.526), channel_id=1, source_target_pairs={{0,8},{4,12},{8,0},{12,4},{1,9},{5,13},{9,1},{13,5},{2,10},{6,14},... | collective-permute-start | bytes 811016 | tf_op jit(solution)/shard_map/ppermute | solution.py:468
  42.6 22.9 %collective-permute-start.9 = (bf16[2,336,768]{2,1,0:T(8,128)(2,1)}, bf16[2,336,768]{2,1,0:T(8,128)(2,1)}, u32[]{:S(2)}, u32[]{:S(2)}) collective-permute-start(bf16[2,336,768]{2,1,0:T(8,128)(2,1)} %get-tuple-element.591.refs_1_), channel_id=1, source_target_pairs={{0,1},{1,0},{2,3},{3,2},{4,5},{5,4},{6,7},{7,6},{8,9},{9,8},{10,11... | collective-permute-start | bytes 3096584 | tf_op jit(solution)/shard_map/ppermute | solution.py:452
  44.2 24.5 %collective-permute-start.10 = (bf16[2,336,768]{2,1,0:T(8,128)(2,1)}, bf16[2,336,768]{2,1,0:T(8,128)(2,1)}, u32[]{:S(2)}, u32[]{:S(2)}) collective-permute-start(bf16[2,336,768]{2,1,0:T(8,128)(2,1)} %get-tuple-element.590.refs_0_), channel_id=1, source_target_pairs={{0,1},{1,0},{2,3},{3,2},{4,5},{5,4},{6,7},{7,6},{8,9},{9,8},{10,11... | collective-permute-start | bytes 3096584 | tf_op jit(solution)/shard_map/ppermute | solution.py:452
  47.3 18.3 %collective-permute-start.11 = (bf16[240,768]{1,0:T(8,128)(2,1)S(1)}, bf16[240,768]{1,0:T(8,128)(2,1)S(1)}, u32[]{:S(2)}, u32[]{:S(2)}) collective-permute-start(bf16[240,768]{1,0:T(8,128)(2,1)S(1)} %copy-done.61), channel_id=1, source_target_pairs={{0,4},{1,5},{2,6},{3,7},{4,8},{5,9},{6,10},{7,11},{8,12},{9,13},{1... | collective-permute-start | bytes 1105928 | tf_op jit(solution)/shard_map/ppermute | solution.py:461
  48.5 17.1 %collective-permute-start.12 = (bf16[128,768]{1,0:T(8,128)(2,1)S(1)}, bf16[128,768]{1,0:T(8,128)(2,1)S(1)}, u32[]{:S(2)}, u32[]{:S(2)}) collective-permute-start(bf16[128,768]{1,0:T(8,128)(2,1)S(1)} %copy-done.74), channel_id=1, source_target_pairs={{0,8},{4,12},{8,0},{12,4},{1,9},{5,13},{9,1},{13,5},{2,10},{6,14},... | collective-permute-start | bytes 589832 | tf_op jit(solution)/shard_map/ppermute | solution.py:468
  68.7 10.0 %collective-permute-start.17 = (bf16[2,336,768]{2,1,0:T(8,128)(2,1)}, bf16[2,336,768]{2,1,0:T(8,128)(2,1)S(1)}, u32[]{:S(2)}, u32[]{:S(2)}) collective-permute-start(bf16[2,336,768]{2,1,0:T(8,128)(2,1)} %collective-permute-done.9.refs_3_), channel_id=1, source_target_pairs={{0,16},{16,0},{1,17},{17,1},{2,18},{18,2},{3,19},{19,3},{4,20},{20... | collective-permute-start | bytes 3096584 | tf_op jit(solution)/shard_map/ppermute | solution.py:472
  69.2 14.9 %collective-permute-start.19 = (bf16[2,336,768]{2,1,0:T(8,128)(2,1)}, bf16[2,336,768]{2,1,0:T(8,128)(2,1)}, u32[]{:S(2)}, u32[]{:S(2)}) collective-permute-start(bf16[2,336,768]{2,1,0:T(8,128)(2,1)} %collective-permute-done.9.refs_3_), channel_id=1, source_target_pairs={{0,2},{1,3},{2,0},{3,1},{4,6},{5,7},{6,4},{7,5},{8,10},{9,11},{10,... | collective-permute-start | bytes 3096584 | tf_op jit(solution)/shard_map/ppermute | solution.py:456
  84.8 25.2 %collective-permute-start.21 = (bf16[2,240,768]{2,1,0:T(8,128)(2,1)}, bf16[2,240,768]{2,1,0:T(8,128)(2,1)}, u32[]{:S(2)}, u32[]{:S(2)}) collective-permute-start(bf16[2,240,768]{2,1,0:T(8,128)(2,1)} %get-tuple-element.640.refs_1_), channel_id=1, source_target_pairs={{0,1},{1,0},{2,3},{3,2},{4,5},{5,4},{6,7},{7,6},{8,9},{9,8},{10,11... | collective-permute-start | bytes 2211848 | tf_op jit(solution)/shard_map/ppermute | solution.py:452
  86.4 23.7 %collective-permute-start.22 = (bf16[2,240,768]{2,1,0:T(8,128)(2,1)}, bf16[2,240,768]{2,1,0:T(8,128)(2,1)}, u32[]{:S(2)}, u32[]{:S(2)}) collective-permute-start(bf16[2,240,768]{2,1,0:T(8,128)(2,1)} %get-tuple-element.639.refs_0_), channel_id=1, source_target_pairs={{0,1},{1,0},{2,3},{3,2},{4,5},{5,4},{6,7},{7,6},{8,9},{9,8},{10,11... | collective-permute-start | bytes 2211848 | tf_op jit(solution)/shard_map/ppermute | solution.py:452
  86.9 23.1 %collective-permute-start.23 = (bf16[336,768]{1,0:T(8,128)(2,1)S(1)}, bf16[336,768]{1,0:T(8,128)(2,1)}, u32[]{:S(2)}, u32[]{:S(2)}) collective-permute-start(bf16[336,768]{1,0:T(8,128)(2,1)S(1)} %copy-done.51), channel_id=1, source_target_pairs={{0,4},{1,5},{2,6},{3,7},{4,8},{5,9},{6,10},{7,11},{8,12},{9,13},{1... | collective-permute-start | bytes 1548296 | tf_op jit(solution)/shard_map/ppermute | solution.py:461
  88.1 22.0 %collective-permute-start.24 = (bf16[176,768]{1,0:T(8,128)(2,1)}, bf16[176,768]{1,0:T(8,128)(2,1)}, u32[]{:S(2)}, u32[]{:S(2)}) collective-permute-start(bf16[176,768]{1,0:T(8,128)(2,1)} %get-tuple-element.609), channel_id=1, source_target_pairs={{0,8},{4,12},{8,0},{12,4},{1,9},{5,13},{9,1},{13,5},{2,10},{6,14},... | collective-permute-start | bytes 811016 | tf_op jit(solution)/shard_map/ppermute | solution.py:468
  110.1 12.7 %collective-permute-start.25 = (bf16[2,240,768]{2,1,0:T(8,128)(2,1)}, bf16[2,240,768]{2,1,0:T(8,128)(2,1)S(1)}, u32[]{:S(2)}, u32[]{:S(2)}) collective-permute-start(bf16[2,240,768]{2,1,0:T(8,128)(2,1)} %collective-permute-done.21.refs_3_), channel_id=1, source_target_pairs={{0,2},{1,3},{2,0},{3,1},{4,6},{5,7},{6,4},{7,5},{8,10},{9,11},{10,... | collective-permute-start | bytes 2211848 | tf_op jit(solution)/shard_map/ppermute | solution.py:456
  111.6 11.2 %collective-permute-start.26 = (bf16[2,240,768]{2,1,0:T(8,128)(2,1)}, bf16[2,240,768]{2,1,0:T(8,128)(2,1)S(1)}, u32[]{:S(2)}, u32[]{:S(2)}) collective-permute-start(bf16[2,240,768]{2,1,0:T(8,128)(2,1)} %collective-permute-done.22.refs_2_), channel_id=1, source_target_pairs={{0,16},{16,0},{1,17},{17,1},{2,18},{18,2},{3,19},{19,3},{4,20},{20... | collective-permute-start | bytes 2211848 | tf_op jit(solution)/shard_map/ppermute | solution.py:472
  126.7 21.3 %collective-permute-start.33 = (bf16[2,336,768]{2,1,0:T(8,128)(2,1)}, bf16[2,336,768]{2,1,0:T(8,128)(2,1)S(1)}, u32[]{:S(2)}, u32[]{:S(2)}) collective-permute-start(bf16[2,336,768]{2,1,0:T(8,128)(2,1)} %get-tuple-element.683.refs_1_), channel_id=1, source_target_pairs={{0,1},{1,0},{2,3},{3,2},{4,5},{5,4},{6,7},{7,6},{8,9},{9,8},{10,11... | collective-permute-start | bytes 3096584 | tf_op jit(solution)/shard_map/ppermute | solution.py:452
  127.7 24.9 %collective-permute-start.34 = (bf16[2,336,768]{2,1,0:T(8,128)(2,1)}, bf16[2,336,768]{2,1,0:T(8,128)(2,1)S(1)}, u32[]{:S(2)}, u32[]{:S(2)}) collective-permute-start(bf16[2,336,768]{2,1,0:T(8,128)(2,1)} %get-tuple-element.682.refs_0_), channel_id=1, source_target_pairs={{0,1},{1,0},{2,3},{3,2},{4,5},{5,4},{6,7},{7,6},{8,9},{9,8},{10,11... | collective-permute-start | bytes 3096584 | tf_op jit(solution)/shard_map/ppermute | solution.py:452
  128.8 19.2 %collective-permute-start.31 = (bf16[240,768]{1,0:T(8,128)(2,1)}, bf16[240,768]{1,0:T(8,128)(2,1)S(1)}, u32[]{:S(2)}, u32[]{:S(2)}) collective-permute-start(bf16[240,768]{1,0:T(8,128)(2,1)} %get-tuple-element.657.own_ref), channel_id=1, source_target_pairs={{0,4},{1,5},{2,6},{3,7},{4,8},{5,9},{6,10},{7,11},{8,12},{9,13},{1... | collective-permute-start | bytes 1105928 | tf_op jit(solution)/shard_map/ppermute | solution.py:461
  130.6 17.3 %collective-permute-start.32 = (bf16[128,768]{1,0:T(8,128)(2,1)}, bf16[128,768]{1,0:T(8,128)(2,1)S(1)}, u32[]{:S(2)}, u32[]{:S(2)}) collective-permute-start(bf16[128,768]{1,0:T(8,128)(2,1)} %get-tuple-element.635), channel_id=1, source_target_pairs={{0,8},{4,12},{8,0},{12,4},{1,9},{5,13},{9,1},{13,5},{2,10},{6,14},... | collective-permute-start | bytes 589832 | tf_op jit(solution)/shard_map/ppermute | solution.py:468
  153.7 14.7 %collective-permute-start.39 = (bf16[2,336,768]{2,1,0:T(8,128)(2,1)S(1)}, bf16[2,336,768]{2,1,0:T(8,128)(2,1)}, u32[]{:S(2)}, u32[]{:S(2)}) collective-permute-start(bf16[2,336,768]{2,1,0:T(8,128)(2,1)S(1)} %collective-permute-done.33.refs_3_), channel_id=1, source_target_pairs={{0,2},{1,3},{2,0},{3,1},{4,6},{5,7},{6,4},{7,5},{8,10},{9,11},{10,... | collective-permute-start | bytes 3096584 | tf_op jit(solution)/shard_map/ppermute | solution.py:456
  171.2 19.8 %collective-permute-start.43 = (bf16[3072,512]{1,0:T(8,128)(2,1)}, bf16[3072,512]{1,0:T(8,128)(2,1)}, u32[]{:S(2)}, u32[]{:S(2)}) collective-permute-start(bf16[3072,512]{1,0:T(8,128)(2,1)} %get-tuple-element.778.hidden_ref.own_high), channel_id=1, source_target_pairs={{0,16},{16,0},{1,17},{17,1},{2,18},{18,2},{3,19},{19,3},{4,20},{20... | collective-permute-start | bytes 9437192 | tf_op jit(solution)/shard_map/ppermute | solution.py:472
  171.4 18.5 %collective-permute-start.44 = (bf16[2,240,768]{2,1,0:T(8,128)(2,1)}, bf16[2,240,768]{2,1,0:T(8,128)(2,1)}, u32[]{:S(2)}, u32[]{:S(2)}) collective-permute-start(bf16[2,240,768]{2,1,0:T(8,128)(2,1)} %get-tuple-element.723.refs_1_), channel_id=1, source_target_pairs={{0,1},{1,0},{2,3},{3,2},{4,5},{5,4},{6,7},{7,6},{8,9},{9,8},{10,11... | collective-permute-start | bytes 2211848 | tf_op jit(solution)/shard_map/ppermute | solution.py:452
  172.3 18.7 %collective-permute-start.45 = (bf16[2,240,768]{2,1,0:T(8,128)(2,1)}, bf16[2,240,768]{2,1,0:T(8,128)(2,1)}, u32[]{:S(2)}, u32[]{:S(2)}) collective-permute-start(bf16[2,240,768]{2,1,0:T(8,128)(2,1)} %get-tuple-element.722.refs_0_), channel_id=1, source_target_pairs={{0,1},{1,0},{2,3},{3,2},{4,5},{5,4},{6,7},{7,6},{8,9},{9,8},{10,11... | collective-permute-start | bytes 2211848 | tf_op jit(solution)/shard_map/ppermute | solution.py:452
  173.4 17.7 %collective-permute-start.42 = (bf16[768,512]{1,0:T(8,128)(2,1)}, bf16[768,512]{1,0:T(8,128)(2,1)S(1)}, u32[]{:S(2)}, u32[]{:S(2)}) collective-permute-start(bf16[768,512]{1,0:T(8,128)(2,1)} %get-tuple-element.851.attended_ref.own_low), channel_id=1, source_target_pairs={{0,16},{16,0},{1,17},{17,1},{2,18},{18,2},{3,19},{19,3},{4,20},{20... | collective-permute-start | bytes 2359304 | tf_op jit(solution)/shard_map/ppermute | solution.py:472
  174.8 16.2 %collective-permute-start.46 = (bf16[512,768]{1,0:T(8,128)(2,1)}, bf16[512,768]{1,0:T(8,128)(2,1)S(1)}, u32[]{:S(2)}, u32[]{:S(2)}) collective-permute-start(bf16[512,768]{1,0:T(8,128)(2,1)} %get-tuple-element.887.normed_ref.right_ref), channel_id=1, source_target_pairs={{0,16},{16,0},{1,17},{17,1},{2,18},{18,2},{3,19},{19,3},{4,20},{20... | collective-permute-start | bytes 2359304 | tf_op jit(solution)/shard_map/ppermute | solution.py:472
  191.9 11.8 %collective-permute-start.47 = (bf16[2,240,768]{2,1,0:T(8,128)(2,1)}, bf16[2,240,768]{2,1,0:T(8,128)(2,1)}, u32[]{:S(2)}, u32[]{:S(2)}) collective-permute-start(bf16[2,240,768]{2,1,0:T(8,128)(2,1)} %collective-permute-done.44.refs_3_), channel_id=1, source_target_pairs={{0,2},{1,3},{2,0},{3,1},{4,6},{5,7},{6,4},{7,5},{8,10},{9,11},{10,... | collective-permute-start | bytes 2211848 | tf_op jit(solution)/shard_map/ppermute | solution.py:456
  193.5 10.3 %collective-permute-start.48 = (bf16[2,240,768]{2,1,0:T(8,128)(2,1)}, bf16[2,240,768]{2,1,0:T(8,128)(2,1)}, u32[]{:S(2)}, u32[]{:S(2)}) collective-permute-start(bf16[2,240,768]{2,1,0:T(8,128)(2,1)} %collective-permute-done.45.refs_2_), channel_id=1, source_target_pairs={{0,16},{16,0},{1,17},{17,1},{2,18},{18,2},{3,19},{19,3},{4,20},{20... | collective-permute-start | bytes 2211848 | tf_op jit(solution)/shard_map/ppermute | solution.py:472
  193.5 10.3 %collective-permute-start.49 = (bf16[2,240,768]{2,1,0:T(8,128)(2,1)}, bf16[2,240,768]{2,1,0:T(8,128)(2,1)}, u32[]{:S(2)}, u32[]{:S(2)}) collective-permute-start(bf16[2,240,768]{2,1,0:T(8,128)(2,1)} %collective-permute-done.44.refs_3_), channel_id=1, source_target_pairs={{0,16},{16,0},{1,17},{17,1},{2,18},{18,2},{3,19},{19,3},{4,20},{20... | collective-permute-start | bytes 2211848 | tf_op jit(solution)/shard_map/ppermute | solution.py:472
  206.3 14.4 %collective-permute-start.53 = (bf16[3072,512]{1,0:T(8,128)(2,1)}, bf16[3072,512]{1,0:T(8,128)(2,1)}, u32[]{:S(2)}, u32[]{:S(2)}) collective-permute-start(bf16[3072,512]{1,0:T(8,128)(2,1)} %get-tuple-element.925.own_high.hidden_ref), channel_id=1, source_target_pairs={{0,16},{16,0},{1,17},{17,1},{2,18},{18,2},{3,19},{19,3},{4,20},{20... | collective-permute-start | bytes 9437192 | tf_op jit(solution)/shard_map/ppermute | solution.py:472
  206.4 14.2 %collective-permute-start.54 = (bf16[512,768]{1,0:T(8,128)(2,1)S(1)}, bf16[512,768]{1,0:T(8,128)(2,1)S(1)}, u32[]{:S(2)}, u32[]{:S(2)}) collective-permute-start(bf16[512,768]{1,0:T(8,128)(2,1)S(1)} %copy-done.4), channel_id=1, source_target_pairs={{0,16},{16,0},{1,17},{17,1},{2,18},{18,2},{3,19},{19,3},{4,20},{20... | collective-permute-start | bytes 2359304 | tf_op jit(solution)/shard_map/ppermute | solution.py:472
  230.1 20.0 %collective-permute-start.56 = (bf16[2,240,768]{2,1,0:T(8,128)(2,1)}, bf16[2,240,768]{2,1,0:T(8,128)(2,1)S(1)}, u32[]{:S(2)}, u32[]{:S(2)}) collective-permute-start(bf16[2,240,768]{2,1,0:T(8,128)(2,1)} %get-tuple-element.767), channel_id=1, source_target_pairs={{0,2},{1,3},{2,0},{3,1},{4,6},{5,7},{6,4},{7,5},{8,10},{9,11},{10,... | collective-permute-start | bytes 2211848 | tf_op jit(solution)/shard_map/ppermute | solution.py:456
  231.6 18.5 %collective-permute-start.57 = (bf16[2,240,768]{2,1,0:T(8,128)(2,1)}, bf16[2,240,768]{2,1,0:T(8,128)(2,1)S(1)}, u32[]{:S(2)}, u32[]{:S(2)}) collective-permute-start(bf16[2,240,768]{2,1,0:T(8,128)(2,1)} %get-tuple-element.769), channel_id=1, source_target_pairs={{0,1},{1,0},{2,3},{3,2},{4,5},{5,4},{6,7},{7,6},{8,9},{9,8},{10,11... | collective-permute-start | bytes 2211848 | tf_op jit(solution)/shard_map/ppermute | solution.py:452
  250.2 33.6 %collective-permute-start.63 = (bf16[2304,512]{1,0:T(8,128)(2,1)}, bf16[2304,512]{1,0:T(8,128)(2,1)}, u32[]{:S(2)}, u32[]{:S(2)}) collective-permute-start(bf16[2304,512]{1,0:T(8,128)(2,1)} %bitcast.74), channel_id=1, source_target_pairs={{0,16},{16,0},{1,17},{17,1},{2,18},{18,2},{3,19},{19,3},{4,20},{20... | collective-permute-start | bytes 7077896 | tf_op jit(solution)/shard_map/ppermute | solution.py:472
  253.0 11.5 %collective-permute-start.59 = (bf16[2,240,768]{2,1,0:T(8,128)(2,1)S(1)}, bf16[2,240,768]{2,1,0:T(8,128)(2,1)S(1)}, u32[]{:S(2)}, u32[]{:S(2)}) collective-permute-start(bf16[2,240,768]{2,1,0:T(8,128)(2,1)S(1)} %add_convert_fusion.3), channel_id=1, source_target_pairs={{0,1},{1,0},{2,3},{3,2},{4,5},{5,4},{6,7},{7,6},{8,9},{9,8},{10,11... | collective-permute-start | bytes 2211848 | tf_op jit(solution)/shard_map/ppermute | solution.py:452
  254.1 10.4 %collective-permute-start.60 = (bf16[2,240,768]{2,1,0:T(8,128)(2,1)S(1)}, bf16[2,240,768]{2,1,0:T(8,128)(2,1)S(1)}, u32[]{:S(2)}, u32[]{:S(2)}) collective-permute-start(bf16[2,240,768]{2,1,0:T(8,128)(2,1)S(1)} %collective-permute-done.57.keep_ref), channel_id=1, source_target_pairs={{0,16},{16,0},{1,17},{17,1},{2,18},{18,2},{3,19},{19,3},{4,20},{20... | collective-permute-start | bytes 2211848 | tf_op jit(solution)/shard_map/ppermute | solution.py:472
  265.6 18.2 %collective-permute-start.61 = (bf16[2,240,768]{2,1,0:T(8,128)(2,1)}, bf16[2,240,768]{2,1,0:T(8,128)(2,1)S(1)}, u32[]{:S(2)}, u32[]{:S(2)}) collective-permute-start(bf16[2,240,768]{2,1,0:T(8,128)(2,1)} %get-tuple-element.794), channel_id=1, source_target_pairs={{0,1},{1,0},{2,3},{3,2},{4,5},{5,4},{6,7},{7,6},{8,9},{9,8},{10,11... | collective-permute-start | bytes 2211848 | tf_op jit(solution)/shard_map/ppermute | solution.py:452
  266.7 17.1 %collective-permute-start.62 = (bf16[2,240,768]{2,1,0:T(8,128)(2,1)}, bf16[2,240,768]{2,1,0:T(8,128)(2,1)S(1)}, u32[]{:S(2)}, u32[]{:S(2)}) collective-permute-start(bf16[2,240,768]{2,1,0:T(8,128)(2,1)} %get-tuple-element.796), channel_id=1, source_target_pairs={{0,2},{1,3},{2,0},{3,1},{4,6},{5,7},{6,4},{7,5},{8,10},{9,11},{10,... | collective-permute-start | bytes 2211848 | tf_op jit(solution)/shard_map/ppermute | solution.py:456
  267.0 16.8 %collective-permute-start.64 = (bf16[2,240,768]{2,1,0:T(8,128)(2,1)}, bf16[2,240,768]{2,1,0:T(8,128)(2,1)S(1)}, u32[]{:S(2)}, u32[]{:S(2)}) collective-permute-start(bf16[2,240,768]{2,1,0:T(8,128)(2,1)} %copy-done.44), channel_id=1, source_target_pairs={{0,16},{16,0},{1,17},{17,1},{2,18},{18,2},{3,19},{19,3},{4,20},{20... | collective-permute-start | bytes 2211848 | tf_op jit(solution)/shard_map/ppermute | solution.py:472
  284.1 14.3 %collective-permute-start.67 = (bf16[3072,512]{1,0:T(8,128)(2,1)}, bf16[3072,512]{1,0:T(8,128)(2,1)}, u32[]{:S(2)}, u32[]{:S(2)}) collective-permute-start(bf16[3072,512]{1,0:T(8,128)(2,1)} %get-tuple-element.884.own_high), channel_id=1, source_target_pairs={{0,16},{16,0},{1,17},{17,1},{2,18},{18,2},{3,19},{19,3},{4,20},{20... | collective-permute-start | bytes 9437192 | tf_op jit(solution)/shard_map/ppermute | solution.py:472
  284.1 14.2 %collective-permute-start.65 = (bf16[2,240,768]{2,1,0:T(8,128)(2,1)S(1)}, bf16[2,240,768]{2,1,0:T(8,128)(2,1)}, u32[]{:S(2)}, u32[]{:S(2)}) collective-permute-start(bf16[2,240,768]{2,1,0:T(8,128)(2,1)S(1)} %add_convert_fusion.2), channel_id=1, source_target_pairs={{0,1},{1,0},{2,3},{3,2},{4,5},{5,4},{6,7},{7,6},{8,9},{9,8},{10,11... | collective-permute-start | bytes 2211848 | tf_op jit(solution)/shard_map/ppermute | solution.py:452
  285.0 13.3 %collective-permute-start.66 = (bf16[2,240,768]{2,1,0:T(8,128)(2,1)S(1)}, bf16[2,240,768]{2,1,0:T(8,128)(2,1)S(1)}, u32[]{:S(2)}, u32[]{:S(2)}) collective-permute-start(bf16[2,240,768]{2,1,0:T(8,128)(2,1)S(1)} %collective-permute-done.61.keep_ref), channel_id=1, source_target_pairs={{0,16},{16,0},{1,17},{17,1},{2,18},{18,2},{3,19},{19,3},{4,20},{20... | collective-permute-start | bytes 2211848 | tf_op jit(solution)/shard_map/ppermute | solution.py:472
  299.2 26.1 %collective-permute-start.68 = (bf16[2,240,768]{2,1,0:T(8,128)(2,1)}, bf16[2,240,768]{2,1,0:T(8,128)(2,1)S(1)}, u32[]{:S(2)}, u32[]{:S(2)}) collective-permute-start(bf16[2,240,768]{2,1,0:T(8,128)(2,1)} %collective-permute-done.65.pass_ref), channel_id=1, source_target_pairs={{0,16},{16,0},{1,17},{17,1},{2,18},{18,2},{3,19},{19,3},{4,20},{20... | collective-permute-start | bytes 2211848 | tf_op jit(solution)/shard_map/ppermute | solution.py:472
  299.2 26.2 %collective-permute-start.69 = (bf16[2,336,768]{2,1,0:T(8,128)(2,1)}, bf16[2,336,768]{2,1,0:T(8,128)(2,1)S(1)}, u32[]{:S(2)}, u32[]{:S(2)}) collective-permute-start(bf16[2,336,768]{2,1,0:T(8,128)(2,1)} %get-tuple-element.840), channel_id=1, source_target_pairs={{0,2},{1,3},{2,0},{3,1},{4,6},{5,7},{6,4},{7,5},{8,10},{9,11},{10,... | collective-permute-start | bytes 3096584 | tf_op jit(solution)/shard_map/ppermute | solution.py:456
  302.0 23.4 %collective-permute-start.70 = (bf16[2,336,768]{2,1,0:T(8,128)(2,1)}, bf16[2,336,768]{2,1,0:T(8,128)(2,1)S(1)}, u32[]{:S(2)}, u32[]{:S(2)}) collective-permute-start(bf16[2,336,768]{2,1,0:T(8,128)(2,1)} %get-tuple-element.861), channel_id=1, source_target_pairs={{0,1},{1,0},{2,3},{3,2},{4,5},{5,4},{6,7},{7,6},{8,9},{9,8},{10,11... | collective-permute-start | bytes 3096584 | tf_op jit(solution)/shard_map/ppermute | solution.py:452
  303.0 22.3 %collective-permute-start.71 = (bf16[240,768]{1,0:T(8,128)(2,1)}, bf16[240,768]{1,0:T(8,128)(2,1)S(1)}, u32[]{:S(2)}, u32[]{:S(2)}) collective-permute-start(bf16[240,768]{1,0:T(8,128)(2,1)} %get-tuple-element.863), channel_id=1, source_target_pairs={{0,4},{1,5},{2,6},{3,7},{4,8},{5,9},{6,10},{7,11},{8,12},{9,13},{1... | collective-permute-start | bytes 1105928 | tf_op jit(solution)/shard_map/ppermute | solution.py:461
  304.2 21.1 %collective-permute-start.72 = (bf16[128,768]{1,0:T(8,128)(2,1)}, bf16[128,768]{1,0:T(8,128)(2,1)S(1)}, u32[]{:S(2)}, u32[]{:S(2)}) collective-permute-start(bf16[128,768]{1,0:T(8,128)(2,1)} %get-tuple-element.865), channel_id=1, source_target_pairs={{0,8},{4,12},{8,0},{12,4},{1,9},{5,13},{9,1},{13,5},{2,10},{6,14},... | collective-permute-start | bytes 589832 | tf_op jit(solution)/shard_map/ppermute | solution.py:468
  331.0 19.2 %collective-permute-start.76 = (bf16[2,336,768]{2,1,0:T(8,128)(2,1)S(1)}, bf16[2,336,768]{2,1,0:T(8,128)(2,1)S(1)}, u32[]{:S(2)}, u32[]{:S(2)}) collective-permute-start(bf16[2,336,768]{2,1,0:T(8,128)(2,1)S(1)} %add_convert_fusion.1), channel_id=1, source_target_pairs={{0,1},{1,0},{2,3},{3,2},{4,5},{5,4},{6,7},{7,6},{8,9},{9,8},{10,11... | collective-permute-start | bytes 3096584 | tf_op jit(solution)/shard_map/ppermute | solution.py:452
  332.2 18.0 %collective-permute-start.77 = (bf16[2,336,768]{2,1,0:T(8,128)(2,1)S(1)}, bf16[2,336,768]{2,1,0:T(8,128)(2,1)S(1)}, u32[]{:S(2)}, u32[]{:S(2)}) collective-permute-start(bf16[2,336,768]{2,1,0:T(8,128)(2,1)S(1)} %collective-permute-done.70.keep_ref), channel_id=1, source_target_pairs={{0,16},{16,0},{1,17},{17,1},{2,18},{18,2},{3,19},{19,3},{4,20},{20... | collective-permute-start | bytes 3096584 | tf_op jit(solution)/shard_map/ppermute | solution.py:472
  332.4 17.8 %collective-permute-start.74 = (bf16[240,768]{1,0:T(8,128)(2,1)}, bf16[240,768]{1,0:T(8,128)(2,1)}, u32[]{:S(2)}, u32[]{:S(2)}) collective-permute-start(bf16[240,768]{1,0:T(8,128)(2,1)} %get-tuple-element.880), channel_id=1, source_target_pairs={{0,4},{1,5},{2,6},{3,7},{4,8},{5,9},{6,10},{7,11},{8,12},{9,13},{1... | collective-permute-start | bytes 1105928 | tf_op jit(solution)/shard_map/ppermute | solution.py:461
  332.5 17.7 %collective-permute-start.75 = (bf16[128,768]{1,0:T(8,128)(2,1)}, bf16[128,768]{1,0:T(8,128)(2,1)}, u32[]{:S(2)}, u32[]{:S(2)}) collective-permute-start(bf16[128,768]{1,0:T(8,128)(2,1)} %get-tuple-element.882), channel_id=1, source_target_pairs={{0,8},{4,12},{8,0},{12,4},{1,9},{5,13},{9,1},{13,5},{2,10},{6,14},... | collective-permute-start | bytes 589832 | tf_op jit(solution)/shard_map/ppermute | solution.py:468
  335.9 14.3 %collective-permute-start.78 = (bf16[128,768]{1,0:T(8,128)(2,1)}, bf16[128,768]{1,0:T(8,128)(2,1)}, u32[]{:S(2)}, u32[]{:S(2)}) collective-permute-start(bf16[128,768]{1,0:T(8,128)(2,1)} %get-tuple-element.984.own_ref), channel_id=1, source_target_pairs={{0,16},{16,0},{1,17},{17,1},{2,18},{18,2},{3,19},{19,3},{4,20},{20... | collective-permute-start | bytes 589832 | tf_op jit(solution)/shard_map/ppermute | solution.py:472
  360.3 25.4 %collective-permute-start.82 = (bf16[2,336,768]{2,1,0:T(8,128)(2,1)}, bf16[2,336,768]{2,1,0:T(8,128)(2,1)S(1)}, u32[]{:S(2)}, u32[]{:S(2)}) collective-permute-start(bf16[2,336,768]{2,1,0:T(8,128)(2,1)} %get-tuple-element.917), channel_id=1, source_target_pairs={{0,2},{1,3},{2,0},{3,1},{4,6},{5,7},{6,4},{7,5},{8,10},{9,11},{10,... | collective-permute-start | bytes 3096584 | tf_op jit(solution)/shard_map/ppermute | solution.py:456
  360.9 24.8 %collective-permute-start.83 = (bf16[2,336,768]{2,1,0:T(8,128)(2,1)}, bf16[2,336,768]{2,1,0:T(8,128)(2,1)}, u32[]{:S(2)}, u32[]{:S(2)}) collective-permute-start(bf16[2,336,768]{2,1,0:T(8,128)(2,1)} %get-tuple-element.935), channel_id=1, source_target_pairs={{0,1},{1,0},{2,3},{3,2},{4,5},{5,4},{6,7},{7,6},{8,9},{9,8},{10,11... | collective-permute-start | bytes 3096584 | tf_op jit(solution)/shard_map/ppermute | solution.py:452
  362.4 22.9 %collective-permute-start.84 = (bf16[336,768]{1,0:T(8,128)(2,1)}, bf16[336,768]{1,0:T(8,128)(2,1)}, u32[]{:S(2)}, u32[]{:S(2)}) collective-permute-start(bf16[336,768]{1,0:T(8,128)(2,1)} %get-tuple-element.936), channel_id=1, source_target_pairs={{0,4},{1,5},{2,6},{3,7},{4,8},{5,9},{6,10},{7,11},{8,12},{9,13},{1... | collective-permute-start | bytes 1548296 | tf_op jit(solution)/shard_map/ppermute | solution.py:461
  362.9 22.4 %collective-permute-start.85 = (bf16[176,768]{1,0:T(8,128)(2,1)}, bf16[176,768]{1,0:T(8,128)(2,1)}, u32[]{:S(2)}, u32[]{:S(2)}) collective-permute-start(bf16[176,768]{1,0:T(8,128)(2,1)} %get-tuple-element.938), channel_id=1, source_target_pairs={{0,8},{4,12},{8,0},{12,4},{1,9},{5,13},{9,1},{13,5},{2,10},{6,14},... | collective-permute-start | bytes 811016 | tf_op jit(solution)/shard_map/ppermute | solution.py:468
  366.3 19.0 %collective-permute-start.87 = (bf16[512,768]{1,0:T(8,128)(2,1)S(1)}, bf16[512,768]{1,0:T(8,128)(2,1)}, u32[]{:S(2)}, u32[]{:S(2)}) collective-permute-start(bf16[512,768]{1,0:T(8,128)(2,1)S(1)} %copy-done.11), channel_id=1, source_target_pairs={{0,16},{16,0},{1,17},{17,1},{2,18},{18,2},{3,19},{19,3},{4,20},{20... | collective-permute-start | bytes 2359304 | tf_op jit(solution)/shard_map/ppermute | solution.py:472
  385.9 14.9 %collective-permute-start.90 = (bf16[2,336,768]{2,1,0:T(8,128)(2,1)S(1)}, bf16[2,336,768]{2,1,0:T(8,128)(2,1)S(1)}, u32[]{:S(2)}, u32[]{:S(2)}) collective-permute-start(bf16[2,336,768]{2,1,0:T(8,128)(2,1)S(1)} %add_convert_fusion), channel_id=1, source_target_pairs={{0,1},{1,0},{2,3},{3,2},{4,5},{5,4},{6,7},{7,6},{8,9},{9,8},{10,11... | collective-permute-start | bytes 3096584 | tf_op jit(solution)/shard_map/ppermute | solution.py:452
  386.8 14.0 %collective-permute-start.91 = (bf16[2,336,768]{2,1,0:T(8,128)(2,1)}, bf16[2,336,768]{2,1,0:T(8,128)(2,1)}, u32[]{:S(2)}, u32[]{:S(2)}) collective-permute-start(bf16[2,336,768]{2,1,0:T(8,128)(2,1)} %collective-permute-done.83.keep_ref), channel_id=1, source_target_pairs={{0,16},{16,0},{1,17},{17,1},{2,18},{18,2},{3,19},{19,3},{4,20},{20... | collective-permute-start | bytes 3096584 | tf_op jit(solution)/shard_map/ppermute | solution.py:472
  388.1 12.7 %collective-permute-start.88 = (bf16[240,768]{1,0:T(8,128)(2,1)}, bf16[240,768]{1,0:T(8,128)(2,1)S(1)}, u32[]{:S(2)}, u32[]{:S(2)}) collective-permute-start(bf16[240,768]{1,0:T(8,128)(2,1)} %collective-permute-done.74.near_ref), channel_id=1, source_target_pairs={{0,16},{16,0},{1,17},{17,1},{2,18},{18,2},{3,19},{19,3},{4,20},{20... | collective-permute-start | bytes 1105928 | tf_op jit(solution)/shard_map/ppermute | solution.py:472
  388.1 12.7 %collective-permute-start.89 = (bf16[128,768]{1,0:T(8,128)(2,1)}, bf16[128,768]{1,0:T(8,128)(2,1)S(1)}, u32[]{:S(2)}, u32[]{:S(2)}) collective-permute-start(bf16[128,768]{1,0:T(8,128)(2,1)} %collective-permute-done.75.far_ref), channel_id=1, source_target_pairs={{0,16},{16,0},{1,17},{17,1},{2,18},{18,2},{3,19},{19,3},{4,20},{20... | collective-permute-start | bytes 589832 | tf_op jit(solution)/shard_map/ppermute | solution.py:472
  388.6 12.2 %collective-permute-start.92 = (f32[16,128]{1,0:T(8,128)S(1)}, f32[16,128]{1,0:T(8,128)S(1)}, u32[]{:S(2)}, u32[]{:S(2)}) collective-permute-start(f32[16,128]{1,0:T(8,128)S(1)} %pad_bitcast_fusion), channel_id=1, source_target_pairs={{0,1},{1,0},{2,3},{3,2},{4,5},{5,4},{6,7},{7,6},{8,9},{9,8},{10,11... | collective-permute-start | bytes 24584 | tf_op jit(solution)/shard_map/ppermute | solution.py:898
  409.6 23.6 %collective-permute-start.99 = (bf16[336,768]{1,0:T(8,128)(2,1)}, bf16[336,768]{1,0:T(8,128)(2,1)}, u32[]{:S(2)}, u32[]{:S(2)}) collective-permute-start(bf16[336,768]{1,0:T(8,128)(2,1)} %get-tuple-element.1001), channel_id=1, source_target_pairs={{0,4},{1,5},{2,6},{3,7},{4,8},{5,9},{6,10},{7,11},{8,12},{9,13},{1... | collective-permute-start | bytes 1548296 | tf_op jit(solution)/shard_map/ppermute | solution.py:461
  411.1 22.1 %collective-permute-start.100 = (bf16[176,768]{1,0:T(8,128)(2,1)}, bf16[176,768]{1,0:T(8,128)(2,1)}, u32[]{:S(2)}, u32[]{:S(2)}) collective-permute-start(bf16[176,768]{1,0:T(8,128)(2,1)} %get-tuple-element.1003), channel_id=1, source_target_pairs={{0,8},{4,12},{8,0},{12,4},{1,9},{5,13},{9,1},{13,5},{2,10},{6,14},... | collective-permute-start | bytes 811016 | tf_op jit(solution)/shard_map/ppermute | solution.py:468
  414.5 13.2 %collective-permute-start.101 = (f32[16,128]{1,0:T(8,128)S(1)}, f32[16,128]{1,0:T(8,128)S(1)}, u32[]{:S(2)}, u32[]{:S(2)}) collective-permute-start(f32[16,128]{1,0:T(8,128)S(1)} %add.99), channel_id=1, source_target_pairs={{0,4},{4,0},{8,12},{12,8},{1,5},{5,1},{9,13},{13,9},{2,6},{6,2},{1... | collective-permute-start | bytes 24584 | tf_op jit(solution)/shard_map/ppermute | solution.py:921
  414.5 18.7 %collective-permute-start.102 = (bf16[176,768]{1,0:T(8,128)(2,1)}, bf16[176,768]{1,0:T(8,128)(2,1)}, u32[]{:S(2)}, u32[]{:S(2)}) collective-permute-start(bf16[176,768]{1,0:T(8,128)(2,1)} %get-tuple-element.1019.own_ref), channel_id=1, source_target_pairs={{0,16},{16,0},{1,17},{17,1},{2,18},{18,2},{3,19},{19,3},{4,20},{20... | collective-permute-start | bytes 811016 | tf_op jit(solution)/shard_map/ppermute | solution.py:472
  (120 other events, 952.5 us)

commit v5 on v4

--- a/solution.py
+++ b/solution.py
@@ -1102,13 +1102,12 @@
         )
         in_0.across()
         small = small + got
-        got = order.move(butterfly(2), small)
+        got = order.move(butterfly(2), small, count=2)
         order.fence()
-        small = small + got
-        got = order.swap(small)
         in_grad = order.run(total, *in_0.ends(), in_grad_1)[None]
         out_grad = out_grad[None]
         small = small + got
+        small = small + order.swap(small)
     else:
         top_1, grad_0, gain_1, heads_1 = order.run(back, *kept_1, feed_1)
         feed_0, low_0 = order.run(feed, grad_0, slope_0, weight_in_0, weight_out_0)

time: 455 us -> 457 us (level)
  transfers between devices with their start and end apart: 107 -> 107, of which waited for: 32 -> 33; matrix products, arithmetic and copies ran while one was open for 3% -> 3% of each run, Pallas kernels for 44% -> 43%
where the time goes in v5:
time: 457 us; the launch traced here: 449 us
  Pallas kernels  206 us (45%)
  waiting for transfers between devices  115 us (25%)
  starting transfers between devices  94.8 us (21%)
  local copies, waits for them, and re-layouts  18.5 us (4%)
  other arithmetic  9.67 us (2%)
  between operations  4.82 us (1%)
    pallas_call x30, Pallas kernels, launch(): pl.pallas_call(kernel, grid=grid, in_specs=in_specs, out_specs=out_specs,...  206 us
    ppermute x8, waiting for transfers between devices, opposite(): lax.ppermute(value, 'z', [(z, (z + 2) % depth) for z in range(depth)])  46.7 us
    ppermute x8, starting transfers between devices, opposite(): lax.ppermute(value, 'z', [(z, (z + 2) % depth) for z in range(depth)])  26.2 us
    ppermute x59, starting transfers between devices, swap(): return lax.ppermute(value, 'section', [(0, 1), (1, 0)])  22.1 us
    ppermute x59, waiting for transfers between devices, swap(): return lax.ppermute(value, 'section', [(0, 1), (1, 0)])  19.7 us
    ppermute x16, starting transfers between devices, sideways(): return lax.ppermute(value, ALL, sends(fine, next_x, next_y))  16.8 us
    ppermute x16, waiting for transfers between devices, sideways(): return lax.ppermute(value, ALL, sends(fine, next_x, next_y))  16.3 us
    ppermute x8, waiting for transfers between devices, turned(): return lax.ppermute(value, ALL, sends(fine, next_y, next_x))  11.4 us
  transfers between devices with their start and end apart: 107, of which 33 were waited for; matrix products, arithmetic and copies ran while one was open for 3% of the time, Pallas kernels for 43%

profile of v5, /device:TPU:0, one launch (start us, length us, event | category | flops | bytes accessed | tf_op | source)
XLA Modules:
  0.0 448.8 jit_solution(7095195078247540313)
XLA Ops:
  5.2 1.9 pick.4
  7.1 3.0 collective-permute-start.3
  10.1 2.6 collective-permute-start.4
  14.2 2.2 collective-permute-done.5
  16.4 15.1 %collective-permute-done.4.far_ref = bf16[176,768]{1,0:T(8,128)(2,1)S(1)} collective-permute-done((bf16[176,768]{1,0:T(8,128)(2,1)}, bf16[176,768]{1,0:T(8,128)(2,1)S(1)}, u32[]{:S(2)}, u32[]{:S(2)}) %collective-permute-start.4) | collective-permute-done | bytes 270368 | tf_op jit(solution)/shard_map/ppermute | solution.py:468
  31.5 3.5 collective-permute-start.6
  39.7 2.9 line.4
  48.5 3.3 collective-permute-start.12
  53.1 2.2 pick.6
  58.1 7.4 %collective-permute-done.12.far_ref = bf16[128,768]{1,0:T(8,128)(2,1)S(1)} collective-permute-done((bf16[128,768]{1,0:T(8,128)(2,1)S(1)}, bf16[128,768]{1,0:T(8,128)(2,1)S(1)}, u32[]{:S(2)}, u32[]{:S(2)}) %collective-permute-start.12) | collective-permute-done | bytes 196640 | tf_op jit(solution)/shard_map/ppermute | solution.py:468
  65.5 3.1 collective-permute-done.10.refs_2_
  71.9 2.5 collective-permute-done.13
  76.2 2.5 line.5
  78.7 2.5 collective-permute-start.18
  81.2 2.9 collective-permute-done.19.refs_6_
  88.1 3.3 collective-permute-start.24
  92.8 14.5 %attend.2 = (bf16[512,768]{1,0:T(8,128)(2,1)}, f32[2,3,256,512]{3,2,1,0:T(8,128)}, bf16[768,512]{1,0:T(8,128)(2,1)}, bf16[768,512]{1,0:T(8,128)(2,1)}, f32[3,8,512]{2,1,0:T(8,128)}, /*index=5*/bf16[5376,768]{1,0:T(8,128)(2,1)}) custom-call(s32[1,2]{1,0:T(1,128)} %copy-done.23, bf16[512,768]{1,0:T(8,128)(2,1)} %dynamic-slice_bitcast_fusion.rows_ref, ...), custom_call_target="tpu_custom_call" | custom-call | flops 14949999616 | bytes 13000000 | tf_op jit(solution)/shard_map/attend/pallas_call | solution.py:40
  107.3 2.7 collective-permute-done.24.far_ref
  111.6 2.2 collective-permute-start.26
  114.4 8.4 %hidden.2 = (bf16[3072,512]{1,0:T(8,128)(2,1)}, bf16[3072,512]{1,0:T(8,128)(2,1)}) custom-call(bf16[512,768]{1,0:T(8,128)(2,1)} %get-tuple-element.887.normed_ref.right_ref, bf16[5376,768]{1,0:T(8,128)(2,1)} %get-tuple-element.854.weight_ref.weight_in_ref), custom_call_target="tpu_custom_call" | custom-call | flops 9200000000 | bytes 8000000 | tf_op jit(solution)/shard_map/hidden/pallas_call | solution.py:40
  123.7 2.9 line.6
  130.6 3.4 collective-permute-start.32
  134.0 11.0 %output.2 = (bf16[512,768]{1,0:T(8,128)(2,1)}, f32[3,8,768]{2,1,0:T(8,128)}, bf16[3840,768]{1,0:T(8,128)(2,1)}) custom-call(s32[1,2]{1,0:T(1,128)} %copy-done.23, bf16[512,768]{1,0:T(8,128)(2,1)} %dynamic-slice_bitcast_fusion.rows_ref, bf16[768,512]{1,0:T(8,128)(2,1)} %get-tuple-element.851.attended_ref.own_low, ...), custom_call_target="tpu_custom_call" | custom-call | flops 10350000128 | bytes 9000000 | tf_op jit(solution)/shard_map/output/pallas_call | solution.py:40
  145.0 2.9 collective-permute-done.32.far_ref
  148.0 4.7 %collective-permute-done.34.refs_2_ = bf16[2,336,768]{2,1,0:T(8,128)(2,1)S(1)} collective-permute-done((bf16[2,336,768]{2,1,0:T(8,128)(2,1)}, bf16[2,336,768]{2,1,0:T(8,128)(2,1)S(1)}, u32[]{:S(2)}, u32[]{:S(2)}) %collective-permute-start.34) | collective-permute-done | bytes 1032224 | tf_op jit(solution)/shard_map/ppermute | solution.py:452
  158.3 2.5 line.7
  161.0 7.3 %collective-permute-done.39.refs_6_ = bf16[2,336,768]{2,1,0:T(8,128)(2,1)} collective-permute-done((bf16[2,336,768]{2,1,0:T(8,128)(2,1)S(1)}, bf16[2,336,768]{2,1,0:T(8,128)(2,1)}, u32[]{:S(2)}, u32[]{:S(2)}) %collective-permute-start.39) | collective-permute-done | bytes 1032224 | tf_op jit(solution)/shard_map/ppermute | solution.py:456
  168.4 2.8 collective-permute-done.41.refs_7_
  175.3 14.5 %attend.3 = (bf16[512,768]{1,0:T(8,128)(2,1)}, f32[2,3,256,512]{3,2,1,0:T(8,128)}, bf16[768,512]{1,0:T(8,128)(2,1)}, bf16[768,512]{1,0:T(8,128)(2,1)}, f32[3,8,512]{2,1,0:T(8,128)}, /*index=5*/bf16[5376,768]{1,0:T(8,128)(2,1)}) custom-call(s32[1,2]{1,0:T(1,128)} %copy-done.23, bf16[512,768]{1,0:T(8,128)(2,1)} %get-tuple-element.993.rows_ref, ...), custom_call_target="tpu_custom_call" | custom-call | flops 14949999616 | bytes 13000000 | tf_op jit(solution)/shard_map/attend/pallas_call | solution.py:40
  194.5 8.5 %hidden.3 = (bf16[3072,512]{1,0:T(8,128)(2,1)}, bf16[3072,512]{1,0:T(8,128)(2,1)}) custom-call(bf16[512,768]{1,0:T(8,128)(2,1)} %get-tuple-element.819.normed_ref.right_ref, bf16[5376,768]{1,0:T(8,128)(2,1)} %get-tuple-element.761.weight_ref.weight_in_ref), custom_call_target="tpu_custom_call" | custom-call | flops 9200000000 | bytes 8000000 | tf_op jit(solution)/shard_map/hidden/pallas_call | solution.py:40
  203.8 2.4 collective-permute-done.52.refs_7_
  207.1 13.4 %feed_back.2 = (f32[512,768]{1,0:T(8,128)}, bf16[3072,512]{1,0:T(8,128)(2,1)}, bf16[3840,768]{1,0:T(8,128)(2,1)}) custom-call(bf16[512,768]{1,0:T(8,128)(2,1)} %copy-done.15, bf16[3072,512]{1,0:T(8,128)(2,1)} %get-tuple-element.720.slope_ref, bf16[5376,768]{1,0:T(8,128)(2,1)} %get-tuple-element.761.weight_ref.weight_in_ref, ...), custom_call_target="tpu_custom_call" | custom-call | flops 12650000384 | bytes 11000000 | tf_op jit(solution)/shard_map/feed_back/pallas_call | solution.py:40
  220.8 7.8 %partial.4 = (bf16[2,240,768]{2,1,0:T(8,128)(2,1)}, bf16[2,240,768]{2,1,0:T(8,128)(2,1)}, bf16[2,240,768]{2,1,0:T(8,128)(2,1)}, bf16[240,768]{1,0:T(8,128)(2,1)}, bf16[2,128,768]{2,1,0:T(8,128)(2,1)}) custom-call(bf16[768,512]{1,0:T(8,128)(2,1)} %get-tuple-element.924.own_low.attended_ref, bf16[3072,512]{1,0:T(8,128)(2,1)} %get-tuple-element.925.own_high.hidden_ref, ...), custom_call_target="tpu_custom_call" | custom-call | flops 6308571648 | bytes 5485714 | tf_op jit(solution)/shard_map/partial/pallas_call | solution.py:40
  232.6 17.5 %attend_back.2 = (bf16[3,3,256,512]{3,2,1,0:T(8,128)(2,1)}, bf16[512,768]{1,0:T(8,128)(2,1)}, f32[8,768]{1,0:T(8,128)}, f32[2,64,128]{2,1,0:T(8,128)}) custom-call(s32[1,2]{1,0:T(1,128)} %copy-done.23, bf16[512,768]{1,0:T(8,128)(2,1)} %get-tuple-element.993.rows_ref, bf16[512,768]{1,0:T(8,128)(2,1)} %copy-done.15, f32[1,768]{1,0:T(1,128)} %get-tuple-element.753.gain_ref, ...), custom_call_target="tpu_custom_call" | custom-call | flops 19549999104 | bytes 17000000 | tf_op jit(solution)/shard_map/attend_back/pallas_call | solution.py:40
  250.9 2.1 collective-permute-done.58.right_other_ref
  254.1 7.6 %partial.5 = (bf16[2,240,768]{2,1,0:T(8,128)(2,1)}, bf16[2,240,768]{2,1,0:T(8,128)(2,1)}, bf16[2,240,768]{2,1,0:T(8,128)(2,1)}, bf16[240,768]{1,0:T(8,128)(2,1)}, bf16[2,128,768]{2,1,0:T(8,128)(2,1)}) custom-call(bf16[768,512]{1,0:T(8,128)(2,1)} %get-tuple-element.851.attended_ref.own_low, bf16[3072,512]{1,0:T(8,128)(2,1)} %get-tuple-element.778.hidden_ref.own_high, ...), custom_call_target="tpu_custom_call" | custom-call | flops 6308571648 | bytes 5485714 | tf_op jit(solution)/shard_map/partial/pallas_call | solution.py:40
  261.8 2.7 collective-permute-done.59.pass_ref
  267.0 12.2 %feed_back.3 = (f32[512,768]{1,0:T(8,128)}, bf16[3072,512]{1,0:T(8,128)(2,1)}) custom-call(bf16[512,768]{1,0:T(8,128)(2,1)} %get-tuple-element.998.right_ref.grad_ref, bf16[3072,512]{1,0:T(8,128)(2,1)} %get-tuple-element.800.slope_ref, bf16[5376,768]{1,0:T(8,128)(2,1)} %get-tuple-element.854.weight_ref.weight_in_ref, ...), custom_call_target="tpu_custom_call" | custom-call | flops 12650000384 | bytes 11000000 | tf_op jit(solution)/shard_map/feed_back/pallas_call | solution.py:40
  279.3 4.6 %collective-permute-done.61.keep_ref = bf16[2,240,768]{2,1,0:T(8,128)(2,1)S(1)} collective-permute-done((bf16[2,240,768]{2,1,0:T(8,128)(2,1)}, bf16[2,240,768]{2,1,0:T(8,128)(2,1)S(1)}, u32[]{:S(2)}, u32[]{:S(2)}) %collective-permute-start.61) | collective-permute-done | bytes 737312 | tf_op jit(solution)/shard_map/ppermute | solution.py:452
  285.8 3.5 depth.4
  289.3 9.0 %partial.6 = (bf16[2,336,768]{2,1,0:T(8,128)(2,1)}, bf16[2,336,768]{2,1,0:T(8,128)(2,1)}, bf16[2,336,768]{2,1,0:T(8,128)(2,1)}, bf16[336,768]{1,0:T(8,128)(2,1)}, bf16[2,176,768]{2,1,0:T(8,128)(2,1)}) custom-call(bf16[2304,512]{1,0:T(8,128)(2,1)} %bitcast.75, bf16[3072,512]{1,0:T(8,128)(2,1)} %get-tuple-element.816.own_high, ...), custom_call_target="tpu_custom_call" | custom-call | flops 8832000000 | bytes 7680000 | tf_op jit(solution)/shard_map/partial/pallas_call | solution.py:40
  304.2 3.4 collective-permute-start.72
  307.6 17.7 %attend_back.3 = (bf16[3,3,256,512]{3,2,1,0:T(8,128)(2,1)}, bf16[512,768]{1,0:T(8,128)(2,1)}, f32[8,768]{1,0:T(8,128)}, f32[2,64,128]{2,1,0:T(8,128)}) custom-call(s32[1,2]{1,0:T(1,128)} %copy-done.23, bf16[512,768]{1,0:T(8,128)(2,1)} %dynamic-slice_bitcast_fusion.rows_ref, bf16[512,768]{1,0:T(8,128)(2,1)} %get-tuple-element.998.right_ref.grad_ref, ...), custom_call_target="tpu_custom_call" | custom-call | flops 19549999104 | bytes 17000000 | tf_op jit(solution)/shard_map/attend_back/pallas_call | solution.py:40
  326.4 3.6 depth.5
  332.5 3.4 collective-permute-start.75
  335.9 8.9 %partial.7 = (bf16[2,336,768]{2,1,0:T(8,128)(2,1)}, bf16[2,336,768]{2,1,0:T(8,128)(2,1)}, bf16[2,336,768]{2,1,0:T(8,128)(2,1)}, bf16[336,768]{1,0:T(8,128)(2,1)}, bf16[2,176,768]{2,1,0:T(8,128)(2,1)}) custom-call(bf16[2304,512]{1,0:T(8,128)(2,1)} %bitcast.77, bf16[3072,512]{1,0:T(8,128)(2,1)} %get-tuple-element.884.own_high, ...), custom_call_target="tpu_custom_call" | custom-call | flops 8832000000 | bytes 7680000 | tf_op jit(solution)/shard_map/partial/pallas_call | solution.py:40
  344.8 5.4 %collective-permute-done.75.far_ref = bf16[128,768]{1,0:T(8,128)(2,1)} collective-permute-done((bf16[128,768]{1,0:T(8,128)(2,1)}, bf16[128,768]{1,0:T(8,128)(2,1)}, u32[]{:S(2)}, u32[]{:S(2)}) %collective-permute-start.75) | collective-permute-done | bytes 196640 | tf_op jit(solution)/shard_map/ppermute | solution.py:468
  352.1 2.8 collective-permute-done.81.far_other
  354.9 4.1 depth.6
  362.9 3.4 collective-permute-start.85
  366.4 9.7 %output.3 = (bf16[512,768]{1,0:T(8,128)(2,1)}, f32[3,8,768]{2,1,0:T(8,128)}) custom-call(s32[1,2]{1,0:T(1,128)} %copy-done.23, bf16[512,768]{1,0:T(8,128)(2,1)} %get-tuple-element.993.rows_ref, bf16[768,512]{1,0:T(8,128)(2,1)} %get-tuple-element.924.own_low.attended_ref, bf16[3072,512]{1,0:T(8,128)(2,1)} %get-tuple-element.925.own_high.hidden_ref, ...), custom_call_target="tpu_custom_call" | custom-call | flops 10350000128 | bytes 9000000 | tf_op jit(solution)/shard_map/output/pallas_call | solution.py:40
  377.7 7.6 %collective-permute-done.85.far_ref = bf16[176,768]{1,0:T(8,128)(2,1)} collective-permute-done((bf16[176,768]{1,0:T(8,128)(2,1)}, bf16[176,768]{1,0:T(8,128)(2,1)}, u32[]{:S(2)}, u32[]{:S(2)}) %collective-permute-start.85) | collective-permute-done | bytes 270368 | tf_op jit(solution)/shard_map/ppermute | solution.py:468
  390.1 2.4 total.4.refs_0_
  392.5 8.3 %collective-permute-done.92 = f32[16,128]{1,0:T(8,128)S(1)} collective-permute-done((f32[16,128]{1,0:T(8,128)S(1)}, f32[16,128]{1,0:T(8,128)S(1)}, u32[]{:S(2)}, u32[]{:S(2)}) %collective-permute-start.92) | collective-permute-done | bytes 8224 | tf_op jit(solution)/shard_map/ppermute | solution.py:898
  401.4 2.3 collective-permute-done.93.pass_other
  405.5 4.0 depth.7
  411.1 3.4 collective-permute-start.100
  416.1 2.8 total.6.refs_0_
  418.9 2.7 total.5
  424.1 3.5 collective-permute-done.101
  427.6 5.6 %collective-permute-done.100.far_ref = bf16[176,768]{1,0:T(8,128)(2,1)} collective-permute-done((bf16[176,768]{1,0:T(8,128)(2,1)}, bf16[176,768]{1,0:T(8,128)(2,1)}, u32[]{:S(2)}, u32[]{:S(2)}) %collective-permute-start.100) | collective-permute-done | bytes 270368 | tf_op jit(solution)/shard_map/ppermute | solution.py:468
  433.2 2.6 collective-permute-start.103
  435.9 4.5 %collective-permute-done.105 = f32[16,128]{1,0:T(8,128)S(1)} collective-permute-done((f32[16,128]{1,0:T(8,128)S(1)}, f32[16,128]{1,0:T(8,128)S(1)}, u32[]{:S(2)}, u32[]{:S(2)}) %collective-permute-start.105) | collective-permute-done | bytes 8224 | tf_op jit(solution)/shard_map/ppermute | solution.py:921
  442.0 3.1 total.7
  (385 shorter events, 96.5 us)
Async XLA Ops:
  7.1 24.4 %collective-permute-start.3 = (bf16[336,768]{1,0:T(8,128)(2,1)}, bf16[336,768]{1,0:T(8,128)(2,1)S(1)}, u32[]{:S(2)}, u32[]{:S(2)}) collective-permute-start(bf16[336,768]{1,0:T(8,128)(2,1)} %get-tuple-element.537.own_ref), channel_id=1, source_target_pairs={{0,4},{1,5},{2,6},{3,7},{4,8},{5,9},{6,10},{7,11},{8,12},{9,13},{1... | collective-permute-start | bytes 1548296 | tf_op jit(solution)/shard_map/ppermute | solution.py:461
  10.1 21.4 %collective-permute-start.4 = (bf16[176,768]{1,0:T(8,128)(2,1)}, bf16[176,768]{1,0:T(8,128)(2,1)S(1)}, u32[]{:S(2)}, u32[]{:S(2)}) collective-permute-start(bf16[176,768]{1,0:T(8,128)(2,1)} %get-tuple-element.526), channel_id=1, source_target_pairs={{0,8},{4,12},{8,0},{12,4},{1,9},{5,13},{9,1},{13,5},{2,10},{6,14},... | collective-permute-start | bytes 811016 | tf_op jit(solution)/shard_map/ppermute | solution.py:468
  42.6 22.9 %collective-permute-start.9 = (bf16[2,336,768]{2,1,0:T(8,128)(2,1)}, bf16[2,336,768]{2,1,0:T(8,128)(2,1)}, u32[]{:S(2)}, u32[]{:S(2)}) collective-permute-start(bf16[2,336,768]{2,1,0:T(8,128)(2,1)} %get-tuple-element.591.refs_1_), channel_id=1, source_target_pairs={{0,1},{1,0},{2,3},{3,2},{4,5},{5,4},{6,7},{7,6},{8,9},{9,8},{10,11... | collective-permute-start | bytes 3096584 | tf_op jit(solution)/shard_map/ppermute | solution.py:452
  44.2 24.5 %collective-permute-start.10 = (bf16[2,336,768]{2,1,0:T(8,128)(2,1)}, bf16[2,336,768]{2,1,0:T(8,128)(2,1)}, u32[]{:S(2)}, u32[]{:S(2)}) collective-permute-start(bf16[2,336,768]{2,1,0:T(8,128)(2,1)} %get-tuple-element.590.refs_0_), channel_id=1, source_target_pairs={{0,1},{1,0},{2,3},{3,2},{4,5},{5,4},{6,7},{7,6},{8,9},{9,8},{10,11... | collective-permute-start | bytes 3096584 | tf_op jit(solution)/shard_map/ppermute | solution.py:452
  47.3 18.3 %collective-permute-start.11 = (bf16[240,768]{1,0:T(8,128)(2,1)S(1)}, bf16[240,768]{1,0:T(8,128)(2,1)S(1)}, u32[]{:S(2)}, u32[]{:S(2)}) collective-permute-start(bf16[240,768]{1,0:T(8,128)(2,1)S(1)} %copy-done.61), channel_id=1, source_target_pairs={{0,4},{1,5},{2,6},{3,7},{4,8},{5,9},{6,10},{7,11},{8,12},{9,13},{1... | collective-permute-start | bytes 1105928 | tf_op jit(solution)/shard_map/ppermute | solution.py:461
  48.5 17.1 %collective-permute-start.12 = (bf16[128,768]{1,0:T(8,128)(2,1)S(1)}, bf16[128,768]{1,0:T(8,128)(2,1)S(1)}, u32[]{:S(2)}, u32[]{:S(2)}) collective-permute-start(bf16[128,768]{1,0:T(8,128)(2,1)S(1)} %copy-done.74), channel_id=1, source_target_pairs={{0,8},{4,12},{8,0},{12,4},{1,9},{5,13},{9,1},{13,5},{2,10},{6,14},... | collective-permute-start | bytes 589832 | tf_op jit(solution)/shard_map/ppermute | solution.py:468
  68.7 10.0 %collective-permute-start.17 = (bf16[2,336,768]{2,1,0:T(8,128)(2,1)}, bf16[2,336,768]{2,1,0:T(8,128)(2,1)S(1)}, u32[]{:S(2)}, u32[]{:S(2)}) collective-permute-start(bf16[2,336,768]{2,1,0:T(8,128)(2,1)} %collective-permute-done.9.refs_3_), channel_id=1, source_target_pairs={{0,16},{16,0},{1,17},{17,1},{2,18},{18,2},{3,19},{19,3},{4,20},{20... | collective-permute-start | bytes 3096584 | tf_op jit(solution)/shard_map/ppermute | solution.py:472
  69.2 14.9 %collective-permute-start.19 = (bf16[2,336,768]{2,1,0:T(8,128)(2,1)}, bf16[2,336,768]{2,1,0:T(8,128)(2,1)}, u32[]{:S(2)}, u32[]{:S(2)}) collective-permute-start(bf16[2,336,768]{2,1,0:T(8,128)(2,1)} %collective-permute-done.9.refs_3_), channel_id=1, source_target_pairs={{0,2},{1,3},{2,0},{3,1},{4,6},{5,7},{6,4},{7,5},{8,10},{9,11},{10,... | collective-permute-start | bytes 3096584 | tf_op jit(solution)/shard_map/ppermute | solution.py:456
  84.8 25.2 %collective-permute-start.21 = (bf16[2,240,768]{2,1,0:T(8,128)(2,1)}, bf16[2,240,768]{2,1,0:T(8,128)(2,1)}, u32[]{:S(2)}, u32[]{:S(2)}) collective-permute-start(bf16[2,240,768]{2,1,0:T(8,128)(2,1)} %get-tuple-element.640.refs_1_), channel_id=1, source_target_pairs={{0,1},{1,0},{2,3},{3,2},{4,5},{5,4},{6,7},{7,6},{8,9},{9,8},{10,11... | collective-permute-start | bytes 2211848 | tf_op jit(solution)/shard_map/ppermute | solution.py:452
  86.4 23.7 %collective-permute-start.22 = (bf16[2,240,768]{2,1,0:T(8,128)(2,1)}, bf16[2,240,768]{2,1,0:T(8,128)(2,1)}, u32[]{:S(2)}, u32[]{:S(2)}) collective-permute-start(bf16[2,240,768]{2,1,0:T(8,128)(2,1)} %get-tuple-element.639.refs_0_), channel_id=1, source_target_pairs={{0,1},{1,0},{2,3},{3,2},{4,5},{5,4},{6,7},{7,6},{8,9},{9,8},{10,11... | collective-permute-start | bytes 2211848 | tf_op jit(solution)/shard_map/ppermute | solution.py:452
  86.9 23.1 %collective-permute-start.23 = (bf16[336,768]{1,0:T(8,128)(2,1)S(1)}, bf16[336,768]{1,0:T(8,128)(2,1)}, u32[]{:S(2)}, u32[]{:S(2)}) collective-permute-start(bf16[336,768]{1,0:T(8,128)(2,1)S(1)} %copy-done.51), channel_id=1, source_target_pairs={{0,4},{1,5},{2,6},{3,7},{4,8},{5,9},{6,10},{7,11},{8,12},{9,13},{1... | collective-permute-start | bytes 1548296 | tf_op jit(solution)/shard_map/ppermute | solution.py:461
  88.1 22.0 %collective-permute-start.24 = (bf16[176,768]{1,0:T(8,128)(2,1)}, bf16[176,768]{1,0:T(8,128)(2,1)}, u32[]{:S(2)}, u32[]{:S(2)}) collective-permute-start(bf16[176,768]{1,0:T(8,128)(2,1)} %get-tuple-element.609), channel_id=1, source_target_pairs={{0,8},{4,12},{8,0},{12,4},{1,9},{5,13},{9,1},{13,5},{2,10},{6,14},... | collective-permute-start | bytes 811016 | tf_op jit(solution)/shard_map/ppermute | solution.py:468
  110.1 12.7 %collective-permute-start.25 = (bf16[2,240,768]{2,1,0:T(8,128)(2,1)}, bf16[2,240,768]{2,1,0:T(8,128)(2,1)S(1)}, u32[]{:S(2)}, u32[]{:S(2)}) collective-permute-start(bf16[2,240,768]{2,1,0:T(8,128)(2,1)} %collective-permute-done.21.refs_3_), channel_id=1, source_target_pairs={{0,2},{1,3},{2,0},{3,1},{4,6},{5,7},{6,4},{7,5},{8,10},{9,11},{10,... | collective-permute-start | bytes 2211848 | tf_op jit(solution)/shard_map/ppermute | solution.py:456
  111.6 11.2 %collective-permute-start.26 = (bf16[2,240,768]{2,1,0:T(8,128)(2,1)}, bf16[2,240,768]{2,1,0:T(8,128)(2,1)S(1)}, u32[]{:S(2)}, u32[]{:S(2)}) collective-permute-start(bf16[2,240,768]{2,1,0:T(8,128)(2,1)} %collective-permute-done.22.refs_2_), channel_id=1, source_target_pairs={{0,16},{16,0},{1,17},{17,1},{2,18},{18,2},{3,19},{19,3},{4,20},{20... | collective-permute-start | bytes 2211848 | tf_op jit(solution)/shard_map/ppermute | solution.py:472
  126.7 21.3 %collective-permute-start.33 = (bf16[2,336,768]{2,1,0:T(8,128)(2,1)}, bf16[2,336,768]{2,1,0:T(8,128)(2,1)S(1)}, u32[]{:S(2)}, u32[]{:S(2)}) collective-permute-start(bf16[2,336,768]{2,1,0:T(8,128)(2,1)} %get-tuple-element.683.refs_1_), channel_id=1, source_target_pairs={{0,1},{1,0},{2,3},{3,2},{4,5},{5,4},{6,7},{7,6},{8,9},{9,8},{10,11... | collective-permute-start | bytes 3096584 | tf_op jit(solution)/shard_map/ppermute | solution.py:452
  127.7 24.9 %collective-permute-start.34 = (bf16[2,336,768]{2,1,0:T(8,128)(2,1)}, bf16[2,336,768]{2,1,0:T(8,128)(2,1)S(1)}, u32[]{:S(2)}, u32[]{:S(2)}) collective-permute-start(bf16[2,336,768]{2,1,0:T(8,128)(2,1)} %get-tuple-element.682.refs_0_), channel_id=1, source_target_pairs={{0,1},{1,0},{2,3},{3,2},{4,5},{5,4},{6,7},{7,6},{8,9},{9,8},{10,11... | collective-permute-start | bytes 3096584 | tf_op jit(solution)/shard_map/ppermute | solution.py:452
  128.8 19.2 %collective-permute-start.31 = (bf16[240,768]{1,0:T(8,128)(2,1)}, bf16[240,768]{1,0:T(8,128)(2,1)S(1)}, u32[]{:S(2)}, u32[]{:S(2)}) collective-permute-start(bf16[240,768]{1,0:T(8,128)(2,1)} %get-tuple-element.657.own_ref), channel_id=1, source_target_pairs={{0,4},{1,5},{2,6},{3,7},{4,8},{5,9},{6,10},{7,11},{8,12},{9,13},{1... | collective-permute-start | bytes 1105928 | tf_op jit(solution)/shard_map/ppermute | solution.py:461
  130.6 17.3 %collective-permute-start.32 = (bf16[128,768]{1,0:T(8,128)(2,1)}, bf16[128,768]{1,0:T(8,128)(2,1)S(1)}, u32[]{:S(2)}, u32[]{:S(2)}) collective-permute-start(bf16[128,768]{1,0:T(8,128)(2,1)} %get-tuple-element.635), channel_id=1, source_target_pairs={{0,8},{4,12},{8,0},{12,4},{1,9},{5,13},{9,1},{13,5},{2,10},{6,14},... | collective-permute-start | bytes 589832 | tf_op jit(solution)/shard_map/ppermute | solution.py:468
  153.7 14.7 %collective-permute-start.39 = (bf16[2,336,768]{2,1,0:T(8,128)(2,1)S(1)}, bf16[2,336,768]{2,1,0:T(8,128)(2,1)}, u32[]{:S(2)}, u32[]{:S(2)}) collective-permute-start(bf16[2,336,768]{2,1,0:T(8,128)(2,1)S(1)} %collective-permute-done.33.refs_3_), channel_id=1, source_target_pairs={{0,2},{1,3},{2,0},{3,1},{4,6},{5,7},{6,4},{7,5},{8,10},{9,11},{10,... | collective-permute-start | bytes 3096584 | tf_op jit(solution)/shard_map/ppermute | solution.py:456
  171.2 19.8 %collective-permute-start.43 = (bf16[3072,512]{1,0:T(8,128)(2,1)}, bf16[3072,512]{1,0:T(8,128)(2,1)}, u32[]{:S(2)}, u32[]{:S(2)}) collective-permute-start(bf16[3072,512]{1,0:T(8,128)(2,1)} %get-tuple-element.778.hidden_ref.own_high), channel_id=1, source_target_pairs={{0,16},{16,0},{1,17},{17,1},{2,18},{18,2},{3,19},{19,3},{4,20},{20... | collective-permute-start | bytes 9437192 | tf_op jit(solution)/shard_map/ppermute | solution.py:472
  171.4 18.5 %collective-permute-start.44 = (bf16[2,240,768]{2,1,0:T(8,128)(2,1)}, bf16[2,240,768]{2,1,0:T(8,128)(2,1)}, u32[]{:S(2)}, u32[]{:S(2)}) collective-permute-start(bf16[2,240,768]{2,1,0:T(8,128)(2,1)} %get-tuple-element.723.refs_1_), channel_id=1, source_target_pairs={{0,1},{1,0},{2,3},{3,2},{4,5},{5,4},{6,7},{7,6},{8,9},{9,8},{10,11... | collective-permute-start | bytes 2211848 | tf_op jit(solution)/shard_map/ppermute | solution.py:452
  172.3 18.7 %collective-permute-start.45 = (bf16[2,240,768]{2,1,0:T(8,128)(2,1)}, bf16[2,240,768]{2,1,0:T(8,128)(2,1)}, u32[]{:S(2)}, u32[]{:S(2)}) collective-permute-start(bf16[2,240,768]{2,1,0:T(8,128)(2,1)} %get-tuple-element.722.refs_0_), channel_id=1, source_target_pairs={{0,1},{1,0},{2,3},{3,2},{4,5},{5,4},{6,7},{7,6},{8,9},{9,8},{10,11... | collective-permute-start | bytes 2211848 | tf_op jit(solution)/shard_map/ppermute | solution.py:452
  173.4 17.7 %collective-permute-start.42 = (bf16[768,512]{1,0:T(8,128)(2,1)}, bf16[768,512]{1,0:T(8,128)(2,1)S(1)}, u32[]{:S(2)}, u32[]{:S(2)}) collective-permute-start(bf16[768,512]{1,0:T(8,128)(2,1)} %get-tuple-element.851.attended_ref.own_low), channel_id=1, source_target_pairs={{0,16},{16,0},{1,17},{17,1},{2,18},{18,2},{3,19},{19,3},{4,20},{20... | collective-permute-start | bytes 2359304 | tf_op jit(solution)/shard_map/ppermute | solution.py:472
  174.8 16.2 %collective-permute-start.46 = (bf16[512,768]{1,0:T(8,128)(2,1)}, bf16[512,768]{1,0:T(8,128)(2,1)S(1)}, u32[]{:S(2)}, u32[]{:S(2)}) collective-permute-start(bf16[512,768]{1,0:T(8,128)(2,1)} %get-tuple-element.887.normed_ref.right_ref), channel_id=1, source_target_pairs={{0,16},{16,0},{1,17},{17,1},{2,18},{18,2},{3,19},{19,3},{4,20},{20... | collective-permute-start | bytes 2359304 | tf_op jit(solution)/shard_map/ppermute | solution.py:472
  191.9 11.8 %collective-permute-start.47 = (bf16[2,240,768]{2,1,0:T(8,128)(2,1)}, bf16[2,240,768]{2,1,0:T(8,128)(2,1)}, u32[]{:S(2)}, u32[]{:S(2)}) collective-permute-start(bf16[2,240,768]{2,1,0:T(8,128)(2,1)} %collective-permute-done.44.refs_3_), channel_id=1, source_target_pairs={{0,2},{1,3},{2,0},{3,1},{4,6},{5,7},{6,4},{7,5},{8,10},{9,11},{10,... | collective-permute-start | bytes 2211848 | tf_op jit(solution)/shard_map/ppermute | solution.py:456
  193.5 10.3 %collective-permute-start.48 = (bf16[2,240,768]{2,1,0:T(8,128)(2,1)}, bf16[2,240,768]{2,1,0:T(8,128)(2,1)}, u32[]{:S(2)}, u32[]{:S(2)}) collective-permute-start(bf16[2,240,768]{2,1,0:T(8,128)(2,1)} %collective-permute-done.45.refs_2_), channel_id=1, source_target_pairs={{0,16},{16,0},{1,17},{17,1},{2,18},{18,2},{3,19},{19,3},{4,20},{20... | collective-permute-start | bytes 2211848 | tf_op jit(solution)/shard_map/ppermute | solution.py:472
  193.5 10.3 %collective-permute-start.49 = (bf16[2,240,768]{2,1,0:T(8,128)(2,1)}, bf16[2,240,768]{2,1,0:T(8,128)(2,1)}, u32[]{:S(2)}, u32[]{:S(2)}) collective-permute-start(bf16[2,240,768]{2,1,0:T(8,128)(2,1)} %collective-permute-done.44.refs_3_), channel_id=1, source_target_pairs={{0,16},{16,0},{1,17},{17,1},{2,18},{18,2},{3,19},{19,3},{4,20},{20... | collective-permute-start | bytes 2211848 | tf_op jit(solution)/shard_map/ppermute | solution.py:472
  206.3 14.4 %collective-permute-start.53 = (bf16[3072,512]{1,0:T(8,128)(2,1)}, bf16[3072,512]{1,0:T(8,128)(2,1)}, u32[]{:S(2)}, u32[]{:S(2)}) collective-permute-start(bf16[3072,512]{1,0:T(8,128)(2,1)} %get-tuple-element.925.own_high.hidden_ref), channel_id=1, source_target_pairs={{0,16},{16,0},{1,17},{17,1},{2,18},{18,2},{3,19},{19,3},{4,20},{20... | collective-permute-start | bytes 9437192 | tf_op jit(solution)/shard_map/ppermute | solution.py:472
  206.4 14.2 %collective-permute-start.54 = (bf16[512,768]{1,0:T(8,128)(2,1)S(1)}, bf16[512,768]{1,0:T(8,128)(2,1)S(1)}, u32[]{:S(2)}, u32[]{:S(2)}) collective-permute-start(bf16[512,768]{1,0:T(8,128)(2,1)S(1)} %copy-done.4), channel_id=1, source_target_pairs={{0,16},{16,0},{1,17},{17,1},{2,18},{18,2},{3,19},{19,3},{4,20},{20... | collective-permute-start | bytes 2359304 | tf_op jit(solution)/shard_map/ppermute | solution.py:472
  230.1 20.0 %collective-permute-start.56 = (bf16[2,240,768]{2,1,0:T(8,128)(2,1)}, bf16[2,240,768]{2,1,0:T(8,128)(2,1)S(1)}, u32[]{:S(2)}, u32[]{:S(2)}) collective-permute-start(bf16[2,240,768]{2,1,0:T(8,128)(2,1)} %get-tuple-element.767), channel_id=1, source_target_pairs={{0,2},{1,3},{2,0},{3,1},{4,6},{5,7},{6,4},{7,5},{8,10},{9,11},{10,... | collective-permute-start | bytes 2211848 | tf_op jit(solution)/shard_map/ppermute | solution.py:456
  231.6 18.5 %collective-permute-start.57 = (bf16[2,240,768]{2,1,0:T(8,128)(2,1)}, bf16[2,240,768]{2,1,0:T(8,128)(2,1)S(1)}, u32[]{:S(2)}, u32[]{:S(2)}) collective-permute-start(bf16[2,240,768]{2,1,0:T(8,128)(2,1)} %get-tuple-element.769), channel_id=1, source_target_pairs={{0,1},{1,0},{2,3},{3,2},{4,5},{5,4},{6,7},{7,6},{8,9},{9,8},{10,11... | collective-permute-start | bytes 2211848 | tf_op jit(solution)/shard_map/ppermute | solution.py:452
  250.2 33.6 %collective-permute-start.63 = (bf16[2304,512]{1,0:T(8,128)(2,1)}, bf16[2304,512]{1,0:T(8,128)(2,1)}, u32[]{:S(2)}, u32[]{:S(2)}) collective-permute-start(bf16[2304,512]{1,0:T(8,128)(2,1)} %bitcast.74), channel_id=1, source_target_pairs={{0,16},{16,0},{1,17},{17,1},{2,18},{18,2},{3,19},{19,3},{4,20},{20... | collective-permute-start | bytes 7077896 | tf_op jit(solution)/shard_map/ppermute | solution.py:472
  253.0 11.5 %collective-permute-start.59 = (bf16[2,240,768]{2,1,0:T(8,128)(2,1)S(1)}, bf16[2,240,768]{2,1,0:T(8,128)(2,1)S(1)}, u32[]{:S(2)}, u32[]{:S(2)}) collective-permute-start(bf16[2,240,768]{2,1,0:T(8,128)(2,1)S(1)} %add_convert_fusion.3), channel_id=1, source_target_pairs={{0,1},{1,0},{2,3},{3,2},{4,5},{5,4},{6,7},{7,6},{8,9},{9,8},{10,11... | collective-permute-start | bytes 2211848 | tf_op jit(solution)/shard_map/ppermute | solution.py:452
  254.1 10.4 %collective-permute-start.60 = (bf16[2,240,768]{2,1,0:T(8,128)(2,1)S(1)}, bf16[2,240,768]{2,1,0:T(8,128)(2,1)S(1)}, u32[]{:S(2)}, u32[]{:S(2)}) collective-permute-start(bf16[2,240,768]{2,1,0:T(8,128)(2,1)S(1)} %collective-permute-done.57.keep_ref), channel_id=1, source_target_pairs={{0,16},{16,0},{1,17},{17,1},{2,18},{18,2},{3,19},{19,3},{4,20},{20... | collective-permute-start | bytes 2211848 | tf_op jit(solution)/shard_map/ppermute | solution.py:472
  265.6 18.2 %collective-permute-start.61 = (bf16[2,240,768]{2,1,0:T(8,128)(2,1)}, bf16[2,240,768]{2,1,0:T(8,128)(2,1)S(1)}, u32[]{:S(2)}, u32[]{:S(2)}) collective-permute-start(bf16[2,240,768]{2,1,0:T(8,128)(2,1)} %get-tuple-element.794), channel_id=1, source_target_pairs={{0,1},{1,0},{2,3},{3,2},{4,5},{5,4},{6,7},{7,6},{8,9},{9,8},{10,11... | collective-permute-start | bytes 2211848 | tf_op jit(solution)/shard_map/ppermute | solution.py:452
  266.7 17.1 %collective-permute-start.62 = (bf16[2,240,768]{2,1,0:T(8,128)(2,1)}, bf16[2,240,768]{2,1,0:T(8,128)(2,1)S(1)}, u32[]{:S(2)}, u32[]{:S(2)}) collective-permute-start(bf16[2,240,768]{2,1,0:T(8,128)(2,1)} %get-tuple-element.796), channel_id=1, source_target_pairs={{0,2},{1,3},{2,0},{3,1},{4,6},{5,7},{6,4},{7,5},{8,10},{9,11},{10,... | collective-permute-start | bytes 2211848 | tf_op jit(solution)/shard_map/ppermute | solution.py:456
  267.0 16.8 %collective-permute-start.64 = (bf16[2,240,768]{2,1,0:T(8,128)(2,1)}, bf16[2,240,768]{2,1,0:T(8,128)(2,1)S(1)}, u32[]{:S(2)}, u32[]{:S(2)}) collective-permute-start(bf16[2,240,768]{2,1,0:T(8,128)(2,1)} %copy-done.44), channel_id=1, source_target_pairs={{0,16},{16,0},{1,17},{17,1},{2,18},{18,2},{3,19},{19,3},{4,20},{20... | collective-permute-start | bytes 2211848 | tf_op jit(solution)/shard_map/ppermute | solution.py:472
  284.1 14.3 %collective-permute-start.67 = (bf16[3072,512]{1,0:T(8,128)(2,1)}, bf16[3072,512]{1,0:T(8,128)(2,1)}, u32[]{:S(2)}, u32[]{:S(2)}) collective-permute-start(bf16[3072,512]{1,0:T(8,128)(2,1)} %get-tuple-element.884.own_high), channel_id=1, source_target_pairs={{0,16},{16,0},{1,17},{17,1},{2,18},{18,2},{3,19},{19,3},{4,20},{20... | collective-permute-start | bytes 9437192 | tf_op jit(solution)/shard_map/ppermute | solution.py:472
  284.1 14.2 %collective-permute-start.65 = (bf16[2,240,768]{2,1,0:T(8,128)(2,1)S(1)}, bf16[2,240,768]{2,1,0:T(8,128)(2,1)}, u32[]{:S(2)}, u32[]{:S(2)}) collective-permute-start(bf16[2,240,768]{2,1,0:T(8,128)(2,1)S(1)} %add_convert_fusion.2), channel_id=1, source_target_pairs={{0,1},{1,0},{2,3},{3,2},{4,5},{5,4},{6,7},{7,6},{8,9},{9,8},{10,11... | collective-permute-start | bytes 2211848 | tf_op jit(solution)/shard_map/ppermute | solution.py:452
  285.0 13.3 %collective-permute-start.66 = (bf16[2,240,768]{2,1,0:T(8,128)(2,1)S(1)}, bf16[2,240,768]{2,1,0:T(8,128)(2,1)S(1)}, u32[]{:S(2)}, u32[]{:S(2)}) collective-permute-start(bf16[2,240,768]{2,1,0:T(8,128)(2,1)S(1)} %collective-permute-done.61.keep_ref), channel_id=1, source_target_pairs={{0,16},{16,0},{1,17},{17,1},{2,18},{18,2},{3,19},{19,3},{4,20},{20... | collective-permute-start | bytes 2211848 | tf_op jit(solution)/shard_map/ppermute | solution.py:472
  299.2 26.1 %collective-permute-start.68 = (bf16[2,240,768]{2,1,0:T(8,128)(2,1)}, bf16[2,240,768]{2,1,0:T(8,128)(2,1)S(1)}, u32[]{:S(2)}, u32[]{:S(2)}) collective-permute-start(bf16[2,240,768]{2,1,0:T(8,128)(2,1)} %collective-permute-done.65.pass_ref), channel_id=1, source_target_pairs={{0,16},{16,0},{1,17},{17,1},{2,18},{18,2},{3,19},{19,3},{4,20},{20... | collective-permute-start | bytes 2211848 | tf_op jit(solution)/shard_map/ppermute | solution.py:472
  299.2 26.2 %collective-permute-start.69 = (bf16[2,336,768]{2,1,0:T(8,128)(2,1)}, bf16[2,336,768]{2,1,0:T(8,128)(2,1)S(1)}, u32[]{:S(2)}, u32[]{:S(2)}) collective-permute-start(bf16[2,336,768]{2,1,0:T(8,128)(2,1)} %get-tuple-element.840), channel_id=1, source_target_pairs={{0,2},{1,3},{2,0},{3,1},{4,6},{5,7},{6,4},{7,5},{8,10},{9,11},{10,... | collective-permute-start | bytes 3096584 | tf_op jit(solution)/shard_map/ppermute | solution.py:456
  302.0 23.4 %collective-permute-start.70 = (bf16[2,336,768]{2,1,0:T(8,128)(2,1)}, bf16[2,336,768]{2,1,0:T(8,128)(2,1)S(1)}, u32[]{:S(2)}, u32[]{:S(2)}) collective-permute-start(bf16[2,336,768]{2,1,0:T(8,128)(2,1)} %get-tuple-element.861), channel_id=1, source_target_pairs={{0,1},{1,0},{2,3},{3,2},{4,5},{5,4},{6,7},{7,6},{8,9},{9,8},{10,11... | collective-permute-start | bytes 3096584 | tf_op jit(solution)/shard_map/ppermute | solution.py:452
  303.0 22.3 %collective-permute-start.71 = (bf16[240,768]{1,0:T(8,128)(2,1)}, bf16[240,768]{1,0:T(8,128)(2,1)S(1)}, u32[]{:S(2)}, u32[]{:S(2)}) collective-permute-start(bf16[240,768]{1,0:T(8,128)(2,1)} %get-tuple-element.863), channel_id=1, source_target_pairs={{0,4},{1,5},{2,6},{3,7},{4,8},{5,9},{6,10},{7,11},{8,12},{9,13},{1... | collective-permute-start | bytes 1105928 | tf_op jit(solution)/shard_map/ppermute | solution.py:461
  304.2 21.1 %collective-permute-start.72 = (bf16[128,768]{1,0:T(8,128)(2,1)}, bf16[128,768]{1,0:T(8,128)(2,1)S(1)}, u32[]{:S(2)}, u32[]{:S(2)}) collective-permute-start(bf16[128,768]{1,0:T(8,128)(2,1)} %get-tuple-element.865), channel_id=1, source_target_pairs={{0,8},{4,12},{8,0},{12,4},{1,9},{5,13},{9,1},{13,5},{2,10},{6,14},... | collective-permute-start | bytes 589832 | tf_op jit(solution)/shard_map/ppermute | solution.py:468
  331.0 19.2 %collective-permute-start.76 = (bf16[2,336,768]{2,1,0:T(8,128)(2,1)S(1)}, bf16[2,336,768]{2,1,0:T(8,128)(2,1)S(1)}, u32[]{:S(2)}, u32[]{:S(2)}) collective-permute-start(bf16[2,336,768]{2,1,0:T(8,128)(2,1)S(1)} %add_convert_fusion.1), channel_id=1, source_target_pairs={{0,1},{1,0},{2,3},{3,2},{4,5},{5,4},{6,7},{7,6},{8,9},{9,8},{10,11... | collective-permute-start | bytes 3096584 | tf_op jit(solution)/shard_map/ppermute | solution.py:452
  332.2 18.0 %collective-permute-start.77 = (bf16[2,336,768]{2,1,0:T(8,128)(2,1)S(1)}, bf16[2,336,768]{2,1,0:T(8,128)(2,1)S(1)}, u32[]{:S(2)}, u32[]{:S(2)}) collective-permute-start(bf16[2,336,768]{2,1,0:T(8,128)(2,1)S(1)} %collective-permute-done.70.keep_ref), channel_id=1, source_target_pairs={{0,16},{16,0},{1,17},{17,1},{2,18},{18,2},{3,19},{19,3},{4,20},{20... | collective-permute-start | bytes 3096584 | tf_op jit(solution)/shard_map/ppermute | solution.py:472
  332.4 17.8 %collective-permute-start.74 = (bf16[240,768]{1,0:T(8,128)(2,1)}, bf16[240,768]{1,0:T(8,128)(2,1)}, u32[]{:S(2)}, u32[]{:S(2)}) collective-permute-start(bf16[240,768]{1,0:T(8,128)(2,1)} %get-tuple-element.880), channel_id=1, source_target_pairs={{0,4},{1,5},{2,6},{3,7},{4,8},{5,9},{6,10},{7,11},{8,12},{9,13},{1... | collective-permute-start | bytes 1105928 | tf_op jit(solution)/shard_map/ppermute | solution.py:461
  332.5 17.7 %collective-permute-start.75 = (bf16[128,768]{1,0:T(8,128)(2,1)}, bf16[128,768]{1,0:T(8,128)(2,1)}, u32[]{:S(2)}, u32[]{:S(2)}) collective-permute-start(bf16[128,768]{1,0:T(8,128)(2,1)} %get-tuple-element.882), channel_id=1, source_target_pairs={{0,8},{4,12},{8,0},{12,4},{1,9},{5,13},{9,1},{13,5},{2,10},{6,14},... | collective-permute-start | bytes 589832 | tf_op jit(solution)/shard_map/ppermute | solution.py:468
  335.9 14.3 %collective-permute-start.78 = (bf16[128,768]{1,0:T(8,128)(2,1)}, bf16[128,768]{1,0:T(8,128)(2,1)}, u32[]{:S(2)}, u32[]{:S(2)}) collective-permute-start(bf16[128,768]{1,0:T(8,128)(2,1)} %get-tuple-element.984.own_ref), channel_id=1, source_target_pairs={{0,16},{16,0},{1,17},{17,1},{2,18},{18,2},{3,19},{19,3},{4,20},{20... | collective-permute-start | bytes 589832 | tf_op jit(solution)/shard_map/ppermute | solution.py:472
  360.3 25.4 %collective-permute-start.82 = (bf16[2,336,768]{2,1,0:T(8,128)(2,1)}, bf16[2,336,768]{2,1,0:T(8,128)(2,1)S(1)}, u32[]{:S(2)}, u32[]{:S(2)}) collective-permute-start(bf16[2,336,768]{2,1,0:T(8,128)(2,1)} %get-tuple-element.917), channel_id=1, source_target_pairs={{0,2},{1,3},{2,0},{3,1},{4,6},{5,7},{6,4},{7,5},{8,10},{9,11},{10,... | collective-permute-start | bytes 3096584 | tf_op jit(solution)/shard_map/ppermute | solution.py:456
  360.9 24.8 %collective-permute-start.83 = (bf16[2,336,768]{2,1,0:T(8,128)(2,1)}, bf16[2,336,768]{2,1,0:T(8,128)(2,1)}, u32[]{:S(2)}, u32[]{:S(2)}) collective-permute-start(bf16[2,336,768]{2,1,0:T(8,128)(2,1)} %get-tuple-element.935), channel_id=1, source_target_pairs={{0,1},{1,0},{2,3},{3,2},{4,5},{5,4},{6,7},{7,6},{8,9},{9,8},{10,11... | collective-permute-start | bytes 3096584 | tf_op jit(solution)/shard_map/ppermute | solution.py:452
  362.4 22.9 %collective-permute-start.84 = (bf16[336,768]{1,0:T(8,128)(2,1)}, bf16[336,768]{1,0:T(8,128)(2,1)}, u32[]{:S(2)}, u32[]{:S(2)}) collective-permute-start(bf16[336,768]{1,0:T(8,128)(2,1)} %get-tuple-element.936), channel_id=1, source_target_pairs={{0,4},{1,5},{2,6},{3,7},{4,8},{5,9},{6,10},{7,11},{8,12},{9,13},{1... | collective-permute-start | bytes 1548296 | tf_op jit(solution)/shard_map/ppermute | solution.py:461
  362.9 22.4 %collective-permute-start.85 = (bf16[176,768]{1,0:T(8,128)(2,1)}, bf16[176,768]{1,0:T(8,128)(2,1)}, u32[]{:S(2)}, u32[]{:S(2)}) collective-permute-start(bf16[176,768]{1,0:T(8,128)(2,1)} %get-tuple-element.938), channel_id=1, source_target_pairs={{0,8},{4,12},{8,0},{12,4},{1,9},{5,13},{9,1},{13,5},{2,10},{6,14},... | collective-permute-start | bytes 811016 | tf_op jit(solution)/shard_map/ppermute | solution.py:468
  366.3 19.0 %collective-permute-start.87 = (bf16[512,768]{1,0:T(8,128)(2,1)S(1)}, bf16[512,768]{1,0:T(8,128)(2,1)}, u32[]{:S(2)}, u32[]{:S(2)}) collective-permute-start(bf16[512,768]{1,0:T(8,128)(2,1)S(1)} %copy-done.11), channel_id=1, source_target_pairs={{0,16},{16,0},{1,17},{17,1},{2,18},{18,2},{3,19},{19,3},{4,20},{20... | collective-permute-start | bytes 2359304 | tf_op jit(solution)/shard_map/ppermute | solution.py:472
  385.9 14.9 %collective-permute-start.90 = (bf16[2,336,768]{2,1,0:T(8,128)(2,1)S(1)}, bf16[2,336,768]{2,1,0:T(8,128)(2,1)S(1)}, u32[]{:S(2)}, u32[]{:S(2)}) collective-permute-start(bf16[2,336,768]{2,1,0:T(8,128)(2,1)S(1)} %add_convert_fusion), channel_id=1, source_target_pairs={{0,1},{1,0},{2,3},{3,2},{4,5},{5,4},{6,7},{7,6},{8,9},{9,8},{10,11... | collective-permute-start | bytes 3096584 | tf_op jit(solution)/shard_map/ppermute | solution.py:452
  386.8 14.0 %collective-permute-start.91 = (bf16[2,336,768]{2,1,0:T(8,128)(2,1)}, bf16[2,336,768]{2,1,0:T(8,128)(2,1)}, u32[]{:S(2)}, u32[]{:S(2)}) collective-permute-start(bf16[2,336,768]{2,1,0:T(8,128)(2,1)} %collective-permute-done.83.keep_ref), channel_id=1, source_target_pairs={{0,16},{16,0},{1,17},{17,1},{2,18},{18,2},{3,19},{19,3},{4,20},{20... | collective-permute-start | bytes 3096584 | tf_op jit(solution)/shard_map/ppermute | solution.py:472
  388.1 12.7 %collective-permute-start.88 = (bf16[240,768]{1,0:T(8,128)(2,1)}, bf16[240,768]{1,0:T(8,128)(2,1)S(1)}, u32[]{:S(2)}, u32[]{:S(2)}) collective-permute-start(bf16[240,768]{1,0:T(8,128)(2,1)} %collective-permute-done.74.near_ref), channel_id=1, source_target_pairs={{0,16},{16,0},{1,17},{17,1},{2,18},{18,2},{3,19},{19,3},{4,20},{20... | collective-permute-start | bytes 1105928 | tf_op jit(solution)/shard_map/ppermute | solution.py:472
  388.1 12.7 %collective-permute-start.89 = (bf16[128,768]{1,0:T(8,128)(2,1)}, bf16[128,768]{1,0:T(8,128)(2,1)S(1)}, u32[]{:S(2)}, u32[]{:S(2)}) collective-permute-start(bf16[128,768]{1,0:T(8,128)(2,1)} %collective-permute-done.75.far_ref), channel_id=1, source_target_pairs={{0,16},{16,0},{1,17},{17,1},{2,18},{18,2},{3,19},{19,3},{4,20},{20... | collective-permute-start | bytes 589832 | tf_op jit(solution)/shard_map/ppermute | solution.py:472
  388.6 12.2 %collective-permute-start.92 = (f32[16,128]{1,0:T(8,128)S(1)}, f32[16,128]{1,0:T(8,128)S(1)}, u32[]{:S(2)}, u32[]{:S(2)}) collective-permute-start(f32[16,128]{1,0:T(8,128)S(1)} %pad_bitcast_fusion), channel_id=1, source_target_pairs={{0,1},{1,0},{2,3},{3,2},{4,5},{5,4},{6,7},{7,6},{8,9},{9,8},{10,11... | collective-permute-start | bytes 24584 | tf_op jit(solution)/shard_map/ppermute | solution.py:898
  409.6 23.6 %collective-permute-start.99 = (bf16[336,768]{1,0:T(8,128)(2,1)}, bf16[336,768]{1,0:T(8,128)(2,1)}, u32[]{:S(2)}, u32[]{:S(2)}) collective-permute-start(bf16[336,768]{1,0:T(8,128)(2,1)} %get-tuple-element.1001), channel_id=1, source_target_pairs={{0,4},{1,5},{2,6},{3,7},{4,8},{5,9},{6,10},{7,11},{8,12},{9,13},{1... | collective-permute-start | bytes 1548296 | tf_op jit(solution)/shard_map/ppermute | solution.py:461
  411.1 22.1 %collective-permute-start.100 = (bf16[176,768]{1,0:T(8,128)(2,1)}, bf16[176,768]{1,0:T(8,128)(2,1)}, u32[]{:S(2)}, u32[]{:S(2)}) collective-permute-start(bf16[176,768]{1,0:T(8,128)(2,1)} %get-tuple-element.1003), channel_id=1, source_target_pairs={{0,8},{4,12},{8,0},{12,4},{1,9},{5,13},{9,1},{13,5},{2,10},{6,14},... | collective-permute-start | bytes 811016 | tf_op jit(solution)/shard_map/ppermute | solution.py:468
  414.5 13.2 %collective-permute-start.101 = (f32[16,128]{1,0:T(8,128)S(1)}, f32[16,128]{1,0:T(8,128)S(1)}, u32[]{:S(2)}, u32[]{:S(2)}) collective-permute-start(f32[16,128]{1,0:T(8,128)S(1)} %add.99), channel_id=1, source_target_pairs={{0,4},{4,0},{8,12},{12,8},{1,5},{5,1},{9,13},{13,9},{2,6},{6,2},{1... | collective-permute-start | bytes 24584 | tf_op jit(solution)/shard_map/ppermute | solution.py:921
  414.5 18.7 %collective-permute-start.102 = (bf16[176,768]{1,0:T(8,128)(2,1)}, bf16[176,768]{1,0:T(8,128)(2,1)}, u32[]{:S(2)}, u32[]{:S(2)}) collective-permute-start(bf16[176,768]{1,0:T(8,128)(2,1)} %get-tuple-element.1018.own_ref), channel_id=1, source_target_pairs={{0,16},{16,0},{1,17},{17,1},{2,18},{18,2},{3,19},{19,3},{4,20},{20... | collective-permute-start | bytes 811016 | tf_op jit(solution)/shard_map/ppermute | solution.py:472
  (120 other events, 951.4 us)
